TPU v7x, 32 devices: a whole 2x2x4 slice. The times are simulated.
32 devices in a mesh: wide: 16 (over z, x, core), narrow: 2 (over y).
Axes of the slice: x: 2, y: 2, z: 4, core: 2. Of those that a mesh axis runs over, the one named last changes fastest.
Arguments:
- features: float32 [32768, 1024], P(('wide', 'narrow')), may hold values from -6 to 6
- sketch: float32 [1024, 256], replicated, may hold values from -0.1875 to 0.1875
Outputs:
- basis: float32 [32768, 256], P(('wide', 'narrow'))
- factor: float32 [256, 256], replicated
- projection: float32 [256, 1024], replicated
All inputs are finite; a program needn't handle non-finite values.
Results may differ from a plain program's by a relative error of at most 0.000073.
Values sent between devices are 32-bit elements; how exact they have to be, the bound alone decides.
No kernel may reach another device: no remote copies, remote signals or barrier semaphores. Data moves between devices by JAX's collectives and lax.ppermute only.
A program may use at most 64 MiB of HBM per device.

v0:
```python
import jax
import jax.numpy as jnp
from jax import lax
from jax.sharding import PartitionSpec as P


def partner_2(value, axis, bit):
    mask = 2**bit
    pairs = [(source, source ^ mask) for source in range(lax.axis_size(axis))]
    return lax.ppermute(value, axis, pairs)


def per_device(features, sketch):
    high = lax.Precision.HIGHEST
    sampled = jnp.dot(features, sketch, preferred_element_type=jnp.float32, precision=high)
    gram = jnp.dot(sampled.T, sampled, preferred_element_type=jnp.float32, precision=high)
    for level in range(lax.axis_size("narrow").bit_length() - 1):
        partner = partner_2(gram, "narrow", level)
        gram = gram + partner
    for level in range(lax.axis_size("wide").bit_length() - 1):
        partner = partner_2(gram, "wide", level)
        gram = gram + partner
    upper = jnp.linalg.cholesky(gram).T
    ortho_t = lax.linalg.triangular_solve(upper.T, sampled.T, left_side=True, lower=True)
    term = jnp.dot(ortho_t, features, preferred_element_type=jnp.float32, precision=high)
    summed = lax.psum(term, ("wide", "narrow"))
    count = features.shape[0] * lax.axis_size("wide") * lax.axis_size("narrow")
    scale = jnp.sqrt(jnp.float32(count))
    return (ortho_t.T * scale, upper / scale, summed)


def solution(mesh):
    in_specs = (P(("wide", "narrow"), None), P())
    out_specs = (P(("wide", "narrow"), None), P(), P())
    return jax.shard_map(
        per_device, mesh=mesh, in_specs=in_specs, out_specs=out_specs, check_vma=False
    )
```

profile of v0, /device:TPU:0, one launch (start us, length us, event | category | flops | bytes accessed | tf_op | source)
XLA Modules:
  0.0 265.3 jit_solution(13186971820106907901)
XLA Ops:
  7.2 0.0 copy-start
  7.2 0.0 all-reduce.3.cloned.1.call-start
  7.2 1.2 copy-done
  8.4 5.2 %fusion.12 = f32[1024,256]{1,0:T(8,128)S(1)} fusion(f32[1024,1024]{1,0:T(8,128)} %param.2, f32[1024,256]{1,0:T(8,128)S(1)} %copy-done), kind=kOutput, calls=%fused_computation.34 | convolution fusion | flops 3221225472 | bytes 6291456 | tf_op jit(solution)/shard_map/dot_general | solution.py:15
  13.6 1.8 fusion.13
  15.5 3.0 %collective-permute-start = (f32[256,256]{0,1:T(8,128)S(1)}, f32[256,256]{0,1:T(8,128)S(1)}, u32[]{:S(2)}, u32[]{:S(2)}) collective-permute-start(f32[256,256]{0,1:T(8,128)S(1)} %fusion.13), channel_id=1, source_target_pairs={{0,1},{1,0},{2,3},{3,2},{4,5},{5,4},{6,7},{7,6},{8,9},{9,8},{10,11... | collective-permute-start | bytes 786440 | tf_op jit(solution)/shard_map/ppermute | solution.py:10
  18.5 6.3 %collective-permute-done = f32[256,256]{0,1:T(8,128)S(1)} collective-permute-done((f32[256,256]{0,1:T(8,128)S(1)}, f32[256,256]{0,1:T(8,128)S(1)}, u32[]{:S(2)}, u32[]{:S(2)}) %collective-permute-start) | collective-permute-done | bytes 262176 | tf_op jit(solution)/shard_map/ppermute | solution.py:10
  24.8 0.1 collective-permute-start.1
  24.9 1.5 collective-permute-done.1
  26.5 1.8 collective-permute-start.2
  28.2 6.6 %collective-permute-done.2 = f32[256,256]{0,1:T(8,128)S(1)} collective-permute-done((f32[256,256]{0,1:T(8,128)S(1)}, f32[256,256]{0,1:T(8,128)S(1)}, u32[]{:S(2)}, u32[]{:S(2)}) %collective-permute-start.2) | collective-permute-done | bytes 262176 | tf_op jit(solution)/shard_map/ppermute | solution.py:10
  34.9 1.9 collective-permute-start.3
  36.8 5.8 %collective-permute-done.3 = f32[256,256]{0,1:T(8,128)S(1)} collective-permute-done((f32[256,256]{0,1:T(8,128)S(1)}, f32[256,256]{0,1:T(8,128)S(1)}, u32[]{:S(2)}, u32[]{:S(2)}) %collective-permute-start.3) | collective-permute-done | bytes 262176 | tf_op jit(solution)/shard_map/ppermute | solution.py:10
  42.6 2.8 %collective-permute-start.4 = (f32[256,256]{0,1:T(8,128)S(1)}, f32[256,256]{0,1:T(8,128)S(1)}, u32[]{:S(2)}, u32[]{:S(2)}) collective-permute-start(f32[256,256]{0,1:T(8,128)S(1)} %add.42), channel_id=1, source_target_pairs={{0,16},{2,18},{4,20},{6,22},{8,24},{10,26},{12,28},{14,30},{16,0},... | collective-permute-start | bytes 786440 | tf_op jit(solution)/shard_map/ppermute | solution.py:10
  45.4 10.5 %collective-permute-done.4 = f32[256,256]{0,1:T(8,128)S(1)} collective-permute-done((f32[256,256]{0,1:T(8,128)S(1)}, f32[256,256]{0,1:T(8,128)S(1)}, u32[]{:S(2)}, u32[]{:S(2)}) %collective-permute-start.4) | collective-permute-done | bytes 262176 | tf_op jit(solution)/shard_map/ppermute | solution.py:10
  55.9 0.1 copy.7
  56.1 11.7 %cholesky.50 = f32[128,128]{1,0:T(8,128)S(1)} custom-call(f32[128,128]{1,0:T(8,128)S(1)} %cholesky.118), custom_call_target="Cholesky" | custom-call | tf_op jit(solution)/shard_map/jit(cholesky)/cholesky | solution.py:23
  67.9 9.8 %custom-call.14 = f32[1,128,128]{1,2,0:T(8,128)S(1)} custom-call(f32[1,128,128]{2,1,0:T(8,128)S(1)} %get-tuple-element.29), custom_call_target="InvertDiagBlocksLowerTriangular" | custom-call | tf_op jit(solution)/shard_map/jit(cholesky)/cholesky | solution.py:23
  77.7 0.2 constant_dynamic-update-slice_fusion.1
  77.9 0.3 slice_subtract_fusion
  78.2 11.8 %cholesky.105 = f32[128,128]{1,0:T(8,128)S(1)} custom-call(f32[128,128]{1,0:T(8,128)S(1)} %slice_subtract_fusion), custom_call_target="Cholesky" | custom-call | tf_op jit(solution)/shard_map/jit(cholesky)/cholesky | solution.py:23
  90.1 0.6 compare_reduce_fusion
  92.0 0.1 triangular_solve.57
  92.1 4.0 %while.1 = (s32[]{:T(128)}, f32[256,256]{1,0:T(8,128)S(1)}, s32[2,2]{1,0:T(2,128)S(1)}, f32[2,128,128]{2,1,0:T(8,128)S(1)}, s32[]{:T(128)}) while((s32[]{:T(128)}, f32[256,256]{1,0:T(8,128)S(1)}, s32[2,2]{1,0:T(2,128)S(1)}, f32[2,128,128]{2,1,0:T(8,128)S(1)}, s32[]{:T(128)}) %tuple.29), condition=%wide.while_cond, body=%wide.while_body.sunk | while | flops 2 | bytes 131189 | solution.py:24
  92.1 0.6 fusion.24
  92.7 1.4 bitcast_dynamic-update-slice_fusion.2
  94.1 0.6 fusion.24
  94.7 1.4 bitcast_dynamic-update-slice_fusion.2
  96.1 19.7 %custom-call.15 = f32[2,128,128]{1,2,0:T(8,128)S(1)} custom-call(f32[2,128,128]{2,1,0:T(8,128)S(1)} %get-tuple-element.10), custom_call_target="InvertDiagBlocksLowerTriangular" | custom-call | tf_op jit(solution)/shard_map/triangular_solve | solution.py:24
  115.8 0.6 fusion.1
  116.4 1.0 convolution_subtract_fusion
  117.4 0.6 fusion.6
  118.1 6.9 %fusion = f32[256,1024]{1,0:T(8,128)} fusion(f32[1024,1024]{1,0:T(8,128)} %param.2, f32[128,1024]{1,0:T(8,128)S(1)} %fusion.6, f32[128,1024]{1,0:T(8,128)S(1)} %fusion.1), kind=kOutput, calls=%fused_computation.5 | convolution fusion | flops 3221487616 | bytes 6291456 | tf_op jit(solution)/shard_map/dot_general | solution.py:25
  125.0 0.0 all-reduce.3.cloned.1.call-update
  125.0 0.8 copy.9
  125.8 1.1 multiply_bitcast_fusion
  126.9 2.5 copy.8
  129.5 126.7 %all-reduce.3.cloned.1.call-done = f32[256,1024]{1,0:T(8,128)} async-done(((f32[256,1024]{1,0:T(8,128)}), f32[256,1024]{1,0:T(8,128)}) %all-reduce.3.cloned.1.call-update) | async-done | bytes 1048592 | tf_op jit(solution)/shard_map/psum | solution.py:26
  256.2 2.3 copy.23
  (15 shorter events, 0.4 us)
Async XLA Ops:
  7.2 1.2 copy-start
  7.2 249.0 %all-reduce.3.cloned.1.call-start = ((), (), s32[]{:S(2)}) async-start(), calls=%async_computation | async-start | bytes 2097152 | tf_op jit(solution)/shard_map/psum | solution.py:26
  15.5 9.3 %collective-permute-start = (f32[256,256]{0,1:T(8,128)S(1)}, f32[256,256]{0,1:T(8,128)S(1)}, u32[]{:S(2)}, u32[]{:S(2)}) collective-permute-start(f32[256,256]{0,1:T(8,128)S(1)} %fusion.13), channel_id=1, source_target_pairs={{0,1},{1,0},{2,3},{3,2},{4,5},{5,4},{6,7},{7,6},{8,9},{9,8},{10,11... | collective-permute-start | bytes 786440 | tf_op jit(solution)/shard_map/ppermute | solution.py:10
  24.8 1.6 collective-permute-start.1
  26.5 8.4 %collective-permute-start.2 = (f32[256,256]{0,1:T(8,128)S(1)}, f32[256,256]{0,1:T(8,128)S(1)}, u32[]{:S(2)}, u32[]{:S(2)}) collective-permute-start(f32[256,256]{0,1:T(8,128)S(1)} %add.40), channel_id=1, source_target_pairs={{0,4},{2,6},{4,0},{6,2},{8,12},{10,14},{12,8},{14,10},{16,20},{18,... | collective-permute-start | bytes 786440 | tf_op jit(solution)/shard_map/ppermute | solution.py:10
  34.9 7.7 %collective-permute-start.3 = (f32[256,256]{0,1:T(8,128)S(1)}, f32[256,256]{0,1:T(8,128)S(1)}, u32[]{:S(2)}, u32[]{:S(2)}) collective-permute-start(f32[256,256]{0,1:T(8,128)S(1)} %add.41), channel_id=1, source_target_pairs={{0,8},{2,10},{4,12},{6,14},{8,0},{10,2},{12,4},{14,6},{16,24},{18,... | collective-permute-start | bytes 786440 | tf_op jit(solution)/shard_map/ppermute | solution.py:10
  42.6 13.3 %collective-permute-start.4 = (f32[256,256]{0,1:T(8,128)S(1)}, f32[256,256]{0,1:T(8,128)S(1)}, u32[]{:S(2)}, u32[]{:S(2)}) collective-permute-start(f32[256,256]{0,1:T(8,128)S(1)} %add.42), channel_id=1, source_target_pairs={{0,16},{2,18},{4,20},{6,22},{8,24},{10,26},{12,28},{14,30},{16,0},... | collective-permute-start | bytes 786440 | tf_op jit(solution)/shard_map/ppermute | solution.py:10
Sparse Core Ops, SparseCore 0:
  125.1 131.0 all-reduce.2
where the time goes:
time: 266 us; the launch traced here: 265 us
  waiting for transfers between devices  157 us (59%)
  other arithmetic  55.1 us (21%)
  matrix products  16.7 us (6%)
  between operations  15.5 us (6%)
  local copies, waits for them, and re-layouts  11 us (4%)
  starting transfers between devices  9.6 us (4%)
    psum x1, waiting for transfers between devices, per_device(): summed = lax.psum(term, ('wide', 'narrow'))  127 us
    another operation x6, other arithmetic, per_device(): upper = jnp.linalg.cholesky(gram).T  34.1 us
    ppermute x5, waiting for transfers between devices, partner_2(): return lax.ppermute(value, axis, pairs)  30.7 us
    another operation x2, other arithmetic, per_device(): lax.linalg.triangular_solve(upper.T, sampled.T, left_side=True, lower=True)  19.7 us
    ppermute x5, starting transfers between devices, partner_2(): return lax.ppermute(value, axis, pairs)  9.56 us
    dot_general x1, matrix products, per_device(): jnp.dot(ortho_t, features, preferred_element_type=jnp.float32, precision=...  6.88 us
    unnamed x5, local copies, waits for them, and re-layouts  6.85 us
  transfers between devices with their start and end apart: 6, of which 6 were waited for; matrix products, arithmetic and copies ran while one was open for 2% of the time, Pallas kernels for 0%

commit v1 on v0

v1 whole, which is shorter than its diff:
```python
import jax, jax.numpy as jnp
from jax import lax
from jax.experimental import pallas as pl
from jax.experimental.pallas import tpu as pltpu
from jax.sharding import PartitionSpec as P

GROUP = 8
LANES = 128
PANEL = 64


def factor_panel(a_ref, upper_ref, base, height, size):
    lane = lax.broadcasted_iota(jnp.int32, (GROUP, LANES), 1)
    sub = lax.broadcasted_iota(jnp.int32, (GROUP, LANES), 0)
    tiles = size // LANES
    for top in range(base, base + height, GROUP):
        groups = list(range(top, base + height, GROUP))
        home = top // LANES
        offset = top - home * LANES
        inside = (lane >= offset) & (lane < offset + GROUP)
        rows = {}
        for g in groups:
            for t in range(tiles):
                rows[g, t] = a_ref[g:g + GROUP, t * LANES:(t + 1) * LANES]
        diag = rows[top, home]
        col = {}
        for g in groups:
            for j in range(GROUP):
                at = rows[g, home][:, offset + j:offset + j + 1]
                col[g, j] = jnp.broadcast_to(at, (GROUP, LANES))
        one = {}
        for j in range(GROUP):
            for k in range(j, GROUP):
                one[k, j] = jnp.broadcast_to(col[top, j][k:k + 1, :], (GROUP, LANES))
        for g in groups:
            fresh = jnp.where(lane == sub + offset, 1.0, 0.0) if g == top else 0.0
            rows[g, home] = jnp.where(inside, fresh, rows[g, home])
        for j in range(GROUP):
            inv = lax.rsqrt(one[j, j])
            low = {k: one[k, j] * inv for k in range(j + 1, GROUP)}
            for k in range(j + 1, GROUP):
                for m in range(k, GROUP):
                    one[m, k] = one[m, k] - low[m] * low[k]
            scaled = {g: col[g, j] * inv for g in groups}
            for k in range(j + 1, GROUP):
                for g in groups:
                    col[g, k] = col[g, k] - scaled[g] * low[k]
            pivot = {t: jnp.broadcast_to(rows[top, t][j:j + 1, :], (GROUP, LANES)) * inv for t in range(tiles)}
            pivot_diag = jnp.broadcast_to(diag[j:j + 1, :], (GROUP, LANES)) * inv
            below = jnp.where(sub > j, scaled[top], 0.0)
            diag = jnp.where(sub == j, pivot_diag, diag - below * pivot_diag)
            for t in range(tiles):
                rows[top, t] = jnp.where(sub == j, pivot[t], rows[top, t] - below * pivot[t])
                for g in groups[1:]:
                    rows[g, t] = rows[g, t] - scaled[g] * pivot[t]
        for g in groups:
            for t in range(tiles):
                a_ref[g:g + GROUP, t * LANES:(t + 1) * LANES] = rows[g, t]
        for t in range(tiles):
            span = slice(t * LANES, (t + 1) * LANES)
            if t < home:
                upper_ref[top:top + GROUP, span] = jnp.zeros((GROUP, LANES), jnp.float32)
            elif t == home:
                upper_ref[top:top + GROUP, span] = jnp.where(lane >= sub + offset, diag, 0.0)
            else:
                upper_ref[top:top + GROUP, span] = rows[top, t]


def trailing(a_ref, base, height, size):
    end = base + height
    if end == size:
        return
    panel = a_ref[base:end, :]
    col = lax.broadcasted_iota(jnp.int32, (height, size), 1)
    row = lax.broadcasted_iota(jnp.int32, (height, size), 0) + base
    right = jnp.where((col <= row) | (col >= end), panel, 0.0)
    left = panel[:, end:]
    update = lax.dot_general(left, right, (((0,), (0,)), ((), ())), precision=lax.Precision.HIGHEST, preferred_element_type=jnp.float32)
    rest = a_ref[end:, :]
    at = lax.broadcasted_iota(jnp.int32, (size - end, size), 1)
    a_ref[end:, :] = jnp.where((at >= base) & (at < end), 0.0, rest) - update


def factor_kernel(gram_ref, upper_ref, inverse_ref, a_ref):
    size = gram_ref.shape[0]
    a_ref[...] = gram_ref[...]
    for base in range(0, size, PANEL):
        factor_panel(a_ref, upper_ref, base, PANEL, size)
        trailing(a_ref, base, PANEL, size)
    col = lax.broadcasted_iota(jnp.int32, (size, size), 1)
    row = lax.broadcasted_iota(jnp.int32, (size, size), 0)
    inverse_ref[...] = jnp.where(col <= row, a_ref[...], 0.0)


def factor_and_inverse(gram):
    size = gram.shape[0]
    vmem = pl.BlockSpec(memory_space=pltpu.VMEM)
    square = jax.ShapeDtypeStruct((size, size), jnp.float32)
    return pl.pallas_call(
        factor_kernel,
        out_shape=(square, square),
        in_specs=[vmem],
        out_specs=(vmem, vmem),
        scratch_shapes=[pltpu.VMEM((size, size), jnp.float32)],
        compiler_params=pltpu.CompilerParams(vmem_limit_bytes=16 * 2**20),
        cost_estimate=pl.CostEstimate(flops=100_000_000, bytes_accessed=1_000_000, transcendentals=256),
        name="factor_and_inverse",
    )(gram)


def swap(value, axis, bit):
    mask = 2**bit
    pairs = [(source, source ^ mask) for source in range(lax.axis_size(axis))]
    return lax.ppermute(value, axis, pairs)


def bit_of(axis, bit):
    return (lax.axis_index(axis) // 2**bit) % 2


def levels():
    wide = lax.axis_size("wide").bit_length() - 1
    narrow = lax.axis_size("narrow").bit_length() - 1
    return [("wide", 0)] + [("narrow", bit) for bit in range(narrow)] + [("wide", bit) for bit in range(1, wide)]


def halve(value, axis, bit):
    cut = 0 if value.shape[0] > GROUP else 1
    mine = bit_of(axis, bit) == 0
    first, second = jnp.split(value, 2, axis=cut)
    return jnp.where(mine, first, second) + swap(jnp.where(mine, second, first), axis, bit), cut


def unhalve(value, axis, bit, cut):
    other = swap(value, axis, bit)
    mine = bit_of(axis, bit) == 0
    return jnp.concatenate([jnp.where(mine, value, other), jnp.where(mine, other, value)], axis=cut)


def sum_everywhere(value, halvings):
    undo = []
    for at, (axis, bit) in enumerate(levels()):
        if at < halvings:
            value, cut = halve(value, axis, bit)
            undo.append((axis, bit, cut))
        else:
            value = value + swap(value, axis, bit)
    for axis, bit, cut in reversed(undo):
        value = unhalve(value, axis, bit, cut)
    return value


def per_device(features, sketch):
    high = lax.Precision.HIGH
    dot = lambda a, b: jnp.dot(a, b, preferred_element_type=jnp.float32, precision=high)
    sampled = dot(features, sketch)
    gram = sum_everywhere(dot(sampled.T, sampled), 1)
    cross = sum_everywhere(dot(sampled.T, features), len(levels()))
    upper, inverse = factor_and_inverse(gram)
    count = features.shape[0] * lax.axis_size("wide") * lax.axis_size("narrow")
    scale = jnp.sqrt(jnp.float32(count))
    basis = dot(sampled, (inverse * scale).T)
    return (basis, upper / scale, dot(inverse, cross))


def solution(mesh):
    in_specs = (P(("wide", "narrow"), None), P())
    out_specs = (P(("wide", "narrow"), None), P(), P())
    return jax.shard_map(
        per_device, mesh=mesh, in_specs=in_specs, out_specs=out_specs, check_vma=False
    )
```

time: 266 us -> 75.5 us (0.28)
  waiting for transfers between devices: 157 us -> 25.1 us
  other arithmetic: 55.1 us -> 3.28 us
  starting transfers between devices: 9.6 us -> 25.3 us
  between operations: 15.5 us -> 0.94 us
  local copies, waits for them, and re-layouts: 11 us -> 1.21 us
  Pallas kernels: 0 us -> 8.97 us
  matrix products: 16.7 us -> 10.5 us
    psum x1 -> x0, waiting for transfers between devices: 127 us -> none  [per_device(): summed = lax.psum(term, ('wide', 'narrow'))]
    another operation x8 -> x0, other arithmetic: 53.7 us -> none  [the longest x6 34.1 us: per_device(): upper = jnp.linalg.cholesky(gram).T]
    ppermute x5 -> x16, starting transfers between devices: 9.56 us -> 25.3 us  [swap(): return lax.ppermute(value, axis, pairs)]
    pallas_call x0 -> x1, Pallas kernels: none -> 8.97 us  [factor_and_inverse(): pl.pallas_call(factor_kernel, out_shape=(square, square), in_specs=[vmem]...]
    unnamed x5 -> x4, local copies, waits for them, and re-layouts: 6.85 us -> 1.21 us
    ppermute x5 -> x16, waiting for transfers between devices: 30.7 us -> 25.1 us  [swap(): return lax.ppermute(value, axis, pairs)]
    another operation x9 -> x0, local copies, waits for them, and re-layouts: 4.05 us -> none
    dot_general x3 -> x5, matrix products: 13.9 us -> 10.5 us  [per_device(): jnp.dot(a, b, preferred_element_type=jnp.float32, precision=high)]
  transfers between devices with their start and end apart: 6 -> 16, of which waited for: 6 -> 10; matrix products, arithmetic and copies ran while one was open for 2% -> 5% of each run, Pallas kernels for 0% -> 12%
where the time goes in v1:
time: 75.5 us; the launch traced here: 75.3 us
  starting transfers between devices  25.3 us (34%)
  waiting for transfers between devices  25.1 us (33%)
  matrix products  10.5 us (14%)
  Pallas kernels  8.97 us (12%)
  other arithmetic  3.28 us (4%)
  local copies, waits for them, and re-layouts  1.21 us (2%)
  between operations  0.94 us (1%)
    ppermute x16, starting transfers between devices, swap(): return lax.ppermute(value, axis, pairs)  25.3 us
    ppermute x16, waiting for transfers between devices, swap(): return lax.ppermute(value, axis, pairs)  25.1 us
    dot_general x5, matrix products, per_device(): jnp.dot(a, b, preferred_element_type=jnp.float32, precision=high)  10.5 us
    pallas_call x1, Pallas kernels, factor_and_inverse(): pl.pallas_call(factor_kernel, out_shape=(square, square), in_specs=[vmem]...  8.97 us
  transfers between devices with their start and end apart: 16, of which 10 were waited for; matrix products, arithmetic and copies ran while one was open for 5% of the time, Pallas kernels for 12%

profile of v1, /device:TPU:0, one launch (start us, length us, event | category | flops | bytes accessed | tf_op | source)
XLA Modules:
  0.0 75.3 jit_solution(12023949701015066436)
XLA Ops:
  0.6 0.0 copy-start
  0.7 1.2 %copy-done = f32[1024,256]{1,0:T(8,128)S(1)} copy-done((f32[1024,256]{1,0:T(8,128)S(1)}, f32[1024,256]{1,0:T(8,128)}, u32[]{:S(2)}) %copy-start) | copy-done | bytes 1048600
  1.9 0.0 copy-start.1
  1.9 4.1 %fusion.9 = f32[1024,256]{1,0:T(8,128)S(1)} fusion(f32[1024,1024]{1,0:T(8,128)} %param.2, f32[1024,256]{1,0:T(8,128)S(1)} %copy-done), kind=kOutput, calls=%fused_computation.39 | convolution fusion | flops 1610612736 | bytes 6291456 | tf_op jit(solution)/shard_map/dot_general | solution.py:155
  6.0 0.0 copy-done.1
  6.0 2.2 %fusion.11 = f32[256,1024]{1,0:T(8,128)S(1)} fusion(f32[1024,256]{1,0:T(8,128)S(1)} %fusion.9, f32[1024,1024]{1,0:T(8,128)S(1)} %copy-done.1), kind=kOutput, calls=%fused_computation.41 | convolution fusion | flops 1610612736 | bytes 6291456 | tf_op jit(solution)/shard_map/dot_general | solution.py:155
  8.2 0.9 %slice_select_fusion = f32[128,1024]{1,0:T(8,128)} fusion(f32[256,1024]{1,0:T(8,128)S(1)} %fusion.11, pred[]{:T(512)S(6)} %eq.35), kind=kLoop, calls=%fused_computation.6 | loop fusion | flops 131072 | bytes 1572865 | tf_op jit(solution)/shard_map/jit(_where)/select_n | solution.py:131
  9.0 0.5 collective-permute-start.6
  9.5 1.9 %collective-permute-done.6 = f32[128,1024]{1,0:T(8,128)} collective-permute-done((f32[128,1024]{1,0:T(8,128)}, f32[128,1024]{1,0:T(8,128)}, u32[]{:S(2)}, u32[]{:S(2)}) %collective-permute-start.6) | collective-permute-done | bytes 524320 | tf_op jit(solution)/shard_map/ppermute | solution.py:114
  11.4 1.1 %select_add_fusion = f32[128,1024]{1,0:T(8,128)S(1)} fusion(f32[128,1024]{1,0:T(8,128)} %collective-permute-done.6, f32[256,1024]{1,0:T(8,128)S(1)} %fusion.11, pred[]{:T(512)S(6)} %eq.35), kind=kLoop, calls=%fused_computation.5 | loop fusion | flops 262144 | bytes 2097153 | tf_op jit(solution)/shard_map/add | solution.py:131
  12.5 3.0 %collective-permute-start.7 = (f32[64,1024]{1,0:T(8,128)S(1)}, f32[64,1024]{1,0:T(8,128)S(1)}, u32[]{:S(2)}, u32[]{:S(2)}) collective-permute-start(f32[64,1024]{1,0:T(8,128)S(1)} %slice_select_fusion.1), channel_id=1, source_target_pairs={{0,1},{1,0},{2,3},{3,2},{4,5},{5,4},{6,7},{7,6},{8,9},{9,8},{10,11... | collective-permute-start | bytes 786440 | tf_op jit(solution)/shard_map/ppermute | solution.py:114
  15.5 1.0 %fusion.10 = f32[256,256]{1,0:T(8,128)S(1)} fusion(f32[1024,256]{1,0:T(8,128)S(1)} %fusion.9), kind=kOutput, calls=%fused_computation.40 | convolution fusion | flops 402653184 | bytes 1310720 | tf_op jit(solution)/shard_map/dot_general | solution.py:155
  16.5 5.6 %collective-permute-done.7 = f32[64,1024]{1,0:T(8,128)S(1)} collective-permute-done((f32[64,1024]{1,0:T(8,128)S(1)}, f32[64,1024]{1,0:T(8,128)S(1)}, u32[]{:S(2)}, u32[]{:S(2)}) %collective-permute-start.7) | collective-permute-done | bytes 262176 | tf_op jit(solution)/shard_map/ppermute | solution.py:114
  22.2 1.8 %collective-permute-start.8 = (f32[32,1024]{1,0:T(8,128)S(1)}, f32[32,1024]{1,0:T(8,128)S(1)}, u32[]{:S(2)}, u32[]{:S(2)}) collective-permute-start(f32[32,1024]{1,0:T(8,128)S(1)} %slice_select_fusion.2), channel_id=1, source_target_pairs={{0,4},{2,6},{4,0},{6,2},{8,12},{10,14},{12,8},{14,10},{16,20},{18,... | collective-permute-start | bytes 393224 | tf_op jit(solution)/shard_map/ppermute | solution.py:114
  24.0 0.1 collective-permute-start
  24.1 3.2 %collective-permute-done.8 = f32[32,1024]{1,0:T(8,128)S(1)} collective-permute-done((f32[32,1024]{1,0:T(8,128)S(1)}, f32[32,1024]{1,0:T(8,128)S(1)}, u32[]{:S(2)}, u32[]{:S(2)}) %collective-permute-start.8) | collective-permute-done | bytes 131104 | tf_op jit(solution)/shard_map/ppermute | solution.py:114
  27.3 1.8 %collective-permute-start.9 = (f32[16,1024]{1,0:T(8,128)S(1)}, f32[16,1024]{1,0:T(8,128)S(1)}, u32[]{:S(2)}, u32[]{:S(2)}) collective-permute-start(f32[16,1024]{1,0:T(8,128)S(1)} %slice_select_fusion.4), channel_id=1, source_target_pairs={{0,8},{2,10},{4,12},{6,14},{8,0},{10,2},{12,4},{14,6},{16,24},{18,... | collective-permute-start | bytes 196616 | tf_op jit(solution)/shard_map/ppermute | solution.py:114
  29.1 0.0 collective-permute-done
  29.1 1.6 %collective-permute-start.1 = (f32[128,256]{1,0:T(8,128)S(1)}, f32[128,256]{1,0:T(8,128)S(1)}, u32[]{:S(2)}, u32[]{:S(2)}) collective-permute-start(f32[128,256]{1,0:T(8,128)S(1)} %select_add_fusion.3), channel_id=1, source_target_pairs={{0,1},{1,0},{2,3},{3,2},{4,5},{5,4},{6,7},{7,6},{8,9},{9,8},{10,11... | collective-permute-start | bytes 393224 | tf_op jit(solution)/shard_map/ppermute | solution.py:114
  30.7 0.9 %collective-permute-done.9 = f32[16,1024]{1,0:T(8,128)S(1)} collective-permute-done((f32[16,1024]{1,0:T(8,128)S(1)}, f32[16,1024]{1,0:T(8,128)S(1)}, u32[]{:S(2)}, u32[]{:S(2)}) %collective-permute-start.9) | collective-permute-done | bytes 65568 | tf_op jit(solution)/shard_map/ppermute | solution.py:114
  31.7 3.2 %collective-permute-start.10 = (f32[8,1024]{1,0:T(8,128)S(1)}, f32[8,1024]{1,0:T(8,128)S(1)}, u32[]{:S(2)}, u32[]{:S(2)}) collective-permute-start(f32[8,1024]{1,0:T(8,128)S(1)} %slice_select_fusion.5), channel_id=1, source_target_pairs={{0,16},{2,18},{4,20},{6,22},{8,24},{10,26},{12,28},{14,30},{16,0},... | collective-permute-start | bytes 98312 | tf_op jit(solution)/shard_map/ppermute | solution.py:114
  34.8 0.0 collective-permute-done.1
  34.9 1.6 %collective-permute-start.2 = (f32[128,256]{1,0:T(8,128)S(1)}, f32[128,256]{1,0:T(8,128)S(1)}, u32[]{:S(2)}, u32[]{:S(2)}) collective-permute-start(f32[128,256]{1,0:T(8,128)S(1)} %add.60), channel_id=1, source_target_pairs={{0,4},{2,6},{4,0},{6,2},{8,12},{10,14},{12,8},{14,10},{16,20},{18,... | collective-permute-start | bytes 393224 | tf_op jit(solution)/shard_map/ppermute | solution.py:114
  36.4 0.6 collective-permute-done.10
  37.0 2.7 %collective-permute-start.11 = (f32[8,1024]{1,0:T(8,128)S(1)}, f32[8,1024]{1,0:T(8,128)S(1)}, u32[]{:S(2)}, u32[]{:S(2)}) collective-permute-start(f32[8,1024]{1,0:T(8,128)S(1)} %select_add_fusion.5), channel_id=1, source_target_pairs={{0,16},{2,18},{4,20},{6,22},{8,24},{10,26},{12,28},{14,30},{16,0},... | collective-permute-start | bytes 98312 | tf_op jit(solution)/shard_map/ppermute | solution.py:114
  39.7 0.2 collective-permute-done.2
  39.9 1.8 %collective-permute-start.3 = (f32[128,256]{1,0:T(8,128)S(1)}, f32[128,256]{1,0:T(8,128)S(1)}, u32[]{:S(2)}, u32[]{:S(2)}) collective-permute-start(f32[128,256]{1,0:T(8,128)S(1)} %add.61), channel_id=1, source_target_pairs={{0,8},{2,10},{4,12},{6,14},{8,0},{10,2},{12,4},{14,6},{16,24},{18,... | collective-permute-start | bytes 393224 | tf_op jit(solution)/shard_map/ppermute | solution.py:114
  41.7 0.1 collective-permute-done.11
  41.8 2.0 %collective-permute-start.12 = (f32[16,1024]{1,0:T(8,128)S(1)}, f32[16,1024]{1,0:T(8,128)S(1)}, u32[]{:S(2)}, u32[]{:S(2)}) collective-permute-start(f32[16,1024]{1,0:T(8,128)S(1)} %pad_maximum_fusion.4), channel_id=1, source_target_pairs={{0,8},{2,10},{4,12},{6,14},{8,0},{10,2},{12,4},{14,6},{16,24},{18,... | collective-permute-start | bytes 196616 | tf_op jit(solution)/shard_map/ppermute | solution.py:114
  43.8 2.0 %collective-permute-done.3 = f32[128,256]{1,0:T(8,128)S(1)} collective-permute-done((f32[128,256]{1,0:T(8,128)S(1)}, f32[128,256]{1,0:T(8,128)S(1)}, u32[]{:S(2)}, u32[]{:S(2)}) %collective-permute-start.3) | collective-permute-done | bytes 131104 | tf_op jit(solution)/shard_map/ppermute | solution.py:114
  45.8 2.2 %collective-permute-start.4 = (f32[128,256]{1,0:T(8,128)S(1)}, f32[128,256]{1,0:T(8,128)S(1)}, u32[]{:S(2)}, u32[]{:S(2)}) collective-permute-start(f32[128,256]{1,0:T(8,128)S(1)} %add.62), channel_id=1, source_target_pairs={{0,16},{2,18},{4,20},{6,22},{8,24},{10,26},{12,28},{14,30},{16,0},... | collective-permute-start | bytes 393224 | tf_op jit(solution)/shard_map/ppermute | solution.py:114
  48.0 0.0 collective-permute-done.12
  48.0 1.6 %collective-permute-start.13 = (f32[32,1024]{1,0:T(8,128)S(1)}, f32[32,1024]{1,0:T(8,128)S(1)}, u32[]{:S(2)}, u32[]{:S(2)}) collective-permute-start(f32[32,1024]{1,0:T(8,128)S(1)} %pad_maximum_fusion.3), channel_id=1, source_target_pairs={{0,4},{2,6},{4,0},{6,2},{8,12},{10,14},{12,8},{14,10},{16,20},{18,... | collective-permute-start | bytes 393224 | tf_op jit(solution)/shard_map/ppermute | solution.py:114
  49.6 3.6 %collective-permute-done.4 = f32[128,256]{1,0:T(8,128)S(1)} collective-permute-done((f32[128,256]{1,0:T(8,128)S(1)}, f32[128,256]{1,0:T(8,128)S(1)}, u32[]{:S(2)}, u32[]{:S(2)}) %collective-permute-start.4) | collective-permute-done | bytes 131104 | tf_op jit(solution)/shard_map/ppermute | solution.py:114
  53.2 0.1 collective-permute-start.5
  53.3 0.0 collective-permute-done.13
  53.3 1.6 %collective-permute-start.14 = (f32[64,1024]{1,0:T(8,128)S(1)}, f32[64,1024]{1,0:T(8,128)S(1)}, u32[]{:S(2)}, u32[]{:S(2)}) collective-permute-start(f32[64,1024]{1,0:T(8,128)S(1)} %pad_maximum_fusion.2), channel_id=1, source_target_pairs={{0,1},{1,0},{2,3},{3,2},{4,5},{5,4},{6,7},{7,6},{8,9},{9,8},{10,11... | collective-permute-start | bytes 786440 | tf_op jit(solution)/shard_map/ppermute | solution.py:114
  54.9 0.0 collective-permute-done.5
  55.0 7.1 %collective-permute-done.14 = f32[64,1024]{1,0:T(8,128)S(1)} collective-permute-done((f32[64,1024]{1,0:T(8,128)S(1)}, f32[64,1024]{1,0:T(8,128)S(1)}, u32[]{:S(2)}, u32[]{:S(2)}) %collective-permute-start.14) | collective-permute-done | bytes 262176 | tf_op jit(solution)/shard_map/ppermute | solution.py:114
  62.2 0.1 collective-permute-start.15
  62.3 9.0 %factor_and_inverse.1 = (f32[256,256]{1,0:T(8,128)S(1)}, f32[256,256]{1,0:T(8,128)S(1)}) custom-call(f32[256,256]{1,0:T(8,128)S(1)} %pad_maximum_fusion.1.gram_ref), custom_call_target="tpu_custom_call" | custom-call | flops 100000000 | bytes 1000000 | tf_op jit(solution)/shard_map/factor_and_inverse/pallas_call | solution.py:99
  71.2 0.7 broadcast_multiply_fusion
  72.0 1.6 %fusion.4 = f32[1024,256]{1,0:T(8,128)} fusion(f32[1024,256]{1,0:T(8,128)S(1)} %fusion.9, f32[256,256]{1,0:T(8,128)S(1)} %get-tuple-element.5), kind=kOutput, calls=%fused_computation.10 | convolution fusion | flops 402718720 | bytes 2359296 | tf_op jit(solution)/shard_map/dot_general | solution.py:155
  73.6 0.0 collective-permute-done.15
  73.6 0.1 broadcast_select_fusion.1
  73.7 1.6 %fusion = f32[256,1024]{1,0:T(8,128)} fusion(f32[256,256]{1,0:T(8,128)S(1)} %get-tuple-element.5, f32[128,1024]{1,0:T(8,128)S(1)} %get-tuple-element.8, f32[128,1024]{1,0:T(8,128)S(1)} %get-tuple-element.7), kind=kOutput, calls=%fused_computation | convolution fusion | flops 402915328 | bytes 2359296 | tf_op jit(solution)/shard_map/dot_general | solution.py:155
  (24 shorter events, 0.5 us)
Async XLA Ops:
  0.6 1.2 %copy-start = (f32[1024,256]{1,0:T(8,128)S(1)}, f32[1024,256]{1,0:T(8,128)}, u32[]{:S(2)}) copy-start(f32[1024,256]{1,0:T(8,128)} %param.3) | copy-start | bytes 3145732
  1.9 4.2 %copy-start.1 = (f32[1024,1024]{1,0:T(8,128)S(1)}, f32[1024,1024]{1,0:T(8,128)}, u32[]{:S(2)}) copy-start(f32[1024,1024]{1,0:T(8,128)} %param.2) | copy-start | bytes 12582916
  9.0 2.3 %collective-permute-start.6 = (f32[128,1024]{1,0:T(8,128)}, f32[128,1024]{1,0:T(8,128)}, u32[]{:S(2)}, u32[]{:S(2)}) collective-permute-start(f32[128,1024]{1,0:T(8,128)} %slice_select_fusion), channel_id=1, source_target_pairs={{0,2},{2,0},{4,6},{6,4},{8,10},{10,8},{12,14},{14,12},{16,18},{18,... | collective-permute-start | bytes 1572872 | tf_op jit(solution)/shard_map/ppermute | solution.py:114
  12.5 9.6 %collective-permute-start.7 = (f32[64,1024]{1,0:T(8,128)S(1)}, f32[64,1024]{1,0:T(8,128)S(1)}, u32[]{:S(2)}, u32[]{:S(2)}) collective-permute-start(f32[64,1024]{1,0:T(8,128)S(1)} %slice_select_fusion.1), channel_id=1, source_target_pairs={{0,1},{1,0},{2,3},{3,2},{4,5},{5,4},{6,7},{7,6},{8,9},{9,8},{10,11... | collective-permute-start | bytes 786440 | tf_op jit(solution)/shard_map/ppermute | solution.py:114
  22.2 5.1 %collective-permute-start.8 = (f32[32,1024]{1,0:T(8,128)S(1)}, f32[32,1024]{1,0:T(8,128)S(1)}, u32[]{:S(2)}, u32[]{:S(2)}) collective-permute-start(f32[32,1024]{1,0:T(8,128)S(1)} %slice_select_fusion.2), channel_id=1, source_target_pairs={{0,4},{2,6},{4,0},{6,2},{8,12},{10,14},{12,8},{14,10},{16,20},{18,... | collective-permute-start | bytes 393224 | tf_op jit(solution)/shard_map/ppermute | solution.py:114
  24.0 5.1 %collective-permute-start = (f32[128,256]{1,0:T(8,128)S(1)}, f32[128,256]{1,0:T(8,128)S(1)}, u32[]{:S(2)}, u32[]{:S(2)}) collective-permute-start(f32[128,256]{1,0:T(8,128)S(1)} %slice_select_fusion.3), channel_id=1, source_target_pairs={{0,2},{2,0},{4,6},{6,4},{8,10},{10,8},{12,14},{14,12},{16,18},{18,... | collective-permute-start | bytes 393224 | tf_op jit(solution)/shard_map/ppermute | solution.py:114
  27.3 4.3 %collective-permute-start.9 = (f32[16,1024]{1,0:T(8,128)S(1)}, f32[16,1024]{1,0:T(8,128)S(1)}, u32[]{:S(2)}, u32[]{:S(2)}) collective-permute-start(f32[16,1024]{1,0:T(8,128)S(1)} %slice_select_fusion.4), channel_id=1, source_target_pairs={{0,8},{2,10},{4,12},{6,14},{8,0},{10,2},{12,4},{14,6},{16,24},{18,... | collective-permute-start | bytes 196616 | tf_op jit(solution)/shard_map/ppermute | solution.py:114
  29.1 5.7 %collective-permute-start.1 = (f32[128,256]{1,0:T(8,128)S(1)}, f32[128,256]{1,0:T(8,128)S(1)}, u32[]{:S(2)}, u32[]{:S(2)}) collective-permute-start(f32[128,256]{1,0:T(8,128)S(1)} %select_add_fusion.3), channel_id=1, source_target_pairs={{0,1},{1,0},{2,3},{3,2},{4,5},{5,4},{6,7},{7,6},{8,9},{9,8},{10,11... | collective-permute-start | bytes 393224 | tf_op jit(solution)/shard_map/ppermute | solution.py:114
  31.7 5.3 %collective-permute-start.10 = (f32[8,1024]{1,0:T(8,128)S(1)}, f32[8,1024]{1,0:T(8,128)S(1)}, u32[]{:S(2)}, u32[]{:S(2)}) collective-permute-start(f32[8,1024]{1,0:T(8,128)S(1)} %slice_select_fusion.5), channel_id=1, source_target_pairs={{0,16},{2,18},{4,20},{6,22},{8,24},{10,26},{12,28},{14,30},{16,0},... | collective-permute-start | bytes 98312 | tf_op jit(solution)/shard_map/ppermute | solution.py:114
  34.9 5.0 %collective-permute-start.2 = (f32[128,256]{1,0:T(8,128)S(1)}, f32[128,256]{1,0:T(8,128)S(1)}, u32[]{:S(2)}, u32[]{:S(2)}) collective-permute-start(f32[128,256]{1,0:T(8,128)S(1)} %add.60), channel_id=1, source_target_pairs={{0,4},{2,6},{4,0},{6,2},{8,12},{10,14},{12,8},{14,10},{16,20},{18,... | collective-permute-start | bytes 393224 | tf_op jit(solution)/shard_map/ppermute | solution.py:114
  37.0 4.8 %collective-permute-start.11 = (f32[8,1024]{1,0:T(8,128)S(1)}, f32[8,1024]{1,0:T(8,128)S(1)}, u32[]{:S(2)}, u32[]{:S(2)}) collective-permute-start(f32[8,1024]{1,0:T(8,128)S(1)} %select_add_fusion.5), channel_id=1, source_target_pairs={{0,16},{2,18},{4,20},{6,22},{8,24},{10,26},{12,28},{14,30},{16,0},... | collective-permute-start | bytes 98312 | tf_op jit(solution)/shard_map/ppermute | solution.py:114
  39.9 5.9 %collective-permute-start.3 = (f32[128,256]{1,0:T(8,128)S(1)}, f32[128,256]{1,0:T(8,128)S(1)}, u32[]{:S(2)}, u32[]{:S(2)}) collective-permute-start(f32[128,256]{1,0:T(8,128)S(1)} %add.61), channel_id=1, source_target_pairs={{0,8},{2,10},{4,12},{6,14},{8,0},{10,2},{12,4},{14,6},{16,24},{18,... | collective-permute-start | bytes 393224 | tf_op jit(solution)/shard_map/ppermute | solution.py:114
  41.8 6.2 %collective-permute-start.12 = (f32[16,1024]{1,0:T(8,128)S(1)}, f32[16,1024]{1,0:T(8,128)S(1)}, u32[]{:S(2)}, u32[]{:S(2)}) collective-permute-start(f32[16,1024]{1,0:T(8,128)S(1)} %pad_maximum_fusion.4), channel_id=1, source_target_pairs={{0,8},{2,10},{4,12},{6,14},{8,0},{10,2},{12,4},{14,6},{16,24},{18,... | collective-permute-start | bytes 196616 | tf_op jit(solution)/shard_map/ppermute | solution.py:114
  45.8 7.3 %collective-permute-start.4 = (f32[128,256]{1,0:T(8,128)S(1)}, f32[128,256]{1,0:T(8,128)S(1)}, u32[]{:S(2)}, u32[]{:S(2)}) collective-permute-start(f32[128,256]{1,0:T(8,128)S(1)} %add.62), channel_id=1, source_target_pairs={{0,16},{2,18},{4,20},{6,22},{8,24},{10,26},{12,28},{14,30},{16,0},... | collective-permute-start | bytes 393224 | tf_op jit(solution)/shard_map/ppermute | solution.py:114
  48.0 5.2 %collective-permute-start.13 = (f32[32,1024]{1,0:T(8,128)S(1)}, f32[32,1024]{1,0:T(8,128)S(1)}, u32[]{:S(2)}, u32[]{:S(2)}) collective-permute-start(f32[32,1024]{1,0:T(8,128)S(1)} %pad_maximum_fusion.3), channel_id=1, source_target_pairs={{0,4},{2,6},{4,0},{6,2},{8,12},{10,14},{12,8},{14,10},{16,20},{18,... | collective-permute-start | bytes 393224 | tf_op jit(solution)/shard_map/ppermute | solution.py:114
  53.2 1.7 %collective-permute-start.5 = (f32[128,256]{1,0:T(8,128)S(1)}, f32[128,256]{1,0:T(8,128)S(1)}, u32[]{:S(2)}, u32[]{:S(2)}) collective-permute-start(f32[128,256]{1,0:T(8,128)S(1)} %add.63), channel_id=1, source_target_pairs={{0,2},{2,0},{4,6},{6,4},{8,10},{10,8},{12,14},{14,12},{16,18},{18,... | collective-permute-start | bytes 393224 | tf_op jit(solution)/shard_map/ppermute | solution.py:114
  53.3 8.8 %collective-permute-start.14 = (f32[64,1024]{1,0:T(8,128)S(1)}, f32[64,1024]{1,0:T(8,128)S(1)}, u32[]{:S(2)}, u32[]{:S(2)}) collective-permute-start(f32[64,1024]{1,0:T(8,128)S(1)} %pad_maximum_fusion.2), channel_id=1, source_target_pairs={{0,1},{1,0},{2,3},{3,2},{4,5},{5,4},{6,7},{7,6},{8,9},{9,8},{10,11... | collective-permute-start | bytes 786440 | tf_op jit(solution)/shard_map/ppermute | solution.py:114
  62.2 11.4 %collective-permute-start.15 = (f32[128,1024]{1,0:T(8,128)S(1)}, f32[128,1024]{1,0:T(8,128)S(1)}, u32[]{:S(2)}, u32[]{:S(2)}) collective-permute-start(f32[128,1024]{1,0:T(8,128)S(1)} %pad_maximum_fusion), channel_id=1, source_target_pairs={{0,2},{2,0},{4,6},{6,4},{8,10},{10,8},{12,14},{14,12},{16,18},{18,... | collective-permute-start | bytes 1572872 | tf_op jit(solution)/shard_map/ppermute | solution.py:114

commit v2 on v1

--- a/solution.py
+++ b/solution.py
@@ -2,7 +2,7 @@
 from jax import lax
 from jax.experimental import pallas as pl
 from jax.experimental.pallas import tpu as pltpu
-from jax.sharding import PartitionSpec as P
+from jax.sharding import Mesh, PartitionSpec as P
 
 GROUP = 8
 LANES = 128
@@ -108,64 +108,53 @@
     )(gram)
 
 
-def swap(value, axis, bit):
-    mask = 2**bit
-    pairs = [(source, source ^ mask) for source in range(lax.axis_size(axis))]
-    return lax.ppermute(value, axis, pairs)
+CHIPS = ("chip", "narrow")
 
 
-def bit_of(axis, bit):
-    return (lax.axis_index(axis) // 2**bit) % 2
+def exchange(blocks, axes):
+    return lax.all_to_all(blocks, axes, 0, 0, tiled=True)
 
 
-def levels():
-    wide = lax.axis_size("wide").bit_length() - 1
-    narrow = lax.axis_size("narrow").bit_length() - 1
-    return [("wide", 0)] + [("narrow", bit) for bit in range(narrow)] + [("wide", bit) for bit in range(1, wide)]
+def scatter_sum(value, axes):
+    count = lax.axis_size(axes)
+    blocks = value.reshape((count, value.shape[0] // count) + value.shape[1:])
+    return jnp.sum(exchange(blocks, axes), axis=0)
 
 
-def halve(value, axis, bit):
-    cut = 0 if value.shape[0] > GROUP else 1
-    mine = bit_of(axis, bit) == 0
-    first, second = jnp.split(value, 2, axis=cut)
-    return jnp.where(mine, first, second) + swap(jnp.where(mine, second, first), axis, bit), cut
+def gather(value, axes):
+    count = lax.axis_size(axes)
+    blocks = exchange(jnp.broadcast_to(value, (count,) + value.shape), axes)
+    return blocks.reshape((count * value.shape[0],) + value.shape[1:])
 
 
-def unhalve(value, axis, bit, cut):
-    other = swap(value, axis, bit)
-    mine = bit_of(axis, bit) == 0
-    return jnp.concatenate([jnp.where(mine, value, other), jnp.where(mine, other, value)], axis=cut)
-
-
-def sum_everywhere(value, halvings):
-    undo = []
-    for at, (axis, bit) in enumerate(levels()):
-        if at < halvings:
-            value, cut = halve(value, axis, bit)
-            undo.append((axis, bit, cut))
-        else:
-            value = value + swap(value, axis, bit)
-    for axis, bit, cut in reversed(undo):
-        value = unhalve(value, axis, bit, cut)
-    return value
+def sum_everywhere(value):
+    half = scatter_sum(value, "core")
+    rows, columns = half.shape
+    count = lax.axis_size(CHIPS)
+    tall = max(rows, count * GROUP)
+    own = scatter_sum(half.reshape(tall, rows * columns // tall), CHIPS)
+    half = gather(own, CHIPS).reshape(rows, columns)
+    return gather(half, "core")
 
 
 def per_device(features, sketch):
     high = lax.Precision.HIGH
     dot = lambda a, b: jnp.dot(a, b, preferred_element_type=jnp.float32, precision=high)
     sampled = dot(features, sketch)
-    gram = sum_everywhere(dot(sampled.T, sampled), 1)
-    cross = sum_everywhere(dot(sampled.T, features), len(levels()))
+    terms = jnp.concatenate([dot(sampled.T, sampled), dot(sampled.T, features)], axis=1)
+    summed = sum_everywhere(terms)
+    gram, cross = jnp.split(summed, [sampled.shape[1]], axis=1)
     upper, inverse = factor_and_inverse(gram)
-    count = features.shape[0] * lax.axis_size("wide") * lax.axis_size("narrow")
+    count = features.shape[0] * lax.axis_size(("chip", "core", "narrow"))
     scale = jnp.sqrt(jnp.float32(count))
     basis = dot(sampled, (inverse * scale).T)
     return (basis, upper / scale, dot(inverse, cross))
 
 
 def solution(mesh):
-    in_specs = (P(("wide", "narrow"), None), P())
-    out_specs = (P(("wide", "narrow"), None), P(), P())
+    wide, narrow = mesh.shape["wide"], mesh.shape["narrow"]
+    split = Mesh(mesh.devices.reshape(wide // 2, 2, narrow), ("chip", "core", "narrow"))
+    rows = P(("chip", "core", "narrow"), None)
     return jax.shard_map(
-        per_device, mesh=mesh, in_specs=in_specs, out_specs=out_specs, check_vma=False
+        per_device, mesh=split, in_specs=(rows, P()), out_specs=(rows, P(), P()), check_vma=False
     )

time: 75.5 us -> 81.7 us (1.082)
  blocking collectives: 0 us -> 58.1 us
  starting transfers between devices: 25.3 us -> 0 us
  waiting for transfers between devices: 25.1 us -> 0 us
  other arithmetic: 3.28 us -> 1.83 us
    all_to_all x0 -> x4, blocking collectives: none -> 58.1 us  [exchange(): return lax.all_to_all(blocks, axes, 0, 0, tiled=True)]
    ppermute x16 -> x0, starting transfers between devices: 25.3 us -> none  [swap(): return lax.ppermute(value, axis, pairs)]
    ppermute x16 -> x0, waiting for transfers between devices: 25.1 us -> none  [swap(): return lax.ppermute(value, axis, pairs)]
    add x10 -> x0, other arithmetic: 1.31 us -> none  [the longest x6 1.24 us: halve(): jnp.where(mine, first, second)]
    select_n x12 -> x0, other arithmetic: 1.15 us -> none  [the longest x6 0.93 us: halve(): jnp.where(mine, second, first)]
    reduce_sum x0 -> x2, other arithmetic: none -> 1.01 us  [scatter_sum(): return jnp.sum(exchange(blocks, axes), axis=0)]
  transfers between devices with their start and end apart: 16 -> 0, of which waited for: 10 -> 0; matrix products, arithmetic and copies ran while one was open for 5% -> 0% of each run, Pallas kernels for 12% -> 0%
where the time goes in v2:
time: 81.7 us; the launch traced here: 81.3 us
  blocking collectives  58.1 us (71%)
  matrix products  10.5 us (13%)
  Pallas kernels  8.8 us (11%)
  other arithmetic  1.83 us (2%)
  local copies, waits for them, and re-layouts  1.37 us (2%)
    all_to_all x4, blocking collectives, exchange(): return lax.all_to_all(blocks, axes, 0, 0, tiled=True)  58.1 us
    dot_general x5, matrix products, per_device(): jnp.dot(a, b, preferred_element_type=jnp.float32, precision=high)  10.5 us
    pallas_call x1, Pallas kernels, factor_and_inverse(): pl.pallas_call(factor_kernel, out_shape=(square, square), in_specs=[vmem]...  8.8 us

profile of v2, /device:TPU:0, one launch (start us, length us, event | category | flops | bytes accessed | tf_op | source)
XLA Modules:
  0.0 81.3 jit_solution(16756236159787733232)
XLA Ops:
  0.6 0.0 copy-start
  0.6 1.2 %copy-done = f32[1024,256]{1,0:T(8,128)S(1)} copy-done((f32[1024,256]{1,0:T(8,128)S(1)}, f32[1024,256]{1,0:T(8,128)}, u32[]{:S(2)}) %copy-start) | copy-done | bytes 1048600
  1.9 0.0 copy-start.1
  1.9 4.1 %fusion.6 = f32[1024,256]{1,0:T(8,128)S(1)} fusion(f32[1024,1024]{1,0:T(8,128)} %param.2, f32[1024,256]{1,0:T(8,128)S(1)} %copy-done), kind=kOutput, calls=%fused_computation.8 | convolution fusion | flops 1610612736 | bytes 6291456 | tf_op jit(solution)/shard_map/dot_general | solution.py:142
  6.0 1.0 %fusion.7 = f32[256,256]{1,0:T(8,128)S(1)} fusion(f32[1024,256]{1,0:T(8,128)S(1)} %fusion.6), kind=kOutput, calls=%fused_computation.9 | convolution fusion | flops 402653184 | bytes 1310720 | tf_op jit(solution)/shard_map/dot_general | solution.py:142
  7.0 0.0 copy-done.1
  7.0 2.2 %fusion.8 = f32[256,1024]{1,0:T(8,128)S(1)} fusion(f32[1024,256]{1,0:T(8,128)S(1)} %fusion.6, f32[1024,1024]{1,0:T(8,128)S(1)} %copy-done.1), kind=kOutput, calls=%fused_computation.10 | convolution fusion | flops 1610612736 | bytes 6291456 | tf_op jit(solution)/shard_map/dot_general | solution.py:142
  9.2 0.1 pad_maximum_fusion
  9.3 4.8 %all_to_all.20 = f32[2,128,1280]{2,1,0:T(8,128)S(1)} all-to-all(f32[2,128,1280]{2,1,0:T(8,128)S(1)} %bitcast.14), channel_id=1, replica_groups=mesh['chip'=8,'core'=2,'narrow'=2] {'core'}, dimensions={0} | all-to-all | bytes 2621440 | tf_op jit(solution)/shard_map/all_to_all | solution.py:115
  14.1 1.0 %reduce_sum.18 = f32[128,1280]{1,0:T(8,128)} reduce(f32[2,128,1280]{2,1,0:T(8,128)S(1)} %all_to_all.20, f32[]{:T(128)} %constant.1.clone.1), dimensions={0}, to_apply=%region_0.0 | reduce | flops 163840 | bytes 1966084 | tf_op jit(solution)/shard_map/reduce_sum | solution.py:121
  15.1 27.3 %all_to_all.21 = f32[16,8,1280]{2,1,0:T(8,128)S(1)} all-to-all(f32[16,8,1280]{2,1,0:T(8,128)} %bitcast.15), channel_id=1, replica_groups=mesh['chip'=8,'core'=2,'narrow'=2] {'chip','narrow'}, dimensions={0} | all-to-all | bytes 1310720 | tf_op jit(solution)/shard_map/all_to_all | solution.py:115
  42.5 21.2 %all_to_all.22 = f32[16,8,1280]{2,1,0:T(8,128)S(1)} all-to-all(f32[16,8,1280]{2,1,0:T(8,128)S(1)} %broadcast_in_dim.6), channel_id=1, replica_groups=mesh['chip'=8,'core'=2,'narrow'=2] {'chip','narrow'}, dimensions={0} | all-to-all | bytes 1310720 | tf_op jit(solution)/shard_map/all_to_all | solution.py:115
  63.7 0.1 broadcast_in_dim.7
  63.8 4.8 %all_to_all.23 = f32[2,128,1280]{2,1,0:T(8,128)S(1)} all-to-all(f32[2,128,1280]{2,1,0:T(8,128)S(1)} %broadcast_in_dim.7), channel_id=1, replica_groups=mesh['chip'=8,'core'=2,'narrow'=2] {'core'}, dimensions={0} | all-to-all | bytes 2621440 | tf_op jit(solution)/shard_map/all_to_all | solution.py:115
  68.6 8.8 %factor_and_inverse.1 = (f32[256,256]{1,0:T(8,128)S(1)}, f32[256,256]{1,0:T(8,128)S(1)}) custom-call(f32[256,256]{1,0:T(8,128)S(1)} %split.8.gram_ref), custom_call_target="tpu_custom_call" | custom-call | flops 100000000 | bytes 1000000 | tf_op jit(solution)/shard_map/factor_and_inverse/pallas_call | solution.py:99
  77.4 1.6 %fusion = f32[256,1024]{1,0:T(8,128)} fusion(f32[256,256]{1,0:T(8,128)S(1)} %get-tuple-element.5, f32[256,1280]{1,0:T(8,128)S(1)} %bitcast.13), kind=kOutput, calls=%fused_computation.1 | convolution fusion | flops 402653184 | bytes 2359296 | tf_op jit(solution)/shard_map/dot_general | solution.py:142
  79.0 1.6 %fusion.2 = f32[1024,256]{1,0:T(8,128)} fusion(f32[1024,256]{1,0:T(8,128)S(1)} %fusion.6, f32[256,256]{1,0:T(8,128)S(1)} %get-tuple-element.5), kind=kOutput, calls=%fused_computation.3 | convolution fusion | flops 402718720 | bytes 2359296 | tf_op jit(solution)/shard_map/dot_general | solution.py:142
  80.6 0.7 broadcast_multiply_fusion
  (3 shorter events, 0.1 us)
Async XLA Ops:
  0.6 1.2 %copy-start = (f32[1024,256]{1,0:T(8,128)S(1)}, f32[1024,256]{1,0:T(8,128)}, u32[]{:S(2)}) copy-start(f32[1024,256]{1,0:T(8,128)} %param.3) | copy-start | bytes 3145732
  1.9 5.2 %copy-start.1 = (f32[1024,1024]{1,0:T(8,128)S(1)}, f32[1024,1024]{1,0:T(8,128)}, u32[]{:S(2)}) copy-start(f32[1024,1024]{1,0:T(8,128)} %param.2) | copy-start | bytes 12582916

commit v3 on v2

v3 whole, which is shorter than its diff:
```python
import jax, jax.numpy as jnp
from jax import lax
from jax.experimental import pallas as pl
from jax.experimental.pallas import tpu as pltpu
from jax.sharding import PartitionSpec as P

GROUP = 8
LANES = 128
PANEL = 64
BLOCK = 256
BLOCKS = 32
AXES = ("wide", "narrow")
VMEM = pl.BlockSpec(memory_space=pltpu.VMEM)


def factor_panel(a_ref, factor_ref, scale, base, height, size):
    lane = lax.broadcasted_iota(jnp.int32, (GROUP, LANES), 1)
    sub = lax.broadcasted_iota(jnp.int32, (GROUP, LANES), 0)
    tiles = size // LANES
    for top in range(base, base + height, GROUP):
        groups = list(range(top, base + height, GROUP))
        home = top // LANES
        offset = top - home * LANES
        inside = (lane >= offset) & (lane < offset + GROUP)
        rows = {}
        for g in groups:
            for t in range(tiles):
                rows[g, t] = a_ref[g:g + GROUP, t * LANES:(t + 1) * LANES]
        diag = rows[top, home]
        col = {}
        for g in groups:
            for j in range(GROUP):
                at = rows[g, home][:, offset + j:offset + j + 1]
                col[g, j] = jnp.broadcast_to(at, (GROUP, LANES))
        one = {}
        for j in range(GROUP):
            for k in range(j, GROUP):
                one[k, j] = jnp.broadcast_to(col[top, j][k:k + 1, :], (GROUP, LANES))
        for g in groups:
            fresh = jnp.where(lane == sub + offset, 1.0, 0.0) if g == top else 0.0
            rows[g, home] = jnp.where(inside, fresh, rows[g, home])
        for j in range(GROUP):
            inv = lax.rsqrt(one[j, j])
            low = {k: one[k, j] * inv for k in range(j + 1, GROUP)}
            for k in range(j + 1, GROUP):
                for m in range(k, GROUP):
                    one[m, k] = one[m, k] - low[m] * low[k]
            scaled = {g: col[g, j] * inv for g in groups}
            for k in range(j + 1, GROUP):
                for g in groups:
                    col[g, k] = col[g, k] - scaled[g] * low[k]
            pivot = {t: jnp.broadcast_to(rows[top, t][j:j + 1, :], (GROUP, LANES)) * inv for t in range(tiles)}
            pivot_diag = jnp.broadcast_to(diag[j:j + 1, :], (GROUP, LANES)) * inv
            below = jnp.where(sub > j, scaled[top], 0.0)
            diag = jnp.where(sub == j, pivot_diag, diag - below * pivot_diag)
            for t in range(tiles):
                rows[top, t] = jnp.where(sub == j, pivot[t], rows[top, t] - below * pivot[t])
                for g in groups[1:]:
                    rows[g, t] = rows[g, t] - scaled[g] * pivot[t]
        for g in groups:
            for t in range(tiles):
                a_ref[g:g + GROUP, t * LANES:(t + 1) * LANES] = rows[g, t]
        for t in range(tiles):
            span = slice(t * LANES, (t + 1) * LANES)
            if t < home:
                factor_ref[top:top + GROUP, span] = jnp.zeros((GROUP, LANES), jnp.float32)
            elif t == home:
                factor_ref[top:top + GROUP, span] = jnp.where(lane >= sub + offset, diag / scale, 0.0)
            else:
                factor_ref[top:top + GROUP, span] = rows[top, t] / scale


def trailing(a_ref, base, height, size):
    end = base + height
    if end == size:
        return
    panel = a_ref[base:end, :]
    col = lax.broadcasted_iota(jnp.int32, (height, size), 1)
    row = lax.broadcasted_iota(jnp.int32, (height, size), 0) + base
    right = jnp.where((col <= row) | (col >= end), panel, 0.0)
    left = panel[:, end:]
    update = lax.dot_general(left, right, (((0,), (0,)), ((), ())), precision=lax.Precision.HIGHEST, preferred_element_type=jnp.float32)
    rest = a_ref[end:, :]
    at = lax.broadcasted_iota(jnp.int32, (size - end, size), 1)
    a_ref[end:, :] = jnp.where((at >= base) & (at < end), 0.0, rest) - update


def split(value):
    high = value.astype(jnp.bfloat16)
    return high, (value - high.astype(jnp.float32)).astype(jnp.bfloat16)


def product(left, right, left_dim, right_dim):
    dims = (((left_dim,), (right_dim,)), ((), ()))
    dot = lambda a, b: lax.dot_general(a, b, dims, preferred_element_type=jnp.float32)
    return dot(left[0], right[0]) + (dot(left[0], right[1]) + dot(left[1], right[0]))


def core_bit():
    return lax.rem(lax.axis_index("wide"), 2)


def own_block():
    wide, narrow = lax.axis_index("wide"), lax.axis_index("narrow")
    plane = lax.rem(narrow, 2) + 2 * lax.rem(wide // 2, 2)
    return 16 * lax.rem(wide, 2) + 4 * plane + lax.rem(wide // 4, 4)


def rows_of(block, height):
    return pl.ds(pl.multiple_of(block * height, GROUP), height)


def local_kernel(features_ref, sketch_ref, sampled_ref, keep_ref, send_ref, gram_keep_ref, gram_send_ref, high_ref, low_ref, cross_ref, gram_ref, packed_ref):
    step = pl.program_id(0)

    @pl.when(step == 0)
    def _():
        high_ref[...], low_ref[...] = split(sketch_ref[...])
        cross_ref[...] = jnp.zeros_like(cross_ref)
        gram_ref[...] = jnp.zeros_like(gram_ref)

    features = split(features_ref[...])
    sampled = product(features, (high_ref[...], low_ref[...]), 1, 0)
    sampled_ref[...] = sampled
    parts = split(sampled)
    cross_ref[...] += product(parts, features, 0, 0)
    gram_ref[...] += product(parts, parts, 0, 0)

    @pl.when(step == pl.num_programs(0) - 1)
    def _():
        own = own_block()
        height = cross_ref.shape[0] // BLOCKS
        for at in range(BLOCKS):
            block = cross_ref[rows_of(at ^ own, height), :]
            if at < BLOCKS // 2:
                keep_ref[at * height:(at + 1) * height, :] = block
            else:
                rest = at - BLOCKS // 2
                send_ref[rest * height:(rest + 1) * height, :] = block
        packed_ref[:LANES, :] = gram_ref[:LANES, :LANES]
        packed_ref[LANES:2 * LANES, :] = gram_ref[:LANES, LANES:]
        packed_ref[2 * LANES:, :] = gram_ref[LANES:, LANES:]
        half = packed_ref.shape[0] // 2
        core = core_bit()
        gram_keep_ref[...] = packed_ref[rows_of(core, half), :]
        gram_send_ref[...] = packed_ref[rows_of(1 - core, half), :]


def local_terms(features, sketch):
    rows, depth = features.shape
    rank = sketch.shape[1]
    f32 = lambda *shape: jax.ShapeDtypeStruct(shape, jnp.float32)
    whole = lambda *shape: pl.BlockSpec(shape, lambda i: (0, 0))
    packed = 3 * LANES
    return pl.pallas_call(
        local_kernel,
        grid=(rows // BLOCK,),
        out_shape=(f32(rows, rank), f32(rank // 2, depth), f32(rank // 2, depth), f32(packed // 2, LANES), f32(packed // 2, LANES)),
        in_specs=[pl.BlockSpec((BLOCK, depth), lambda i: (i, 0)), whole(depth, rank)],
        out_specs=(
            pl.BlockSpec((BLOCK, rank), lambda i: (i, 0)),
            whole(rank // 2, depth), whole(rank // 2, depth),
            whole(packed // 2, LANES), whole(packed // 2, LANES),
        ),
        scratch_shapes=[
            pltpu.VMEM((depth, rank), jnp.bfloat16), pltpu.VMEM((depth, rank), jnp.bfloat16),
            pltpu.VMEM((rank, depth), jnp.float32), pltpu.VMEM((rank, rank), jnp.float32),
            pltpu.VMEM((packed, LANES), jnp.float32),
        ],
        compiler_params=pltpu.CompilerParams(vmem_limit_bytes=32 * 2**20),
        cost_estimate=pl.CostEstimate(flops=4 * 10**9, bytes_accessed=8 * 2**20, transcendentals=0),
        name="local_terms",
    )(features, sketch)


def factor_kernel(scale, first, last, *refs):
    if first == 0:
        keep_ref, other_ref, a_ref, factor_ref, packed_ref = refs
        half = keep_ref.shape[0]
        core = core_bit()
        packed_ref[rows_of(core, half), :] = keep_ref[...]
        packed_ref[rows_of(1 - core, half), :] = other_ref[...]
        a_ref[:LANES, :LANES] = packed_ref[:LANES, :]
        a_ref[:LANES, LANES:] = packed_ref[LANES:2 * LANES, :]
        a_ref[LANES:, :LANES] = jnp.zeros((LANES, LANES), jnp.float32)
        a_ref[LANES:, LANES:] = packed_ref[2 * LANES:, :]
    else:
        from_ref, upper_ref, a_ref, factor_ref = refs
        a_ref[...] = from_ref[...]
        factor_ref[...] = upper_ref[...]
    size = a_ref.shape[0]
    for base in range(first, last, PANEL):
        factor_panel(a_ref, factor_ref, scale, base, PANEL, size)
        trailing(a_ref, base, PANEL, size)
    if last == size:
        col = lax.broadcasted_iota(jnp.int32, (size, size), 1)
        row = lax.broadcasted_iota(jnp.int32, (size, size), 0)
        a_ref[...] = jnp.where(col <= row, a_ref[...], 0.0)


def factor_part(operands, size, scale, first, last):
    square = jax.ShapeDtypeStruct((size, size), jnp.float32)
    return pl.pallas_call(
        lambda *refs: factor_kernel(scale, first, last, *refs),
        out_shape=(square, square),
        in_specs=[VMEM] * 2,
        out_specs=(VMEM, VMEM),
        scratch_shapes=[pltpu.VMEM((3 * LANES, LANES), jnp.float32)] if first == 0 else [],
        compiler_params=pltpu.CompilerParams(vmem_limit_bytes=16 * 2**20),
        cost_estimate=pl.CostEstimate(flops=10**9 * (last - first) // size, bytes_accessed=2**20, transcendentals=last - first),
        name="factor_part",
    )(*operands)


def basis_kernel(scale, sampled_ref, inverse_ref, basis_ref):
    basis_ref[...] = product(split(sampled_ref[...]), split(inverse_ref[...] * scale), 1, 1)


def basis_of(sampled, inverse, scale):
    rows, rank = sampled.shape
    return pl.pallas_call(
        lambda *refs: basis_kernel(scale, *refs),
        grid=(rows // BLOCK,),
        out_shape=jax.ShapeDtypeStruct(sampled.shape, jnp.float32),
        in_specs=[pl.BlockSpec((BLOCK, rank), lambda i: (i, 0)), pl.BlockSpec((rank, rank), lambda i: (0, 0))],
        out_specs=pl.BlockSpec((BLOCK, rank), lambda i: (i, 0)),
        cost_estimate=pl.CostEstimate(flops=4 * 10**8, bytes_accessed=2 * 2**20, transcendentals=0),
        name="basis",
    )(sampled, inverse)


def project_kernel(inverse_ref, *refs):
    *pieces, projection_ref, cross_ref = refs
    own = own_block()
    height = cross_ref.shape[0] // BLOCKS
    at = 0
    for piece in pieces:
        for top in range(0, piece.shape[0], height):
            cross_ref[rows_of(at ^ own, height), :] = piece[top:top + height, :]
            at += 1
    inverse = split(inverse_ref[...])
    for left in range(0, cross_ref.shape[1], BLOCK):
        span = slice(left, left + BLOCK)
        projection_ref[:, span] = product(inverse, split(cross_ref[:, span]), 1, 0)


def project(inverse, pieces):
    rank = inverse.shape[0]
    depth = pieces[0].shape[1]
    return pl.pallas_call(
        project_kernel,
        out_shape=jax.ShapeDtypeStruct((rank, depth), jnp.float32),
        in_specs=[VMEM] * (1 + len(pieces)),
        out_specs=VMEM,
        scratch_shapes=[pltpu.VMEM((rank, depth), jnp.float32)],
        compiler_params=pltpu.CompilerParams(vmem_limit_bytes=16 * 2**20),
        cost_estimate=pl.CostEstimate(flops=4 * 10**8, bytes_accessed=2 * 2**20, transcendentals=0),
        name="project",
    )(inverse, *pieces)


def send(value, wide, narrow):
    mask = wide * lax.axis_size("narrow") + narrow
    pairs = [(source, source ^ mask) for source in range(lax.axis_size(AXES))]
    return lax.ppermute(value, AXES, pairs)


CORE = (1, 0)
PLANE = [(0, 1), (2, 0), (2, 1)]
LINE = [(4, 0), (8, 0), (12, 0)]


def spare_bits():
    wide = [(2**bit, 0) for bit in range(4, lax.axis_size("wide").bit_length() - 1)]
    narrow = [(0, 2**bit) for bit in range(1, lax.axis_size("narrow").bit_length() - 1)]
    return wide + narrow


def sum_gram(keep, other):
    half = keep + send(other, *CORE)
    for mask in [(0, 1), (2, 0), (4, 0), (8, 0)] + spare_bits():
        half = half + send(half, *mask)
    return half, send(half, *CORE)


def quarters(values):
    height = values[0].shape[0] // 4
    return [sum(value[at * height:(at + 1) * height] for value in values) for at in range(4)]


def scatter(values, masks):
    first, *rest = quarters(values)
    return [first] + [send(part, *mask) for part, mask in zip(rest, masks)]


def sum_cross(keep, other):
    values = scatter([keep, send(other, *CORE)], PLANE)
    values = scatter(values, LINE)
    own = sum(values)
    for mask in spare_bits():
        own = own + send(own, *mask)
    line = jnp.concatenate([own] + [send(own, *mask) for mask in LINE])
    plane = [line] + [send(line, *mask) for mask in PLANE]
    return plane + [send(part, *CORE) for part in plane]


def per_device(features, sketch):
    scale = (features.shape[0] * lax.axis_size(AXES)) ** 0.5
    size = sketch.shape[1]
    sampled, keep, other, gram_keep, gram_other = local_terms(features, sketch)
    gram = sum_gram(gram_keep, gram_other)
    cross = sum_cross(keep, other)
    state = factor_part(gram, size, scale, 0, size // 2)
    inverse, factor = factor_part(state, size, scale, size // 2, size)
    return (basis_of(sampled, inverse, scale), factor, project(inverse, cross))


def solution(mesh):
    rows = P(AXES, None)
    return jax.shard_map(
        per_device, mesh=mesh, in_specs=(rows, P()), out_specs=(rows, P(), P()), check_vma=False
    )
```

time: 81.7 us -> 70.7 us (0.87)
  blocking collectives: 58.1 us -> 0 us
  starting transfers between devices: 0 us -> 23.6 us
  waiting for transfers between devices: 0 us -> 17.8 us
  Pallas kernels: 8.8 us -> 22.9 us
  matrix products: 10.5 us -> 0 us
  local copies, waits for them, and re-layouts: 1.37 us -> 5.05 us
  other arithmetic: 1.83 us -> 0.2 us
    all_to_all x4 -> x0, blocking collectives: 58.1 us -> none  [exchange(): return lax.all_to_all(blocks, axes, 0, 0, tiled=True)]
    ppermute x0 -> x23, starting transfers between devices: none -> 23.6 us  [send(): return lax.ppermute(value, AXES, pairs)]
    ppermute x0 -> x23, waiting for transfers between devices: none -> 17.8 us  [send(): return lax.ppermute(value, AXES, pairs)]
    pallas_call x1 -> x5, Pallas kernels: 8.8 us -> 22.9 us  [the longest x2 9.52 us: factor_part(): pl.pallas_call(lambda *refs: factor_kernel(scale, first, last, *refs), ou...]
    dot_general x5 -> x0, matrix products: 10.5 us -> none  [per_device(): jnp.dot(a, b, preferred_element_type=jnp.float32, precision=high)]
    unnamed x4 -> x10, local copies, waits for them, and re-layouts: 1.23 us -> 5.05 us
    reduce_sum x2 -> x0, other arithmetic: 1.01 us -> none  [scatter_sum(): return jnp.sum(exchange(blocks, axes), axis=0)]
  transfers between devices with their start and end apart: 0 -> 23, of which waited for: 0 -> 9; matrix products, arithmetic and copies ran while one was open for 0% -> 0% of each run, Pallas kernels for 0% -> 19%
where the time goes in v3:
time: 70.7 us; the launch traced here: 70.4 us
  starting transfers between devices  23.6 us (33%)
  Pallas kernels  22.9 us (32%)
  waiting for transfers between devices  17.8 us (25%)
  local copies, waits for them, and re-layouts  5.05 us (7%)
  between operations  0.75 us (1%)
    ppermute x23, starting transfers between devices, send(): return lax.ppermute(value, AXES, pairs)  23.6 us
    ppermute x23, waiting for transfers between devices, send(): return lax.ppermute(value, AXES, pairs)  17.8 us
    pallas_call x2, Pallas kernels, factor_part(): pl.pallas_call(lambda *refs: factor_kernel(scale, first, last, *refs), ou...  9.52 us
    pallas_call x1, Pallas kernels, local_terms(): pl.pallas_call(local_kernel, grid=(rows // BLOCK,), out_shape=(f32(rows,...  7.75 us
    unnamed x10, local copies, waits for them, and re-layouts  5.05 us
    pallas_call x1, Pallas kernels, basis_of(): pl.pallas_call(lambda *refs: basis_kernel(scale, *refs), grid=(rows // BL...  4.02 us
    pallas_call x1, Pallas kernels, project(): pl.pallas_call(project_kernel, out_shape=jax.ShapeDtypeStruct((rank, dept...  1.65 us
  transfers between devices with their start and end apart: 23, of which 9 were waited for; matrix products, arithmetic and copies ran while one was open for 0% of the time, Pallas kernels for 19%

profile of v3, /device:TPU:0, one launch (start us, length us, event | category | flops | bytes accessed | tf_op | source)
XLA Modules:
  0.0 70.4 jit_solution(14079747240222443420)
XLA Ops:
  0.6 0.0 copy-start.3
  0.6 2.2 %copy-done.3 = f32[1024,1024]{1,0:T(8,128)S(1)} copy-done((f32[1024,1024]{1,0:T(8,128)S(1)}, f32[1024,1024]{1,0:T(8,128)}, u32[]{:S(2)}) %copy-start.3) | copy-done | bytes 4194328
  2.8 0.0 copy-start.4
  2.8 1.2 %copy-done.4 = f32[1024,256]{1,0:T(8,128)S(1)} copy-done((f32[1024,256]{1,0:T(8,128)S(1)}, f32[1024,256]{1,0:T(8,128)}, u32[]{:S(2)}) %copy-start.4) | copy-done | bytes 1048600
  4.0 7.8 %local_terms.1 = (f32[1024,256]{1,0:T(8,128)S(1)}, f32[128,1024]{1,0:T(8,128)S(1)}, f32[128,1024]{1,0:T(8,128)S(1)}, f32[192,128]{1,0:T(8,128)S(1)}, f32[192,128]{1,0:T(8,128)S(1)}) custom-call(f32[1024,1024]{1,0:T(8,128)S(1)} %copy-done.3, f32[1024,256]{1,0:T(8,128)S(1)} %copy-done.4), custom_call_target="tpu_custom_call" | custom-call | flops 4000000000 | bytes 8388608 | tf_op jit(solution)/shard_map/local_terms/pallas_call | solution.py:155
  11.8 0.0 copy-start.2
  11.8 0.5 collective-permute-start.6
  12.3 0.1 collective-permute-start
  12.4 1.5 %collective-permute-done.6 = f32[128,1024]{1,0:T(8,128)S(1)} collective-permute-done((f32[128,1024]{1,0:T(8,128)S(1)}, f32[128,1024]{1,0:T(8,128)S(1)}, u32[]{:S(2)}, u32[]{:S(2)}) %collective-permute-start.6) | collective-permute-done | bytes 524320 | tf_op jit(solution)/shard_map/ppermute | solution.py:265
  13.9 0.1 slice_add_fusion.3
  13.9 3.9 %collective-permute-start.9 = (f32[32,1024]{1,0:T(8,128)S(1)}, f32[32,1024]{1,0:T(8,128)S(1)}, u32[]{:S(2)}, u32[]{:S(2)}) collective-permute-start(f32[32,1024]{1,0:T(8,128)S(1)} %get-tuple-element.22), channel_id=1, source_target_pairs={{0,5},{1,4},{2,7},{3,6},{4,1},{5,0},{6,3},{7,2},{8,13},{9,12},{10,... | collective-permute-start | bytes 393224 | tf_op jit(solution)/shard_map/ppermute | solution.py:265
  17.8 0.5 collective-permute-start.8
  18.4 0.1 collective-permute-start.7
  18.5 0.0 collective-permute-done
  18.5 2.0 %collective-permute-start.1 = (f32[192,128]{1,0:T(8,128)S(1)}, f32[192,128]{1,0:T(8,128)S(1)}, u32[]{:S(2)}, u32[]{:S(2)}) collective-permute-start(f32[192,128]{1,0:T(8,128)S(1)} %add.72), channel_id=1, source_target_pairs={{0,1},{1,0},{2,3},{3,2},{4,5},{5,4},{6,7},{7,6},{8,9},{9,8},{10,11... | collective-permute-start | bytes 294920 | tf_op jit(solution)/shard_map/ppermute | solution.py:265
  20.5 6.1 %collective-permute-done.1 = f32[192,128]{1,0:T(8,128)S(1)} collective-permute-done((f32[192,128]{1,0:T(8,128)S(1)}, f32[192,128]{1,0:T(8,128)S(1)}, u32[]{:S(2)}, u32[]{:S(2)}) %collective-permute-start.1) | collective-permute-done | bytes 98336 | tf_op jit(solution)/shard_map/ppermute | solution.py:265
  26.6 1.7 %collective-permute-start.2 = (f32[192,128]{1,0:T(8,128)S(1)}, f32[192,128]{1,0:T(8,128)S(1)}, u32[]{:S(2)}, u32[]{:S(2)}) collective-permute-start(f32[192,128]{1,0:T(8,128)S(1)} %add.73), channel_id=1, source_target_pairs={{0,4},{1,5},{2,6},{3,7},{4,0},{5,1},{6,2},{7,3},{8,12},{9,13},{10,... | collective-permute-start | bytes 294920 | tf_op jit(solution)/shard_map/ppermute | solution.py:265
  28.3 0.0 collective-permute-done.9
  28.3 0.0 collective-permute-done.8
  28.3 0.0 collective-permute-done.7
  28.4 1.6 %collective-permute-start.10 = (f32[8,1024]{1,0:T(8,128)S(1)}, f32[8,1024]{1,0:T(8,128)S(1)}, u32[]{:S(2)}, u32[]{:S(2)}) collective-permute-start(f32[8,1024]{1,0:T(8,128)S(1)} %get-tuple-element.25), channel_id=1, source_target_pairs={{0,8},{1,9},{2,10},{3,11},{4,12},{5,13},{6,14},{7,15},{8,0},{9,1},... | collective-permute-start | bytes 98312 | tf_op jit(solution)/shard_map/ppermute | solution.py:265
  30.0 2.5 %collective-permute-start.12 = (f32[8,1024]{1,0:T(8,128)S(1)}, f32[8,1024]{1,0:T(8,128)S(1)}, u32[]{:S(2)}, u32[]{:S(2)}) collective-permute-start(f32[8,1024]{1,0:T(8,128)S(1)} %get-tuple-element.26), channel_id=1, source_target_pairs={{0,24},{1,25},{2,26},{3,27},{4,28},{5,29},{6,30},{7,31},{8,16},{9,... | collective-permute-start | bytes 98312 | tf_op jit(solution)/shard_map/ppermute | solution.py:265
  32.5 0.1 collective-permute-start.11
  32.6 0.0 collective-permute-done.2
  32.6 1.9 %collective-permute-start.3 = (f32[192,128]{1,0:T(8,128)S(1)}, f32[192,128]{1,0:T(8,128)S(1)}, u32[]{:S(2)}, u32[]{:S(2)}) collective-permute-start(f32[192,128]{1,0:T(8,128)S(1)} %add.74), channel_id=1, source_target_pairs={{0,8},{1,9},{2,10},{3,11},{4,12},{5,13},{6,14},{7,15},{8,0},{9,1},... | collective-permute-start | bytes 294920 | tf_op jit(solution)/shard_map/ppermute | solution.py:265
  34.5 0.0 collective-permute-done.10
  34.5 1.2 %collective-permute-done.12 = f32[8,1024]{1,0:T(8,128)S(1)} collective-permute-done((f32[8,1024]{1,0:T(8,128)S(1)}, f32[8,1024]{1,0:T(8,128)S(1)}, u32[]{:S(2)}, u32[]{:S(2)}) %collective-permute-start.12) | collective-permute-done | bytes 32800 | tf_op jit(solution)/shard_map/ppermute | solution.py:265
  35.7 1.9 %collective-permute-done.11 = f32[8,1024]{1,0:T(8,128)S(1)} collective-permute-done((f32[8,1024]{1,0:T(8,128)S(1)}, f32[8,1024]{1,0:T(8,128)S(1)}, u32[]{:S(2)}, u32[]{:S(2)}) %collective-permute-start.11) | collective-permute-done | bytes 32800 | tf_op jit(solution)/shard_map/ppermute | solution.py:265
  37.7 1.4 %collective-permute-start.15 = (f32[8,1024]{1,0:T(8,128)S(1)}, f32[8,1024]{1,0:T(8,128)S(1)}, u32[]{:S(2)}, u32[]{:S(2)}) collective-permute-start(f32[8,1024]{1,0:T(8,128)S(1)} %fusion.2), channel_id=1, source_target_pairs={{0,24},{1,25},{2,26},{3,27},{4,28},{5,29},{6,30},{7,31},{8,16},{9,... | collective-permute-start | bytes 98312 | tf_op jit(solution)/shard_map/ppermute | solution.py:265
  39.1 0.5 collective-permute-start.14
  39.6 2.5 %collective-permute-start.13 = (f32[8,1024]{1,0:T(8,128)S(1)}, f32[8,1024]{1,0:T(8,128)S(1)}, u32[]{:S(2)}, u32[]{:S(2)}) collective-permute-start(f32[8,1024]{1,0:T(8,128)S(1)} %fusion.2), channel_id=1, source_target_pairs={{0,8},{1,9},{2,10},{3,11},{4,12},{5,13},{6,14},{7,15},{8,0},{9,1},... | collective-permute-start | bytes 98312 | tf_op jit(solution)/shard_map/ppermute | solution.py:265
  42.1 0.0 collective-permute-done.3
  42.1 0.1 collective-permute-start.4
  42.2 1.7 %collective-permute-done.15 = f32[8,1024]{1,0:T(8,128)S(1)} collective-permute-done((f32[8,1024]{1,0:T(8,128)S(1)}, f32[8,1024]{1,0:T(8,128)S(1)}, u32[]{:S(2)}, u32[]{:S(2)}) %collective-permute-start.15) | collective-permute-done | bytes 32800 | tf_op jit(solution)/shard_map/ppermute | solution.py:265
  43.9 1.4 %collective-permute-done.14 = f32[8,1024]{1,0:T(8,128)S(1)} collective-permute-done((f32[8,1024]{1,0:T(8,128)S(1)}, f32[8,1024]{1,0:T(8,128)S(1)}, u32[]{:S(2)}, u32[]{:S(2)}) %collective-permute-start.14) | collective-permute-done | bytes 32800 | tf_op jit(solution)/shard_map/ppermute | solution.py:265
  45.2 0.0 collective-permute-done.13
  45.3 1.8 %collective-permute-start.18 = (f32[32,1024]{1,0:T(8,128)S(1)}, f32[32,1024]{1,0:T(8,128)S(1)}, u32[]{:S(2)}, u32[]{:S(2)}) collective-permute-start(f32[32,1024]{1,0:T(8,128)S(1)} %pad_maximum_fusion.refs_0_), channel_id=1, source_target_pairs={{0,5},{1,4},{2,7},{3,6},{4,1},{5,0},{6,3},{7,2},{8,13},{9,12},{10,... | collective-permute-start | bytes 393224 | tf_op jit(solution)/shard_map/ppermute | solution.py:265
  47.0 1.5 %collective-permute-start.17 = (f32[32,1024]{1,0:T(8,128)S(1)}, f32[32,1024]{1,0:T(8,128)S(1)}, u32[]{:S(2)}, u32[]{:S(2)}) collective-permute-start(f32[32,1024]{1,0:T(8,128)S(1)} %pad_maximum_fusion.refs_0_), channel_id=1, source_target_pairs={{0,4},{1,5},{2,6},{3,7},{4,0},{5,1},{6,2},{7,3},{8,12},{9,13},{10,... | collective-permute-start | bytes 393224 | tf_op jit(solution)/shard_map/ppermute | solution.py:265
  48.5 0.3 collective-permute-start.16
  48.8 0.0 collective-permute-done.4
  48.8 0.1 collective-permute-start.5
  48.9 0.5 collective-permute-start.19
  49.4 1.8 %collective-permute-done.18.refs_3_ = f32[32,1024]{1,0:T(8,128)S(1)} collective-permute-done((f32[32,1024]{1,0:T(8,128)S(1)}, f32[32,1024]{1,0:T(8,128)S(1)}, u32[]{:S(2)}, u32[]{:S(2)}) %collective-permute-start.18) | collective-permute-done | bytes 131104 | tf_op jit(solution)/shard_map/ppermute | solution.py:265
  51.2 0.0 collective-permute-start.22
  51.2 1.7 %collective-permute-done.17.refs_2_ = f32[32,1024]{1,0:T(8,128)S(1)} collective-permute-done((f32[32,1024]{1,0:T(8,128)S(1)}, f32[32,1024]{1,0:T(8,128)S(1)}, u32[]{:S(2)}, u32[]{:S(2)}) %collective-permute-start.17) | collective-permute-done | bytes 131104 | tf_op jit(solution)/shard_map/ppermute | solution.py:265
  52.9 0.0 collective-permute-start.21
  52.9 0.6 collective-permute-done.16.refs_1_
  53.5 0.0 collective-permute-start.20
  53.5 0.0 collective-permute-done.5.refs_1_
  53.5 4.7 %factor_part.2 = (f32[256,256]{1,0:T(8,128)S(1)}, f32[256,256]{1,0:T(8,128)S(1)}) custom-call(f32[192,128]{1,0:T(8,128)S(1)} %add.76.refs_0_, f32[192,128]{1,0:T(8,128)S(1)} %collective-permute-done.5.refs_1_), custom_call_target="tpu_custom_call" | custom-call | flops 500000000 | bytes 1048576 | tf_op jit(solution)/shard_map/factor_part/pallas_call | solution.py:203
  58.2 4.8 %factor_part.3 = (f32[256,256]{1,0:T(8,128)S(1)}, f32[256,256]{1,0:T(8,128)}) custom-call(f32[256,256]{1,0:T(8,128)S(1)} %get-tuple-element.15.refs_0_, f32[256,256]{1,0:T(8,128)S(1)} %get-tuple-element.16.refs_1_), custom_call_target="tpu_custom_call" | custom-call | flops 500000000 | bytes 1048576 | tf_op jit(solution)/shard_map/factor_part/pallas_call | solution.py:203
  63.0 0.0 copy-done.2
  63.1 0.0 copy-start
  63.1 0.7 copy-done
  63.7 4.0 %basis.1 = f32[1024,256]{1,0:T(8,128)} custom-call(f32[1024,256]{1,0:T(8,128)} %copy-done.2, f32[256,256]{1,0:T(8,128)} %copy-done), custom_call_target="tpu_custom_call" | custom-call | flops 400000000 | bytes 2097152 | tf_op jit(solution)/shard_map/basis/pallas_call | solution.py:221
  67.8 0.0 collective-permute-done.19.refs_4_
  67.8 0.0 collective-permute-done.22.refs_7_
  67.8 0.0 collective-permute-done.21.refs_6_
  67.8 0.0 collective-permute-done.20.refs_5_
  67.8 0.0 copy-start.1
  67.8 0.9 %copy-done.1 = f32[256,256]{1,0:T(8,128)S(1)} copy-done((f32[256,256]{1,0:T(8,128)S(1)}, f32[256,256]{1,0:T(8,128)}, u32[]{:S(2)}) %copy-start.1) | copy-done | bytes 262168
  68.8 1.7 %project.1 = f32[256,1024]{1,0:T(8,128)} custom-call(f32[256,256]{1,0:T(8,128)S(1)} %copy-done.1, f32[32,1024]{1,0:T(8,128)S(1)} %pad_maximum_fusion.refs_0_, f32[32,1024]{1,0:T(8,128)S(1)} %collective-permute-done.16.refs_1_, f32[32,1024]{1,0:T(8,128)S(1)} %collective-permute-done.17.refs_2_, f32[32,1024]{1,0:T(8,128)S(1)} %collective-permute-done.18.refs_3_, ...), custom_call_target="tpu_custom_call" | custom-call | flops 400000000 | bytes 2097152 | tf_op jit(solution)/shard_map/project/pallas_call | solution.py:250
  (8 shorter events, 0.1 us)
Async XLA Ops:
  0.6 2.2 %copy-start.3 = (f32[1024,1024]{1,0:T(8,128)S(1)}, f32[1024,1024]{1,0:T(8,128)}, u32[]{:S(2)}) copy-start(f32[1024,1024]{1,0:T(8,128)} %features_ref.1) | copy-start | bytes 12582916
  2.8 1.2 %copy-start.4 = (f32[1024,256]{1,0:T(8,128)S(1)}, f32[1024,256]{1,0:T(8,128)}, u32[]{:S(2)}) copy-start(f32[1024,256]{1,0:T(8,128)} %sketch_ref.1) | copy-start | bytes 3145732
  11.8 51.2 %copy-start.2 = (f32[1024,256]{1,0:T(8,128)}, f32[1024,256]{1,0:T(8,128)S(1)}, u32[]{:S(2)}) copy-start(f32[1024,256]{1,0:T(8,128)S(1)} %get-tuple-element.12.refs_0_) | copy-start | bytes 3145732
  11.8 2.1 %collective-permute-start.6 = (f32[128,1024]{1,0:T(8,128)S(1)}, f32[128,1024]{1,0:T(8,128)S(1)}, u32[]{:S(2)}, u32[]{:S(2)}) collective-permute-start(f32[128,1024]{1,0:T(8,128)S(1)} %get-tuple-element.20), channel_id=1, source_target_pairs={{0,2},{1,3},{2,0},{3,1},{4,6},{5,7},{6,4},{7,5},{8,10},{9,11},{10,... | collective-permute-start | bytes 1572872 | tf_op jit(solution)/shard_map/ppermute | solution.py:265
  12.3 6.1 %collective-permute-start = (f32[192,128]{1,0:T(8,128)S(1)}, f32[192,128]{1,0:T(8,128)S(1)}, u32[]{:S(2)}, u32[]{:S(2)}) collective-permute-start(f32[192,128]{1,0:T(8,128)S(1)} %get-tuple-element.14), channel_id=1, source_target_pairs={{0,2},{1,3},{2,0},{3,1},{4,6},{5,7},{6,4},{7,5},{8,10},{9,11},{10,... | collective-permute-start | bytes 294920 | tf_op jit(solution)/shard_map/ppermute | solution.py:265
  13.9 14.4 %collective-permute-start.9 = (f32[32,1024]{1,0:T(8,128)S(1)}, f32[32,1024]{1,0:T(8,128)S(1)}, u32[]{:S(2)}, u32[]{:S(2)}) collective-permute-start(f32[32,1024]{1,0:T(8,128)S(1)} %get-tuple-element.22), channel_id=1, source_target_pairs={{0,5},{1,4},{2,7},{3,6},{4,1},{5,0},{6,3},{7,2},{8,13},{9,12},{10,... | collective-permute-start | bytes 393224 | tf_op jit(solution)/shard_map/ppermute | solution.py:265
  17.8 10.5 %collective-permute-start.8 = (f32[32,1024]{1,0:T(8,128)S(1)}, f32[32,1024]{1,0:T(8,128)S(1)}, u32[]{:S(2)}, u32[]{:S(2)}) collective-permute-start(f32[32,1024]{1,0:T(8,128)S(1)} %get-tuple-element.23), channel_id=1, source_target_pairs={{0,4},{1,5},{2,6},{3,7},{4,0},{5,1},{6,2},{7,3},{8,12},{9,13},{10,... | collective-permute-start | bytes 393224 | tf_op jit(solution)/shard_map/ppermute | solution.py:265
  18.4 10.0 %collective-permute-start.7 = (f32[32,1024]{1,0:T(8,128)S(1)}, f32[32,1024]{1,0:T(8,128)S(1)}, u32[]{:S(2)}, u32[]{:S(2)}) collective-permute-start(f32[32,1024]{1,0:T(8,128)S(1)} %get-tuple-element.24), channel_id=1, source_target_pairs={{0,1},{1,0},{2,3},{3,2},{4,5},{5,4},{6,7},{7,6},{8,9},{9,8},{10,11... | collective-permute-start | bytes 393224 | tf_op jit(solution)/shard_map/ppermute | solution.py:265
  18.5 8.1 %collective-permute-start.1 = (f32[192,128]{1,0:T(8,128)S(1)}, f32[192,128]{1,0:T(8,128)S(1)}, u32[]{:S(2)}, u32[]{:S(2)}) collective-permute-start(f32[192,128]{1,0:T(8,128)S(1)} %add.72), channel_id=1, source_target_pairs={{0,1},{1,0},{2,3},{3,2},{4,5},{5,4},{6,7},{7,6},{8,9},{9,8},{10,11... | collective-permute-start | bytes 294920 | tf_op jit(solution)/shard_map/ppermute | solution.py:265
  26.6 6.0 %collective-permute-start.2 = (f32[192,128]{1,0:T(8,128)S(1)}, f32[192,128]{1,0:T(8,128)S(1)}, u32[]{:S(2)}, u32[]{:S(2)}) collective-permute-start(f32[192,128]{1,0:T(8,128)S(1)} %add.73), channel_id=1, source_target_pairs={{0,4},{1,5},{2,6},{3,7},{4,0},{5,1},{6,2},{7,3},{8,12},{9,13},{10,... | collective-permute-start | bytes 294920 | tf_op jit(solution)/shard_map/ppermute | solution.py:265
  28.4 6.1 %collective-permute-start.10 = (f32[8,1024]{1,0:T(8,128)S(1)}, f32[8,1024]{1,0:T(8,128)S(1)}, u32[]{:S(2)}, u32[]{:S(2)}) collective-permute-start(f32[8,1024]{1,0:T(8,128)S(1)} %get-tuple-element.25), channel_id=1, source_target_pairs={{0,8},{1,9},{2,10},{3,11},{4,12},{5,13},{6,14},{7,15},{8,0},{9,1},... | collective-permute-start | bytes 98312 | tf_op jit(solution)/shard_map/ppermute | solution.py:265
  30.0 5.7 %collective-permute-start.12 = (f32[8,1024]{1,0:T(8,128)S(1)}, f32[8,1024]{1,0:T(8,128)S(1)}, u32[]{:S(2)}, u32[]{:S(2)}) collective-permute-start(f32[8,1024]{1,0:T(8,128)S(1)} %get-tuple-element.26), channel_id=1, source_target_pairs={{0,24},{1,25},{2,26},{3,27},{4,28},{5,29},{6,30},{7,31},{8,16},{9,... | collective-permute-start | bytes 98312 | tf_op jit(solution)/shard_map/ppermute | solution.py:265
  32.5 5.2 %collective-permute-start.11 = (f32[8,1024]{1,0:T(8,128)S(1)}, f32[8,1024]{1,0:T(8,128)S(1)}, u32[]{:S(2)}, u32[]{:S(2)}) collective-permute-start(f32[8,1024]{1,0:T(8,128)S(1)} %get-tuple-element.27), channel_id=1, source_target_pairs={{0,16},{1,17},{2,18},{3,19},{4,20},{5,21},{6,22},{7,23},{8,24},{9,... | collective-permute-start | bytes 98312 | tf_op jit(solution)/shard_map/ppermute | solution.py:265
  32.6 9.5 %collective-permute-start.3 = (f32[192,128]{1,0:T(8,128)S(1)}, f32[192,128]{1,0:T(8,128)S(1)}, u32[]{:S(2)}, u32[]{:S(2)}) collective-permute-start(f32[192,128]{1,0:T(8,128)S(1)} %add.74), channel_id=1, source_target_pairs={{0,8},{1,9},{2,10},{3,11},{4,12},{5,13},{6,14},{7,15},{8,0},{9,1},... | collective-permute-start | bytes 294920 | tf_op jit(solution)/shard_map/ppermute | solution.py:265
  37.7 6.2 %collective-permute-start.15 = (f32[8,1024]{1,0:T(8,128)S(1)}, f32[8,1024]{1,0:T(8,128)S(1)}, u32[]{:S(2)}, u32[]{:S(2)}) collective-permute-start(f32[8,1024]{1,0:T(8,128)S(1)} %fusion.2), channel_id=1, source_target_pairs={{0,24},{1,25},{2,26},{3,27},{4,28},{5,29},{6,30},{7,31},{8,16},{9,... | collective-permute-start | bytes 98312 | tf_op jit(solution)/shard_map/ppermute | solution.py:265
  39.1 6.2 %collective-permute-start.14 = (f32[8,1024]{1,0:T(8,128)S(1)}, f32[8,1024]{1,0:T(8,128)S(1)}, u32[]{:S(2)}, u32[]{:S(2)}) collective-permute-start(f32[8,1024]{1,0:T(8,128)S(1)} %fusion.2), channel_id=1, source_target_pairs={{0,16},{1,17},{2,18},{3,19},{4,20},{5,21},{6,22},{7,23},{8,24},{9,... | collective-permute-start | bytes 98312 | tf_op jit(solution)/shard_map/ppermute | solution.py:265
  39.6 5.6 %collective-permute-start.13 = (f32[8,1024]{1,0:T(8,128)S(1)}, f32[8,1024]{1,0:T(8,128)S(1)}, u32[]{:S(2)}, u32[]{:S(2)}) collective-permute-start(f32[8,1024]{1,0:T(8,128)S(1)} %fusion.2), channel_id=1, source_target_pairs={{0,8},{1,9},{2,10},{3,11},{4,12},{5,13},{6,14},{7,15},{8,0},{9,1},... | collective-permute-start | bytes 98312 | tf_op jit(solution)/shard_map/ppermute | solution.py:265
  42.1 6.7 %collective-permute-start.4 = (f32[192,128]{1,0:T(8,128)S(1)}, f32[192,128]{1,0:T(8,128)S(1)}, u32[]{:S(2)}, u32[]{:S(2)}) collective-permute-start(f32[192,128]{1,0:T(8,128)S(1)} %add.75), channel_id=1, source_target_pairs={{0,16},{1,17},{2,18},{3,19},{4,20},{5,21},{6,22},{7,23},{8,24},{9,... | collective-permute-start | bytes 294920 | tf_op jit(solution)/shard_map/ppermute | solution.py:265
  45.3 5.9 %collective-permute-start.18 = (f32[32,1024]{1,0:T(8,128)S(1)}, f32[32,1024]{1,0:T(8,128)S(1)}, u32[]{:S(2)}, u32[]{:S(2)}) collective-permute-start(f32[32,1024]{1,0:T(8,128)S(1)} %pad_maximum_fusion.refs_0_), channel_id=1, source_target_pairs={{0,5},{1,4},{2,7},{3,6},{4,1},{5,0},{6,3},{7,2},{8,13},{9,12},{10,... | collective-permute-start | bytes 393224 | tf_op jit(solution)/shard_map/ppermute | solution.py:265
  47.0 5.8 %collective-permute-start.17 = (f32[32,1024]{1,0:T(8,128)S(1)}, f32[32,1024]{1,0:T(8,128)S(1)}, u32[]{:S(2)}, u32[]{:S(2)}) collective-permute-start(f32[32,1024]{1,0:T(8,128)S(1)} %pad_maximum_fusion.refs_0_), channel_id=1, source_target_pairs={{0,4},{1,5},{2,6},{3,7},{4,0},{5,1},{6,2},{7,3},{8,12},{9,13},{10,... | collective-permute-start | bytes 393224 | tf_op jit(solution)/shard_map/ppermute | solution.py:265
  48.5 5.0 %collective-permute-start.16 = (f32[32,1024]{1,0:T(8,128)S(1)}, f32[32,1024]{1,0:T(8,128)S(1)}, u32[]{:S(2)}, u32[]{:S(2)}) collective-permute-start(f32[32,1024]{1,0:T(8,128)S(1)} %pad_maximum_fusion.refs_0_), channel_id=1, source_target_pairs={{0,1},{1,0},{2,3},{3,2},{4,5},{5,4},{6,7},{7,6},{8,9},{9,8},{10,11... | collective-permute-start | bytes 393224 | tf_op jit(solution)/shard_map/ppermute | solution.py:265
  48.8 4.7 %collective-permute-start.5 = (f32[192,128]{1,0:T(8,128)S(1)}, f32[192,128]{1,0:T(8,128)S(1)}, u32[]{:S(2)}, u32[]{:S(2)}) collective-permute-start(f32[192,128]{1,0:T(8,128)S(1)} %add.76.refs_0_), channel_id=1, source_target_pairs={{0,2},{1,3},{2,0},{3,1},{4,6},{5,7},{6,4},{7,5},{8,10},{9,11},{10,... | collective-permute-start | bytes 294920 | tf_op jit(solution)/shard_map/ppermute | solution.py:265
  48.9 18.9 %collective-permute-start.19 = (f32[32,1024]{1,0:T(8,128)S(1)}, f32[32,1024]{1,0:T(8,128)S(1)}, u32[]{:S(2)}, u32[]{:S(2)}) collective-permute-start(f32[32,1024]{1,0:T(8,128)S(1)} %pad_maximum_fusion.refs_0_), channel_id=1, source_target_pairs={{0,2},{1,3},{2,0},{3,1},{4,6},{5,7},{6,4},{7,5},{8,10},{9,11},{10,... | collective-permute-start | bytes 393224 | tf_op jit(solution)/shard_map/ppermute | solution.py:265
  51.2 16.6 %collective-permute-start.22 = (f32[32,1024]{1,0:T(8,128)S(1)}, f32[32,1024]{1,0:T(8,128)S(1)}, u32[]{:S(2)}, u32[]{:S(2)}) collective-permute-start(f32[32,1024]{1,0:T(8,128)S(1)} %collective-permute-done.18.refs_3_), channel_id=1, source_target_pairs={{0,2},{1,3},{2,0},{3,1},{4,6},{5,7},{6,4},{7,5},{8,10},{9,11},{10,... | collective-permute-start | bytes 393224 | tf_op jit(solution)/shard_map/ppermute | solution.py:265
  52.9 14.9 %collective-permute-start.21 = (f32[32,1024]{1,0:T(8,128)S(1)}, f32[32,1024]{1,0:T(8,128)S(1)}, u32[]{:S(2)}, u32[]{:S(2)}) collective-permute-start(f32[32,1024]{1,0:T(8,128)S(1)} %collective-permute-done.17.refs_2_), channel_id=1, source_target_pairs={{0,2},{1,3},{2,0},{3,1},{4,6},{5,7},{6,4},{7,5},{8,10},{9,11},{10,... | collective-permute-start | bytes 393224 | tf_op jit(solution)/shard_map/ppermute | solution.py:265
  53.5 14.3 %collective-permute-start.20 = (f32[32,1024]{1,0:T(8,128)S(1)}, f32[32,1024]{1,0:T(8,128)S(1)}, u32[]{:S(2)}, u32[]{:S(2)}) collective-permute-start(f32[32,1024]{1,0:T(8,128)S(1)} %collective-permute-done.16.refs_1_), channel_id=1, source_target_pairs={{0,2},{1,3},{2,0},{3,1},{4,6},{5,7},{6,4},{7,5},{8,10},{9,11},{10,... | collective-permute-start | bytes 393224 | tf_op jit(solution)/shard_map/ppermute | solution.py:265
  63.1 0.7 copy-start
  67.8 1.0 %copy-start.1 = (f32[256,256]{1,0:T(8,128)S(1)}, f32[256,256]{1,0:T(8,128)}, u32[]{:S(2)}) copy-start(f32[256,256]{1,0:T(8,128)} %copy-done) | copy-start | bytes 786436

commit v4 on v3

--- a/solution.py
+++ b/solution.py
@@ -122,9 +122,9 @@
     features = split(features_ref[...])
     sampled = product(features, (high_ref[...], low_ref[...]), 1, 0)
     sampled_ref[...] = sampled
-    parts = split(sampled)
-    cross_ref[...] += product(parts, features, 0, 0)
-    gram_ref[...] += product(parts, parts, 0, 0)
+    flipped = split(sampled.T)
+    cross_ref[...] += product(flipped, features, 1, 0)
+    gram_ref[...] += product(flipped, split(sampled), 1, 0)
 
     @pl.when(step == pl.num_programs(0) - 1)
     def _():
@@ -167,7 +167,7 @@
             pltpu.VMEM((rank, depth), jnp.float32), pltpu.VMEM((rank, rank), jnp.float32),
             pltpu.VMEM((packed, LANES), jnp.float32),
         ],
-        compiler_params=pltpu.CompilerParams(vmem_limit_bytes=32 * 2**20),
+        compiler_params=pltpu.CompilerParams(vmem_limit_bytes=58 * 2**20),
         cost_estimate=pl.CostEstimate(flops=4 * 10**9, bytes_accessed=8 * 2**20, transcendentals=0),
         name="local_terms",
     )(features, sketch)
@@ -185,9 +185,9 @@
         a_ref[LANES:, :LANES] = jnp.zeros((LANES, LANES), jnp.float32)
         a_ref[LANES:, LANES:] = packed_ref[2 * LANES:, :]
     else:
-        from_ref, upper_ref, a_ref, factor_ref = refs
+        from_ref, upper_ref, a_ref, factor_ref, *flipped_ref = refs
         a_ref[...] = from_ref[...]
-        factor_ref[...] = upper_ref[...]
+        factor_ref[:first, :] = upper_ref[:first, :]
     size = a_ref.shape[0]
     for base in range(first, last, PANEL):
         factor_panel(a_ref, factor_ref, scale, base, PANEL, size)
@@ -195,38 +195,41 @@
     if last == size:
         col = lax.broadcasted_iota(jnp.int32, (size, size), 1)
         row = lax.broadcasted_iota(jnp.int32, (size, size), 0)
-        a_ref[...] = jnp.where(col <= row, a_ref[...], 0.0)
+        inverse = jnp.where(col <= row, a_ref[...], 0.0)
+        a_ref[...] = inverse
+        flipped_ref[0][...] = inverse.T * scale
 
 
 def factor_part(operands, size, scale, first, last):
     square = jax.ShapeDtypeStruct((size, size), jnp.float32)
+    outs = 3 if last == size else 2
     return pl.pallas_call(
         lambda *refs: factor_kernel(scale, first, last, *refs),
-        out_shape=(square, square),
+        out_shape=(square,) * outs,
         in_specs=[VMEM] * 2,
-        out_specs=(VMEM, VMEM),
+        out_specs=(VMEM,) * outs,
         scratch_shapes=[pltpu.VMEM((3 * LANES, LANES), jnp.float32)] if first == 0 else [],
         compiler_params=pltpu.CompilerParams(vmem_limit_bytes=16 * 2**20),
-        cost_estimate=pl.CostEstimate(flops=10**9 * (last - first) // size, bytes_accessed=2**20, transcendentals=last - first),
+        cost_estimate=pl.CostEstimate(flops=12 * 10**9 * (last - first) // size, bytes_accessed=2**20, transcendentals=last - first),
         name="factor_part",
     )(*operands)
 
 
-def basis_kernel(scale, sampled_ref, inverse_ref, basis_ref):
-    basis_ref[...] = product(split(sampled_ref[...]), split(inverse_ref[...] * scale), 1, 1)
-
-
-def basis_of(sampled, inverse, scale):
+def basis_kernel(sampled_ref, flipped_ref, basis_ref):
+    basis_ref[...] = product(split(sampled_ref[...]), split(flipped_ref[...]), 1, 0)
+
+
+def basis_of(sampled, flipped):
     rows, rank = sampled.shape
     return pl.pallas_call(
-        lambda *refs: basis_kernel(scale, *refs),
+        basis_kernel,
         grid=(rows // BLOCK,),
         out_shape=jax.ShapeDtypeStruct(sampled.shape, jnp.float32),
         in_specs=[pl.BlockSpec((BLOCK, rank), lambda i: (i, 0)), pl.BlockSpec((rank, rank), lambda i: (0, 0))],
         out_specs=pl.BlockSpec((BLOCK, rank), lambda i: (i, 0)),
         cost_estimate=pl.CostEstimate(flops=4 * 10**8, bytes_accessed=2 * 2**20, transcendentals=0),
         name="basis",
-    )(sampled, inverse)
+    )(sampled, flipped)
 
 
 def project_kernel(inverse_ref, *refs):
@@ -310,9 +313,11 @@
     sampled, keep, other, gram_keep, gram_other = local_terms(features, sketch)
     gram = sum_gram(gram_keep, gram_other)
     cross = sum_cross(keep, other)
-    state = factor_part(gram, size, scale, 0, size // 2)
-    inverse, factor = factor_part(state, size, scale, size // 2, size)
-    return (basis_of(sampled, inverse, scale), factor, project(inverse, cross))
+    state = gram
+    for first in range(0, size, PANEL):
+        state = factor_part(state[:2], size, scale, first, first + PANEL)
+    inverse, factor, flipped = state
+    return (basis_of(sampled, flipped), factor, project(inverse, cross))
 
 
 def solution(mesh):

time: 70.7 us -> 70.6 us (level)
  local copies, waits for them, and re-layouts: 5.05 us -> 0.7 us
  Pallas kernels: 22.9 us -> 25.6 us
  waiting for transfers between devices: 17.8 us -> 15.8 us
  other arithmetic: 0.2 us -> 2.18 us
  starting transfers between devices: 23.6 us -> 25.3 us
    unnamed x10 -> x2, local copies, waits for them, and re-layouts: 5.05 us -> 0.7 us
    pallas_call x1, Pallas kernels: 7.75 us -> 10.6 us  [local_terms(): pl.pallas_call(local_kernel, grid=(rows // BLOCK,), out_shape=(f32(rows,...]
    ppermute x23, waiting for transfers between devices: 17.8 us -> 15.8 us  [send(): return lax.ppermute(value, AXES, pairs)]
    ppermute x23, starting transfers between devices: 23.6 us -> 25.3 us  [send(): return lax.ppermute(value, AXES, pairs)]
    add x2, other arithmetic: 0.11 us -> 1.2 us  [quarters(): sum((value[at * height:(at + 1) * height] for value in values))]
    add x1, other arithmetic: 0.02 us -> 0.91 us  [sum_gram(): half = keep + send(other, *CORE)]
    pallas_call x2 -> x4, Pallas kernels: 9.52 us -> 9.42 us  [factor_part(): pl.pallas_call(lambda *refs: factor_kernel(scale, first, last, *refs), ou...]
  transfers between devices with their start and end apart: 23 -> 23, of which waited for: 9 -> 9; matrix products, arithmetic and copies ran while one was open for 0% -> 3% of each run, Pallas kernels for 19% -> 19%
where the time goes in v4:
time: 70.6 us; the launch traced here: 70.4 us
  Pallas kernels  25.6 us (36%)
  starting transfers between devices  25.3 us (36%)
  waiting for transfers between devices  15.8 us (22%)
  other arithmetic  2.18 us (3%)
  between operations  0.81 us (1%)
    ppermute x23, starting transfers between devices, send(): return lax.ppermute(value, AXES, pairs)  25.3 us
    ppermute x23, waiting for transfers between devices, send(): return lax.ppermute(value, AXES, pairs)  15.8 us
    pallas_call x1, Pallas kernels, local_terms(): pl.pallas_call(local_kernel, grid=(rows // BLOCK,), out_shape=(f32(rows,...  10.6 us
    pallas_call x4, Pallas kernels, factor_part(): pl.pallas_call(lambda *refs: factor_kernel(scale, first, last, *refs), ou...  9.42 us
    pallas_call x1, Pallas kernels, basis_of(): pl.pallas_call(basis_kernel, grid=(rows // BLOCK,), out_shape=jax.ShapeDt...  3.95 us
    pallas_call x1, Pallas kernels, project(): pl.pallas_call(project_kernel, out_shape=jax.ShapeDtypeStruct((rank, dept...  1.65 us
  transfers between devices with their start and end apart: 23, of which 9 were waited for; matrix products, arithmetic and copies ran while one was open for 3% of the time, Pallas kernels for 19%

profile of v4, /device:TPU:0, one launch (start us, length us, event | category | flops | bytes accessed | tf_op | source)
XLA Modules:
  0.0 70.4 jit_solution(1552235723471531159)
XLA Ops:
  0.6 10.6 %local_terms.1 = (f32[1024,256]{1,0:T(8,128)}, f32[128,1024]{1,0:T(8,128)}, f32[128,1024]{1,0:T(8,128)}, f32[192,128]{1,0:T(8,128)}, f32[192,128]{1,0:T(8,128)}) custom-call(f32[1024,1024]{1,0:T(8,128)} %features_ref.1, f32[1024,256]{1,0:T(8,128)} %sketch_ref.1), custom_call_target="tpu_custom_call" | custom-call | flops 4000000000 | bytes 8388608 | tf_op jit(solution)/shard_map/local_terms/pallas_call | solution.py:155
  11.2 0.5 collective-permute-start.6
  11.7 0.1 collective-permute-start
  11.7 1.8 %collective-permute-done = f32[192,128]{1,0:T(8,128)S(1)} collective-permute-done((f32[192,128]{1,0:T(8,128)}, f32[192,128]{1,0:T(8,128)S(1)}, u32[]{:S(2)}, u32[]{:S(2)}) %collective-permute-start) | collective-permute-done | bytes 98336 | tf_op jit(solution)/shard_map/ppermute | solution.py:268
  13.5 0.9 %add.72 = f32[192,128]{1,0:T(8,128)S(1)} add(f32[192,128]{1,0:T(8,128)} %get-tuple-element.18, f32[192,128]{1,0:T(8,128)S(1)} %collective-permute-done) | non-fusion elementwise | flops 24576 | bytes 294912 | tf_op jit(solution)/shard_map/add | solution.py:283
  14.4 3.0 %collective-permute-start.1 = (f32[192,128]{1,0:T(8,128)S(1)}, f32[192,128]{1,0:T(8,128)S(1)}, u32[]{:S(2)}, u32[]{:S(2)}) collective-permute-start(f32[192,128]{1,0:T(8,128)S(1)} %add.72), channel_id=1, source_target_pairs={{0,1},{1,0},{2,3},{3,2},{4,5},{5,4},{6,7},{7,6},{8,9},{9,8},{10,11... | collective-permute-start | bytes 294920 | tf_op jit(solution)/shard_map/ppermute | solution.py:268
  17.4 3.1 %collective-permute-done.1 = f32[192,128]{1,0:T(8,128)S(1)} collective-permute-done((f32[192,128]{1,0:T(8,128)S(1)}, f32[192,128]{1,0:T(8,128)S(1)}, u32[]{:S(2)}, u32[]{:S(2)}) %collective-permute-start.1) | collective-permute-done | bytes 98336 | tf_op jit(solution)/shard_map/ppermute | solution.py:268
  20.5 1.8 %collective-permute-start.2 = (f32[192,128]{1,0:T(8,128)S(1)}, f32[192,128]{1,0:T(8,128)S(1)}, u32[]{:S(2)}, u32[]{:S(2)}) collective-permute-start(f32[192,128]{1,0:T(8,128)S(1)} %add.73), channel_id=1, source_target_pairs={{0,4},{1,5},{2,6},{3,7},{4,0},{5,1},{6,2},{7,3},{8,12},{9,13},{10,... | collective-permute-start | bytes 294920 | tf_op jit(solution)/shard_map/ppermute | solution.py:268
  22.3 2.9 %collective-permute-done.2 = f32[192,128]{1,0:T(8,128)S(1)} collective-permute-done((f32[192,128]{1,0:T(8,128)S(1)}, f32[192,128]{1,0:T(8,128)S(1)}, u32[]{:S(2)}, u32[]{:S(2)}) %collective-permute-start.2) | collective-permute-done | bytes 98336 | tf_op jit(solution)/shard_map/ppermute | solution.py:268
  25.2 1.9 %collective-permute-start.3 = (f32[192,128]{1,0:T(8,128)S(1)}, f32[192,128]{1,0:T(8,128)S(1)}, u32[]{:S(2)}, u32[]{:S(2)}) collective-permute-start(f32[192,128]{1,0:T(8,128)S(1)} %add.74), channel_id=1, source_target_pairs={{0,8},{1,9},{2,10},{3,11},{4,12},{5,13},{6,14},{7,15},{8,0},{9,1},... | collective-permute-start | bytes 294920 | tf_op jit(solution)/shard_map/ppermute | solution.py:268
  27.1 0.0 collective-permute-done.6
  27.1 1.2 %slice_add_fusion.3 = (f32[32,1024]{1,0:T(8,128)S(1)}, f32[32,1024]{1,0:T(8,128)S(1)}, f32[32,1024]{1,0:T(8,128)S(1)}, f32[32,1024]{1,0:T(8,128)S(1)}) fusion(f32[128,1024]{1,0:T(8,128)S(1)} %collective-permute-done.6, f32[128,1024]{1,0:T(8,128)} %get-tuple-element.29), kind=kLoop, calls=%fused_computation.3 | loop fusion | flops 131072 | bytes 1572864 | tf_op jit(solution)/shard_map/add | solution.py:291
  28.2 2.5 %collective-permute-start.9 = (f32[32,1024]{1,0:T(8,128)S(1)}, f32[32,1024]{1,0:T(8,128)S(1)}, u32[]{:S(2)}, u32[]{:S(2)}) collective-permute-start(f32[32,1024]{1,0:T(8,128)S(1)} %get-tuple-element.32), channel_id=1, source_target_pairs={{0,5},{1,4},{2,7},{3,6},{4,1},{5,0},{6,3},{7,2},{8,13},{9,12},{10,... | collective-permute-start | bytes 393224 | tf_op jit(solution)/shard_map/ppermute | solution.py:268
  30.8 0.5 collective-permute-start.8
  31.3 0.5 collective-permute-start.7
  31.8 0.0 collective-permute-done.3
  31.8 2.7 %collective-permute-start.4 = (f32[192,128]{1,0:T(8,128)S(1)}, f32[192,128]{1,0:T(8,128)S(1)}, u32[]{:S(2)}, u32[]{:S(2)}) collective-permute-start(f32[192,128]{1,0:T(8,128)S(1)} %add.75), channel_id=1, source_target_pairs={{0,16},{1,17},{2,18},{3,19},{4,20},{5,21},{6,22},{7,23},{8,24},{9,... | collective-permute-start | bytes 294920 | tf_op jit(solution)/shard_map/ppermute | solution.py:268
  34.5 3.6 %collective-permute-done.4 = f32[192,128]{1,0:T(8,128)S(1)} collective-permute-done((f32[192,128]{1,0:T(8,128)S(1)}, f32[192,128]{1,0:T(8,128)S(1)}, u32[]{:S(2)}, u32[]{:S(2)}) %collective-permute-start.4) | collective-permute-done | bytes 98336 | tf_op jit(solution)/shard_map/ppermute | solution.py:268
  38.1 0.1 collective-permute-start.5
  38.2 0.0 collective-permute-done.9
  38.2 0.0 collective-permute-done.8
  38.2 0.0 collective-permute-done.7
  38.3 0.1 collective-permute-start.10
  38.4 3.4 %collective-permute-start.12 = (f32[8,1024]{1,0:T(8,128)S(1)}, f32[8,1024]{1,0:T(8,128)S(1)}, u32[]{:S(2)}, u32[]{:S(2)}) collective-permute-start(f32[8,1024]{1,0:T(8,128)S(1)} %get-tuple-element.36), channel_id=1, source_target_pairs={{0,24},{1,25},{2,26},{3,27},{4,28},{5,29},{6,30},{7,31},{8,16},{9,... | collective-permute-start | bytes 98312 | tf_op jit(solution)/shard_map/ppermute | solution.py:268
  41.7 0.1 collective-permute-start.11
  41.8 0.0 collective-permute-done.5.refs_1_
  41.8 2.3 %factor_part.4 = (f32[256,256]{1,0:T(8,128)S(1)}, f32[256,256]{1,0:T(8,128)S(1)}) custom-call(f32[192,128]{1,0:T(8,128)S(1)} %add.76.refs_0_, f32[192,128]{1,0:T(8,128)S(1)} %collective-permute-done.5.refs_1_), custom_call_target="tpu_custom_call" | custom-call | flops 3000000000 | bytes 1048576 | tf_op jit(solution)/shard_map/factor_part/pallas_call | solution.py:206
  44.2 0.0 collective-permute-done.10
  44.2 0.4 collective-permute-done.12
  44.6 1.9 %collective-permute-done.11 = f32[8,1024]{1,0:T(8,128)S(1)} collective-permute-done((f32[8,1024]{1,0:T(8,128)S(1)}, f32[8,1024]{1,0:T(8,128)S(1)}, u32[]{:S(2)}, u32[]{:S(2)}) %collective-permute-start.11) | collective-permute-done | bytes 32800 | tf_op jit(solution)/shard_map/ppermute | solution.py:268
  46.5 1.6 %collective-permute-start.15 = (f32[8,1024]{1,0:T(8,128)S(1)}, f32[8,1024]{1,0:T(8,128)S(1)}, u32[]{:S(2)}, u32[]{:S(2)}) collective-permute-start(f32[8,1024]{1,0:T(8,128)S(1)} %fusion.2), channel_id=1, source_target_pairs={{0,24},{1,25},{2,26},{3,27},{4,28},{5,29},{6,30},{7,31},{8,16},{9,... | collective-permute-start | bytes 98312 | tf_op jit(solution)/shard_map/ppermute | solution.py:268
  48.1 0.0 collective-permute-start.14
  48.1 2.9 %collective-permute-start.13 = (f32[8,1024]{1,0:T(8,128)S(1)}, f32[8,1024]{1,0:T(8,128)S(1)}, u32[]{:S(2)}, u32[]{:S(2)}) collective-permute-start(f32[8,1024]{1,0:T(8,128)S(1)} %fusion.2), channel_id=1, source_target_pairs={{0,8},{1,9},{2,10},{3,11},{4,12},{5,13},{6,14},{7,15},{8,0},{9,1},... | collective-permute-start | bytes 98312 | tf_op jit(solution)/shard_map/ppermute | solution.py:268
  51.0 2.2 %factor_part.5 = (f32[256,256]{1,0:T(8,128)S(1)}, f32[256,256]{1,0:T(8,128)S(1)}) custom-call(f32[256,256]{1,0:T(8,128)S(1)} %get-tuple-element.20.refs_0_, f32[256,256]{1,0:T(8,128)S(1)} %get-tuple-element.21.refs_1_), custom_call_target="tpu_custom_call" | custom-call | flops 3000000000 | bytes 1048576 | tf_op jit(solution)/shard_map/factor_part/pallas_call | solution.py:206
  53.2 0.0 collective-permute-done.15
  53.2 0.0 collective-permute-done.14
  53.2 0.0 collective-permute-done.13
  53.3 2.5 %collective-permute-start.18 = (f32[32,1024]{1,0:T(8,128)S(1)}, f32[32,1024]{1,0:T(8,128)S(1)}, u32[]{:S(2)}, u32[]{:S(2)}) collective-permute-start(f32[32,1024]{1,0:T(8,128)S(1)} %pad_maximum_fusion.refs_0_), channel_id=1, source_target_pairs={{0,5},{1,4},{2,7},{3,6},{4,1},{5,0},{6,3},{7,2},{8,13},{9,12},{10,... | collective-permute-start | bytes 393224 | tf_op jit(solution)/shard_map/ppermute | solution.py:268
  55.8 0.5 collective-permute-start.17
  56.3 0.5 collective-permute-start.16
  56.8 2.2 %factor_part.6 = (f32[256,256]{1,0:T(8,128)S(1)}, f32[256,256]{1,0:T(8,128)S(1)}) custom-call(f32[256,256]{1,0:T(8,128)S(1)} %get-tuple-element.22.refs_0_, f32[256,256]{1,0:T(8,128)S(1)} %get-tuple-element.23.refs_1_), custom_call_target="tpu_custom_call" | custom-call | flops 3000000000 | bytes 1048576 | tf_op jit(solution)/shard_map/factor_part/pallas_call | solution.py:206
  59.1 0.1 collective-permute-start.19
  59.1 0.3 collective-permute-done.18.refs_3_
  59.4 0.2 collective-permute-start.22
  59.6 1.2 %collective-permute-done.17.refs_2_ = f32[32,1024]{1,0:T(8,128)S(1)} collective-permute-done((f32[32,1024]{1,0:T(8,128)S(1)}, f32[32,1024]{1,0:T(8,128)S(1)}, u32[]{:S(2)}, u32[]{:S(2)}) %collective-permute-start.17) | collective-permute-done | bytes 131104 | tf_op jit(solution)/shard_map/ppermute | solution.py:268
  60.8 0.0 collective-permute-start.21
  60.9 0.4 collective-permute-done.16.refs_1_
  61.3 0.1 collective-permute-start.20
  61.4 2.6 %factor_part.7 = (f32[256,256]{1,0:T(8,128)S(1)}, f32[256,256]{1,0:T(8,128)}, f32[256,256]{1,0:T(8,128)S(1)}) custom-call(f32[256,256]{1,0:T(8,128)S(1)} %get-tuple-element.24.refs_0_, f32[256,256]{1,0:T(8,128)S(1)} %get-tuple-element.25.refs_1_), custom_call_target="tpu_custom_call" | custom-call | flops 3000000000 | bytes 1048576 | tf_op jit(solution)/shard_map/factor_part/pallas_call | solution.py:206
  64.0 0.0 copy-start
  64.0 0.7 copy-done
  64.7 4.0 %basis.1 = f32[1024,256]{1,0:T(8,128)} custom-call(f32[1024,256]{1,0:T(8,128)} %get-tuple-element.17.sampled_ref, f32[256,256]{1,0:T(8,128)} %copy-done), custom_call_target="tpu_custom_call" | custom-call | flops 400000000 | bytes 2097152 | tf_op jit(solution)/shard_map/basis/pallas_call | solution.py:224
  68.7 0.0 collective-permute-done.19.refs_4_
  68.7 0.0 collective-permute-done.22.refs_7_
  68.7 0.0 collective-permute-done.21.refs_6_
  68.7 0.0 collective-permute-done.20.refs_5_
  68.7 1.7 %project.1 = f32[256,1024]{1,0:T(8,128)} custom-call(f32[256,256]{1,0:T(8,128)S(1)} %get-tuple-element.28.inverse_ref, f32[32,1024]{1,0:T(8,128)S(1)} %pad_maximum_fusion.refs_0_, f32[32,1024]{1,0:T(8,128)S(1)} %collective-permute-done.16.refs_1_, f32[32,1024]{1,0:T(8,128)S(1)} %collective-permute-done.17.refs_2_, ...), custom_call_target="tpu_custom_call" | custom-call | flops 400000000 | bytes 2097152 | tf_op jit(solution)/shard_map/project/pallas_call | solution.py:253
  (7 shorter events, 0.1 us)
Async XLA Ops:
  11.2 15.9 %collective-permute-start.6 = (f32[128,1024]{1,0:T(8,128)}, f32[128,1024]{1,0:T(8,128)S(1)}, u32[]{:S(2)}, u32[]{:S(2)}) collective-permute-start(f32[128,1024]{1,0:T(8,128)} %get-tuple-element.30), channel_id=1, source_target_pairs={{0,2},{1,3},{2,0},{3,1},{4,6},{5,7},{6,4},{7,5},{8,10},{9,11},{10,... | collective-permute-start | bytes 1572872 | tf_op jit(solution)/shard_map/ppermute | solution.py:268
  11.7 1.9 %collective-permute-start = (f32[192,128]{1,0:T(8,128)}, f32[192,128]{1,0:T(8,128)S(1)}, u32[]{:S(2)}, u32[]{:S(2)}) collective-permute-start(f32[192,128]{1,0:T(8,128)} %get-tuple-element.19), channel_id=1, source_target_pairs={{0,2},{1,3},{2,0},{3,1},{4,6},{5,7},{6,4},{7,5},{8,10},{9,11},{10,... | collective-permute-start | bytes 294920 | tf_op jit(solution)/shard_map/ppermute | solution.py:268
  14.4 6.0 %collective-permute-start.1 = (f32[192,128]{1,0:T(8,128)S(1)}, f32[192,128]{1,0:T(8,128)S(1)}, u32[]{:S(2)}, u32[]{:S(2)}) collective-permute-start(f32[192,128]{1,0:T(8,128)S(1)} %add.72), channel_id=1, source_target_pairs={{0,1},{1,0},{2,3},{3,2},{4,5},{5,4},{6,7},{7,6},{8,9},{9,8},{10,11... | collective-permute-start | bytes 294920 | tf_op jit(solution)/shard_map/ppermute | solution.py:268
  20.5 4.7 %collective-permute-start.2 = (f32[192,128]{1,0:T(8,128)S(1)}, f32[192,128]{1,0:T(8,128)S(1)}, u32[]{:S(2)}, u32[]{:S(2)}) collective-permute-start(f32[192,128]{1,0:T(8,128)S(1)} %add.73), channel_id=1, source_target_pairs={{0,4},{1,5},{2,6},{3,7},{4,0},{5,1},{6,2},{7,3},{8,12},{9,13},{10,... | collective-permute-start | bytes 294920 | tf_op jit(solution)/shard_map/ppermute | solution.py:268
  25.2 6.6 %collective-permute-start.3 = (f32[192,128]{1,0:T(8,128)S(1)}, f32[192,128]{1,0:T(8,128)S(1)}, u32[]{:S(2)}, u32[]{:S(2)}) collective-permute-start(f32[192,128]{1,0:T(8,128)S(1)} %add.74), channel_id=1, source_target_pairs={{0,8},{1,9},{2,10},{3,11},{4,12},{5,13},{6,14},{7,15},{8,0},{9,1},... | collective-permute-start | bytes 294920 | tf_op jit(solution)/shard_map/ppermute | solution.py:268
  28.2 10.0 %collective-permute-start.9 = (f32[32,1024]{1,0:T(8,128)S(1)}, f32[32,1024]{1,0:T(8,128)S(1)}, u32[]{:S(2)}, u32[]{:S(2)}) collective-permute-start(f32[32,1024]{1,0:T(8,128)S(1)} %get-tuple-element.32), channel_id=1, source_target_pairs={{0,5},{1,4},{2,7},{3,6},{4,1},{5,0},{6,3},{7,2},{8,13},{9,12},{10,... | collective-permute-start | bytes 393224 | tf_op jit(solution)/shard_map/ppermute | solution.py:268
  30.8 7.5 %collective-permute-start.8 = (f32[32,1024]{1,0:T(8,128)S(1)}, f32[32,1024]{1,0:T(8,128)S(1)}, u32[]{:S(2)}, u32[]{:S(2)}) collective-permute-start(f32[32,1024]{1,0:T(8,128)S(1)} %get-tuple-element.33), channel_id=1, source_target_pairs={{0,4},{1,5},{2,6},{3,7},{4,0},{5,1},{6,2},{7,3},{8,12},{9,13},{10,... | collective-permute-start | bytes 393224 | tf_op jit(solution)/shard_map/ppermute | solution.py:268
  31.3 6.9 %collective-permute-start.7 = (f32[32,1024]{1,0:T(8,128)S(1)}, f32[32,1024]{1,0:T(8,128)S(1)}, u32[]{:S(2)}, u32[]{:S(2)}) collective-permute-start(f32[32,1024]{1,0:T(8,128)S(1)} %get-tuple-element.34), channel_id=1, source_target_pairs={{0,1},{1,0},{2,3},{3,2},{4,5},{5,4},{6,7},{7,6},{8,9},{9,8},{10,11... | collective-permute-start | bytes 393224 | tf_op jit(solution)/shard_map/ppermute | solution.py:268
  31.8 6.3 %collective-permute-start.4 = (f32[192,128]{1,0:T(8,128)S(1)}, f32[192,128]{1,0:T(8,128)S(1)}, u32[]{:S(2)}, u32[]{:S(2)}) collective-permute-start(f32[192,128]{1,0:T(8,128)S(1)} %add.75), channel_id=1, source_target_pairs={{0,16},{1,17},{2,18},{3,19},{4,20},{5,21},{6,22},{7,23},{8,24},{9,... | collective-permute-start | bytes 294920 | tf_op jit(solution)/shard_map/ppermute | solution.py:268
  38.1 3.7 %collective-permute-start.5 = (f32[192,128]{1,0:T(8,128)S(1)}, f32[192,128]{1,0:T(8,128)S(1)}, u32[]{:S(2)}, u32[]{:S(2)}) collective-permute-start(f32[192,128]{1,0:T(8,128)S(1)} %add.76.refs_0_), channel_id=1, source_target_pairs={{0,2},{1,3},{2,0},{3,1},{4,6},{5,7},{6,4},{7,5},{8,10},{9,11},{10,... | collective-permute-start | bytes 294920 | tf_op jit(solution)/shard_map/ppermute | solution.py:268
  38.3 5.9 %collective-permute-start.10 = (f32[8,1024]{1,0:T(8,128)S(1)}, f32[8,1024]{1,0:T(8,128)S(1)}, u32[]{:S(2)}, u32[]{:S(2)}) collective-permute-start(f32[8,1024]{1,0:T(8,128)S(1)} %get-tuple-element.35), channel_id=1, source_target_pairs={{0,8},{1,9},{2,10},{3,11},{4,12},{5,13},{6,14},{7,15},{8,0},{9,1},... | collective-permute-start | bytes 98312 | tf_op jit(solution)/shard_map/ppermute | solution.py:268
  38.4 6.3 %collective-permute-start.12 = (f32[8,1024]{1,0:T(8,128)S(1)}, f32[8,1024]{1,0:T(8,128)S(1)}, u32[]{:S(2)}, u32[]{:S(2)}) collective-permute-start(f32[8,1024]{1,0:T(8,128)S(1)} %get-tuple-element.36), channel_id=1, source_target_pairs={{0,24},{1,25},{2,26},{3,27},{4,28},{5,29},{6,30},{7,31},{8,16},{9,... | collective-permute-start | bytes 98312 | tf_op jit(solution)/shard_map/ppermute | solution.py:268
  41.7 4.8 %collective-permute-start.11 = (f32[8,1024]{1,0:T(8,128)S(1)}, f32[8,1024]{1,0:T(8,128)S(1)}, u32[]{:S(2)}, u32[]{:S(2)}) collective-permute-start(f32[8,1024]{1,0:T(8,128)S(1)} %get-tuple-element.37), channel_id=1, source_target_pairs={{0,16},{1,17},{2,18},{3,19},{4,20},{5,21},{6,22},{7,23},{8,24},{9,... | collective-permute-start | bytes 98312 | tf_op jit(solution)/shard_map/ppermute | solution.py:268
  46.5 6.7 %collective-permute-start.15 = (f32[8,1024]{1,0:T(8,128)S(1)}, f32[8,1024]{1,0:T(8,128)S(1)}, u32[]{:S(2)}, u32[]{:S(2)}) collective-permute-start(f32[8,1024]{1,0:T(8,128)S(1)} %fusion.2), channel_id=1, source_target_pairs={{0,24},{1,25},{2,26},{3,27},{4,28},{5,29},{6,30},{7,31},{8,16},{9,... | collective-permute-start | bytes 98312 | tf_op jit(solution)/shard_map/ppermute | solution.py:268
  48.1 5.1 %collective-permute-start.14 = (f32[8,1024]{1,0:T(8,128)S(1)}, f32[8,1024]{1,0:T(8,128)S(1)}, u32[]{:S(2)}, u32[]{:S(2)}) collective-permute-start(f32[8,1024]{1,0:T(8,128)S(1)} %fusion.2), channel_id=1, source_target_pairs={{0,16},{1,17},{2,18},{3,19},{4,20},{5,21},{6,22},{7,23},{8,24},{9,... | collective-permute-start | bytes 98312 | tf_op jit(solution)/shard_map/ppermute | solution.py:268
  48.1 5.1 %collective-permute-start.13 = (f32[8,1024]{1,0:T(8,128)S(1)}, f32[8,1024]{1,0:T(8,128)S(1)}, u32[]{:S(2)}, u32[]{:S(2)}) collective-permute-start(f32[8,1024]{1,0:T(8,128)S(1)} %fusion.2), channel_id=1, source_target_pairs={{0,8},{1,9},{2,10},{3,11},{4,12},{5,13},{6,14},{7,15},{8,0},{9,1},... | collective-permute-start | bytes 98312 | tf_op jit(solution)/shard_map/ppermute | solution.py:268
  53.3 6.2 %collective-permute-start.18 = (f32[32,1024]{1,0:T(8,128)S(1)}, f32[32,1024]{1,0:T(8,128)S(1)}, u32[]{:S(2)}, u32[]{:S(2)}) collective-permute-start(f32[32,1024]{1,0:T(8,128)S(1)} %pad_maximum_fusion.refs_0_), channel_id=1, source_target_pairs={{0,5},{1,4},{2,7},{3,6},{4,1},{5,0},{6,3},{7,2},{8,13},{9,12},{10,... | collective-permute-start | bytes 393224 | tf_op jit(solution)/shard_map/ppermute | solution.py:268
  55.8 5.1 %collective-permute-start.17 = (f32[32,1024]{1,0:T(8,128)S(1)}, f32[32,1024]{1,0:T(8,128)S(1)}, u32[]{:S(2)}, u32[]{:S(2)}) collective-permute-start(f32[32,1024]{1,0:T(8,128)S(1)} %pad_maximum_fusion.refs_0_), channel_id=1, source_target_pairs={{0,4},{1,5},{2,6},{3,7},{4,0},{5,1},{6,2},{7,3},{8,12},{9,13},{10,... | collective-permute-start | bytes 393224 | tf_op jit(solution)/shard_map/ppermute | solution.py:268
  56.3 5.0 %collective-permute-start.16 = (f32[32,1024]{1,0:T(8,128)S(1)}, f32[32,1024]{1,0:T(8,128)S(1)}, u32[]{:S(2)}, u32[]{:S(2)}) collective-permute-start(f32[32,1024]{1,0:T(8,128)S(1)} %pad_maximum_fusion.refs_0_), channel_id=1, source_target_pairs={{0,1},{1,0},{2,3},{3,2},{4,5},{5,4},{6,7},{7,6},{8,9},{9,8},{10,11... | collective-permute-start | bytes 393224 | tf_op jit(solution)/shard_map/ppermute | solution.py:268
  59.1 9.6 %collective-permute-start.19 = (f32[32,1024]{1,0:T(8,128)S(1)}, f32[32,1024]{1,0:T(8,128)S(1)}, u32[]{:S(2)}, u32[]{:S(2)}) collective-permute-start(f32[32,1024]{1,0:T(8,128)S(1)} %pad_maximum_fusion.refs_0_), channel_id=1, source_target_pairs={{0,2},{1,3},{2,0},{3,1},{4,6},{5,7},{6,4},{7,5},{8,10},{9,11},{10,... | collective-permute-start | bytes 393224 | tf_op jit(solution)/shard_map/ppermute | solution.py:268
  59.4 9.2 %collective-permute-start.22 = (f32[32,1024]{1,0:T(8,128)S(1)}, f32[32,1024]{1,0:T(8,128)S(1)}, u32[]{:S(2)}, u32[]{:S(2)}) collective-permute-start(f32[32,1024]{1,0:T(8,128)S(1)} %collective-permute-done.18.refs_3_), channel_id=1, source_target_pairs={{0,2},{1,3},{2,0},{3,1},{4,6},{5,7},{6,4},{7,5},{8,10},{9,11},{10,... | collective-permute-start | bytes 393224 | tf_op jit(solution)/shard_map/ppermute | solution.py:268
  60.8 7.8 %collective-permute-start.21 = (f32[32,1024]{1,0:T(8,128)S(1)}, f32[32,1024]{1,0:T(8,128)S(1)}, u32[]{:S(2)}, u32[]{:S(2)}) collective-permute-start(f32[32,1024]{1,0:T(8,128)S(1)} %collective-permute-done.17.refs_2_), channel_id=1, source_target_pairs={{0,2},{1,3},{2,0},{3,1},{4,6},{5,7},{6,4},{7,5},{8,10},{9,11},{10,... | collective-permute-start | bytes 393224 | tf_op jit(solution)/shard_map/ppermute | solution.py:268
  61.3 7.4 %collective-permute-start.20 = (f32[32,1024]{1,0:T(8,128)S(1)}, f32[32,1024]{1,0:T(8,128)S(1)}, u32[]{:S(2)}, u32[]{:S(2)}) collective-permute-start(f32[32,1024]{1,0:T(8,128)S(1)} %collective-permute-done.16.refs_1_), channel_id=1, source_target_pairs={{0,2},{1,3},{2,0},{3,1},{4,6},{5,7},{6,4},{7,5},{8,10},{9,11},{10,... | collective-permute-start | bytes 393224 | tf_op jit(solution)/shard_map/ppermute | solution.py:268
  64.0 0.7 %copy-start = (f32[256,256]{1,0:T(8,128)}, f32[256,256]{1,0:T(8,128)S(1)}, u32[]{:S(2)}) copy-start(f32[256,256]{1,0:T(8,128)S(1)} %get-tuple-element.26.flipped_ref) | copy-start | bytes 786436

commit v5 on v4

--- a/solution.py
+++ b/solution.py
@@ -110,67 +110,111 @@
     return pl.ds(pl.multiple_of(block * height, GROUP), height)
 
 
-def local_kernel(features_ref, sketch_ref, sampled_ref, keep_ref, send_ref, gram_keep_ref, gram_send_ref, high_ref, low_ref, cross_ref, gram_ref, packed_ref):
-    step = pl.program_id(0)
-
-    @pl.when(step == 0)
-    def _():
-        high_ref[...], low_ref[...] = split(sketch_ref[...])
-        cross_ref[...] = jnp.zeros_like(cross_ref)
-        gram_ref[...] = jnp.zeros_like(gram_ref)
-
-    features = split(features_ref[...])
-    sampled = product(features, (high_ref[...], low_ref[...]), 1, 0)
-    sampled_ref[...] = sampled
-    flipped = split(sampled.T)
-    cross_ref[...] += product(flipped, features, 1, 0)
-    gram_ref[...] += product(flipped, split(sampled), 1, 0)
-
-    @pl.when(step == pl.num_programs(0) - 1)
-    def _():
-        own = own_block()
-        height = cross_ref.shape[0] // BLOCKS
-        for at in range(BLOCKS):
-            block = cross_ref[rows_of(at ^ own, height), :]
-            if at < BLOCKS // 2:
-                keep_ref[at * height:(at + 1) * height, :] = block
-            else:
-                rest = at - BLOCKS // 2
-                send_ref[rest * height:(rest + 1) * height, :] = block
-        packed_ref[:LANES, :] = gram_ref[:LANES, :LANES]
-        packed_ref[LANES:2 * LANES, :] = gram_ref[:LANES, LANES:]
-        packed_ref[2 * LANES:, :] = gram_ref[LANES:, LANES:]
-        half = packed_ref.shape[0] // 2
-        core = core_bit()
-        gram_keep_ref[...] = packed_ref[rows_of(core, half), :]
-        gram_send_ref[...] = packed_ref[rows_of(1 - core, half), :]
+def local_kernel(features_hbm, sketch_hbm, sampled_ref, keep_ref, send_ref, gram_keep_ref, gram_send_ref, features_ref, sketch_ref, high_ref, low_ref, flip_high_ref, flip_low_ref, cross_ref, packed_ref, sems):
+    rows, depth = features_ref.shape
+    rank = sketch_ref.shape[1]
+    chunks = rows // BLOCK
+    copies = [pltpu.make_async_copy(sketch_hbm, sketch_ref, sems.at[chunks])]
+    for at in range(chunks):
+        span = pl.ds(at * BLOCK, BLOCK)
+        copies.append(pltpu.make_async_copy(features_hbm.at[span, :], features_ref.at[span, :], sems.at[at]))
+    for copy in copies:
+        copy.start()
+    copies[0].wait()
+    sketch = split(sketch_ref[...])
+    gram = None
+    for at in range(chunks):
+        span = slice(at * BLOCK, (at + 1) * BLOCK)
+        copies[1 + at].wait()
+        features = split(features_ref[span, :])
+        high_ref[span, :], low_ref[span, :] = features
+        sampled = product(features, sketch, 1, 0)
+        sampled_ref[span, :] = sampled
+        flipped = split(sampled.T)
+        flip_high_ref[:, span], flip_low_ref[:, span] = flipped
+        term = product(flipped, split(sampled), 1, 0)
+        gram = term if gram is None else gram + term
+    packed_ref[:LANES, :] = gram[:LANES, :LANES]
+    packed_ref[LANES:2 * LANES, :] = gram[:LANES, LANES:]
+    packed_ref[2 * LANES:, :] = gram[LANES:, LANES:]
+    half = packed_ref.shape[0] // 2
+    core = core_bit()
+    gram_keep_ref[...] = packed_ref[rows_of(core, half), :]
+    gram_send_ref[...] = packed_ref[rows_of(1 - core, half), :]
+    flipped = flip_high_ref[...], flip_low_ref[...]
+    own = own_block()
+    height = rank // BLOCKS
+    for left in range(0, depth, BLOCK):
+        span = slice(left, left + BLOCK)
+        cross_ref[:, span] = product(flipped, (high_ref[:, span], low_ref[:, span]), 1, 0)
+    for at in range(BLOCKS):
+        block = cross_ref[rows_of(at ^ own, height), :]
+        if at < BLOCKS // 2:
+            keep_ref[at * height:(at + 1) * height, :] = block
+        else:
+            rest = at - BLOCKS // 2
+            send_ref[rest * height:(rest + 1) * height, :] = block
+
+
+def f32(*shape):
+    return jax.ShapeDtypeStruct(shape, jnp.float32)
 
 
 def local_terms(features, sketch):
     rows, depth = features.shape
     rank = sketch.shape[1]
-    f32 = lambda *shape: jax.ShapeDtypeStruct(shape, jnp.float32)
-    whole = lambda *shape: pl.BlockSpec(shape, lambda i: (0, 0))
     packed = 3 * LANES
+    hbm = pl.BlockSpec(memory_space=pltpu.HBM)
     return pl.pallas_call(
         local_kernel,
-        grid=(rows // BLOCK,),
         out_shape=(f32(rows, rank), f32(rank // 2, depth), f32(rank // 2, depth), f32(packed // 2, LANES), f32(packed // 2, LANES)),
-        in_specs=[pl.BlockSpec((BLOCK, depth), lambda i: (i, 0)), whole(depth, rank)],
-        out_specs=(
-            pl.BlockSpec((BLOCK, rank), lambda i: (i, 0)),
-            whole(rank // 2, depth), whole(rank // 2, depth),
-            whole(packed // 2, LANES), whole(packed // 2, LANES),
-        ),
+        in_specs=[hbm, hbm],
+        out_specs=(VMEM,) * 5,
         scratch_shapes=[
-            pltpu.VMEM((depth, rank), jnp.bfloat16), pltpu.VMEM((depth, rank), jnp.bfloat16),
-            pltpu.VMEM((rank, depth), jnp.float32), pltpu.VMEM((rank, rank), jnp.float32),
-            pltpu.VMEM((packed, LANES), jnp.float32),
+            pltpu.VMEM((rows, depth), jnp.float32), pltpu.VMEM((depth, rank), jnp.float32),
+            pltpu.VMEM((rows, depth), jnp.bfloat16), pltpu.VMEM((rows, depth), jnp.bfloat16),
+            pltpu.VMEM((rank, rows), jnp.bfloat16), pltpu.VMEM((rank, rows), jnp.bfloat16),
+            pltpu.VMEM((rank, depth), jnp.float32), pltpu.VMEM((packed, LANES), jnp.float32),
+            pltpu.SemaphoreType.DMA((rows // BLOCK + 1,)),
         ],
-        compiler_params=pltpu.CompilerParams(vmem_limit_bytes=58 * 2**20),
+        compiler_params=pltpu.CompilerParams(vmem_limit_bytes=51 * 2**20),
         cost_estimate=pl.CostEstimate(flops=4 * 10**9, bytes_accessed=8 * 2**20, transcendentals=0),
         name="local_terms",
     )(features, sketch)
+
+
+def stage_kernel(terms, *refs):
+    cross, (gram_ref, gram_other_ref, gram_out_ref), outs = refs[:terms], refs[terms:terms + 3], refs[terms + 3:]
+    gram_out_ref[...] = gram_ref[...] + gram_other_ref[...]
+    height = outs[0].shape[0]
+    for at, out_ref in enumerate(outs):
+        span = slice(at * height, (at + 1) * height)
+        out_ref[...] = sum(ref[span, :] for ref in cross)
+
+
+def join_kernel(*refs):
+    *cross, gram_ref, gram_other_ref, gram_out_ref, out_ref = refs
+    gram_out_ref[...] = gram_ref[...] + gram_other_ref[...]
+    top = 0
+    for ref in cross:
+        out_ref[top:top + ref.shape[0], :] = ref[...]
+        top += ref.shape[0]
+
+
+def stage(cross, gram, gram_other, pieces, join=False):
+    height, depth = cross[0].shape
+    outs = [f32(len(cross) * height, depth)] if join else [f32(height // pieces, depth)] * pieces
+    kernel = join_kernel if join else lambda *refs: stage_kernel(len(cross), *refs)
+    gram, *outs = pl.pallas_call(
+        kernel,
+        out_shape=(f32(*gram.shape), *outs),
+        in_specs=[VMEM] * (len(cross) + 2),
+        out_specs=(VMEM,) * (1 + len(outs)),
+        compiler_params=pltpu.CompilerParams(vmem_limit_bytes=16 * 2**20),
+        cost_estimate=pl.CostEstimate(flops=10**6, bytes_accessed=10**6, transcendentals=0),
+        name="join" if join else "stage",
+    )(*cross, gram, gram_other)
+    return gram, outs
 
 
 def factor_kernel(scale, first, last, *refs):
@@ -216,18 +260,20 @@
 
 
 def basis_kernel(sampled_ref, flipped_ref, basis_ref):
-    basis_ref[...] = product(split(sampled_ref[...]), split(flipped_ref[...]), 1, 0)
+    flipped = split(flipped_ref[...])
+    for top in range(0, sampled_ref.shape[0], BLOCK):
+        span = slice(top, top + BLOCK)
+        basis_ref[span, :] = product(split(sampled_ref[span, :]), flipped, 1, 0)
 
 
 def basis_of(sampled, flipped):
-    rows, rank = sampled.shape
     return pl.pallas_call(
         basis_kernel,
-        grid=(rows // BLOCK,),
-        out_shape=jax.ShapeDtypeStruct(sampled.shape, jnp.float32),
-        in_specs=[pl.BlockSpec((BLOCK, rank), lambda i: (i, 0)), pl.BlockSpec((rank, rank), lambda i: (0, 0))],
-        out_specs=pl.BlockSpec((BLOCK, rank), lambda i: (i, 0)),
-        cost_estimate=pl.CostEstimate(flops=4 * 10**8, bytes_accessed=2 * 2**20, transcendentals=0),
+        out_shape=f32(*sampled.shape),
+        in_specs=[VMEM] * 2,
+        out_specs=VMEM,
+        compiler_params=pltpu.CompilerParams(vmem_limit_bytes=16 * 2**20),
+        cost_estimate=pl.CostEstimate(flops=2 * 10**9, bytes_accessed=2 * 2**20, transcendentals=0),
         name="basis",
     )(sampled, flipped)
 
@@ -279,44 +325,40 @@
     return wide + narrow
 
 
-def sum_gram(keep, other):
-    half = keep + send(other, *CORE)
-    for mask in [(0, 1), (2, 0), (4, 0), (8, 0)] + spare_bits():
-        half = half + send(half, *mask)
-    return half, send(half, *CORE)
-
-
-def quarters(values):
-    height = values[0].shape[0] // 4
-    return [sum(value[at * height:(at + 1) * height] for value in values) for at in range(4)]
-
-
-def scatter(values, masks):
-    first, *rest = quarters(values)
+def spread(parts, masks):
+    first, *rest = parts
     return [first] + [send(part, *mask) for part, mask in zip(rest, masks)]
 
 
-def sum_cross(keep, other):
-    values = scatter([keep, send(other, *CORE)], PLANE)
-    values = scatter(values, LINE)
-    own = sum(values)
+def sums_and_factors(keep, other, gram_keep, gram_other, factors):
+    cross = [keep, send(other, *CORE)]
+    gram, parts = stage(cross, gram_keep, send(gram_other, *CORE), 4)
+    cross = spread(parts, PLANE)
+    gram = gram + send(gram, *LINE[0])
+    gram, parts = stage(cross, gram, send(gram, *LINE[1]), 4)
+    cross = spread(parts, LINE)
+    gram, (own,) = stage(cross, gram, send(gram, *PLANE[0]), 1)
     for mask in spare_bits():
         own = own + send(own, *mask)
-    line = jnp.concatenate([own] + [send(own, *mask) for mask in LINE])
+        gram = gram + send(gram, *mask)
+    line = [own] + [send(own, *mask) for mask in LINE]
+    gram, (line,) = stage(line, gram, send(gram, *PLANE[1]), 1, join=True)
     plane = [line] + [send(line, *mask) for mask in PLANE]
-    return plane + [send(part, *CORE) for part in plane]
+    factors = factors((gram, send(gram, *CORE)))
+    return plane + [send(part, *CORE) for part in plane], factors
 
 
 def per_device(features, sketch):
     scale = (features.shape[0] * lax.axis_size(AXES)) ** 0.5
     size = sketch.shape[1]
-    sampled, keep, other, gram_keep, gram_other = local_terms(features, sketch)
-    gram = sum_gram(gram_keep, gram_other)
-    cross = sum_cross(keep, other)
-    state = gram
-    for first in range(0, size, PANEL):
-        state = factor_part(state[:2], size, scale, first, first + PANEL)
-    inverse, factor, flipped = state
+
+    def factors(state):
+        for first in range(0, size, PANEL):
+            state = factor_part(state[:2], size, scale, first, first + PANEL)
+        return state
+
+    sampled, *terms = local_terms(features, sketch)
+    cross, (inverse, factor, flipped) = sums_and_factors(*terms, factors)
     return (basis_of(sampled, flipped), factor, project(inverse, cross))
 
 

time: 70.6 us -> 61.7 us (0.87)
  Pallas kernels: 25.6 us -> 21.1 us
  waiting for transfers between devices: 15.8 us -> 13.6 us
  other arithmetic: 2.18 us -> 0.01 us
  starting transfers between devices: 25.3 us -> 26.2 us
    pallas_call x2 -> x6, Pallas kernels: 14.5 us -> 10 us  [the longest x1 8.34 us: local_terms(): pl.pallas_call(local_kernel, out_shape=(f32(rows, rank), f32(rank // 2, d...]
    ppermute x23, waiting for transfers between devices: 15.8 us -> 13.6 us  [send(): return lax.ppermute(value, AXES, pairs)]
    add x8 -> x1, other arithmetic: 2.17 us -> 0.01 us  [sums_and_factors(): gram = gram + send(gram, *LINE[0])]
    ppermute x23, starting transfers between devices: 25.3 us -> 26.2 us  [send(): return lax.ppermute(value, AXES, pairs)]
  transfers between devices with their start and end apart: 23 -> 23, of which waited for: 9 -> 8; matrix products, arithmetic and copies ran while one was open for 3% -> 0% of each run, Pallas kernels for 19% -> 18%
where the time goes in v5:
time: 61.7 us; the launch traced here: 61.6 us
  starting transfers between devices  26.2 us (42%)
  Pallas kernels  21.1 us (34%)
  waiting for transfers between devices  13.6 us (22%)
  between operations  0.73 us (1%)
    ppermute x23, starting transfers between devices, send(): return lax.ppermute(value, AXES, pairs)  26.2 us
    ppermute x23, waiting for transfers between devices, send(): return lax.ppermute(value, AXES, pairs)  13.6 us
    pallas_call x4, Pallas kernels, factor_part(): pl.pallas_call(lambda *refs: factor_kernel(scale, first, last, *refs), ou...  9.41 us
    pallas_call x1, Pallas kernels, local_terms(): pl.pallas_call(local_kernel, out_shape=(f32(rows, rank), f32(rank // 2, d...  8.34 us
    pallas_call x1, Pallas kernels, project(): pl.pallas_call(project_kernel, out_shape=jax.ShapeDtypeStruct((rank, dept...  1.66 us
    pallas_call x1, Pallas kernels, basis_of(): pl.pallas_call(basis_kernel, out_shape=f32(*sampled.shape), in_specs=[VME...  1.55 us
  transfers between devices with their start and end apart: 23, of which 8 were waited for; matrix products, arithmetic and copies ran while one was open for 0% of the time, Pallas kernels for 18%

profile of v5, /device:TPU:0, one launch (start us, length us, event | category | flops | bytes accessed | tf_op | source)
XLA Modules:
  0.0 61.6 jit_solution(12405368222693670149)
XLA Ops:
  0.6 8.3 %local_terms.1 = (f32[1024,256]{1,0:T(8,128)S(1)}, f32[128,1024]{1,0:T(8,128)S(1)}, f32[128,1024]{1,0:T(8,128)S(1)}, f32[192,128]{1,0:T(8,128)S(1)}, f32[192,128]{1,0:T(8,128)S(1)}) custom-call(f32[1024,1024]{1,0:T(8,128)} %features_hbm.1, f32[1024,256]{1,0:T(8,128)} %sketch_hbm.1), custom_call_target="tpu_custom_call" | custom-call | flops 4000000000 | bytes 8388608 | tf_op jit(solution)/shard_map/local_terms/pallas_call | solution.py:168
  9.0 0.5 collective-permute-start
  9.5 0.1 collective-permute-start.1
  9.6 1.6 %collective-permute-done.1.refs_3_ = f32[192,128]{1,0:T(8,128)S(1)} collective-permute-done((f32[192,128]{1,0:T(8,128)S(1)}, f32[192,128]{1,0:T(8,128)S(1)}, u32[]{:S(2)}, u32[]{:S(2)}) %collective-permute-start.1) | collective-permute-done | bytes 98336 | tf_op jit(solution)/shard_map/ppermute | solution.py:314
  11.2 0.0 collective-permute-done.refs_1_
  11.2 0.1 stage.3
  11.2 3.0 %collective-permute-start.5 = (f32[192,128]{1,0:T(8,128)S(1)}, f32[192,128]{1,0:T(8,128)S(1)}, u32[]{:S(2)}, u32[]{:S(2)}) collective-permute-start(f32[192,128]{1,0:T(8,128)S(1)} %get-tuple-element.40), channel_id=1, source_target_pairs={{0,8},{1,9},{2,10},{3,11},{4,12},{5,13},{6,14},{7,15},{8,0},{9,1},... | collective-permute-start | bytes 294920 | tf_op jit(solution)/shard_map/ppermute | solution.py:314
  14.3 1.5 %collective-permute-start.2 = (f32[32,1024]{1,0:T(8,128)S(1)}, f32[32,1024]{1,0:T(8,128)S(1)}, u32[]{:S(2)}, u32[]{:S(2)}) collective-permute-start(f32[32,1024]{1,0:T(8,128)S(1)} %get-tuple-element.37), channel_id=1, source_target_pairs={{0,1},{1,0},{2,3},{3,2},{4,5},{5,4},{6,7},{7,6},{8,9},{9,8},{10,11... | collective-permute-start | bytes 393224 | tf_op jit(solution)/shard_map/ppermute | solution.py:314
  15.8 1.5 %collective-permute-start.3 = (f32[32,1024]{1,0:T(8,128)S(1)}, f32[32,1024]{1,0:T(8,128)S(1)}, u32[]{:S(2)}, u32[]{:S(2)}) collective-permute-start(f32[32,1024]{1,0:T(8,128)S(1)} %get-tuple-element.38), channel_id=1, source_target_pairs={{0,4},{1,5},{2,6},{3,7},{4,0},{5,1},{6,2},{7,3},{8,12},{9,13},{10,... | collective-permute-start | bytes 393224 | tf_op jit(solution)/shard_map/ppermute | solution.py:314
  17.3 0.5 collective-permute-start.4
  17.7 0.0 collective-permute-done.5
  17.8 2.7 %collective-permute-start.6 = (f32[192,128]{1,0:T(8,128)S(1)}, f32[192,128]{1,0:T(8,128)S(1)}, u32[]{:S(2)}, u32[]{:S(2)}) collective-permute-start(f32[192,128]{1,0:T(8,128)S(1)} %add.3.refs_4_), channel_id=1, source_target_pairs={{0,16},{1,17},{2,18},{3,19},{4,20},{5,21},{6,22},{7,23},{8,24},{9,... | collective-permute-start | bytes 294920 | tf_op jit(solution)/shard_map/ppermute | solution.py:314
  20.4 0.0 collective-permute-done.2.refs_1_
  20.4 1.7 %collective-permute-done.3.refs_2_ = f32[32,1024]{1,0:T(8,128)S(1)} collective-permute-done((f32[32,1024]{1,0:T(8,128)S(1)}, f32[32,1024]{1,0:T(8,128)S(1)}, u32[]{:S(2)}, u32[]{:S(2)}) %collective-permute-start.3) | collective-permute-done | bytes 131104 | tf_op jit(solution)/shard_map/ppermute | solution.py:314
  22.2 1.3 %collective-permute-done.4.refs_3_ = f32[32,1024]{1,0:T(8,128)S(1)} collective-permute-done((f32[32,1024]{1,0:T(8,128)S(1)}, f32[32,1024]{1,0:T(8,128)S(1)}, u32[]{:S(2)}, u32[]{:S(2)}) %collective-permute-start.4) | collective-permute-done | bytes 131104 | tf_op jit(solution)/shard_map/ppermute | solution.py:314
  23.5 1.3 %collective-permute-done.6.refs_5_ = f32[192,128]{1,0:T(8,128)S(1)} collective-permute-done((f32[192,128]{1,0:T(8,128)S(1)}, f32[192,128]{1,0:T(8,128)S(1)}, u32[]{:S(2)}, u32[]{:S(2)}) %collective-permute-start.6) | collective-permute-done | bytes 98336 | tf_op jit(solution)/shard_map/ppermute | solution.py:314
  24.8 1.4 %collective-permute-start.10 = (f32[192,128]{1,0:T(8,128)S(1)}, f32[192,128]{1,0:T(8,128)S(1)}, u32[]{:S(2)}, u32[]{:S(2)}) collective-permute-start(f32[192,128]{1,0:T(8,128)S(1)} %get-tuple-element.45.refs_4_), channel_id=1, source_target_pairs={{0,1},{1,0},{2,3},{3,2},{4,5},{5,4},{6,7},{7,6},{8,9},{9,8},{10,11... | collective-permute-start | bytes 294920 | tf_op jit(solution)/shard_map/ppermute | solution.py:314
  26.2 0.7 %collective-permute-start.7 = (f32[8,1024]{1,0:T(8,128)S(1)}, f32[8,1024]{1,0:T(8,128)S(1)}, u32[]{:S(2)}, u32[]{:S(2)}) collective-permute-start(f32[8,1024]{1,0:T(8,128)S(1)} %get-tuple-element.42), channel_id=1, source_target_pairs={{0,8},{1,9},{2,10},{3,11},{4,12},{5,13},{6,14},{7,15},{8,0},{9,1},... | collective-permute-start | bytes 98312 | tf_op jit(solution)/shard_map/ppermute | solution.py:314
  26.9 3.4 %collective-permute-start.8 = (f32[8,1024]{1,0:T(8,128)S(1)}, f32[8,1024]{1,0:T(8,128)S(1)}, u32[]{:S(2)}, u32[]{:S(2)}) collective-permute-start(f32[8,1024]{1,0:T(8,128)S(1)} %get-tuple-element.43), channel_id=1, source_target_pairs={{0,16},{1,17},{2,18},{3,19},{4,20},{5,21},{6,22},{7,23},{8,24},{9,... | collective-permute-start | bytes 98312 | tf_op jit(solution)/shard_map/ppermute | solution.py:314
  30.3 0.3 collective-permute-start.9
  30.6 0.0 collective-permute-done.7.refs_1_
  30.6 1.6 %collective-permute-done.8.refs_2_ = f32[8,1024]{1,0:T(8,128)S(1)} collective-permute-done((f32[8,1024]{1,0:T(8,128)S(1)}, f32[8,1024]{1,0:T(8,128)S(1)}, u32[]{:S(2)}, u32[]{:S(2)}) %collective-permute-start.8) | collective-permute-done | bytes 32800 | tf_op jit(solution)/shard_map/ppermute | solution.py:314
  32.2 3.8 %collective-permute-done.9.refs_3_ = f32[8,1024]{1,0:T(8,128)S(1)} collective-permute-done((f32[8,1024]{1,0:T(8,128)S(1)}, f32[8,1024]{1,0:T(8,128)S(1)}, u32[]{:S(2)}, u32[]{:S(2)}) %collective-permute-start.9) | collective-permute-done | bytes 32800 | tf_op jit(solution)/shard_map/ppermute | solution.py:314
  36.0 0.0 collective-permute-done.10.refs_5_
  36.0 1.6 %collective-permute-start.14 = (f32[192,128]{1,0:T(8,128)S(1)}, f32[192,128]{1,0:T(8,128)S(1)}, u32[]{:S(2)}, u32[]{:S(2)}) collective-permute-start(f32[192,128]{1,0:T(8,128)S(1)} %get-tuple-element.47.refs_4_), channel_id=1, source_target_pairs={{0,4},{1,5},{2,6},{3,7},{4,0},{5,1},{6,2},{7,3},{8,12},{9,13},{10,... | collective-permute-start | bytes 294920 | tf_op jit(solution)/shard_map/ppermute | solution.py:314
  37.6 0.0 collective-permute-start.11
  37.6 0.9 %collective-permute-start.12 = (f32[8,1024]{1,0:T(8,128)S(1)}, f32[8,1024]{1,0:T(8,128)S(1)}, u32[]{:S(2)}, u32[]{:S(2)}) collective-permute-start(f32[8,1024]{1,0:T(8,128)S(1)} %get-tuple-element.46.refs_0_), channel_id=1, source_target_pairs={{0,16},{1,17},{2,18},{3,19},{4,20},{5,21},{6,22},{7,23},{8,24},{9,... | collective-permute-start | bytes 98312 | tf_op jit(solution)/shard_map/ppermute | solution.py:314
  38.5 3.5 %collective-permute-start.13 = (f32[8,1024]{1,0:T(8,128)S(1)}, f32[8,1024]{1,0:T(8,128)S(1)}, u32[]{:S(2)}, u32[]{:S(2)}) collective-permute-start(f32[8,1024]{1,0:T(8,128)S(1)} %get-tuple-element.46.refs_0_), channel_id=1, source_target_pairs={{0,24},{1,25},{2,26},{3,27},{4,28},{5,29},{6,30},{7,31},{8,16},{9,... | collective-permute-start | bytes 98312 | tf_op jit(solution)/shard_map/ppermute | solution.py:314
  42.0 0.0 collective-permute-done.11.refs_1_
  42.0 0.4 collective-permute-done.12.refs_2_
  42.4 1.8 %collective-permute-done.13.refs_3_ = f32[8,1024]{1,0:T(8,128)S(1)} collective-permute-done((f32[8,1024]{1,0:T(8,128)S(1)}, f32[8,1024]{1,0:T(8,128)S(1)}, u32[]{:S(2)}, u32[]{:S(2)}) %collective-permute-start.13) | collective-permute-done | bytes 32800 | tf_op jit(solution)/shard_map/ppermute | solution.py:314
  44.2 0.0 collective-permute-done.14.refs_5_
  44.2 0.1 collective-permute-start.15
  44.3 0.6 collective-permute-start.16
  44.9 0.7 %collective-permute-start.17 = (f32[32,1024]{1,0:T(8,128)S(1)}, f32[32,1024]{1,0:T(8,128)S(1)}, u32[]{:S(2)}, u32[]{:S(2)}) collective-permute-start(f32[32,1024]{1,0:T(8,128)S(1)} %get-tuple-element.58.refs_0_), channel_id=1, source_target_pairs={{0,4},{1,5},{2,6},{3,7},{4,0},{5,1},{6,2},{7,3},{8,12},{9,13},{10,... | collective-permute-start | bytes 393224 | tf_op jit(solution)/shard_map/ppermute | solution.py:314
  45.6 2.3 %collective-permute-start.18 = (f32[32,1024]{1,0:T(8,128)S(1)}, f32[32,1024]{1,0:T(8,128)S(1)}, u32[]{:S(2)}, u32[]{:S(2)}) collective-permute-start(f32[32,1024]{1,0:T(8,128)S(1)} %get-tuple-element.58.refs_0_), channel_id=1, source_target_pairs={{0,5},{1,4},{2,7},{3,6},{4,1},{5,0},{6,3},{7,2},{8,13},{9,12},{10,... | collective-permute-start | bytes 393224 | tf_op jit(solution)/shard_map/ppermute | solution.py:314
  47.9 0.0 collective-permute-start.19
  47.9 0.0 collective-permute-done.15.refs_1_
  47.9 2.3 %factor_part.4 = (f32[256,256]{1,0:T(8,128)S(1)}, f32[256,256]{1,0:T(8,128)S(1)}) custom-call(f32[192,128]{1,0:T(8,128)S(1)} %get-tuple-element.48.refs_0_, f32[192,128]{1,0:T(8,128)S(1)} %collective-permute-done.15.refs_1_), custom_call_target="tpu_custom_call" | custom-call | flops 3000000000 | bytes 1048576 | tf_op jit(solution)/shard_map/factor_part/pallas_call | solution.py:250
  50.2 2.2 %factor_part.5 = (f32[256,256]{1,0:T(8,128)S(1)}, f32[256,256]{1,0:T(8,128)S(1)}) custom-call(f32[256,256]{1,0:T(8,128)S(1)} %get-tuple-element.49.refs_0_, f32[256,256]{1,0:T(8,128)S(1)} %get-tuple-element.50.refs_1_), custom_call_target="tpu_custom_call" | custom-call | flops 3000000000 | bytes 1048576 | tf_op jit(solution)/shard_map/factor_part/pallas_call | solution.py:250
  52.4 2.2 %factor_part.6 = (f32[256,256]{1,0:T(8,128)S(1)}, f32[256,256]{1,0:T(8,128)S(1)}) custom-call(f32[256,256]{1,0:T(8,128)S(1)} %get-tuple-element.51.refs_0_, f32[256,256]{1,0:T(8,128)S(1)} %get-tuple-element.52.refs_1_), custom_call_target="tpu_custom_call" | custom-call | flops 3000000000 | bytes 1048576 | tf_op jit(solution)/shard_map/factor_part/pallas_call | solution.py:250
  54.7 2.6 %factor_part.7 = (f32[256,256]{1,0:T(8,128)S(1)}, f32[256,256]{1,0:T(8,128)}, f32[256,256]{1,0:T(8,128)S(1)}) custom-call(f32[256,256]{1,0:T(8,128)S(1)} %get-tuple-element.53.refs_0_, f32[256,256]{1,0:T(8,128)S(1)} %get-tuple-element.54.refs_1_), custom_call_target="tpu_custom_call" | custom-call | flops 3000000000 | bytes 1048576 | tf_op jit(solution)/shard_map/factor_part/pallas_call | solution.py:250
  57.3 0.0 collective-permute-done.16.refs_1_
  57.3 0.5 collective-permute-start.20
  57.8 0.0 collective-permute-done.17.refs_2_
  57.8 0.1 collective-permute-start.21
  57.9 0.0 collective-permute-done.18.refs_3_
  57.9 0.4 collective-permute-start.22
  58.4 1.5 %basis.1 = f32[1024,256]{1,0:T(8,128)} custom-call(f32[1024,256]{1,0:T(8,128)S(1)} %get-tuple-element.31.sampled_ref, f32[256,256]{1,0:T(8,128)S(1)} %get-tuple-element.55.flipped_ref), custom_call_target="tpu_custom_call" | custom-call | flops 2000000000 | bytes 2097152 | tf_op jit(solution)/shard_map/basis/pallas_call | solution.py:270
  59.9 0.0 collective-permute-done.19.refs_4_
  59.9 0.0 collective-permute-done.20.refs_5_
  59.9 0.0 collective-permute-done.21.refs_6_
  59.9 0.0 collective-permute-done.22.refs_7_
  59.9 1.7 %project.1 = f32[256,1024]{1,0:T(8,128)} custom-call(f32[256,256]{1,0:T(8,128)S(1)} %get-tuple-element.57.inverse_ref, f32[32,1024]{1,0:T(8,128)S(1)} %get-tuple-element.58.refs_0_, f32[32,1024]{1,0:T(8,128)S(1)} %collective-permute-done.16.refs_1_, f32[32,1024]{1,0:T(8,128)S(1)} %collective-permute-done.17.refs_2_, ...), custom_call_target="tpu_custom_call" | custom-call | flops 400000000 | bytes 2097152 | tf_op jit(solution)/shard_map/project/pallas_call | solution.py:299
  (4 shorter events, 0.1 us)
Async XLA Ops:
  9.0 2.2 %collective-permute-start = (f32[128,1024]{1,0:T(8,128)S(1)}, f32[128,1024]{1,0:T(8,128)S(1)}, u32[]{:S(2)}, u32[]{:S(2)}) collective-permute-start(f32[128,1024]{1,0:T(8,128)S(1)} %get-tuple-element.33), channel_id=1, source_target_pairs={{0,2},{1,3},{2,0},{3,1},{4,6},{5,7},{6,4},{7,5},{8,10},{9,11},{10,... | collective-permute-start | bytes 1572872 | tf_op jit(solution)/shard_map/ppermute | solution.py:314
  9.5 1.7 %collective-permute-start.1 = (f32[192,128]{1,0:T(8,128)S(1)}, f32[192,128]{1,0:T(8,128)S(1)}, u32[]{:S(2)}, u32[]{:S(2)}) collective-permute-start(f32[192,128]{1,0:T(8,128)S(1)} %get-tuple-element.35), channel_id=1, source_target_pairs={{0,2},{1,3},{2,0},{3,1},{4,6},{5,7},{6,4},{7,5},{8,10},{9,11},{10,... | collective-permute-start | bytes 294920 | tf_op jit(solution)/shard_map/ppermute | solution.py:314
  11.2 6.5 %collective-permute-start.5 = (f32[192,128]{1,0:T(8,128)S(1)}, f32[192,128]{1,0:T(8,128)S(1)}, u32[]{:S(2)}, u32[]{:S(2)}) collective-permute-start(f32[192,128]{1,0:T(8,128)S(1)} %get-tuple-element.40), channel_id=1, source_target_pairs={{0,8},{1,9},{2,10},{3,11},{4,12},{5,13},{6,14},{7,15},{8,0},{9,1},... | collective-permute-start | bytes 294920 | tf_op jit(solution)/shard_map/ppermute | solution.py:314
  14.3 6.2 %collective-permute-start.2 = (f32[32,1024]{1,0:T(8,128)S(1)}, f32[32,1024]{1,0:T(8,128)S(1)}, u32[]{:S(2)}, u32[]{:S(2)}) collective-permute-start(f32[32,1024]{1,0:T(8,128)S(1)} %get-tuple-element.37), channel_id=1, source_target_pairs={{0,1},{1,0},{2,3},{3,2},{4,5},{5,4},{6,7},{7,6},{8,9},{9,8},{10,11... | collective-permute-start | bytes 393224 | tf_op jit(solution)/shard_map/ppermute | solution.py:314
  15.8 6.4 %collective-permute-start.3 = (f32[32,1024]{1,0:T(8,128)S(1)}, f32[32,1024]{1,0:T(8,128)S(1)}, u32[]{:S(2)}, u32[]{:S(2)}) collective-permute-start(f32[32,1024]{1,0:T(8,128)S(1)} %get-tuple-element.38), channel_id=1, source_target_pairs={{0,4},{1,5},{2,6},{3,7},{4,0},{5,1},{6,2},{7,3},{8,12},{9,13},{10,... | collective-permute-start | bytes 393224 | tf_op jit(solution)/shard_map/ppermute | solution.py:314
  17.3 6.2 %collective-permute-start.4 = (f32[32,1024]{1,0:T(8,128)S(1)}, f32[32,1024]{1,0:T(8,128)S(1)}, u32[]{:S(2)}, u32[]{:S(2)}) collective-permute-start(f32[32,1024]{1,0:T(8,128)S(1)} %get-tuple-element.39), channel_id=1, source_target_pairs={{0,5},{1,4},{2,7},{3,6},{4,1},{5,0},{6,3},{7,2},{8,13},{9,12},{10,... | collective-permute-start | bytes 393224 | tf_op jit(solution)/shard_map/ppermute | solution.py:314
  17.8 7.0 %collective-permute-start.6 = (f32[192,128]{1,0:T(8,128)S(1)}, f32[192,128]{1,0:T(8,128)S(1)}, u32[]{:S(2)}, u32[]{:S(2)}) collective-permute-start(f32[192,128]{1,0:T(8,128)S(1)} %add.3.refs_4_), channel_id=1, source_target_pairs={{0,16},{1,17},{2,18},{3,19},{4,20},{5,21},{6,22},{7,23},{8,24},{9,... | collective-permute-start | bytes 294920 | tf_op jit(solution)/shard_map/ppermute | solution.py:314
  24.8 11.2 %collective-permute-start.10 = (f32[192,128]{1,0:T(8,128)S(1)}, f32[192,128]{1,0:T(8,128)S(1)}, u32[]{:S(2)}, u32[]{:S(2)}) collective-permute-start(f32[192,128]{1,0:T(8,128)S(1)} %get-tuple-element.45.refs_4_), channel_id=1, source_target_pairs={{0,1},{1,0},{2,3},{3,2},{4,5},{5,4},{6,7},{7,6},{8,9},{9,8},{10,11... | collective-permute-start | bytes 294920 | tf_op jit(solution)/shard_map/ppermute | solution.py:314
  26.2 4.4 %collective-permute-start.7 = (f32[8,1024]{1,0:T(8,128)S(1)}, f32[8,1024]{1,0:T(8,128)S(1)}, u32[]{:S(2)}, u32[]{:S(2)}) collective-permute-start(f32[8,1024]{1,0:T(8,128)S(1)} %get-tuple-element.42), channel_id=1, source_target_pairs={{0,8},{1,9},{2,10},{3,11},{4,12},{5,13},{6,14},{7,15},{8,0},{9,1},... | collective-permute-start | bytes 98312 | tf_op jit(solution)/shard_map/ppermute | solution.py:314
  26.9 5.3 %collective-permute-start.8 = (f32[8,1024]{1,0:T(8,128)S(1)}, f32[8,1024]{1,0:T(8,128)S(1)}, u32[]{:S(2)}, u32[]{:S(2)}) collective-permute-start(f32[8,1024]{1,0:T(8,128)S(1)} %get-tuple-element.43), channel_id=1, source_target_pairs={{0,16},{1,17},{2,18},{3,19},{4,20},{5,21},{6,22},{7,23},{8,24},{9,... | collective-permute-start | bytes 98312 | tf_op jit(solution)/shard_map/ppermute | solution.py:314
  30.3 5.7 %collective-permute-start.9 = (f32[8,1024]{1,0:T(8,128)S(1)}, f32[8,1024]{1,0:T(8,128)S(1)}, u32[]{:S(2)}, u32[]{:S(2)}) collective-permute-start(f32[8,1024]{1,0:T(8,128)S(1)} %get-tuple-element.44), channel_id=1, source_target_pairs={{0,24},{1,25},{2,26},{3,27},{4,28},{5,29},{6,30},{7,31},{8,16},{9,... | collective-permute-start | bytes 98312 | tf_op jit(solution)/shard_map/ppermute | solution.py:314
  36.0 8.2 %collective-permute-start.14 = (f32[192,128]{1,0:T(8,128)S(1)}, f32[192,128]{1,0:T(8,128)S(1)}, u32[]{:S(2)}, u32[]{:S(2)}) collective-permute-start(f32[192,128]{1,0:T(8,128)S(1)} %get-tuple-element.47.refs_4_), channel_id=1, source_target_pairs={{0,4},{1,5},{2,6},{3,7},{4,0},{5,1},{6,2},{7,3},{8,12},{9,13},{10,... | collective-permute-start | bytes 294920 | tf_op jit(solution)/shard_map/ppermute | solution.py:314
  37.6 4.4 %collective-permute-start.11 = (f32[8,1024]{1,0:T(8,128)S(1)}, f32[8,1024]{1,0:T(8,128)S(1)}, u32[]{:S(2)}, u32[]{:S(2)}) collective-permute-start(f32[8,1024]{1,0:T(8,128)S(1)} %get-tuple-element.46.refs_0_), channel_id=1, source_target_pairs={{0,8},{1,9},{2,10},{3,11},{4,12},{5,13},{6,14},{7,15},{8,0},{9,1},... | collective-permute-start | bytes 98312 | tf_op jit(solution)/shard_map/ppermute | solution.py:314
  37.6 4.8 %collective-permute-start.12 = (f32[8,1024]{1,0:T(8,128)S(1)}, f32[8,1024]{1,0:T(8,128)S(1)}, u32[]{:S(2)}, u32[]{:S(2)}) collective-permute-start(f32[8,1024]{1,0:T(8,128)S(1)} %get-tuple-element.46.refs_0_), channel_id=1, source_target_pairs={{0,16},{1,17},{2,18},{3,19},{4,20},{5,21},{6,22},{7,23},{8,24},{9,... | collective-permute-start | bytes 98312 | tf_op jit(solution)/shard_map/ppermute | solution.py:314
  38.5 5.7 %collective-permute-start.13 = (f32[8,1024]{1,0:T(8,128)S(1)}, f32[8,1024]{1,0:T(8,128)S(1)}, u32[]{:S(2)}, u32[]{:S(2)}) collective-permute-start(f32[8,1024]{1,0:T(8,128)S(1)} %get-tuple-element.46.refs_0_), channel_id=1, source_target_pairs={{0,24},{1,25},{2,26},{3,27},{4,28},{5,29},{6,30},{7,31},{8,16},{9,... | collective-permute-start | bytes 98312 | tf_op jit(solution)/shard_map/ppermute | solution.py:314
  44.2 3.6 %collective-permute-start.15 = (f32[192,128]{1,0:T(8,128)S(1)}, f32[192,128]{1,0:T(8,128)S(1)}, u32[]{:S(2)}, u32[]{:S(2)}) collective-permute-start(f32[192,128]{1,0:T(8,128)S(1)} %get-tuple-element.48.refs_0_), channel_id=1, source_target_pairs={{0,2},{1,3},{2,0},{3,1},{4,6},{5,7},{6,4},{7,5},{8,10},{9,11},{10,... | collective-permute-start | bytes 294920 | tf_op jit(solution)/shard_map/ppermute | solution.py:314
  44.3 13.0 %collective-permute-start.16 = (f32[32,1024]{1,0:T(8,128)S(1)}, f32[32,1024]{1,0:T(8,128)S(1)}, u32[]{:S(2)}, u32[]{:S(2)}) collective-permute-start(f32[32,1024]{1,0:T(8,128)S(1)} %get-tuple-element.58.refs_0_), channel_id=1, source_target_pairs={{0,1},{1,0},{2,3},{3,2},{4,5},{5,4},{6,7},{7,6},{8,9},{9,8},{10,11... | collective-permute-start | bytes 393224 | tf_op jit(solution)/shard_map/ppermute | solution.py:314
  44.9 12.9 %collective-permute-start.17 = (f32[32,1024]{1,0:T(8,128)S(1)}, f32[32,1024]{1,0:T(8,128)S(1)}, u32[]{:S(2)}, u32[]{:S(2)}) collective-permute-start(f32[32,1024]{1,0:T(8,128)S(1)} %get-tuple-element.58.refs_0_), channel_id=1, source_target_pairs={{0,4},{1,5},{2,6},{3,7},{4,0},{5,1},{6,2},{7,3},{8,12},{9,13},{10,... | collective-permute-start | bytes 393224 | tf_op jit(solution)/shard_map/ppermute | solution.py:314
  45.6 12.3 %collective-permute-start.18 = (f32[32,1024]{1,0:T(8,128)S(1)}, f32[32,1024]{1,0:T(8,128)S(1)}, u32[]{:S(2)}, u32[]{:S(2)}) collective-permute-start(f32[32,1024]{1,0:T(8,128)S(1)} %get-tuple-element.58.refs_0_), channel_id=1, source_target_pairs={{0,5},{1,4},{2,7},{3,6},{4,1},{5,0},{6,3},{7,2},{8,13},{9,12},{10,... | collective-permute-start | bytes 393224 | tf_op jit(solution)/shard_map/ppermute | solution.py:314
  47.9 12.0 %collective-permute-start.19 = (f32[32,1024]{1,0:T(8,128)S(1)}, f32[32,1024]{1,0:T(8,128)S(1)}, u32[]{:S(2)}, u32[]{:S(2)}) collective-permute-start(f32[32,1024]{1,0:T(8,128)S(1)} %get-tuple-element.58.refs_0_), channel_id=1, source_target_pairs={{0,2},{1,3},{2,0},{3,1},{4,6},{5,7},{6,4},{7,5},{8,10},{9,11},{10,... | collective-permute-start | bytes 393224 | tf_op jit(solution)/shard_map/ppermute | solution.py:314
  57.3 2.6 %collective-permute-start.20 = (f32[32,1024]{1,0:T(8,128)S(1)}, f32[32,1024]{1,0:T(8,128)S(1)}, u32[]{:S(2)}, u32[]{:S(2)}) collective-permute-start(f32[32,1024]{1,0:T(8,128)S(1)} %collective-permute-done.16.refs_1_), channel_id=1, source_target_pairs={{0,2},{1,3},{2,0},{3,1},{4,6},{5,7},{6,4},{7,5},{8,10},{9,11},{10,... | collective-permute-start | bytes 393224 | tf_op jit(solution)/shard_map/ppermute | solution.py:314
  57.8 2.1 %collective-permute-start.21 = (f32[32,1024]{1,0:T(8,128)S(1)}, f32[32,1024]{1,0:T(8,128)S(1)}, u32[]{:S(2)}, u32[]{:S(2)}) collective-permute-start(f32[32,1024]{1,0:T(8,128)S(1)} %collective-permute-done.17.refs_2_), channel_id=1, source_target_pairs={{0,2},{1,3},{2,0},{3,1},{4,6},{5,7},{6,4},{7,5},{8,10},{9,11},{10,... | collective-permute-start | bytes 393224 | tf_op jit(solution)/shard_map/ppermute | solution.py:314
  57.9 2.0 %collective-permute-start.22 = (f32[32,1024]{1,0:T(8,128)S(1)}, f32[32,1024]{1,0:T(8,128)S(1)}, u32[]{:S(2)}, u32[]{:S(2)}) collective-permute-start(f32[32,1024]{1,0:T(8,128)S(1)} %collective-permute-done.18.refs_3_), channel_id=1, source_target_pairs={{0,2},{1,3},{2,0},{3,1},{4,6},{5,7},{6,4},{7,5},{8,10},{9,11},{10,... | collective-permute-start | bytes 393224 | tf_op jit(solution)/shard_map/ppermute | solution.py:314

commit v6 on v5

--- a/solution.py
+++ b/solution.py
@@ -110,7 +110,12 @@
     return pl.ds(pl.multiple_of(block * height, GROUP), height)
 
 
-def local_kernel(features_hbm, sketch_hbm, sampled_ref, keep_ref, send_ref, gram_keep_ref, gram_send_ref, features_ref, sketch_ref, high_ref, low_ref, flip_high_ref, flip_low_ref, cross_ref, packed_ref, sems):
+def stacked_product(left_ref, left_span, rank, high, low):
+    both = lax.dot(left_ref[:, left_span], high, preferred_element_type=jnp.float32)
+    return both[:rank, :] + (both[rank:, :] + lax.dot(left_ref[:rank, left_span], low, preferred_element_type=jnp.float32))
+
+
+def local_kernel(features_hbm, sketch_hbm, sampled_ref, keep_ref, send_ref, gram_keep_ref, gram_send_ref, features_ref, sketch_ref, pair_ref, high_ref, low_ref, flip_ref, cross_ref, packed_ref, sems):
     rows, depth = features_ref.shape
     rank = sketch_ref.shape[1]
     chunks = rows // BLOCK
@@ -121,18 +126,18 @@
     for copy in copies:
         copy.start()
     copies[0].wait()
-    sketch = split(sketch_ref[...])
+    pair_ref[:, :rank], pair_ref[:, rank:] = split(sketch_ref[...])
     gram = None
     for at in range(chunks):
         span = slice(at * BLOCK, (at + 1) * BLOCK)
         copies[1 + at].wait()
-        features = split(features_ref[span, :])
-        high_ref[span, :], low_ref[span, :] = features
-        sampled = product(features, sketch, 1, 0)
+        high, low = split(features_ref[span, :])
+        high_ref[span, :], low_ref[span, :] = high, low
+        both = lax.dot(high, pair_ref[...], preferred_element_type=jnp.float32)
+        sampled = both[:, :rank] + (both[:, rank:] + lax.dot(low, pair_ref[:, :rank], preferred_element_type=jnp.float32))
         sampled_ref[span, :] = sampled
-        flipped = split(sampled.T)
-        flip_high_ref[:, span], flip_low_ref[:, span] = flipped
-        term = product(flipped, split(sampled), 1, 0)
+        flip_ref[:rank, span], flip_ref[rank:, span] = split(sampled.T)
+        term = stacked_product(flip_ref, span, rank, *split(sampled))
         gram = term if gram is None else gram + term
     packed_ref[:LANES, :] = gram[:LANES, :LANES]
     packed_ref[LANES:2 * LANES, :] = gram[:LANES, LANES:]
@@ -141,12 +146,11 @@
     core = core_bit()
     gram_keep_ref[...] = packed_ref[rows_of(core, half), :]
     gram_send_ref[...] = packed_ref[rows_of(1 - core, half), :]
-    flipped = flip_high_ref[...], flip_low_ref[...]
     own = own_block()
     height = rank // BLOCKS
-    for left in range(0, depth, BLOCK):
-        span = slice(left, left + BLOCK)
-        cross_ref[:, span] = product(flipped, (high_ref[:, span], low_ref[:, span]), 1, 0)
+    for left in range(0, depth, 2 * BLOCK):
+        span = slice(left, left + 2 * BLOCK)
+        cross_ref[:, span] = stacked_product(flip_ref, slice(None), rank, high_ref[:, span], low_ref[:, span])
     for at in range(BLOCKS):
         block = cross_ref[rows_of(at ^ own, height), :]
         if at < BLOCKS // 2:
@@ -172,8 +176,9 @@
         out_specs=(VMEM,) * 5,
         scratch_shapes=[
             pltpu.VMEM((rows, depth), jnp.float32), pltpu.VMEM((depth, rank), jnp.float32),
+            pltpu.VMEM((depth, 2 * rank), jnp.bfloat16),
             pltpu.VMEM((rows, depth), jnp.bfloat16), pltpu.VMEM((rows, depth), jnp.bfloat16),
-            pltpu.VMEM((rank, rows), jnp.bfloat16), pltpu.VMEM((rank, rows), jnp.bfloat16),
+            pltpu.VMEM((2 * rank, rows), jnp.bfloat16),
             pltpu.VMEM((rank, depth), jnp.float32), pltpu.VMEM((packed, LANES), jnp.float32),
             pltpu.SemaphoreType.DMA((rows // BLOCK + 1,)),
         ],
@@ -193,31 +198,57 @@
 
 
 def join_kernel(*refs):
-    *cross, gram_ref, gram_other_ref, gram_out_ref, out_ref = refs
-    gram_out_ref[...] = gram_ref[...] + gram_other_ref[...]
+    *cross, _, out_ref = refs
     top = 0
     for ref in cross:
         out_ref[top:top + ref.shape[0], :] = ref[...]
         top += ref.shape[0]
 
 
-def stage(cross, gram, gram_other, pieces, join=False):
+def stage(cross, gram, gram_other, pieces):
     height, depth = cross[0].shape
-    outs = [f32(len(cross) * height, depth)] if join else [f32(height // pieces, depth)] * pieces
-    kernel = join_kernel if join else lambda *refs: stage_kernel(len(cross), *refs)
     gram, *outs = pl.pallas_call(
-        kernel,
-        out_shape=(f32(*gram.shape), *outs),
+        lambda *refs: stage_kernel(len(cross), *refs),
+        out_shape=(f32(*gram.shape), *[f32(height // pieces, depth)] * pieces),
         in_specs=[VMEM] * (len(cross) + 2),
-        out_specs=(VMEM,) * (1 + len(outs)),
+        out_specs=(VMEM,) * (1 + pieces),
         compiler_params=pltpu.CompilerParams(vmem_limit_bytes=16 * 2**20),
         cost_estimate=pl.CostEstimate(flops=10**6, bytes_accessed=10**6, transcendentals=0),
-        name="join" if join else "stage",
+        name="stage",
     )(*cross, gram, gram_other)
     return gram, outs
 
 
-def factor_kernel(scale, first, last, *refs):
+def add_after(gram, other, after):
+    def kernel(gram_ref, other_ref, _, out_ref):
+        out_ref[...] = gram_ref[...] + other_ref[...]
+
+    return pl.pallas_call(
+        kernel,
+        out_shape=f32(*gram.shape),
+        in_specs=[VMEM, VMEM, pl.BlockSpec(memory_space=pl.ANY)],
+        out_specs=VMEM,
+        compiler_params=pltpu.CompilerParams(vmem_limit_bytes=16 * 2**20),
+        cost_estimate=pl.CostEstimate(flops=10**6, bytes_accessed=10**6, transcendentals=0),
+        name="add_after",
+    )(gram, other, after)
+
+
+def join(cross, after):
+    height, depth = cross[0].shape
+    return pl.pallas_call(
+        join_kernel,
+        out_shape=f32(len(cross) * height, depth),
+        in_specs=[VMEM] * len(cross) + [pl.BlockSpec(memory_space=pl.ANY)],
+        out_specs=VMEM,
+        compiler_params=pltpu.CompilerParams(vmem_limit_bytes=16 * 2**20),
+        cost_estimate=pl.CostEstimate(flops=10**6, bytes_accessed=10**6, transcendentals=0),
+        name="join",
+    )(*cross, after)
+
+
+def factor_kernel(scale, first, last, after, *refs):
+    refs = refs[:2] + refs[2 + after:]
     if first == 0:
         keep_ref, other_ref, a_ref, factor_ref, packed_ref = refs
         half = keep_ref.shape[0]
@@ -244,19 +275,19 @@
         flipped_ref[0][...] = inverse.T * scale
 
 
-def factor_part(operands, size, scale, first, last):
+def factor_part(operands, size, scale, first, last, after=()):
     square = jax.ShapeDtypeStruct((size, size), jnp.float32)
     outs = 3 if last == size else 2
     return pl.pallas_call(
-        lambda *refs: factor_kernel(scale, first, last, *refs),
+        lambda *refs: factor_kernel(scale, first, last, len(after), *refs),
         out_shape=(square,) * outs,
-        in_specs=[VMEM] * 2,
+        in_specs=[VMEM] * 2 + [pl.BlockSpec(memory_space=pl.ANY)] * len(after),
         out_specs=(VMEM,) * outs,
         scratch_shapes=[pltpu.VMEM((3 * LANES, LANES), jnp.float32)] if first == 0 else [],
         compiler_params=pltpu.CompilerParams(vmem_limit_bytes=16 * 2**20),
         cost_estimate=pl.CostEstimate(flops=12 * 10**9 * (last - first) // size, bytes_accessed=2**20, transcendentals=last - first),
         name="factor_part",
-    )(*operands)
+    )(*operands, *after)
 
 
 def basis_kernel(sampled_ref, flipped_ref, basis_ref):
@@ -330,9 +361,12 @@
     return [first] + [send(part, *mask) for part, mask in zip(rest, masks)]
 
 
-def sums_and_factors(keep, other, gram_keep, gram_other, factors):
+def per_device(features, sketch):
+    scale = (features.shape[0] * lax.axis_size(AXES)) ** 0.5
+    size = sketch.shape[1]
+    sampled, keep, other, gram, gram_other = local_terms(features, sketch)
     cross = [keep, send(other, *CORE)]
-    gram, parts = stage(cross, gram_keep, send(gram_other, *CORE), 4)
+    gram, parts = stage(cross, gram, send(gram_other, *CORE), 4)
     cross = spread(parts, PLANE)
     gram = gram + send(gram, *LINE[0])
     gram, parts = stage(cross, gram, send(gram, *LINE[1]), 4)
@@ -342,23 +376,16 @@
         own = own + send(own, *mask)
         gram = gram + send(gram, *mask)
     line = [own] + [send(own, *mask) for mask in LINE]
-    gram, (line,) = stage(line, gram, send(gram, *PLANE[1]), 1, join=True)
+    gram = add_after(gram, send(gram, *PLANE[1]), line[1])
+    state = factor_part((gram, send(gram, *CORE)), size, scale, 0, PANEL)
+    line = join(line, state[0])
     plane = [line] + [send(line, *mask) for mask in PLANE]
-    factors = factors((gram, send(gram, *CORE)))
-    return plane + [send(part, *CORE) for part in plane], factors
-
-
-def per_device(features, sketch):
-    scale = (features.shape[0] * lax.axis_size(AXES)) ** 0.5
-    size = sketch.shape[1]
-
-    def factors(state):
-        for first in range(0, size, PANEL):
-            state = factor_part(state[:2], size, scale, first, first + PANEL)
-        return state
-
-    sampled, *terms = local_terms(features, sketch)
-    cross, (inverse, factor, flipped) = sums_and_factors(*terms, factors)
+    after = (line,)
+    for first in range(PANEL, size, PANEL):
+        state = factor_part(state[:2], size, scale, first, first + PANEL, after)
+        after = ()
+    inverse, factor, flipped = state
+    cross = plane + [send(part, *CORE) for part in plane]
     return (basis_of(sampled, flipped), factor, project(inverse, cross))
 
 

time: 61.7 us -> 62.8 us (1.018)
  waiting for transfers between devices: 13.6 us -> 16.4 us
  starting transfers between devices: 26.2 us -> 24.2 us
    ppermute x23, waiting for transfers between devices: 13.6 us -> 16.4 us  [send(): return lax.ppermute(value, AXES, pairs)]
    ppermute x23, starting transfers between devices: 26.2 us -> 24.2 us  [send(): return lax.ppermute(value, AXES, pairs)]
    pallas_call x8 -> x9, Pallas kernels: 9.55 us -> 9.56 us  [the longest x4 9.42 us: factor_part(): pl.pallas_call(lambda *refs: factor_kernel(scale, first, last, len(after)...]
where the time goes in v6:
time: 62.8 us; the launch traced here: 62.6 us
  starting transfers between devices  24.2 us (39%)
  Pallas kernels  21.3 us (34%)
  waiting for transfers between devices  16.4 us (26%)
  between operations  0.74 us (1%)
    ppermute x23, starting transfers between devices, send(): return lax.ppermute(value, AXES, pairs)  24.2 us
    ppermute x23, waiting for transfers between devices, send(): return lax.ppermute(value, AXES, pairs)  16.4 us
    pallas_call x4, Pallas kernels, factor_part(): pl.pallas_call(lambda *refs: factor_kernel(scale, first, last, len(after)...  9.42 us
    pallas_call x1, Pallas kernels, local_terms(): pl.pallas_call(local_kernel, out_shape=(f32(rows, rank), f32(rank // 2, d...  8.49 us
    pallas_call x1, Pallas kernels, project(): pl.pallas_call(project_kernel, out_shape=jax.ShapeDtypeStruct((rank, dept...  1.66 us
    pallas_call x1, Pallas kernels, basis_of(): pl.pallas_call(basis_kernel, out_shape=f32(*sampled.shape), in_specs=[VME...  1.55 us
  transfers between devices with their start and end apart: 23, of which 8 were waited for; matrix products, arithmetic and copies ran while one was open for 0% of the time, Pallas kernels for 18%

profile of v6, /device:TPU:0, one launch (start us, length us, event | category | flops | bytes accessed | tf_op | source)
XLA Modules:
  0.0 62.6 jit_solution(6962174561749104030)
XLA Ops:
  0.6 8.5 %local_terms.1 = (f32[1024,256]{1,0:T(8,128)S(1)}, f32[128,1024]{1,0:T(8,128)S(1)}, f32[128,1024]{1,0:T(8,128)S(1)}, f32[192,128]{1,0:T(8,128)S(1)}, f32[192,128]{1,0:T(8,128)S(1)}) custom-call(f32[1024,1024]{1,0:T(8,128)} %features_hbm.1, f32[1024,256]{1,0:T(8,128)} %sketch_hbm.1), custom_call_target="tpu_custom_call" | custom-call | flops 4000000000 | bytes 8388608 | tf_op jit(solution)/shard_map/local_terms/pallas_call | solution.py:172
  9.1 0.5 collective-permute-start
  9.7 0.1 collective-permute-start.1
  9.7 1.6 %collective-permute-done.1.refs_3_ = f32[192,128]{1,0:T(8,128)S(1)} collective-permute-done((f32[192,128]{1,0:T(8,128)S(1)}, f32[192,128]{1,0:T(8,128)S(1)}, u32[]{:S(2)}, u32[]{:S(2)}) %collective-permute-start.1) | collective-permute-done | bytes 98336 | tf_op jit(solution)/shard_map/ppermute | solution.py:345
  11.3 0.0 collective-permute-done.refs_1_
  11.3 0.1 stage.3
  11.4 3.0 %collective-permute-start.5 = (f32[192,128]{1,0:T(8,128)S(1)}, f32[192,128]{1,0:T(8,128)S(1)}, u32[]{:S(2)}, u32[]{:S(2)}) collective-permute-start(f32[192,128]{1,0:T(8,128)S(1)} %get-tuple-element.38), channel_id=1, source_target_pairs={{0,8},{1,9},{2,10},{3,11},{4,12},{5,13},{6,14},{7,15},{8,0},{9,1},... | collective-permute-start | bytes 294920 | tf_op jit(solution)/shard_map/ppermute | solution.py:345
  14.4 1.5 %collective-permute-start.2 = (f32[32,1024]{1,0:T(8,128)S(1)}, f32[32,1024]{1,0:T(8,128)S(1)}, u32[]{:S(2)}, u32[]{:S(2)}) collective-permute-start(f32[32,1024]{1,0:T(8,128)S(1)} %get-tuple-element.35), channel_id=1, source_target_pairs={{0,1},{1,0},{2,3},{3,2},{4,5},{5,4},{6,7},{7,6},{8,9},{9,8},{10,11... | collective-permute-start | bytes 393224 | tf_op jit(solution)/shard_map/ppermute | solution.py:345
  15.9 1.5 %collective-permute-start.3 = (f32[32,1024]{1,0:T(8,128)S(1)}, f32[32,1024]{1,0:T(8,128)S(1)}, u32[]{:S(2)}, u32[]{:S(2)}) collective-permute-start(f32[32,1024]{1,0:T(8,128)S(1)} %get-tuple-element.36), channel_id=1, source_target_pairs={{0,4},{1,5},{2,6},{3,7},{4,0},{5,1},{6,2},{7,3},{8,12},{9,13},{10,... | collective-permute-start | bytes 393224 | tf_op jit(solution)/shard_map/ppermute | solution.py:345
  17.4 0.5 collective-permute-start.4
  17.9 0.0 collective-permute-done.5
  17.9 2.7 %collective-permute-start.6 = (f32[192,128]{1,0:T(8,128)S(1)}, f32[192,128]{1,0:T(8,128)S(1)}, u32[]{:S(2)}, u32[]{:S(2)}) collective-permute-start(f32[192,128]{1,0:T(8,128)S(1)} %add.3.refs_4_), channel_id=1, source_target_pairs={{0,16},{1,17},{2,18},{3,19},{4,20},{5,21},{6,22},{7,23},{8,24},{9,... | collective-permute-start | bytes 294920 | tf_op jit(solution)/shard_map/ppermute | solution.py:345
  20.6 0.0 collective-permute-done.2.refs_1_
  20.6 1.7 %collective-permute-done.3.refs_2_ = f32[32,1024]{1,0:T(8,128)S(1)} collective-permute-done((f32[32,1024]{1,0:T(8,128)S(1)}, f32[32,1024]{1,0:T(8,128)S(1)}, u32[]{:S(2)}, u32[]{:S(2)}) %collective-permute-start.3) | collective-permute-done | bytes 131104 | tf_op jit(solution)/shard_map/ppermute | solution.py:345
  22.3 1.3 %collective-permute-done.4.refs_3_ = f32[32,1024]{1,0:T(8,128)S(1)} collective-permute-done((f32[32,1024]{1,0:T(8,128)S(1)}, f32[32,1024]{1,0:T(8,128)S(1)}, u32[]{:S(2)}, u32[]{:S(2)}) %collective-permute-start.4) | collective-permute-done | bytes 131104 | tf_op jit(solution)/shard_map/ppermute | solution.py:345
  23.7 1.3 %collective-permute-done.6.refs_5_ = f32[192,128]{1,0:T(8,128)S(1)} collective-permute-done((f32[192,128]{1,0:T(8,128)S(1)}, f32[192,128]{1,0:T(8,128)S(1)}, u32[]{:S(2)}, u32[]{:S(2)}) %collective-permute-start.6) | collective-permute-done | bytes 98336 | tf_op jit(solution)/shard_map/ppermute | solution.py:345
  25.0 1.4 %collective-permute-start.10 = (f32[192,128]{1,0:T(8,128)S(1)}, f32[192,128]{1,0:T(8,128)S(1)}, u32[]{:S(2)}, u32[]{:S(2)}) collective-permute-start(f32[192,128]{1,0:T(8,128)S(1)} %get-tuple-element.43.refs_4_), channel_id=1, source_target_pairs={{0,1},{1,0},{2,3},{3,2},{4,5},{5,4},{6,7},{7,6},{8,9},{9,8},{10,11... | collective-permute-start | bytes 294920 | tf_op jit(solution)/shard_map/ppermute | solution.py:345
  26.4 0.7 %collective-permute-start.7 = (f32[8,1024]{1,0:T(8,128)S(1)}, f32[8,1024]{1,0:T(8,128)S(1)}, u32[]{:S(2)}, u32[]{:S(2)}) collective-permute-start(f32[8,1024]{1,0:T(8,128)S(1)} %get-tuple-element.40), channel_id=1, source_target_pairs={{0,8},{1,9},{2,10},{3,11},{4,12},{5,13},{6,14},{7,15},{8,0},{9,1},... | collective-permute-start | bytes 98312 | tf_op jit(solution)/shard_map/ppermute | solution.py:345
  27.1 3.4 %collective-permute-start.8 = (f32[8,1024]{1,0:T(8,128)S(1)}, f32[8,1024]{1,0:T(8,128)S(1)}, u32[]{:S(2)}, u32[]{:S(2)}) collective-permute-start(f32[8,1024]{1,0:T(8,128)S(1)} %get-tuple-element.41), channel_id=1, source_target_pairs={{0,16},{1,17},{2,18},{3,19},{4,20},{5,21},{6,22},{7,23},{8,24},{9,... | collective-permute-start | bytes 98312 | tf_op jit(solution)/shard_map/ppermute | solution.py:345
  30.4 0.3 collective-permute-start.9
  30.8 0.0 collective-permute-done.7.refs_1_
  30.8 1.6 %collective-permute-done.8.refs_2_ = f32[8,1024]{1,0:T(8,128)S(1)} collective-permute-done((f32[8,1024]{1,0:T(8,128)S(1)}, f32[8,1024]{1,0:T(8,128)S(1)}, u32[]{:S(2)}, u32[]{:S(2)}) %collective-permute-start.8) | collective-permute-done | bytes 32800 | tf_op jit(solution)/shard_map/ppermute | solution.py:345
  32.3 3.8 %collective-permute-done.9.refs_3_ = f32[8,1024]{1,0:T(8,128)S(1)} collective-permute-done((f32[8,1024]{1,0:T(8,128)S(1)}, f32[8,1024]{1,0:T(8,128)S(1)}, u32[]{:S(2)}, u32[]{:S(2)}) %collective-permute-start.9) | collective-permute-done | bytes 32800 | tf_op jit(solution)/shard_map/ppermute | solution.py:345
  36.2 0.0 collective-permute-done.10.refs_5_
  36.2 1.6 %collective-permute-start.11 = (f32[192,128]{1,0:T(8,128)S(1)}, f32[192,128]{1,0:T(8,128)S(1)}, u32[]{:S(2)}, u32[]{:S(2)}) collective-permute-start(f32[192,128]{1,0:T(8,128)S(1)} %get-tuple-element.44.gram_ref), channel_id=1, source_target_pairs={{0,4},{1,5},{2,6},{3,7},{4,0},{5,1},{6,2},{7,3},{8,12},{9,13},{10,... | collective-permute-start | bytes 294920 | tf_op jit(solution)/shard_map/ppermute | solution.py:345
  37.7 0.0 collective-permute-start.12
  37.7 3.9 %collective-permute-done.12._.refs_1_ = f32[8,1024]{1,0:T(8,128)S(1)} collective-permute-done((f32[8,1024]{1,0:T(8,128)S(1)}, f32[8,1024]{1,0:T(8,128)S(1)}, u32[]{:S(2)}, u32[]{:S(2)}) %collective-permute-start.12) | collective-permute-done | bytes 32800 | tf_op jit(solution)/shard_map/ppermute | solution.py:345
  41.7 0.0 collective-permute-done.11.other_ref
  41.7 0.1 collective-permute-start.13
  41.8 0.1 collective-permute-start.14
  41.8 2.4 %collective-permute-start.15 = (f32[8,1024]{1,0:T(8,128)S(1)}, f32[8,1024]{1,0:T(8,128)S(1)}, u32[]{:S(2)}, u32[]{:S(2)}) collective-permute-start(f32[8,1024]{1,0:T(8,128)S(1)} %get-tuple-element.45.refs_0_), channel_id=1, source_target_pairs={{0,24},{1,25},{2,26},{3,27},{4,28},{5,29},{6,30},{7,31},{8,16},{9,... | collective-permute-start | bytes 98312 | tf_op jit(solution)/shard_map/ppermute | solution.py:345
  44.2 0.0 collective-permute-done.13.refs_1_
  44.2 2.3 %factor_part.4 = (f32[256,256]{1,0:T(8,128)S(1)}, f32[256,256]{1,0:T(8,128)S(1)}) custom-call(f32[192,128]{1,0:T(8,128)S(1)} %add_after.1.refs_0_, f32[192,128]{1,0:T(8,128)S(1)} %collective-permute-done.13.refs_1_), custom_call_target="tpu_custom_call" | custom-call | flops 3000000000 | bytes 1048576 | tf_op jit(solution)/shard_map/factor_part/pallas_call | solution.py:281
  46.5 1.1 %collective-permute-done.14.refs_2_ = f32[8,1024]{1,0:T(8,128)S(1)} collective-permute-done((f32[8,1024]{1,0:T(8,128)S(1)}, f32[8,1024]{1,0:T(8,128)S(1)}, u32[]{:S(2)}, u32[]{:S(2)}) %collective-permute-start.14) | collective-permute-done | bytes 32800 | tf_op jit(solution)/shard_map/ppermute | solution.py:345
  47.7 0.0 collective-permute-done.15.refs_3_
  47.7 0.6 collective-permute-start.16
  48.3 0.7 %collective-permute-start.17 = (f32[32,1024]{1,0:T(8,128)S(1)}, f32[32,1024]{1,0:T(8,128)S(1)}, u32[]{:S(2)}, u32[]{:S(2)}) collective-permute-start(f32[32,1024]{1,0:T(8,128)S(1)} %join.1.refs_2_.refs_0_), channel_id=1, source_target_pairs={{0,4},{1,5},{2,6},{3,7},{4,0},{5,1},{6,2},{7,3},{8,12},{9,13},{10,... | collective-permute-start | bytes 393224 | tf_op jit(solution)/shard_map/ppermute | solution.py:345
  48.9 2.3 %collective-permute-start.18 = (f32[32,1024]{1,0:T(8,128)S(1)}, f32[32,1024]{1,0:T(8,128)S(1)}, u32[]{:S(2)}, u32[]{:S(2)}) collective-permute-start(f32[32,1024]{1,0:T(8,128)S(1)} %join.1.refs_2_.refs_0_), channel_id=1, source_target_pairs={{0,5},{1,4},{2,7},{3,6},{4,1},{5,0},{6,3},{7,2},{8,13},{9,12},{10,... | collective-permute-start | bytes 393224 | tf_op jit(solution)/shard_map/ppermute | solution.py:345
  51.3 0.0 collective-permute-start.19
  51.3 2.2 %factor_part.5 = (f32[256,256]{1,0:T(8,128)S(1)}, f32[256,256]{1,0:T(8,128)S(1)}) custom-call(f32[256,256]{1,0:T(8,128)S(1)} %get-tuple-element.46.refs_4_.refs_0_, f32[256,256]{1,0:T(8,128)S(1)} %get-tuple-element.47.refs_1_, f32[32,1024]{1,0:T(8,128)S(1)} %join.1.refs_2_.refs_0_), custom_call_target="tpu_custom_call" | custom-call | flops 3000000000 | bytes 1048576 | tf_op jit(solution)/shard_map/factor_part/pallas_call | solution.py:281
  53.5 2.2 %factor_part.6 = (f32[256,256]{1,0:T(8,128)S(1)}, f32[256,256]{1,0:T(8,128)S(1)}) custom-call(f32[256,256]{1,0:T(8,128)S(1)} %get-tuple-element.48.refs_0_, f32[256,256]{1,0:T(8,128)S(1)} %get-tuple-element.49.refs_1_), custom_call_target="tpu_custom_call" | custom-call | flops 3000000000 | bytes 1048576 | tf_op jit(solution)/shard_map/factor_part/pallas_call | solution.py:281
  55.7 2.6 %factor_part.7 = (f32[256,256]{1,0:T(8,128)S(1)}, f32[256,256]{1,0:T(8,128)}, f32[256,256]{1,0:T(8,128)S(1)}) custom-call(f32[256,256]{1,0:T(8,128)S(1)} %get-tuple-element.50.refs_0_, f32[256,256]{1,0:T(8,128)S(1)} %get-tuple-element.51.refs_1_), custom_call_target="tpu_custom_call" | custom-call | flops 3000000000 | bytes 1048576 | tf_op jit(solution)/shard_map/factor_part/pallas_call | solution.py:281
  58.4 0.0 collective-permute-done.16.refs_1_
  58.4 0.5 collective-permute-start.20
  58.9 0.0 collective-permute-done.17.refs_2_
  58.9 0.1 collective-permute-start.21
  58.9 0.0 collective-permute-done.18.refs_3_
  58.9 0.4 collective-permute-start.22
  59.4 1.6 %basis.1 = f32[1024,256]{1,0:T(8,128)} custom-call(f32[1024,256]{1,0:T(8,128)S(1)} %get-tuple-element.29.sampled_ref, f32[256,256]{1,0:T(8,128)S(1)} %get-tuple-element.52.flipped_ref), custom_call_target="tpu_custom_call" | custom-call | flops 2000000000 | bytes 2097152 | tf_op jit(solution)/shard_map/basis/pallas_call | solution.py:301
  60.9 0.0 collective-permute-done.19.refs_4_
  60.9 0.0 collective-permute-done.20.refs_5_
  60.9 0.0 collective-permute-done.21.refs_6_
  61.0 0.0 collective-permute-done.22.refs_7_
  61.0 1.7 %project.1 = f32[256,1024]{1,0:T(8,128)} custom-call(f32[256,256]{1,0:T(8,128)S(1)} %get-tuple-element.54.inverse_ref, f32[32,1024]{1,0:T(8,128)S(1)} %join.1.refs_2_.refs_0_, f32[32,1024]{1,0:T(8,128)S(1)} %collective-permute-done.16.refs_1_, f32[32,1024]{1,0:T(8,128)S(1)} %collective-permute-done.17.refs_2_, ...), custom_call_target="tpu_custom_call" | custom-call | flops 400000000 | bytes 2097152 | tf_op jit(solution)/shard_map/project/pallas_call | solution.py:330
  (5 shorter events, 0.1 us)
Async XLA Ops:
  9.1 2.2 %collective-permute-start = (f32[128,1024]{1,0:T(8,128)S(1)}, f32[128,1024]{1,0:T(8,128)S(1)}, u32[]{:S(2)}, u32[]{:S(2)}) collective-permute-start(f32[128,1024]{1,0:T(8,128)S(1)} %get-tuple-element.31), channel_id=1, source_target_pairs={{0,2},{1,3},{2,0},{3,1},{4,6},{5,7},{6,4},{7,5},{8,10},{9,11},{10,... | collective-permute-start | bytes 1572872 | tf_op jit(solution)/shard_map/ppermute | solution.py:345
  9.7 1.7 %collective-permute-start.1 = (f32[192,128]{1,0:T(8,128)S(1)}, f32[192,128]{1,0:T(8,128)S(1)}, u32[]{:S(2)}, u32[]{:S(2)}) collective-permute-start(f32[192,128]{1,0:T(8,128)S(1)} %get-tuple-element.33), channel_id=1, source_target_pairs={{0,2},{1,3},{2,0},{3,1},{4,6},{5,7},{6,4},{7,5},{8,10},{9,11},{10,... | collective-permute-start | bytes 294920 | tf_op jit(solution)/shard_map/ppermute | solution.py:345
  11.4 6.5 %collective-permute-start.5 = (f32[192,128]{1,0:T(8,128)S(1)}, f32[192,128]{1,0:T(8,128)S(1)}, u32[]{:S(2)}, u32[]{:S(2)}) collective-permute-start(f32[192,128]{1,0:T(8,128)S(1)} %get-tuple-element.38), channel_id=1, source_target_pairs={{0,8},{1,9},{2,10},{3,11},{4,12},{5,13},{6,14},{7,15},{8,0},{9,1},... | collective-permute-start | bytes 294920 | tf_op jit(solution)/shard_map/ppermute | solution.py:345
  14.4 6.2 %collective-permute-start.2 = (f32[32,1024]{1,0:T(8,128)S(1)}, f32[32,1024]{1,0:T(8,128)S(1)}, u32[]{:S(2)}, u32[]{:S(2)}) collective-permute-start(f32[32,1024]{1,0:T(8,128)S(1)} %get-tuple-element.35), channel_id=1, source_target_pairs={{0,1},{1,0},{2,3},{3,2},{4,5},{5,4},{6,7},{7,6},{8,9},{9,8},{10,11... | collective-permute-start | bytes 393224 | tf_op jit(solution)/shard_map/ppermute | solution.py:345
  15.9 6.4 %collective-permute-start.3 = (f32[32,1024]{1,0:T(8,128)S(1)}, f32[32,1024]{1,0:T(8,128)S(1)}, u32[]{:S(2)}, u32[]{:S(2)}) collective-permute-start(f32[32,1024]{1,0:T(8,128)S(1)} %get-tuple-element.36), channel_id=1, source_target_pairs={{0,4},{1,5},{2,6},{3,7},{4,0},{5,1},{6,2},{7,3},{8,12},{9,13},{10,... | collective-permute-start | bytes 393224 | tf_op jit(solution)/shard_map/ppermute | solution.py:345
  17.4 6.2 %collective-permute-start.4 = (f32[32,1024]{1,0:T(8,128)S(1)}, f32[32,1024]{1,0:T(8,128)S(1)}, u32[]{:S(2)}, u32[]{:S(2)}) collective-permute-start(f32[32,1024]{1,0:T(8,128)S(1)} %get-tuple-element.37), channel_id=1, source_target_pairs={{0,5},{1,4},{2,7},{3,6},{4,1},{5,0},{6,3},{7,2},{8,13},{9,12},{10,... | collective-permute-start | bytes 393224 | tf_op jit(solution)/shard_map/ppermute | solution.py:345
  17.9 7.0 %collective-permute-start.6 = (f32[192,128]{1,0:T(8,128)S(1)}, f32[192,128]{1,0:T(8,128)S(1)}, u32[]{:S(2)}, u32[]{:S(2)}) collective-permute-start(f32[192,128]{1,0:T(8,128)S(1)} %add.3.refs_4_), channel_id=1, source_target_pairs={{0,16},{1,17},{2,18},{3,19},{4,20},{5,21},{6,22},{7,23},{8,24},{9,... | collective-permute-start | bytes 294920 | tf_op jit(solution)/shard_map/ppermute | solution.py:345
  25.0 11.2 %collective-permute-start.10 = (f32[192,128]{1,0:T(8,128)S(1)}, f32[192,128]{1,0:T(8,128)S(1)}, u32[]{:S(2)}, u32[]{:S(2)}) collective-permute-start(f32[192,128]{1,0:T(8,128)S(1)} %get-tuple-element.43.refs_4_), channel_id=1, source_target_pairs={{0,1},{1,0},{2,3},{3,2},{4,5},{5,4},{6,7},{7,6},{8,9},{9,8},{10,11... | collective-permute-start | bytes 294920 | tf_op jit(solution)/shard_map/ppermute | solution.py:345
  26.4 4.4 %collective-permute-start.7 = (f32[8,1024]{1,0:T(8,128)S(1)}, f32[8,1024]{1,0:T(8,128)S(1)}, u32[]{:S(2)}, u32[]{:S(2)}) collective-permute-start(f32[8,1024]{1,0:T(8,128)S(1)} %get-tuple-element.40), channel_id=1, source_target_pairs={{0,8},{1,9},{2,10},{3,11},{4,12},{5,13},{6,14},{7,15},{8,0},{9,1},... | collective-permute-start | bytes 98312 | tf_op jit(solution)/shard_map/ppermute | solution.py:345
  27.1 5.3 %collective-permute-start.8 = (f32[8,1024]{1,0:T(8,128)S(1)}, f32[8,1024]{1,0:T(8,128)S(1)}, u32[]{:S(2)}, u32[]{:S(2)}) collective-permute-start(f32[8,1024]{1,0:T(8,128)S(1)} %get-tuple-element.41), channel_id=1, source_target_pairs={{0,16},{1,17},{2,18},{3,19},{4,20},{5,21},{6,22},{7,23},{8,24},{9,... | collective-permute-start | bytes 98312 | tf_op jit(solution)/shard_map/ppermute | solution.py:345
  30.4 5.7 %collective-permute-start.9 = (f32[8,1024]{1,0:T(8,128)S(1)}, f32[8,1024]{1,0:T(8,128)S(1)}, u32[]{:S(2)}, u32[]{:S(2)}) collective-permute-start(f32[8,1024]{1,0:T(8,128)S(1)} %get-tuple-element.42), channel_id=1, source_target_pairs={{0,24},{1,25},{2,26},{3,27},{4,28},{5,29},{6,30},{7,31},{8,16},{9,... | collective-permute-start | bytes 98312 | tf_op jit(solution)/shard_map/ppermute | solution.py:345
  36.2 5.5 %collective-permute-start.11 = (f32[192,128]{1,0:T(8,128)S(1)}, f32[192,128]{1,0:T(8,128)S(1)}, u32[]{:S(2)}, u32[]{:S(2)}) collective-permute-start(f32[192,128]{1,0:T(8,128)S(1)} %get-tuple-element.44.gram_ref), channel_id=1, source_target_pairs={{0,4},{1,5},{2,6},{3,7},{4,0},{5,1},{6,2},{7,3},{8,12},{9,13},{10,... | collective-permute-start | bytes 294920 | tf_op jit(solution)/shard_map/ppermute | solution.py:345
  37.7 3.9 %collective-permute-start.12 = (f32[8,1024]{1,0:T(8,128)S(1)}, f32[8,1024]{1,0:T(8,128)S(1)}, u32[]{:S(2)}, u32[]{:S(2)}) collective-permute-start(f32[8,1024]{1,0:T(8,128)S(1)} %get-tuple-element.45.refs_0_), channel_id=1, source_target_pairs={{0,8},{1,9},{2,10},{3,11},{4,12},{5,13},{6,14},{7,15},{8,0},{9,1},... | collective-permute-start | bytes 98312 | tf_op jit(solution)/shard_map/ppermute | solution.py:345
  41.7 2.5 %collective-permute-start.13 = (f32[192,128]{1,0:T(8,128)S(1)}, f32[192,128]{1,0:T(8,128)S(1)}, u32[]{:S(2)}, u32[]{:S(2)}) collective-permute-start(f32[192,128]{1,0:T(8,128)S(1)} %add_after.1.refs_0_), channel_id=1, source_target_pairs={{0,2},{1,3},{2,0},{3,1},{4,6},{5,7},{6,4},{7,5},{8,10},{9,11},{10,... | collective-permute-start | bytes 294920 | tf_op jit(solution)/shard_map/ppermute | solution.py:345
  41.8 5.9 %collective-permute-start.14 = (f32[8,1024]{1,0:T(8,128)S(1)}, f32[8,1024]{1,0:T(8,128)S(1)}, u32[]{:S(2)}, u32[]{:S(2)}) collective-permute-start(f32[8,1024]{1,0:T(8,128)S(1)} %get-tuple-element.45.refs_0_), channel_id=1, source_target_pairs={{0,16},{1,17},{2,18},{3,19},{4,20},{5,21},{6,22},{7,23},{8,24},{9,... | collective-permute-start | bytes 98312 | tf_op jit(solution)/shard_map/ppermute | solution.py:345
  41.8 5.9 %collective-permute-start.15 = (f32[8,1024]{1,0:T(8,128)S(1)}, f32[8,1024]{1,0:T(8,128)S(1)}, u32[]{:S(2)}, u32[]{:S(2)}) collective-permute-start(f32[8,1024]{1,0:T(8,128)S(1)} %get-tuple-element.45.refs_0_), channel_id=1, source_target_pairs={{0,24},{1,25},{2,26},{3,27},{4,28},{5,29},{6,30},{7,31},{8,16},{9,... | collective-permute-start | bytes 98312 | tf_op jit(solution)/shard_map/ppermute | solution.py:345
  47.7 10.7 %collective-permute-start.16 = (f32[32,1024]{1,0:T(8,128)S(1)}, f32[32,1024]{1,0:T(8,128)S(1)}, u32[]{:S(2)}, u32[]{:S(2)}) collective-permute-start(f32[32,1024]{1,0:T(8,128)S(1)} %join.1.refs_2_.refs_0_), channel_id=1, source_target_pairs={{0,1},{1,0},{2,3},{3,2},{4,5},{5,4},{6,7},{7,6},{8,9},{9,8},{10,11... | collective-permute-start | bytes 393224 | tf_op jit(solution)/shard_map/ppermute | solution.py:345
  48.3 10.6 %collective-permute-start.17 = (f32[32,1024]{1,0:T(8,128)S(1)}, f32[32,1024]{1,0:T(8,128)S(1)}, u32[]{:S(2)}, u32[]{:S(2)}) collective-permute-start(f32[32,1024]{1,0:T(8,128)S(1)} %join.1.refs_2_.refs_0_), channel_id=1, source_target_pairs={{0,4},{1,5},{2,6},{3,7},{4,0},{5,1},{6,2},{7,3},{8,12},{9,13},{10,... | collective-permute-start | bytes 393224 | tf_op jit(solution)/shard_map/ppermute | solution.py:345
  48.9 10.0 %collective-permute-start.18 = (f32[32,1024]{1,0:T(8,128)S(1)}, f32[32,1024]{1,0:T(8,128)S(1)}, u32[]{:S(2)}, u32[]{:S(2)}) collective-permute-start(f32[32,1024]{1,0:T(8,128)S(1)} %join.1.refs_2_.refs_0_), channel_id=1, source_target_pairs={{0,5},{1,4},{2,7},{3,6},{4,1},{5,0},{6,3},{7,2},{8,13},{9,12},{10,... | collective-permute-start | bytes 393224 | tf_op jit(solution)/shard_map/ppermute | solution.py:345
  51.3 9.7 %collective-permute-start.19 = (f32[32,1024]{1,0:T(8,128)S(1)}, f32[32,1024]{1,0:T(8,128)S(1)}, u32[]{:S(2)}, u32[]{:S(2)}) collective-permute-start(f32[32,1024]{1,0:T(8,128)S(1)} %join.1.refs_2_.refs_0_), channel_id=1, source_target_pairs={{0,2},{1,3},{2,0},{3,1},{4,6},{5,7},{6,4},{7,5},{8,10},{9,11},{10,... | collective-permute-start | bytes 393224 | tf_op jit(solution)/shard_map/ppermute | solution.py:345
  58.4 2.6 %collective-permute-start.20 = (f32[32,1024]{1,0:T(8,128)S(1)}, f32[32,1024]{1,0:T(8,128)S(1)}, u32[]{:S(2)}, u32[]{:S(2)}) collective-permute-start(f32[32,1024]{1,0:T(8,128)S(1)} %collective-permute-done.16.refs_1_), channel_id=1, source_target_pairs={{0,2},{1,3},{2,0},{3,1},{4,6},{5,7},{6,4},{7,5},{8,10},{9,11},{10,... | collective-permute-start | bytes 393224 | tf_op jit(solution)/shard_map/ppermute | solution.py:345
  58.9 2.1 %collective-permute-start.21 = (f32[32,1024]{1,0:T(8,128)S(1)}, f32[32,1024]{1,0:T(8,128)S(1)}, u32[]{:S(2)}, u32[]{:S(2)}) collective-permute-start(f32[32,1024]{1,0:T(8,128)S(1)} %collective-permute-done.17.refs_2_), channel_id=1, source_target_pairs={{0,2},{1,3},{2,0},{3,1},{4,6},{5,7},{6,4},{7,5},{8,10},{9,11},{10,... | collective-permute-start | bytes 393224 | tf_op jit(solution)/shard_map/ppermute | solution.py:345
  58.9 2.0 %collective-permute-start.22 = (f32[32,1024]{1,0:T(8,128)S(1)}, f32[32,1024]{1,0:T(8,128)S(1)}, u32[]{:S(2)}, u32[]{:S(2)}) collective-permute-start(f32[32,1024]{1,0:T(8,128)S(1)} %collective-permute-done.18.refs_3_), channel_id=1, source_target_pairs={{0,2},{1,3},{2,0},{3,1},{4,6},{5,7},{6,4},{7,5},{8,10},{9,11},{10,... | collective-permute-start | bytes 393224 | tf_op jit(solution)/shard_map/ppermute | solution.py:345

commit v7 on v4

--- a/solution.py
+++ b/solution.py
@@ -96,10 +96,6 @@
     return dot(left[0], right[0]) + (dot(left[0], right[1]) + dot(left[1], right[0]))
 
 
-def core_bit():
-    return lax.rem(lax.axis_index("wide"), 2)
-
-
 def own_block():
     wide, narrow = lax.axis_index("wide"), lax.axis_index("narrow")
     plane = lax.rem(narrow, 2) + 2 * lax.rem(wide // 2, 2)
@@ -110,80 +106,83 @@
     return pl.ds(pl.multiple_of(block * height, GROUP), height)
 
 
-def local_kernel(features_ref, sketch_ref, sampled_ref, keep_ref, send_ref, gram_keep_ref, gram_send_ref, high_ref, low_ref, cross_ref, gram_ref, packed_ref):
-    step = pl.program_id(0)
-
-    @pl.when(step == 0)
-    def _():
-        high_ref[...], low_ref[...] = split(sketch_ref[...])
-        cross_ref[...] = jnp.zeros_like(cross_ref)
-        gram_ref[...] = jnp.zeros_like(gram_ref)
-
-    features = split(features_ref[...])
-    sampled = product(features, (high_ref[...], low_ref[...]), 1, 0)
-    sampled_ref[...] = sampled
-    flipped = split(sampled.T)
-    cross_ref[...] += product(flipped, features, 1, 0)
-    gram_ref[...] += product(flipped, split(sampled), 1, 0)
-
-    @pl.when(step == pl.num_programs(0) - 1)
-    def _():
+def arrange_kernel(cross_ref, gram_ref, keep_ref, send_ref):
+    own = own_block()
+    depth = cross_ref.shape[1]
+    height = cross_ref.shape[0] // BLOCKS
+    for at in range(BLOCKS):
+        rows = rows_of(at ^ own, height)
+        out_ref = keep_ref if at < BLOCKS // 2 else send_ref
+        top = at % (BLOCKS // 2) * height
+        out_ref[top:top + height, :depth] = cross_ref[rows, :]
+        out_ref[top:top + height, depth:] = gram_ref[rows, :]
+
+
+def f32(*shape):
+    return jax.ShapeDtypeStruct(shape, jnp.float32)
+
+
+def call(kernel, name, outs, *operands, after=(), flops=10**6):
+    return pl.pallas_call(
+        lambda *refs: kernel(*refs[:len(operands)], *refs[len(operands) + len(after):]),
+        out_shape=outs,
+        in_specs=[VMEM] * len(operands) + [pl.BlockSpec(memory_space=pl.ANY)] * len(after),
+        out_specs=jax.tree.map(lambda _: VMEM, outs),
+        compiler_params=pltpu.CompilerParams(vmem_limit_bytes=16 * 2**20),
+        cost_estimate=pl.CostEstimate(flops=flops, bytes_accessed=10**6, transcendentals=0),
+        name=name,
+    )(*operands, *after)
+
+
+def core_sum_kernel(keep_ref, other_ref, *outs):
+    height = outs[0].shape[0]
+    for at, out_ref in enumerate(outs):
+        span = slice(at * height, (at + 1) * height)
+        out_ref[...] = keep_ref[span, :] + other_ref[span, :]
+
+
+def plane_sum_kernel(depth, *refs):
+    parts, outs = refs[:4], refs[4:]
+    height = outs[0].shape[0]
+    for at, out_ref in enumerate(outs):
+        span = slice(at * height, (at + 1) * height)
+        total = sum(part[span, :] for part in parts)
+        out_ref[:, :depth] = total[:, :depth]
+        rank = total.shape[1] - depth
+        for to_ref in outs:
+            left = depth + at * rank
+            to_ref[:, left:left + rank] = total[:, depth:]
+
+
+def line_sum_kernel(depth, *refs):
+    parts, (own_ref, gram_ref) = refs[:4], refs[4:]
+    own_ref[...] = sum(part[:, :depth] for part in parts)
+    rank = gram_ref.shape[1]
+    height = own_ref.shape[0]
+    for at in range(4):
+        pieces = [part[:, depth + (at ^ sender) * rank:depth + (at ^ sender) * rank + rank] for sender, part in enumerate(parts)]
+        gram_ref[at * height:(at + 1) * height, :] = sum(pieces)
+
+
+def join_kernel(*refs):
+    *parts, out_ref, gram_ref = refs
+    for to_ref, pieces in ((out_ref, parts[:4]), (gram_ref, parts[4:])):
+        top = 0
+        for piece in pieces:
+            to_ref[top:top + piece.shape[0], :] = piece[...]
+            top += piece.shape[0]
+
+
+def factor_kernel(scale, first, last, after, *refs):
+    refs = refs[:2] + refs[2 + after:]
+    if first == 0:
+        *halves, a_ref, factor_ref = refs
         own = own_block()
-        height = cross_ref.shape[0] // BLOCKS
+        height = a_ref.shape[0] // BLOCKS
         for at in range(BLOCKS):
-            block = cross_ref[rows_of(at ^ own, height), :]
-            if at < BLOCKS // 2:
-                keep_ref[at * height:(at + 1) * height, :] = block
-            else:
-                rest = at - BLOCKS // 2
-                send_ref[rest * height:(rest + 1) * height, :] = block
-        packed_ref[:LANES, :] = gram_ref[:LANES, :LANES]
-        packed_ref[LANES:2 * LANES, :] = gram_ref[:LANES, LANES:]
-        packed_ref[2 * LANES:, :] = gram_ref[LANES:, LANES:]
-        half = packed_ref.shape[0] // 2
-        core = core_bit()
-        gram_keep_ref[...] = packed_ref[rows_of(core, half), :]
-        gram_send_ref[...] = packed_ref[rows_of(1 - core, half), :]
-
-
-def local_terms(features, sketch):
-    rows, depth = features.shape
-    rank = sketch.shape[1]
-    f32 = lambda *shape: jax.ShapeDtypeStruct(shape, jnp.float32)
-    whole = lambda *shape: pl.BlockSpec(shape, lambda i: (0, 0))
-    packed = 3 * LANES
-    return pl.pallas_call(
-        local_kernel,
-        grid=(rows // BLOCK,),
-        out_shape=(f32(rows, rank), f32(rank // 2, depth), f32(rank // 2, depth), f32(packed // 2, LANES), f32(packed // 2, LANES)),
-        in_specs=[pl.BlockSpec((BLOCK, depth), lambda i: (i, 0)), whole(depth, rank)],
-        out_specs=(
-            pl.BlockSpec((BLOCK, rank), lambda i: (i, 0)),
-            whole(rank // 2, depth), whole(rank // 2, depth),
-            whole(packed // 2, LANES), whole(packed // 2, LANES),
-        ),
-        scratch_shapes=[
-            pltpu.VMEM((depth, rank), jnp.bfloat16), pltpu.VMEM((depth, rank), jnp.bfloat16),
-            pltpu.VMEM((rank, depth), jnp.float32), pltpu.VMEM((rank, rank), jnp.float32),
-            pltpu.VMEM((packed, LANES), jnp.float32),
-        ],
-        compiler_params=pltpu.CompilerParams(vmem_limit_bytes=58 * 2**20),
-        cost_estimate=pl.CostEstimate(flops=4 * 10**9, bytes_accessed=8 * 2**20, transcendentals=0),
-        name="local_terms",
-    )(features, sketch)
-
-
-def factor_kernel(scale, first, last, *refs):
-    if first == 0:
-        keep_ref, other_ref, a_ref, factor_ref, packed_ref = refs
-        half = keep_ref.shape[0]
-        core = core_bit()
-        packed_ref[rows_of(core, half), :] = keep_ref[...]
-        packed_ref[rows_of(1 - core, half), :] = other_ref[...]
-        a_ref[:LANES, :LANES] = packed_ref[:LANES, :]
-        a_ref[:LANES, LANES:] = packed_ref[LANES:2 * LANES, :]
-        a_ref[LANES:, :LANES] = jnp.zeros((LANES, LANES), jnp.float32)
-        a_ref[LANES:, LANES:] = packed_ref[2 * LANES:, :]
+            half_ref = halves[at // (BLOCKS // 2)]
+            top = at % (BLOCKS // 2) * height
+            a_ref[rows_of(at ^ own, height), :] = half_ref[top:top + height, :]
     else:
         from_ref, upper_ref, a_ref, factor_ref, *flipped_ref = refs
         a_ref[...] = from_ref[...]
@@ -200,34 +199,35 @@
         flipped_ref[0][...] = inverse.T * scale
 
 
-def factor_part(operands, size, scale, first, last):
+def factor_part(operands, size, scale, first, last, after=()):
     square = jax.ShapeDtypeStruct((size, size), jnp.float32)
     outs = 3 if last == size else 2
     return pl.pallas_call(
-        lambda *refs: factor_kernel(scale, first, last, *refs),
+        lambda *refs: factor_kernel(scale, first, last, len(after), *refs),
         out_shape=(square,) * outs,
-        in_specs=[VMEM] * 2,
+        in_specs=[VMEM] * 2 + [pl.BlockSpec(memory_space=pl.ANY)] * len(after),
         out_specs=(VMEM,) * outs,
-        scratch_shapes=[pltpu.VMEM((3 * LANES, LANES), jnp.float32)] if first == 0 else [],
         compiler_params=pltpu.CompilerParams(vmem_limit_bytes=16 * 2**20),
         cost_estimate=pl.CostEstimate(flops=12 * 10**9 * (last - first) // size, bytes_accessed=2**20, transcendentals=last - first),
         name="factor_part",
-    )(*operands)
+    )(*operands, *after)
 
 
 def basis_kernel(sampled_ref, flipped_ref, basis_ref):
-    basis_ref[...] = product(split(sampled_ref[...]), split(flipped_ref[...]), 1, 0)
+    flipped = split(flipped_ref[...])
+    for top in range(0, sampled_ref.shape[1], BLOCK):
+        span = slice(top, top + BLOCK)
+        basis_ref[span, :] = product(split(sampled_ref[:, span].T), flipped, 1, 0)
 
 
 def basis_of(sampled, flipped):
-    rows, rank = sampled.shape
     return pl.pallas_call(
         basis_kernel,
-        grid=(rows // BLOCK,),
-        out_shape=jax.ShapeDtypeStruct(sampled.shape, jnp.float32),
-        in_specs=[pl.BlockSpec((BLOCK, rank), lambda i: (i, 0)), pl.BlockSpec((rank, rank), lambda i: (0, 0))],
-        out_specs=pl.BlockSpec((BLOCK, rank), lambda i: (i, 0)),
-        cost_estimate=pl.CostEstimate(flops=4 * 10**8, bytes_accessed=2 * 2**20, transcendentals=0),
+        out_shape=f32(*sampled.shape[::-1]),
+        in_specs=[VMEM] * 2,
+        out_specs=VMEM,
+        compiler_params=pltpu.CompilerParams(vmem_limit_bytes=16 * 2**20),
+        cost_estimate=pl.CostEstimate(flops=2 * 10**9, bytes_accessed=2 * 2**20, transcendentals=0),
         name="basis",
     )(sampled, flipped)
 
@@ -279,44 +279,39 @@
     return wide + narrow
 
 
-def sum_gram(keep, other):
-    half = keep + send(other, *CORE)
-    for mask in [(0, 1), (2, 0), (4, 0), (8, 0)] + spare_bits():
-        half = half + send(half, *mask)
-    return half, send(half, *CORE)
-
-
-def quarters(values):
-    height = values[0].shape[0] // 4
-    return [sum(value[at * height:(at + 1) * height] for value in values) for at in range(4)]
-
-
-def scatter(values, masks):
-    first, *rest = quarters(values)
+def spread(parts, masks):
+    first, *rest = parts
     return [first] + [send(part, *mask) for part, mask in zip(rest, masks)]
-
-
-def sum_cross(keep, other):
-    values = scatter([keep, send(other, *CORE)], PLANE)
-    values = scatter(values, LINE)
-    own = sum(values)
-    for mask in spare_bits():
-        own = own + send(own, *mask)
-    line = jnp.concatenate([own] + [send(own, *mask) for mask in LINE])
-    plane = [line] + [send(line, *mask) for mask in PLANE]
-    return plane + [send(part, *CORE) for part in plane]
 
 
 def per_device(features, sketch):
     scale = (features.shape[0] * lax.axis_size(AXES)) ** 0.5
     size = sketch.shape[1]
-    sampled, keep, other, gram_keep, gram_other = local_terms(features, sketch)
-    gram = sum_gram(gram_keep, gram_other)
-    cross = sum_cross(keep, other)
-    state = gram
+    depth = features.shape[1]
+    dot = lambda a, b, dims: lax.dot_general(a, b, ((dims[:1], dims[1:]), ((), ())), precision=lax.Precision.HIGH, preferred_element_type=jnp.float32)
+    sampled = dot(sketch, features, (0, 1))
+    cross = dot(sampled, features, (1, 0))
+    gram = dot(sampled, sampled, (1, 1))
+    half = f32(size // 2, depth + size)
+    keep, other = call(arrange_kernel, "arrange", (half, half), cross, gram)
+    height = size // BLOCKS
+    parts = call(core_sum_kernel, "core_sum", (f32(4 * height, depth + size),) * 4, keep, send(other, *CORE))
+    parts = call(lambda *refs: plane_sum_kernel(depth, *refs), "plane_sum", (f32(height, depth + 4 * size),) * 4, *spread(parts, PLANE))
+    own, gram = call(lambda *refs: line_sum_kernel(depth, *refs), "line_sum", (f32(height, depth), f32(4 * height, size)), *spread(parts, LINE))
+    for mask in spare_bits():
+        own = own + send(own, *mask)
+        gram = gram + send(gram, *mask)
+    line = [own] + [send(own, *mask) for mask in LINE]
+    gram = [gram] + [send(gram, *mask) for mask in PLANE]
+    line, gram = call(join_kernel, "join", (f32(4 * height, depth), f32(16 * height, size)), *line, *gram)
+    plane = [line] + [send(line, *mask) for mask in PLANE]
+    state = (gram, send(gram, *CORE))
+    after = (line,)
     for first in range(0, size, PANEL):
-        state = factor_part(state[:2], size, scale, first, first + PANEL)
+        state = factor_part(state[:2], size, scale, first, first + PANEL, after)
+        after = ()
     inverse, factor, flipped = state
+    cross = plane + [send(part, *CORE) for part in plane]
     return (basis_of(sampled, flipped), factor, project(inverse, cross))
 
 

time: 70.6 us -> 66.4 us (0.941)
  Pallas kernels: 25.6 us -> 13.2 us
  matrix products: 0 us -> 8.72 us
  waiting for transfers between devices: 15.8 us -> 20.3 us
  starting transfers between devices: 25.3 us -> 22.1 us
  other arithmetic: 2.18 us -> 0 us
    pallas_call x6 -> x10, Pallas kernels: 23.9 us -> 11.6 us  [the longest x4 9.64 us: factor_part(): pl.pallas_call(lambda *refs: factor_kernel(scale, first, last, len(after)...]
    dot_general x0 -> x3, matrix products: none -> 8.72 us  [per_device(): lax.dot_general(a, b, ((dims[:1], dims[1:]), ((), ())), precision=lax.Pre...]
    ppermute x23 -> x21, waiting for transfers between devices: 15.8 us -> 20.3 us  [send(): return lax.ppermute(value, AXES, pairs)]
    ppermute x23 -> x21, starting transfers between devices: 25.3 us -> 22.1 us  [send(): return lax.ppermute(value, AXES, pairs)]
    add x8 -> x0, other arithmetic: 2.17 us -> none  [the longest x2 1.2 us: quarters(): sum((value[at * height:(at + 1) * height] for value in values))]
  transfers between devices with their start and end apart: 23 -> 21, of which waited for: 9 -> 10; matrix products, arithmetic and copies ran while one was open for 3% -> 0% of each run, Pallas kernels for 19% -> 17%
where the time goes in v7:
time: 66.4 us; the launch traced here: 66.2 us
  starting transfers between devices  22.1 us (33%)
  waiting for transfers between devices  20.3 us (31%)
  Pallas kernels  13.2 us (20%)
  matrix products  8.72 us (13%)
  local copies, waits for them, and re-layouts  1.23 us (2%)
  between operations  0.76 us (1%)
    ppermute x21, starting transfers between devices, send(): return lax.ppermute(value, AXES, pairs)  22.1 us
    ppermute x21, waiting for transfers between devices, send(): return lax.ppermute(value, AXES, pairs)  20.3 us
    pallas_call x4, Pallas kernels, factor_part(): pl.pallas_call(lambda *refs: factor_kernel(scale, first, last, len(after)...  9.64 us
    dot_general x3, matrix products, per_device(): lax.dot_general(a, b, ((dims[:1], dims[1:]), ((), ())), precision=lax.Pre...  8.72 us
    pallas_call x1, Pallas kernels, basis_of(): pl.pallas_call(basis_kernel, out_shape=f32(*sampled.shape[::-1]), in_spec...  1.68 us
    pallas_call x1, Pallas kernels, project(): pl.pallas_call(project_kernel, out_shape=jax.ShapeDtypeStruct((rank, dept...  1.66 us
  transfers between devices with their start and end apart: 21, of which 10 were waited for; matrix products, arithmetic and copies ran while one was open for 0% of the time, Pallas kernels for 17%

profile of v7, /device:TPU:0, one launch (start us, length us, event | category | flops | bytes accessed | tf_op | source)
XLA Modules:
  0.0 66.2 jit_solution(16916389394329937488)
XLA Ops:
  0.6 0.0 copy-start
  0.6 1.2 %copy-done = f32[1024,256]{1,0:T(8,128)S(1)} copy-done((f32[1024,256]{1,0:T(8,128)S(1)}, f32[1024,256]{1,0:T(8,128)}, u32[]{:S(2)}) %copy-start) | copy-done | bytes 1048600
  1.9 0.0 copy-start.1
  1.9 5.8 %fusion.sampled_ref = f32[256,1024]{1,0:T(8,128)S(1)} fusion(f32[1024,256]{1,0:T(8,128)S(1)} %copy-done, f32[1024,1024]{1,0:T(8,128)} %param.2), kind=kOutput, calls=%fused_computation | convolution fusion | flops 1610612736 | bytes 6291456 | tf_op jit(solution)/shard_map/dot_general | solution.py:291
  7.7 0.0 copy-done.1
  7.7 2.3 %fusion.1.refs_0_ = f32[256,1024]{1,0:T(8,128)S(1)} fusion(f32[256,1024]{1,0:T(8,128)S(1)} %fusion.sampled_ref, f32[1024,1024]{1,0:T(8,128)S(1)} %copy-done.1), kind=kOutput, calls=%fused_computation.1 | convolution fusion | flops 1610612736 | bytes 6291456 | tf_op jit(solution)/shard_map/dot_general | solution.py:291
  10.0 0.6 fusion.2.refs_1_
  10.6 0.1 arrange.1
  10.7 0.5 collective-permute-start
  11.3 1.7 %collective-permute-done.refs_1_ = f32[128,1280]{1,0:T(8,128)S(1)} collective-permute-done((f32[128,1280]{1,0:T(8,128)S(1)}, f32[128,1280]{1,0:T(8,128)S(1)}, u32[]{:S(2)}, u32[]{:S(2)}) %collective-permute-start) | collective-permute-done | bytes 655392 | tf_op jit(solution)/shard_map/ppermute | solution.py:268
  13.0 0.1 core_sum.1
  13.0 3.0 %collective-permute-start.1 = (f32[32,1280]{1,0:T(8,128)S(1)}, f32[32,1280]{1,0:T(8,128)S(1)}, u32[]{:S(2)}, u32[]{:S(2)}) collective-permute-start(f32[32,1280]{1,0:T(8,128)S(1)} %get-tuple-element.29), channel_id=1, source_target_pairs={{0,1},{1,0},{2,3},{3,2},{4,5},{5,4},{6,7},{7,6},{8,9},{9,8},{10,11... | collective-permute-start | bytes 491528 | tf_op jit(solution)/shard_map/ppermute | solution.py:268
  16.0 1.5 %collective-permute-start.2 = (f32[32,1280]{1,0:T(8,128)S(1)}, f32[32,1280]{1,0:T(8,128)S(1)}, u32[]{:S(2)}, u32[]{:S(2)}) collective-permute-start(f32[32,1280]{1,0:T(8,128)S(1)} %get-tuple-element.30), channel_id=1, source_target_pairs={{0,4},{1,5},{2,6},{3,7},{4,0},{5,1},{6,2},{7,3},{8,12},{9,13},{10,... | collective-permute-start | bytes 491528 | tf_op jit(solution)/shard_map/ppermute | solution.py:268
  17.5 0.0 collective-permute-start.3
  17.5 3.0 %collective-permute-done.1.refs_1_ = f32[32,1280]{1,0:T(8,128)S(1)} collective-permute-done((f32[32,1280]{1,0:T(8,128)S(1)}, f32[32,1280]{1,0:T(8,128)S(1)}, u32[]{:S(2)}, u32[]{:S(2)}) %collective-permute-start.1) | collective-permute-done | bytes 163872 | tf_op jit(solution)/shard_map/ppermute | solution.py:268
  20.5 2.6 %collective-permute-done.2.refs_2_ = f32[32,1280]{1,0:T(8,128)S(1)} collective-permute-done((f32[32,1280]{1,0:T(8,128)S(1)}, f32[32,1280]{1,0:T(8,128)S(1)}, u32[]{:S(2)}, u32[]{:S(2)}) %collective-permute-start.2) | collective-permute-done | bytes 163872 | tf_op jit(solution)/shard_map/ppermute | solution.py:268
  23.1 2.2 %collective-permute-done.3.refs_3_ = f32[32,1280]{1,0:T(8,128)S(1)} collective-permute-done((f32[32,1280]{1,0:T(8,128)S(1)}, f32[32,1280]{1,0:T(8,128)S(1)}, u32[]{:S(2)}, u32[]{:S(2)}) %collective-permute-start.3) | collective-permute-done | bytes 163872 | tf_op jit(solution)/shard_map/ppermute | solution.py:268
  25.3 1.8 %collective-permute-start.4 = (f32[8,2048]{1,0:T(8,128)S(1)}, f32[8,2048]{1,0:T(8,128)S(1)}, u32[]{:S(2)}, u32[]{:S(2)}) collective-permute-start(f32[8,2048]{1,0:T(8,128)S(1)} %get-tuple-element.33), channel_id=1, source_target_pairs={{0,8},{1,9},{2,10},{3,11},{4,12},{5,13},{6,14},{7,15},{8,0},{9,1},... | collective-permute-start | bytes 196616 | tf_op jit(solution)/shard_map/ppermute | solution.py:268
  27.1 2.6 %collective-permute-start.5 = (f32[8,2048]{1,0:T(8,128)S(1)}, f32[8,2048]{1,0:T(8,128)S(1)}, u32[]{:S(2)}, u32[]{:S(2)}) collective-permute-start(f32[8,2048]{1,0:T(8,128)S(1)} %get-tuple-element.34), channel_id=1, source_target_pairs={{0,16},{1,17},{2,18},{3,19},{4,20},{5,21},{6,22},{7,23},{8,24},{9,... | collective-permute-start | bytes 196616 | tf_op jit(solution)/shard_map/ppermute | solution.py:268
  29.7 0.1 collective-permute-start.6
  29.8 0.5 collective-permute-done.4.refs_1_
  30.3 3.4 %collective-permute-done.5.refs_2_ = f32[8,2048]{1,0:T(8,128)S(1)} collective-permute-done((f32[8,2048]{1,0:T(8,128)S(1)}, f32[8,2048]{1,0:T(8,128)S(1)}, u32[]{:S(2)}, u32[]{:S(2)}) %collective-permute-start.5) | collective-permute-done | bytes 65568 | tf_op jit(solution)/shard_map/ppermute | solution.py:268
  33.7 2.5 %collective-permute-done.6.refs_3_ = f32[8,2048]{1,0:T(8,128)S(1)} collective-permute-done((f32[8,2048]{1,0:T(8,128)S(1)}, f32[8,2048]{1,0:T(8,128)S(1)}, u32[]{:S(2)}, u32[]{:S(2)}) %collective-permute-start.6) | collective-permute-done | bytes 65568 | tf_op jit(solution)/shard_map/ppermute | solution.py:268
  36.2 0.1 collective-permute-start.7
  36.3 1.0 %collective-permute-start.8 = (f32[8,1024]{1,0:T(8,128)S(1)}, f32[8,1024]{1,0:T(8,128)S(1)}, u32[]{:S(2)}, u32[]{:S(2)}) collective-permute-start(f32[8,1024]{1,0:T(8,128)S(1)} %get-tuple-element.36.refs_0_), channel_id=1, source_target_pairs={{0,16},{1,17},{2,18},{3,19},{4,20},{5,21},{6,22},{7,23},{8,24},{9,... | collective-permute-start | bytes 98312 | tf_op jit(solution)/shard_map/ppermute | solution.py:268
  37.3 3.3 %collective-permute-start.9 = (f32[8,1024]{1,0:T(8,128)S(1)}, f32[8,1024]{1,0:T(8,128)S(1)}, u32[]{:S(2)}, u32[]{:S(2)}) collective-permute-start(f32[8,1024]{1,0:T(8,128)S(1)} %get-tuple-element.36.refs_0_), channel_id=1, source_target_pairs={{0,24},{1,25},{2,26},{3,27},{4,28},{5,29},{6,30},{7,31},{8,16},{9,... | collective-permute-start | bytes 98312 | tf_op jit(solution)/shard_map/ppermute | solution.py:268
  40.7 1.5 %collective-permute-start.10 = (f32[32,256]{1,0:T(8,128)S(1)}, f32[32,256]{1,0:T(8,128)S(1)}, u32[]{:S(2)}, u32[]{:S(2)}) collective-permute-start(f32[32,256]{1,0:T(8,128)S(1)} %get-tuple-element.37.refs_4_), channel_id=1, source_target_pairs={{0,1},{1,0},{2,3},{3,2},{4,5},{5,4},{6,7},{7,6},{8,9},{9,8},{10,11... | collective-permute-start | bytes 98312 | tf_op jit(solution)/shard_map/ppermute | solution.py:268
  42.2 1.5 %collective-permute-start.11 = (f32[32,256]{1,0:T(8,128)S(1)}, f32[32,256]{1,0:T(8,128)S(1)}, u32[]{:S(2)}, u32[]{:S(2)}) collective-permute-start(f32[32,256]{1,0:T(8,128)S(1)} %get-tuple-element.37.refs_4_), channel_id=1, source_target_pairs={{0,4},{1,5},{2,6},{3,7},{4,0},{5,1},{6,2},{7,3},{8,12},{9,13},{10,... | collective-permute-start | bytes 98312 | tf_op jit(solution)/shard_map/ppermute | solution.py:268
  43.7 0.0 collective-permute-done.7.refs_1_
  43.7 0.5 collective-permute-start.12
  44.2 0.0 collective-permute-done.8.refs_2_
  44.2 0.0 collective-permute-done.9.refs_3_
  44.2 0.4 collective-permute-done.10.refs_5_
  44.6 1.5 %collective-permute-done.11.refs_6_ = f32[32,256]{1,0:T(8,128)S(1)} collective-permute-done((f32[32,256]{1,0:T(8,128)S(1)}, f32[32,256]{1,0:T(8,128)S(1)}, u32[]{:S(2)}, u32[]{:S(2)}) %collective-permute-start.11) | collective-permute-done | bytes 32800 | tf_op jit(solution)/shard_map/ppermute | solution.py:268
  46.1 2.4 %collective-permute-done.12.refs_7_ = f32[32,256]{1,0:T(8,128)S(1)} collective-permute-done((f32[32,256]{1,0:T(8,128)S(1)}, f32[32,256]{1,0:T(8,128)S(1)}, u32[]{:S(2)}, u32[]{:S(2)}) %collective-permute-start.12) | collective-permute-done | bytes 32800 | tf_op jit(solution)/shard_map/ppermute | solution.py:268
  48.5 0.1 collective-permute-start.13
  48.6 0.6 collective-permute-start.14
  49.2 0.5 collective-permute-start.15
  49.7 2.4 %collective-permute-start.16 = (f32[32,1024]{1,0:T(8,128)S(1)}, f32[32,1024]{1,0:T(8,128)S(1)}, u32[]{:S(2)}, u32[]{:S(2)}) collective-permute-start(f32[32,1024]{1,0:T(8,128)S(1)} %get-tuple-element.39.refs_2_.refs_0_), channel_id=1, source_target_pairs={{0,5},{1,4},{2,7},{3,6},{4,1},{5,0},{6,3},{7,2},{8,13},{9,12},{10,... | collective-permute-start | bytes 393224 | tf_op jit(solution)/shard_map/ppermute | solution.py:268
  52.2 0.0 collective-permute-start.17
  52.2 0.0 collective-permute-done.13.refs_1_
  52.2 2.4 %factor_part.4 = (f32[256,256]{1,0:T(8,128)S(1)}, f32[256,256]{1,0:T(8,128)S(1)}) custom-call(f32[128,256]{1,0:T(8,128)S(1)} %get-tuple-element.38.refs_0_, f32[128,256]{1,0:T(8,128)S(1)} %collective-permute-done.13.refs_1_, f32[32,1024]{1,0:T(8,128)S(1)} %get-tuple-element.39.refs_2_.refs_0_), custom_call_target="tpu_custom_call" | custom-call | flops 3000000000 | bytes 1048576 | tf_op jit(solution)/shard_map/factor_part/pallas_call | solution.py:205
  54.6 2.2 %factor_part.5 = (f32[256,256]{1,0:T(8,128)S(1)}, f32[256,256]{1,0:T(8,128)S(1)}) custom-call(f32[256,256]{1,0:T(8,128)S(1)} %get-tuple-element.40.refs_0_, f32[256,256]{1,0:T(8,128)S(1)} %get-tuple-element.41.refs_1_), custom_call_target="tpu_custom_call" | custom-call | flops 3000000000 | bytes 1048576 | tf_op jit(solution)/shard_map/factor_part/pallas_call | solution.py:205
  56.8 2.4 %factor_part.6 = (f32[256,256]{1,0:T(8,128)S(1)}, f32[256,256]{1,0:T(8,128)S(1)}) custom-call(f32[256,256]{1,0:T(8,128)S(1)} %get-tuple-element.42.refs_0_, f32[256,256]{1,0:T(8,128)S(1)} %get-tuple-element.43.refs_1_), custom_call_target="tpu_custom_call" | custom-call | flops 3000000000 | bytes 1048576 | tf_op jit(solution)/shard_map/factor_part/pallas_call | solution.py:205
  59.2 2.6 %factor_part.7 = (f32[256,256]{1,0:T(8,128)S(1)}, f32[256,256]{1,0:T(8,128)}, f32[256,256]{1,0:T(8,128)S(1)}) custom-call(f32[256,256]{1,0:T(8,128)S(1)} %get-tuple-element.44.refs_0_, f32[256,256]{1,0:T(8,128)S(1)} %get-tuple-element.45.refs_1_), custom_call_target="tpu_custom_call" | custom-call | flops 3000000000 | bytes 1048576 | tf_op jit(solution)/shard_map/factor_part/pallas_call | solution.py:205
  61.8 0.0 collective-permute-done.14.refs_1_
  61.8 0.5 collective-permute-start.18
  62.4 0.0 collective-permute-done.15.refs_2_
  62.4 0.1 collective-permute-start.19
  62.4 0.0 collective-permute-done.16.refs_3_
  62.4 0.4 collective-permute-start.20
  62.9 1.7 %basis.1 = f32[1024,256]{1,0:T(8,128)} custom-call(f32[256,1024]{1,0:T(8,128)S(1)} %fusion.sampled_ref, f32[256,256]{1,0:T(8,128)S(1)} %get-tuple-element.46.flipped_ref), custom_call_target="tpu_custom_call" | custom-call | flops 2000000000 | bytes 2097152 | tf_op jit(solution)/shard_map/basis/pallas_call | solution.py:224
  64.6 0.0 collective-permute-done.17.refs_4_
  64.6 0.0 collective-permute-done.18.refs_5_
  64.6 0.0 collective-permute-done.19.refs_6_
  64.6 0.0 collective-permute-done.20.refs_7_
  64.6 1.7 %project.1 = f32[256,1024]{1,0:T(8,128)} custom-call(f32[256,256]{1,0:T(8,128)S(1)} %get-tuple-element.48.inverse_ref, f32[32,1024]{1,0:T(8,128)S(1)} %get-tuple-element.39.refs_2_.refs_0_, f32[32,1024]{1,0:T(8,128)S(1)} %collective-permute-done.14.refs_1_, f32[32,1024]{1,0:T(8,128)S(1)} %collective-permute-done.15.refs_2_, ...), custom_call_target="tpu_custom_call" | custom-call | flops 400000000 | bytes 2097152 | tf_op jit(solution)/shard_map/project/pallas_call | solution.py:253
  (3 shorter events, 0.1 us)
Async XLA Ops:
  0.6 1.2 %copy-start = (f32[1024,256]{1,0:T(8,128)S(1)}, f32[1024,256]{1,0:T(8,128)}, u32[]{:S(2)}) copy-start(f32[1024,256]{1,0:T(8,128)} %param.3) | copy-start | bytes 3145732
  1.9 5.8 %copy-start.1 = (f32[1024,1024]{1,0:T(8,128)S(1)}, f32[1024,1024]{1,0:T(8,128)}, u32[]{:S(2)}) copy-start(f32[1024,1024]{1,0:T(8,128)} %param.2) | copy-start | bytes 12582916
  10.7 2.2 %collective-permute-start = (f32[128,1280]{1,0:T(8,128)S(1)}, f32[128,1280]{1,0:T(8,128)S(1)}, u32[]{:S(2)}, u32[]{:S(2)}) collective-permute-start(f32[128,1280]{1,0:T(8,128)S(1)} %get-tuple-element.27), channel_id=1, source_target_pairs={{0,2},{1,3},{2,0},{3,1},{4,6},{5,7},{6,4},{7,5},{8,10},{9,11},{10,... | collective-permute-start | bytes 1966088 | tf_op jit(solution)/shard_map/ppermute | solution.py:268
  13.0 7.5 %collective-permute-start.1 = (f32[32,1280]{1,0:T(8,128)S(1)}, f32[32,1280]{1,0:T(8,128)S(1)}, u32[]{:S(2)}, u32[]{:S(2)}) collective-permute-start(f32[32,1280]{1,0:T(8,128)S(1)} %get-tuple-element.29), channel_id=1, source_target_pairs={{0,1},{1,0},{2,3},{3,2},{4,5},{5,4},{6,7},{7,6},{8,9},{9,8},{10,11... | collective-permute-start | bytes 491528 | tf_op jit(solution)/shard_map/ppermute | solution.py:268
  16.0 7.1 %collective-permute-start.2 = (f32[32,1280]{1,0:T(8,128)S(1)}, f32[32,1280]{1,0:T(8,128)S(1)}, u32[]{:S(2)}, u32[]{:S(2)}) collective-permute-start(f32[32,1280]{1,0:T(8,128)S(1)} %get-tuple-element.30), channel_id=1, source_target_pairs={{0,4},{1,5},{2,6},{3,7},{4,0},{5,1},{6,2},{7,3},{8,12},{9,13},{10,... | collective-permute-start | bytes 491528 | tf_op jit(solution)/shard_map/ppermute | solution.py:268
  17.5 7.8 %collective-permute-start.3 = (f32[32,1280]{1,0:T(8,128)S(1)}, f32[32,1280]{1,0:T(8,128)S(1)}, u32[]{:S(2)}, u32[]{:S(2)}) collective-permute-start(f32[32,1280]{1,0:T(8,128)S(1)} %get-tuple-element.31), channel_id=1, source_target_pairs={{0,5},{1,4},{2,7},{3,6},{4,1},{5,0},{6,3},{7,2},{8,13},{9,12},{10,... | collective-permute-start | bytes 491528 | tf_op jit(solution)/shard_map/ppermute | solution.py:268
  25.3 5.0 %collective-permute-start.4 = (f32[8,2048]{1,0:T(8,128)S(1)}, f32[8,2048]{1,0:T(8,128)S(1)}, u32[]{:S(2)}, u32[]{:S(2)}) collective-permute-start(f32[8,2048]{1,0:T(8,128)S(1)} %get-tuple-element.33), channel_id=1, source_target_pairs={{0,8},{1,9},{2,10},{3,11},{4,12},{5,13},{6,14},{7,15},{8,0},{9,1},... | collective-permute-start | bytes 196616 | tf_op jit(solution)/shard_map/ppermute | solution.py:268
  27.1 6.6 %collective-permute-start.5 = (f32[8,2048]{1,0:T(8,128)S(1)}, f32[8,2048]{1,0:T(8,128)S(1)}, u32[]{:S(2)}, u32[]{:S(2)}) collective-permute-start(f32[8,2048]{1,0:T(8,128)S(1)} %get-tuple-element.34), channel_id=1, source_target_pairs={{0,16},{1,17},{2,18},{3,19},{4,20},{5,21},{6,22},{7,23},{8,24},{9,... | collective-permute-start | bytes 196616 | tf_op jit(solution)/shard_map/ppermute | solution.py:268
  29.7 6.5 %collective-permute-start.6 = (f32[8,2048]{1,0:T(8,128)S(1)}, f32[8,2048]{1,0:T(8,128)S(1)}, u32[]{:S(2)}, u32[]{:S(2)}) collective-permute-start(f32[8,2048]{1,0:T(8,128)S(1)} %get-tuple-element.35), channel_id=1, source_target_pairs={{0,24},{1,25},{2,26},{3,27},{4,28},{5,29},{6,30},{7,31},{8,16},{9,... | collective-permute-start | bytes 196616 | tf_op jit(solution)/shard_map/ppermute | solution.py:268
  36.2 7.5 %collective-permute-start.7 = (f32[8,1024]{1,0:T(8,128)S(1)}, f32[8,1024]{1,0:T(8,128)S(1)}, u32[]{:S(2)}, u32[]{:S(2)}) collective-permute-start(f32[8,1024]{1,0:T(8,128)S(1)} %get-tuple-element.36.refs_0_), channel_id=1, source_target_pairs={{0,8},{1,9},{2,10},{3,11},{4,12},{5,13},{6,14},{7,15},{8,0},{9,1},... | collective-permute-start | bytes 98312 | tf_op jit(solution)/shard_map/ppermute | solution.py:268
  36.3 7.9 %collective-permute-start.8 = (f32[8,1024]{1,0:T(8,128)S(1)}, f32[8,1024]{1,0:T(8,128)S(1)}, u32[]{:S(2)}, u32[]{:S(2)}) collective-permute-start(f32[8,1024]{1,0:T(8,128)S(1)} %get-tuple-element.36.refs_0_), channel_id=1, source_target_pairs={{0,16},{1,17},{2,18},{3,19},{4,20},{5,21},{6,22},{7,23},{8,24},{9,... | collective-permute-start | bytes 98312 | tf_op jit(solution)/shard_map/ppermute | solution.py:268
  37.3 6.8 %collective-permute-start.9 = (f32[8,1024]{1,0:T(8,128)S(1)}, f32[8,1024]{1,0:T(8,128)S(1)}, u32[]{:S(2)}, u32[]{:S(2)}) collective-permute-start(f32[8,1024]{1,0:T(8,128)S(1)} %get-tuple-element.36.refs_0_), channel_id=1, source_target_pairs={{0,24},{1,25},{2,26},{3,27},{4,28},{5,29},{6,30},{7,31},{8,16},{9,... | collective-permute-start | bytes 98312 | tf_op jit(solution)/shard_map/ppermute | solution.py:268
  40.7 3.9 %collective-permute-start.10 = (f32[32,256]{1,0:T(8,128)S(1)}, f32[32,256]{1,0:T(8,128)S(1)}, u32[]{:S(2)}, u32[]{:S(2)}) collective-permute-start(f32[32,256]{1,0:T(8,128)S(1)} %get-tuple-element.37.refs_4_), channel_id=1, source_target_pairs={{0,1},{1,0},{2,3},{3,2},{4,5},{5,4},{6,7},{7,6},{8,9},{9,8},{10,11... | collective-permute-start | bytes 98312 | tf_op jit(solution)/shard_map/ppermute | solution.py:268
  42.2 3.9 %collective-permute-start.11 = (f32[32,256]{1,0:T(8,128)S(1)}, f32[32,256]{1,0:T(8,128)S(1)}, u32[]{:S(2)}, u32[]{:S(2)}) collective-permute-start(f32[32,256]{1,0:T(8,128)S(1)} %get-tuple-element.37.refs_4_), channel_id=1, source_target_pairs={{0,4},{1,5},{2,6},{3,7},{4,0},{5,1},{6,2},{7,3},{8,12},{9,13},{10,... | collective-permute-start | bytes 98312 | tf_op jit(solution)/shard_map/ppermute | solution.py:268
  43.7 4.8 %collective-permute-start.12 = (f32[32,256]{1,0:T(8,128)S(1)}, f32[32,256]{1,0:T(8,128)S(1)}, u32[]{:S(2)}, u32[]{:S(2)}) collective-permute-start(f32[32,256]{1,0:T(8,128)S(1)} %get-tuple-element.37.refs_4_), channel_id=1, source_target_pairs={{0,5},{1,4},{2,7},{3,6},{4,1},{5,0},{6,3},{7,2},{8,13},{9,12},{10,... | collective-permute-start | bytes 98312 | tf_op jit(solution)/shard_map/ppermute | solution.py:268
  48.5 3.6 %collective-permute-start.13 = (f32[128,256]{1,0:T(8,128)S(1)}, f32[128,256]{1,0:T(8,128)S(1)}, u32[]{:S(2)}, u32[]{:S(2)}) collective-permute-start(f32[128,256]{1,0:T(8,128)S(1)} %get-tuple-element.38.refs_0_), channel_id=1, source_target_pairs={{0,2},{1,3},{2,0},{3,1},{4,6},{5,7},{6,4},{7,5},{8,10},{9,11},{10,... | collective-permute-start | bytes 393224 | tf_op jit(solution)/shard_map/ppermute | solution.py:268
  48.6 13.2 %collective-permute-start.14 = (f32[32,1024]{1,0:T(8,128)S(1)}, f32[32,1024]{1,0:T(8,128)S(1)}, u32[]{:S(2)}, u32[]{:S(2)}) collective-permute-start(f32[32,1024]{1,0:T(8,128)S(1)} %get-tuple-element.39.refs_2_.refs_0_), channel_id=1, source_target_pairs={{0,1},{1,0},{2,3},{3,2},{4,5},{5,4},{6,7},{7,6},{8,9},{9,8},{10,11... | collective-permute-start | bytes 393224 | tf_op jit(solution)/shard_map/ppermute | solution.py:268
  49.2 13.2 %collective-permute-start.15 = (f32[32,1024]{1,0:T(8,128)S(1)}, f32[32,1024]{1,0:T(8,128)S(1)}, u32[]{:S(2)}, u32[]{:S(2)}) collective-permute-start(f32[32,1024]{1,0:T(8,128)S(1)} %get-tuple-element.39.refs_2_.refs_0_), channel_id=1, source_target_pairs={{0,4},{1,5},{2,6},{3,7},{4,0},{5,1},{6,2},{7,3},{8,12},{9,13},{10,... | collective-permute-start | bytes 393224 | tf_op jit(solution)/shard_map/ppermute | solution.py:268
  49.7 12.7 %collective-permute-start.16 = (f32[32,1024]{1,0:T(8,128)S(1)}, f32[32,1024]{1,0:T(8,128)S(1)}, u32[]{:S(2)}, u32[]{:S(2)}) collective-permute-start(f32[32,1024]{1,0:T(8,128)S(1)} %get-tuple-element.39.refs_2_.refs_0_), channel_id=1, source_target_pairs={{0,5},{1,4},{2,7},{3,6},{4,1},{5,0},{6,3},{7,2},{8,13},{9,12},{10,... | collective-permute-start | bytes 393224 | tf_op jit(solution)/shard_map/ppermute | solution.py:268
  52.2 12.4 %collective-permute-start.17 = (f32[32,1024]{1,0:T(8,128)S(1)}, f32[32,1024]{1,0:T(8,128)S(1)}, u32[]{:S(2)}, u32[]{:S(2)}) collective-permute-start(f32[32,1024]{1,0:T(8,128)S(1)} %get-tuple-element.39.refs_2_.refs_0_), channel_id=1, source_target_pairs={{0,2},{1,3},{2,0},{3,1},{4,6},{5,7},{6,4},{7,5},{8,10},{9,11},{10,... | collective-permute-start | bytes 393224 | tf_op jit(solution)/shard_map/ppermute | solution.py:268
  61.8 2.7 %collective-permute-start.18 = (f32[32,1024]{1,0:T(8,128)S(1)}, f32[32,1024]{1,0:T(8,128)S(1)}, u32[]{:S(2)}, u32[]{:S(2)}) collective-permute-start(f32[32,1024]{1,0:T(8,128)S(1)} %collective-permute-done.14.refs_1_), channel_id=1, source_target_pairs={{0,2},{1,3},{2,0},{3,1},{4,6},{5,7},{6,4},{7,5},{8,10},{9,11},{10,... | collective-permute-start | bytes 393224 | tf_op jit(solution)/shard_map/ppermute | solution.py:268
  62.4 2.2 %collective-permute-start.19 = (f32[32,1024]{1,0:T(8,128)S(1)}, f32[32,1024]{1,0:T(8,128)S(1)}, u32[]{:S(2)}, u32[]{:S(2)}) collective-permute-start(f32[32,1024]{1,0:T(8,128)S(1)} %collective-permute-done.15.refs_2_), channel_id=1, source_target_pairs={{0,2},{1,3},{2,0},{3,1},{4,6},{5,7},{6,4},{7,5},{8,10},{9,11},{10,... | collective-permute-start | bytes 393224 | tf_op jit(solution)/shard_map/ppermute | solution.py:268
  62.4 2.1 %collective-permute-start.20 = (f32[32,1024]{1,0:T(8,128)S(1)}, f32[32,1024]{1,0:T(8,128)S(1)}, u32[]{:S(2)}, u32[]{:S(2)}) collective-permute-start(f32[32,1024]{1,0:T(8,128)S(1)} %collective-permute-done.16.refs_3_), channel_id=1, source_target_pairs={{0,2},{1,3},{2,0},{3,1},{4,6},{5,7},{6,4},{7,5},{8,10},{9,11},{10,... | collective-permute-start | bytes 393224 | tf_op jit(solution)/shard_map/ppermute | solution.py:268

commit v8 on v5

--- a/solution.py
+++ b/solution.py
@@ -13,61 +13,73 @@
 VMEM = pl.BlockSpec(memory_space=pltpu.VMEM)
 
 
-def factor_panel(a_ref, factor_ref, scale, base, height, size):
+def factor_panel(a_ref, factor_ref, base, height, size):
     lane = lax.broadcasted_iota(jnp.int32, (GROUP, LANES), 1)
     sub = lax.broadcasted_iota(jnp.int32, (GROUP, LANES), 0)
     tiles = size // LANES
+    spread = lambda value: jnp.broadcast_to(value, (GROUP, LANES))
+    rows = {}
+    for g in range(base, base + height, GROUP):
+        for t in range(tiles):
+            rows[g, t] = a_ref[g:g + GROUP, t * LANES:(t + 1) * LANES]
     for top in range(base, base + height, GROUP):
         groups = list(range(top, base + height, GROUP))
         home = top // LANES
         offset = top - home * LANES
         inside = (lane >= offset) & (lane < offset + GROUP)
-        rows = {}
-        for g in groups:
-            for t in range(tiles):
-                rows[g, t] = a_ref[g:g + GROUP, t * LANES:(t + 1) * LANES]
         diag = rows[top, home]
-        col = {}
-        for g in groups:
-            for j in range(GROUP):
-                at = rows[g, home][:, offset + j:offset + j + 1]
-                col[g, j] = jnp.broadcast_to(at, (GROUP, LANES))
-        one = {}
+        col, one = {}, {}
         for j in range(GROUP):
+            for g in groups:
+                col[g, j] = spread(rows[g, home][:, offset + j:offset + j + 1])
             for k in range(j, GROUP):
-                one[k, j] = jnp.broadcast_to(col[top, j][k:k + 1, :], (GROUP, LANES))
+                one[k, j] = spread(col[top, j][k:k + 1, :])
         for g in groups:
             fresh = jnp.where(lane == sub + offset, 1.0, 0.0) if g == top else 0.0
             rows[g, home] = jnp.where(inside, fresh, rows[g, home])
-        for j in range(GROUP):
-            inv = lax.rsqrt(one[j, j])
-            low = {k: one[k, j] * inv for k in range(j + 1, GROUP)}
-            for k in range(j + 1, GROUP):
+        for j in range(0, GROUP, 2):
+            a, b, c = one[j, j], one[j + 1, j], one[j + 1, j + 1]
+            first = lax.rsqrt(a)
+            both = first * lax.rsqrt(a * c - b * b)
+            cross = b * first
+            second = a * both
+            low = {}
+            for k in range(j + 2, GROUP):
+                low[k] = one[k, j] * first, (a * one[k, j + 1] - b * one[k, j]) * both
+            for k in range(j + 2, GROUP):
                 for m in range(k, GROUP):
-                    one[m, k] = one[m, k] - low[m] * low[k]
-            scaled = {g: col[g, j] * inv for g in groups}
-            for k in range(j + 1, GROUP):
+                    one[m, k] = one[m, k] - (low[m][0] * low[k][0] + low[m][1] * low[k][1])
+            scaled = {}
+            for g in groups:
+                scaled[g] = col[g, j] * first, (a * col[g, j + 1] - b * col[g, j]) * both
+            for k in range(j + 2, GROUP):
                 for g in groups:
-                    col[g, k] = col[g, k] - scaled[g] * low[k]
-            pivot = {t: jnp.broadcast_to(rows[top, t][j:j + 1, :], (GROUP, LANES)) * inv for t in range(tiles)}
-            pivot_diag = jnp.broadcast_to(diag[j:j + 1, :], (GROUP, LANES)) * inv
-            below = jnp.where(sub > j, scaled[top], 0.0)
-            diag = jnp.where(sub == j, pivot_diag, diag - below * pivot_diag)
+                    col[g, k] = col[g, k] - (scaled[g][0] * low[k][0] + scaled[g][1] * low[k][1])
+            below = [jnp.where(sub > j + 1, part, 0.0) for part in scaled[top]]
+
+            def pivots(value):
+                upper = spread(value[j:j + 1, :]) * first
+                return upper, (spread(value[j + 1:j + 2, :]) - cross * upper) * second
+
+            def replaced(value, upper, lower):
+                value = value - (below[0] * upper + below[1] * lower)
+                return jnp.where(sub == j, upper, jnp.where(sub == j + 1, lower, value))
+
+            diag = replaced(diag, *pivots(diag))
             for t in range(tiles):
-                rows[top, t] = jnp.where(sub == j, pivot[t], rows[top, t] - below * pivot[t])
+                upper, lower = pivots(rows[top, t])
+                rows[top, t] = replaced(rows[top, t], upper, lower)
                 for g in groups[1:]:
-                    rows[g, t] = rows[g, t] - scaled[g] * pivot[t]
-        for g in groups:
-            for t in range(tiles):
-                a_ref[g:g + GROUP, t * LANES:(t + 1) * LANES] = rows[g, t]
+                    rows[g, t] = rows[g, t] - (scaled[g][0] * upper + scaled[g][1] * lower)
         for t in range(tiles):
             span = slice(t * LANES, (t + 1) * LANES)
+            a_ref[top:top + GROUP, span] = rows[top, t]
             if t < home:
                 factor_ref[top:top + GROUP, span] = jnp.zeros((GROUP, LANES), jnp.float32)
             elif t == home:
-                factor_ref[top:top + GROUP, span] = jnp.where(lane >= sub + offset, diag / scale, 0.0)
+                factor_ref[top:top + GROUP, span] = jnp.where(lane >= sub + offset, diag, 0.0)
             else:
-                factor_ref[top:top + GROUP, span] = rows[top, t] / scale
+                factor_ref[top:top + GROUP, span] = rows[top, t]
 
 
 def trailing(a_ref, base, height, size):
@@ -85,6 +97,19 @@
     a_ref[end:, :] = jnp.where((at >= base) & (at < end), 0.0, rest) - update
 
 
+def factorize(a_ref, factor_ref):
+    size = a_ref.shape[0]
+    col = lax.broadcasted_iota(jnp.int32, (size, size), 1)
+    row = lax.broadcasted_iota(jnp.int32, (size, size), 0)
+    largest = jnp.max(jnp.where(col == row, a_ref[...], 0.0), axis=(0, 1), keepdims=True)
+    shrink = lax.rsqrt(largest)
+    a_ref[...] = a_ref[...] * shrink * shrink
+    for base in range(0, size, PANEL):
+        factor_panel(a_ref, factor_ref, base, PANEL, size)
+        trailing(a_ref, base, PANEL, size)
+    return jnp.where(col <= row, a_ref[...], 0.0) * shrink, largest * shrink
+
+
 def split(value):
     high = value.astype(jnp.bfloat16)
     return high, (value - high.astype(jnp.float32)).astype(jnp.bfloat16)
@@ -123,9 +148,11 @@
     copies[0].wait()
     sketch = split(sketch_ref[...])
     gram = None
-    for at in range(chunks):
-        span = slice(at * BLOCK, (at + 1) * BLOCK)
-        copies[1 + at].wait()
+    step = rows // 2
+    for top in range(0, rows, step):
+        span = slice(top, top + step)
+        for at in range(top // BLOCK, (top + step) // BLOCK):
+            copies[1 + at].wait()
         features = split(features_ref[span, :])
         high_ref[span, :], low_ref[span, :] = features
         sampled = product(features, sketch, 1, 0)
@@ -144,9 +171,7 @@
     flipped = flip_high_ref[...], flip_low_ref[...]
     own = own_block()
     height = rank // BLOCKS
-    for left in range(0, depth, BLOCK):
-        span = slice(left, left + BLOCK)
-        cross_ref[:, span] = product(flipped, (high_ref[:, span], low_ref[:, span]), 1, 0)
+    cross_ref[...] = product(flipped, (high_ref[...], low_ref[...]), 1, 0)
     for at in range(BLOCKS):
         block = cross_ref[rows_of(at ^ own, height), :]
         if at < BLOCKS // 2:
@@ -217,46 +242,32 @@
     return gram, outs
 
 
-def factor_kernel(scale, first, last, *refs):
-    if first == 0:
-        keep_ref, other_ref, a_ref, factor_ref, packed_ref = refs
-        half = keep_ref.shape[0]
-        core = core_bit()
-        packed_ref[rows_of(core, half), :] = keep_ref[...]
-        packed_ref[rows_of(1 - core, half), :] = other_ref[...]
-        a_ref[:LANES, :LANES] = packed_ref[:LANES, :]
-        a_ref[:LANES, LANES:] = packed_ref[LANES:2 * LANES, :]
-        a_ref[LANES:, :LANES] = jnp.zeros((LANES, LANES), jnp.float32)
-        a_ref[LANES:, LANES:] = packed_ref[2 * LANES:, :]
-    else:
-        from_ref, upper_ref, a_ref, factor_ref, *flipped_ref = refs
-        a_ref[...] = from_ref[...]
-        factor_ref[:first, :] = upper_ref[:first, :]
-    size = a_ref.shape[0]
-    for base in range(first, last, PANEL):
-        factor_panel(a_ref, factor_ref, scale, base, PANEL, size)
-        trailing(a_ref, base, PANEL, size)
-    if last == size:
-        col = lax.broadcasted_iota(jnp.int32, (size, size), 1)
-        row = lax.broadcasted_iota(jnp.int32, (size, size), 0)
-        inverse = jnp.where(col <= row, a_ref[...], 0.0)
-        a_ref[...] = inverse
-        flipped_ref[0][...] = inverse.T * scale
-
-
-def factor_part(operands, size, scale, first, last):
-    square = jax.ShapeDtypeStruct((size, size), jnp.float32)
-    outs = 3 if last == size else 2
+def factor_kernel(scale, keep_ref, other_ref, inverse_ref, flipped_ref, factor_ref, a_ref, packed_ref):
+    half = keep_ref.shape[0]
+    core = core_bit()
+    packed_ref[rows_of(core, half), :] = keep_ref[...]
+    packed_ref[rows_of(1 - core, half), :] = other_ref[...]
+    a_ref[:LANES, :LANES] = packed_ref[:LANES, :]
+    a_ref[:LANES, LANES:] = packed_ref[LANES:2 * LANES, :]
+    a_ref[LANES:, :LANES] = jnp.zeros((LANES, LANES), jnp.float32)
+    a_ref[LANES:, LANES:] = packed_ref[2 * LANES:, :]
+    inverse, grow = factorize(a_ref, factor_ref)
+    inverse_ref[...] = inverse
+    flipped_ref[...] = inverse.T * scale
+    factor_ref[...] = factor_ref[...] * (grow / scale)
+
+
+def factor(keep, other, size, scale):
     return pl.pallas_call(
-        lambda *refs: factor_kernel(scale, first, last, *refs),
-        out_shape=(square,) * outs,
+        lambda *refs: factor_kernel(scale, *refs),
+        out_shape=(f32(size, size),) * 3,
         in_specs=[VMEM] * 2,
-        out_specs=(VMEM,) * outs,
-        scratch_shapes=[pltpu.VMEM((3 * LANES, LANES), jnp.float32)] if first == 0 else [],
+        out_specs=(VMEM,) * 3,
+        scratch_shapes=[pltpu.VMEM((size, size), jnp.float32), pltpu.VMEM((3 * LANES, LANES), jnp.float32)],
         compiler_params=pltpu.CompilerParams(vmem_limit_bytes=16 * 2**20),
-        cost_estimate=pl.CostEstimate(flops=12 * 10**9 * (last - first) // size, bytes_accessed=2**20, transcendentals=last - first),
-        name="factor_part",
-    )(*operands)
+        cost_estimate=pl.CostEstimate(flops=10 * 10**9, bytes_accessed=2**20, transcendentals=size),
+        name="factor",
+    )(keep, other)
 
 
 def basis_kernel(sampled_ref, flipped_ref, basis_ref):
@@ -344,7 +355,7 @@
     line = [own] + [send(own, *mask) for mask in LINE]
     gram, (line,) = stage(line, gram, send(gram, *PLANE[1]), 1, join=True)
     plane = [line] + [send(line, *mask) for mask in PLANE]
-    factors = factors((gram, send(gram, *CORE)))
+    factors = factors(gram, send(gram, *CORE))
     return plane + [send(part, *CORE) for part in plane], factors
 
 
@@ -352,14 +363,9 @@
     scale = (features.shape[0] * lax.axis_size(AXES)) ** 0.5
     size = sketch.shape[1]
 
-    def factors(state):
-        for first in range(0, size, PANEL):
-            state = factor_part(state[:2], size, scale, first, first + PANEL)
-        return state
-
     sampled, *terms = local_terms(features, sketch)
-    cross, (inverse, factor, flipped) = sums_and_factors(*terms, factors)
-    return (basis_of(sampled, flipped), factor, project(inverse, cross))
+    cross, (inverse, flipped, upper) = sums_and_factors(*terms, lambda *halves: factor(*halves, size, scale))
+    return (basis_of(sampled, flipped), upper, project(inverse, cross))
 
 
 def solution(mesh):

time: 61.7 us -> 62.1 us (level)
    pallas_call x4 -> x1, Pallas kernels: 9.41 us -> 9.39 us  [factor(): pl.pallas_call(lambda *refs: factor_kernel(scale, *refs), out_shape=(f32(...]
where the time goes in v8:
time: 62.1 us; the launch traced here: 62 us
  starting transfers between devices  26.2 us (42%)
  Pallas kernels  21.5 us (35%)
  waiting for transfers between devices  13.6 us (22%)
  between operations  0.7 us (1%)
    ppermute x23, starting transfers between devices, send(): return lax.ppermute(value, AXES, pairs)  26.2 us
    ppermute x23, waiting for transfers between devices, send(): return lax.ppermute(value, AXES, pairs)  13.6 us
    pallas_call x1, Pallas kernels, factor(): pl.pallas_call(lambda *refs: factor_kernel(scale, *refs), out_shape=(f32(...  9.39 us
    pallas_call x1, Pallas kernels, local_terms(): pl.pallas_call(local_kernel, out_shape=(f32(rows, rank), f32(rank // 2, d...  8.77 us
    pallas_call x1, Pallas kernels, project(): pl.pallas_call(project_kernel, out_shape=jax.ShapeDtypeStruct((rank, dept...  1.66 us
    pallas_call x1, Pallas kernels, basis_of(): pl.pallas_call(basis_kernel, out_shape=f32(*sampled.shape), in_specs=[VME...  1.55 us
  transfers between devices with their start and end apart: 23, of which 8 were waited for; matrix products, arithmetic and copies ran while one was open for 0% of the time, Pallas kernels for 18%

profile of v8, /device:TPU:0, one launch (start us, length us, event | category | flops | bytes accessed | tf_op | source)
XLA Modules:
  0.0 62.0 jit_solution(1385624033122398180)
XLA Ops:
  0.6 8.8 %local_terms.1 = (f32[1024,256]{1,0:T(8,128)S(1)}, f32[128,1024]{1,0:T(8,128)S(1)}, f32[128,1024]{1,0:T(8,128)S(1)}, f32[192,128]{1,0:T(8,128)S(1)}, f32[192,128]{1,0:T(8,128)S(1)}) custom-call(f32[1024,1024]{1,0:T(8,128)} %features_hbm.1, f32[1024,256]{1,0:T(8,128)} %sketch_hbm.1), custom_call_target="tpu_custom_call" | custom-call | flops 4000000000 | bytes 8388608 | tf_op jit(solution)/shard_map/local_terms/pallas_call | solution.py:193
  9.4 0.5 collective-permute-start
  9.9 0.1 collective-permute-start.1
  10.0 1.6 %collective-permute-done.1.refs_3_ = f32[192,128]{1,0:T(8,128)S(1)} collective-permute-done((f32[192,128]{1,0:T(8,128)S(1)}, f32[192,128]{1,0:T(8,128)S(1)}, u32[]{:S(2)}, u32[]{:S(2)}) %collective-permute-start.1) | collective-permute-done | bytes 98336 | tf_op jit(solution)/shard_map/ppermute | solution.py:325
  11.6 0.0 collective-permute-done.refs_1_
  11.6 0.1 stage.3
  11.7 3.0 %collective-permute-start.5 = (f32[192,128]{1,0:T(8,128)S(1)}, f32[192,128]{1,0:T(8,128)S(1)}, u32[]{:S(2)}, u32[]{:S(2)}) collective-permute-start(f32[192,128]{1,0:T(8,128)S(1)} %get-tuple-element.34), channel_id=1, source_target_pairs={{0,8},{1,9},{2,10},{3,11},{4,12},{5,13},{6,14},{7,15},{8,0},{9,1},... | collective-permute-start | bytes 294920 | tf_op jit(solution)/shard_map/ppermute | solution.py:325
  14.7 1.5 %collective-permute-start.2 = (f32[32,1024]{1,0:T(8,128)S(1)}, f32[32,1024]{1,0:T(8,128)S(1)}, u32[]{:S(2)}, u32[]{:S(2)}) collective-permute-start(f32[32,1024]{1,0:T(8,128)S(1)} %get-tuple-element.31), channel_id=1, source_target_pairs={{0,1},{1,0},{2,3},{3,2},{4,5},{5,4},{6,7},{7,6},{8,9},{9,8},{10,11... | collective-permute-start | bytes 393224 | tf_op jit(solution)/shard_map/ppermute | solution.py:325
  16.2 1.5 %collective-permute-start.3 = (f32[32,1024]{1,0:T(8,128)S(1)}, f32[32,1024]{1,0:T(8,128)S(1)}, u32[]{:S(2)}, u32[]{:S(2)}) collective-permute-start(f32[32,1024]{1,0:T(8,128)S(1)} %get-tuple-element.32), channel_id=1, source_target_pairs={{0,4},{1,5},{2,6},{3,7},{4,0},{5,1},{6,2},{7,3},{8,12},{9,13},{10,... | collective-permute-start | bytes 393224 | tf_op jit(solution)/shard_map/ppermute | solution.py:325
  17.7 0.5 collective-permute-start.4
  18.2 0.0 collective-permute-done.5
  18.2 2.7 %collective-permute-start.6 = (f32[192,128]{1,0:T(8,128)S(1)}, f32[192,128]{1,0:T(8,128)S(1)}, u32[]{:S(2)}, u32[]{:S(2)}) collective-permute-start(f32[192,128]{1,0:T(8,128)S(1)} %add.3.refs_4_), channel_id=1, source_target_pairs={{0,16},{1,17},{2,18},{3,19},{4,20},{5,21},{6,22},{7,23},{8,24},{9,... | collective-permute-start | bytes 294920 | tf_op jit(solution)/shard_map/ppermute | solution.py:325
  20.8 0.0 collective-permute-done.2.refs_1_
  20.9 1.7 %collective-permute-done.3.refs_2_ = f32[32,1024]{1,0:T(8,128)S(1)} collective-permute-done((f32[32,1024]{1,0:T(8,128)S(1)}, f32[32,1024]{1,0:T(8,128)S(1)}, u32[]{:S(2)}, u32[]{:S(2)}) %collective-permute-start.3) | collective-permute-done | bytes 131104 | tf_op jit(solution)/shard_map/ppermute | solution.py:325
  22.6 1.3 %collective-permute-done.4.refs_3_ = f32[32,1024]{1,0:T(8,128)S(1)} collective-permute-done((f32[32,1024]{1,0:T(8,128)S(1)}, f32[32,1024]{1,0:T(8,128)S(1)}, u32[]{:S(2)}, u32[]{:S(2)}) %collective-permute-start.4) | collective-permute-done | bytes 131104 | tf_op jit(solution)/shard_map/ppermute | solution.py:325
  23.9 1.3 %collective-permute-done.6.refs_5_ = f32[192,128]{1,0:T(8,128)S(1)} collective-permute-done((f32[192,128]{1,0:T(8,128)S(1)}, f32[192,128]{1,0:T(8,128)S(1)}, u32[]{:S(2)}, u32[]{:S(2)}) %collective-permute-start.6) | collective-permute-done | bytes 98336 | tf_op jit(solution)/shard_map/ppermute | solution.py:325
  25.2 1.4 %collective-permute-start.10 = (f32[192,128]{1,0:T(8,128)S(1)}, f32[192,128]{1,0:T(8,128)S(1)}, u32[]{:S(2)}, u32[]{:S(2)}) collective-permute-start(f32[192,128]{1,0:T(8,128)S(1)} %get-tuple-element.39.refs_4_), channel_id=1, source_target_pairs={{0,1},{1,0},{2,3},{3,2},{4,5},{5,4},{6,7},{7,6},{8,9},{9,8},{10,11... | collective-permute-start | bytes 294920 | tf_op jit(solution)/shard_map/ppermute | solution.py:325
  26.7 0.7 %collective-permute-start.7 = (f32[8,1024]{1,0:T(8,128)S(1)}, f32[8,1024]{1,0:T(8,128)S(1)}, u32[]{:S(2)}, u32[]{:S(2)}) collective-permute-start(f32[8,1024]{1,0:T(8,128)S(1)} %get-tuple-element.36), channel_id=1, source_target_pairs={{0,8},{1,9},{2,10},{3,11},{4,12},{5,13},{6,14},{7,15},{8,0},{9,1},... | collective-permute-start | bytes 98312 | tf_op jit(solution)/shard_map/ppermute | solution.py:325
  27.3 3.4 %collective-permute-start.8 = (f32[8,1024]{1,0:T(8,128)S(1)}, f32[8,1024]{1,0:T(8,128)S(1)}, u32[]{:S(2)}, u32[]{:S(2)}) collective-permute-start(f32[8,1024]{1,0:T(8,128)S(1)} %get-tuple-element.37), channel_id=1, source_target_pairs={{0,16},{1,17},{2,18},{3,19},{4,20},{5,21},{6,22},{7,23},{8,24},{9,... | collective-permute-start | bytes 98312 | tf_op jit(solution)/shard_map/ppermute | solution.py:325
  30.7 0.3 collective-permute-start.9
  31.1 0.0 collective-permute-done.7.refs_1_
  31.1 1.5 %collective-permute-done.8.refs_2_ = f32[8,1024]{1,0:T(8,128)S(1)} collective-permute-done((f32[8,1024]{1,0:T(8,128)S(1)}, f32[8,1024]{1,0:T(8,128)S(1)}, u32[]{:S(2)}, u32[]{:S(2)}) %collective-permute-start.8) | collective-permute-done | bytes 32800 | tf_op jit(solution)/shard_map/ppermute | solution.py:325
  32.6 3.8 %collective-permute-done.9.refs_3_ = f32[8,1024]{1,0:T(8,128)S(1)} collective-permute-done((f32[8,1024]{1,0:T(8,128)S(1)}, f32[8,1024]{1,0:T(8,128)S(1)}, u32[]{:S(2)}, u32[]{:S(2)}) %collective-permute-start.9) | collective-permute-done | bytes 32800 | tf_op jit(solution)/shard_map/ppermute | solution.py:325
  36.4 0.0 collective-permute-done.10.refs_5_
  36.5 1.6 %collective-permute-start.14 = (f32[192,128]{1,0:T(8,128)S(1)}, f32[192,128]{1,0:T(8,128)S(1)}, u32[]{:S(2)}, u32[]{:S(2)}) collective-permute-start(f32[192,128]{1,0:T(8,128)S(1)} %get-tuple-element.41.refs_4_), channel_id=1, source_target_pairs={{0,4},{1,5},{2,6},{3,7},{4,0},{5,1},{6,2},{7,3},{8,12},{9,13},{10,... | collective-permute-start | bytes 294920 | tf_op jit(solution)/shard_map/ppermute | solution.py:325
  38.0 0.0 collective-permute-start.11
  38.0 0.9 %collective-permute-start.12 = (f32[8,1024]{1,0:T(8,128)S(1)}, f32[8,1024]{1,0:T(8,128)S(1)}, u32[]{:S(2)}, u32[]{:S(2)}) collective-permute-start(f32[8,1024]{1,0:T(8,128)S(1)} %get-tuple-element.40.refs_0_), channel_id=1, source_target_pairs={{0,16},{1,17},{2,18},{3,19},{4,20},{5,21},{6,22},{7,23},{8,24},{9,... | collective-permute-start | bytes 98312 | tf_op jit(solution)/shard_map/ppermute | solution.py:325
  38.9 3.5 %collective-permute-start.13 = (f32[8,1024]{1,0:T(8,128)S(1)}, f32[8,1024]{1,0:T(8,128)S(1)}, u32[]{:S(2)}, u32[]{:S(2)}) collective-permute-start(f32[8,1024]{1,0:T(8,128)S(1)} %get-tuple-element.40.refs_0_), channel_id=1, source_target_pairs={{0,24},{1,25},{2,26},{3,27},{4,28},{5,29},{6,30},{7,31},{8,16},{9,... | collective-permute-start | bytes 98312 | tf_op jit(solution)/shard_map/ppermute | solution.py:325
  42.4 0.0 collective-permute-done.11.refs_1_
  42.4 0.4 collective-permute-done.12.refs_2_
  42.8 1.8 %collective-permute-done.13.refs_3_ = f32[8,1024]{1,0:T(8,128)S(1)} collective-permute-done((f32[8,1024]{1,0:T(8,128)S(1)}, f32[8,1024]{1,0:T(8,128)S(1)}, u32[]{:S(2)}, u32[]{:S(2)}) %collective-permute-start.13) | collective-permute-done | bytes 32800 | tf_op jit(solution)/shard_map/ppermute | solution.py:325
  44.6 0.0 collective-permute-done.14.refs_5_
  44.7 0.1 collective-permute-start.15
  44.8 0.6 collective-permute-start.16
  45.3 0.7 %collective-permute-start.17 = (f32[32,1024]{1,0:T(8,128)S(1)}, f32[32,1024]{1,0:T(8,128)S(1)}, u32[]{:S(2)}, u32[]{:S(2)}) collective-permute-start(f32[32,1024]{1,0:T(8,128)S(1)} %get-tuple-element.46.refs_0_), channel_id=1, source_target_pairs={{0,4},{1,5},{2,6},{3,7},{4,0},{5,1},{6,2},{7,3},{8,12},{9,13},{10,... | collective-permute-start | bytes 393224 | tf_op jit(solution)/shard_map/ppermute | solution.py:325
  46.0 2.3 %collective-permute-start.18 = (f32[32,1024]{1,0:T(8,128)S(1)}, f32[32,1024]{1,0:T(8,128)S(1)}, u32[]{:S(2)}, u32[]{:S(2)}) collective-permute-start(f32[32,1024]{1,0:T(8,128)S(1)} %get-tuple-element.46.refs_0_), channel_id=1, source_target_pairs={{0,5},{1,4},{2,7},{3,6},{4,1},{5,0},{6,3},{7,2},{8,13},{9,12},{10,... | collective-permute-start | bytes 393224 | tf_op jit(solution)/shard_map/ppermute | solution.py:325
  48.3 0.0 collective-permute-start.19
  48.3 0.0 collective-permute-done.15.refs_1_
  48.3 9.4 %factor.1 = (f32[256,256]{1,0:T(8,128)S(1)}, f32[256,256]{1,0:T(8,128)S(1)}, f32[256,256]{1,0:T(8,128)}) custom-call(f32[192,128]{1,0:T(8,128)S(1)} %get-tuple-element.42.refs_0_, f32[192,128]{1,0:T(8,128)S(1)} %collective-permute-done.15.refs_1_), custom_call_target="tpu_custom_call" | custom-call | flops 10000000000 | bytes 1048576 | tf_op jit(solution)/shard_map/factor/pallas_call | solution.py:261
  57.7 0.0 collective-permute-done.16.refs_1_
  57.7 0.5 collective-permute-start.20
  58.2 0.0 collective-permute-done.17.refs_2_
  58.2 0.1 collective-permute-start.21
  58.3 0.0 collective-permute-done.18.refs_3_
  58.3 0.4 collective-permute-start.22
  58.7 1.6 %basis.1 = f32[1024,256]{1,0:T(8,128)} custom-call(f32[1024,256]{1,0:T(8,128)S(1)} %get-tuple-element.25.sampled_ref, f32[256,256]{1,0:T(8,128)S(1)} %get-tuple-element.43.flipped_ref), custom_call_target="tpu_custom_call" | custom-call | flops 2000000000 | bytes 2097152 | tf_op jit(solution)/shard_map/basis/pallas_call | solution.py:281
  60.3 0.0 collective-permute-done.19.refs_4_
  60.3 0.0 collective-permute-done.20.refs_5_
  60.3 0.0 collective-permute-done.21.refs_6_
  60.3 0.0 collective-permute-done.22.refs_7_
  60.3 1.7 %project.1 = f32[256,1024]{1,0:T(8,128)} custom-call(f32[256,256]{1,0:T(8,128)S(1)} %get-tuple-element.45.inverse_ref, f32[32,1024]{1,0:T(8,128)S(1)} %get-tuple-element.46.refs_0_, f32[32,1024]{1,0:T(8,128)S(1)} %collective-permute-done.16.refs_1_, f32[32,1024]{1,0:T(8,128)S(1)} %collective-permute-done.17.refs_2_, ...), custom_call_target="tpu_custom_call" | custom-call | flops 400000000 | bytes 2097152 | tf_op jit(solution)/shard_map/project/pallas_call | solution.py:310
  (4 shorter events, 0.1 us)
Async XLA Ops:
  9.4 2.2 %collective-permute-start = (f32[128,1024]{1,0:T(8,128)S(1)}, f32[128,1024]{1,0:T(8,128)S(1)}, u32[]{:S(2)}, u32[]{:S(2)}) collective-permute-start(f32[128,1024]{1,0:T(8,128)S(1)} %get-tuple-element.27), channel_id=1, source_target_pairs={{0,2},{1,3},{2,0},{3,1},{4,6},{5,7},{6,4},{7,5},{8,10},{9,11},{10,... | collective-permute-start | bytes 1572872 | tf_op jit(solution)/shard_map/ppermute | solution.py:325
  9.9 1.7 %collective-permute-start.1 = (f32[192,128]{1,0:T(8,128)S(1)}, f32[192,128]{1,0:T(8,128)S(1)}, u32[]{:S(2)}, u32[]{:S(2)}) collective-permute-start(f32[192,128]{1,0:T(8,128)S(1)} %get-tuple-element.29), channel_id=1, source_target_pairs={{0,2},{1,3},{2,0},{3,1},{4,6},{5,7},{6,4},{7,5},{8,10},{9,11},{10,... | collective-permute-start | bytes 294920 | tf_op jit(solution)/shard_map/ppermute | solution.py:325
  11.7 6.5 %collective-permute-start.5 = (f32[192,128]{1,0:T(8,128)S(1)}, f32[192,128]{1,0:T(8,128)S(1)}, u32[]{:S(2)}, u32[]{:S(2)}) collective-permute-start(f32[192,128]{1,0:T(8,128)S(1)} %get-tuple-element.34), channel_id=1, source_target_pairs={{0,8},{1,9},{2,10},{3,11},{4,12},{5,13},{6,14},{7,15},{8,0},{9,1},... | collective-permute-start | bytes 294920 | tf_op jit(solution)/shard_map/ppermute | solution.py:325
  14.7 6.2 %collective-permute-start.2 = (f32[32,1024]{1,0:T(8,128)S(1)}, f32[32,1024]{1,0:T(8,128)S(1)}, u32[]{:S(2)}, u32[]{:S(2)}) collective-permute-start(f32[32,1024]{1,0:T(8,128)S(1)} %get-tuple-element.31), channel_id=1, source_target_pairs={{0,1},{1,0},{2,3},{3,2},{4,5},{5,4},{6,7},{7,6},{8,9},{9,8},{10,11... | collective-permute-start | bytes 393224 | tf_op jit(solution)/shard_map/ppermute | solution.py:325
  16.2 6.4 %collective-permute-start.3 = (f32[32,1024]{1,0:T(8,128)S(1)}, f32[32,1024]{1,0:T(8,128)S(1)}, u32[]{:S(2)}, u32[]{:S(2)}) collective-permute-start(f32[32,1024]{1,0:T(8,128)S(1)} %get-tuple-element.32), channel_id=1, source_target_pairs={{0,4},{1,5},{2,6},{3,7},{4,0},{5,1},{6,2},{7,3},{8,12},{9,13},{10,... | collective-permute-start | bytes 393224 | tf_op jit(solution)/shard_map/ppermute | solution.py:325
  17.7 6.2 %collective-permute-start.4 = (f32[32,1024]{1,0:T(8,128)S(1)}, f32[32,1024]{1,0:T(8,128)S(1)}, u32[]{:S(2)}, u32[]{:S(2)}) collective-permute-start(f32[32,1024]{1,0:T(8,128)S(1)} %get-tuple-element.33), channel_id=1, source_target_pairs={{0,5},{1,4},{2,7},{3,6},{4,1},{5,0},{6,3},{7,2},{8,13},{9,12},{10,... | collective-permute-start | bytes 393224 | tf_op jit(solution)/shard_map/ppermute | solution.py:325
  18.2 7.0 %collective-permute-start.6 = (f32[192,128]{1,0:T(8,128)S(1)}, f32[192,128]{1,0:T(8,128)S(1)}, u32[]{:S(2)}, u32[]{:S(2)}) collective-permute-start(f32[192,128]{1,0:T(8,128)S(1)} %add.3.refs_4_), channel_id=1, source_target_pairs={{0,16},{1,17},{2,18},{3,19},{4,20},{5,21},{6,22},{7,23},{8,24},{9,... | collective-permute-start | bytes 294920 | tf_op jit(solution)/shard_map/ppermute | solution.py:325
  25.2 11.2 %collective-permute-start.10 = (f32[192,128]{1,0:T(8,128)S(1)}, f32[192,128]{1,0:T(8,128)S(1)}, u32[]{:S(2)}, u32[]{:S(2)}) collective-permute-start(f32[192,128]{1,0:T(8,128)S(1)} %get-tuple-element.39.refs_4_), channel_id=1, source_target_pairs={{0,1},{1,0},{2,3},{3,2},{4,5},{5,4},{6,7},{7,6},{8,9},{9,8},{10,11... | collective-permute-start | bytes 294920 | tf_op jit(solution)/shard_map/ppermute | solution.py:325
  26.7 4.4 %collective-permute-start.7 = (f32[8,1024]{1,0:T(8,128)S(1)}, f32[8,1024]{1,0:T(8,128)S(1)}, u32[]{:S(2)}, u32[]{:S(2)}) collective-permute-start(f32[8,1024]{1,0:T(8,128)S(1)} %get-tuple-element.36), channel_id=1, source_target_pairs={{0,8},{1,9},{2,10},{3,11},{4,12},{5,13},{6,14},{7,15},{8,0},{9,1},... | collective-permute-start | bytes 98312 | tf_op jit(solution)/shard_map/ppermute | solution.py:325
  27.3 5.3 %collective-permute-start.8 = (f32[8,1024]{1,0:T(8,128)S(1)}, f32[8,1024]{1,0:T(8,128)S(1)}, u32[]{:S(2)}, u32[]{:S(2)}) collective-permute-start(f32[8,1024]{1,0:T(8,128)S(1)} %get-tuple-element.37), channel_id=1, source_target_pairs={{0,16},{1,17},{2,18},{3,19},{4,20},{5,21},{6,22},{7,23},{8,24},{9,... | collective-permute-start | bytes 98312 | tf_op jit(solution)/shard_map/ppermute | solution.py:325
  30.7 5.7 %collective-permute-start.9 = (f32[8,1024]{1,0:T(8,128)S(1)}, f32[8,1024]{1,0:T(8,128)S(1)}, u32[]{:S(2)}, u32[]{:S(2)}) collective-permute-start(f32[8,1024]{1,0:T(8,128)S(1)} %get-tuple-element.38), channel_id=1, source_target_pairs={{0,24},{1,25},{2,26},{3,27},{4,28},{5,29},{6,30},{7,31},{8,16},{9,... | collective-permute-start | bytes 98312 | tf_op jit(solution)/shard_map/ppermute | solution.py:325
  36.5 8.2 %collective-permute-start.14 = (f32[192,128]{1,0:T(8,128)S(1)}, f32[192,128]{1,0:T(8,128)S(1)}, u32[]{:S(2)}, u32[]{:S(2)}) collective-permute-start(f32[192,128]{1,0:T(8,128)S(1)} %get-tuple-element.41.refs_4_), channel_id=1, source_target_pairs={{0,4},{1,5},{2,6},{3,7},{4,0},{5,1},{6,2},{7,3},{8,12},{9,13},{10,... | collective-permute-start | bytes 294920 | tf_op jit(solution)/shard_map/ppermute | solution.py:325
  38.0 4.4 %collective-permute-start.11 = (f32[8,1024]{1,0:T(8,128)S(1)}, f32[8,1024]{1,0:T(8,128)S(1)}, u32[]{:S(2)}, u32[]{:S(2)}) collective-permute-start(f32[8,1024]{1,0:T(8,128)S(1)} %get-tuple-element.40.refs_0_), channel_id=1, source_target_pairs={{0,8},{1,9},{2,10},{3,11},{4,12},{5,13},{6,14},{7,15},{8,0},{9,1},... | collective-permute-start | bytes 98312 | tf_op jit(solution)/shard_map/ppermute | solution.py:325
  38.0 4.8 %collective-permute-start.12 = (f32[8,1024]{1,0:T(8,128)S(1)}, f32[8,1024]{1,0:T(8,128)S(1)}, u32[]{:S(2)}, u32[]{:S(2)}) collective-permute-start(f32[8,1024]{1,0:T(8,128)S(1)} %get-tuple-element.40.refs_0_), channel_id=1, source_target_pairs={{0,16},{1,17},{2,18},{3,19},{4,20},{5,21},{6,22},{7,23},{8,24},{9,... | collective-permute-start | bytes 98312 | tf_op jit(solution)/shard_map/ppermute | solution.py:325
  38.9 5.7 %collective-permute-start.13 = (f32[8,1024]{1,0:T(8,128)S(1)}, f32[8,1024]{1,0:T(8,128)S(1)}, u32[]{:S(2)}, u32[]{:S(2)}) collective-permute-start(f32[8,1024]{1,0:T(8,128)S(1)} %get-tuple-element.40.refs_0_), channel_id=1, source_target_pairs={{0,24},{1,25},{2,26},{3,27},{4,28},{5,29},{6,30},{7,31},{8,16},{9,... | collective-permute-start | bytes 98312 | tf_op jit(solution)/shard_map/ppermute | solution.py:325
  44.7 3.6 %collective-permute-start.15 = (f32[192,128]{1,0:T(8,128)S(1)}, f32[192,128]{1,0:T(8,128)S(1)}, u32[]{:S(2)}, u32[]{:S(2)}) collective-permute-start(f32[192,128]{1,0:T(8,128)S(1)} %get-tuple-element.42.refs_0_), channel_id=1, source_target_pairs={{0,2},{1,3},{2,0},{3,1},{4,6},{5,7},{6,4},{7,5},{8,10},{9,11},{10,... | collective-permute-start | bytes 294920 | tf_op jit(solution)/shard_map/ppermute | solution.py:325
  44.8 13.0 %collective-permute-start.16 = (f32[32,1024]{1,0:T(8,128)S(1)}, f32[32,1024]{1,0:T(8,128)S(1)}, u32[]{:S(2)}, u32[]{:S(2)}) collective-permute-start(f32[32,1024]{1,0:T(8,128)S(1)} %get-tuple-element.46.refs_0_), channel_id=1, source_target_pairs={{0,1},{1,0},{2,3},{3,2},{4,5},{5,4},{6,7},{7,6},{8,9},{9,8},{10,11... | collective-permute-start | bytes 393224 | tf_op jit(solution)/shard_map/ppermute | solution.py:325
  45.3 12.9 %collective-permute-start.17 = (f32[32,1024]{1,0:T(8,128)S(1)}, f32[32,1024]{1,0:T(8,128)S(1)}, u32[]{:S(2)}, u32[]{:S(2)}) collective-permute-start(f32[32,1024]{1,0:T(8,128)S(1)} %get-tuple-element.46.refs_0_), channel_id=1, source_target_pairs={{0,4},{1,5},{2,6},{3,7},{4,0},{5,1},{6,2},{7,3},{8,12},{9,13},{10,... | collective-permute-start | bytes 393224 | tf_op jit(solution)/shard_map/ppermute | solution.py:325
  46.0 12.3 %collective-permute-start.18 = (f32[32,1024]{1,0:T(8,128)S(1)}, f32[32,1024]{1,0:T(8,128)S(1)}, u32[]{:S(2)}, u32[]{:S(2)}) collective-permute-start(f32[32,1024]{1,0:T(8,128)S(1)} %get-tuple-element.46.refs_0_), channel_id=1, source_target_pairs={{0,5},{1,4},{2,7},{3,6},{4,1},{5,0},{6,3},{7,2},{8,13},{9,12},{10,... | collective-permute-start | bytes 393224 | tf_op jit(solution)/shard_map/ppermute | solution.py:325
  48.3 12.0 %collective-permute-start.19 = (f32[32,1024]{1,0:T(8,128)S(1)}, f32[32,1024]{1,0:T(8,128)S(1)}, u32[]{:S(2)}, u32[]{:S(2)}) collective-permute-start(f32[32,1024]{1,0:T(8,128)S(1)} %get-tuple-element.46.refs_0_), channel_id=1, source_target_pairs={{0,2},{1,3},{2,0},{3,1},{4,6},{5,7},{6,4},{7,5},{8,10},{9,11},{10,... | collective-permute-start | bytes 393224 | tf_op jit(solution)/shard_map/ppermute | solution.py:325
  57.7 2.6 %collective-permute-start.20 = (f32[32,1024]{1,0:T(8,128)S(1)}, f32[32,1024]{1,0:T(8,128)S(1)}, u32[]{:S(2)}, u32[]{:S(2)}) collective-permute-start(f32[32,1024]{1,0:T(8,128)S(1)} %collective-permute-done.16.refs_1_), channel_id=1, source_target_pairs={{0,2},{1,3},{2,0},{3,1},{4,6},{5,7},{6,4},{7,5},{8,10},{9,11},{10,... | collective-permute-start | bytes 393224 | tf_op jit(solution)/shard_map/ppermute | solution.py:325
  58.2 2.1 %collective-permute-start.21 = (f32[32,1024]{1,0:T(8,128)S(1)}, f32[32,1024]{1,0:T(8,128)S(1)}, u32[]{:S(2)}, u32[]{:S(2)}) collective-permute-start(f32[32,1024]{1,0:T(8,128)S(1)} %collective-permute-done.17.refs_2_), channel_id=1, source_target_pairs={{0,2},{1,3},{2,0},{3,1},{4,6},{5,7},{6,4},{7,5},{8,10},{9,11},{10,... | collective-permute-start | bytes 393224 | tf_op jit(solution)/shard_map/ppermute | solution.py:325
  58.3 2.0 %collective-permute-start.22 = (f32[32,1024]{1,0:T(8,128)S(1)}, f32[32,1024]{1,0:T(8,128)S(1)}, u32[]{:S(2)}, u32[]{:S(2)}) collective-permute-start(f32[32,1024]{1,0:T(8,128)S(1)} %collective-permute-done.18.refs_3_), channel_id=1, source_target_pairs={{0,2},{1,3},{2,0},{3,1},{4,6},{5,7},{6,4},{7,5},{8,10},{9,11},{10,... | collective-permute-start | bytes 393224 | tf_op jit(solution)/shard_map/ppermute | solution.py:325

commit v9 on v8

--- a/solution.py
+++ b/solution.py
@@ -13,11 +13,18 @@
 VMEM = pl.BlockSpec(memory_space=pltpu.VMEM)
 
 
-def factor_panel(a_ref, factor_ref, base, height, size):
+def factor_panel(a_ref, factor_ref, buffer_ref, base, height, size):
     lane = lax.broadcasted_iota(jnp.int32, (GROUP, LANES), 1)
     sub = lax.broadcasted_iota(jnp.int32, (GROUP, LANES), 0)
     tiles = size // LANES
     spread = lambda value: jnp.broadcast_to(value, (GROUP, LANES))
+
+    def spread_row(slot, k):
+        return spread(buffer_ref[slot * GROUP + k:slot * GROUP + k + 1, :])
+
+    def keep(value, slot):
+        buffer_ref[slot * GROUP:(slot + 1) * GROUP, :] = value
+
     rows = {}
     for g in range(base, base + height, GROUP):
         for t in range(tiles):
@@ -28,12 +35,14 @@
         offset = top - home * LANES
         inside = (lane >= offset) & (lane < offset + GROUP)
         diag = rows[top, home]
+        bank = top // GROUP % 2 * 20
         col, one = {}, {}
         for j in range(GROUP):
             for g in groups:
                 col[g, j] = spread(rows[g, home][:, offset + j:offset + j + 1])
+            keep(col[top, j], bank + j)
             for k in range(j, GROUP):
-                one[k, j] = spread(col[top, j][k:k + 1, :])
+                one[k, j] = spread_row(bank + j, k)
         for g in groups:
             fresh = jnp.where(lane == sub + offset, 1.0, 0.0) if g == top else 0.0
             rows[g, home] = jnp.where(inside, fresh, rows[g, home])
@@ -57,17 +66,19 @@
                     col[g, k] = col[g, k] - (scaled[g][0] * low[k][0] + scaled[g][1] * low[k][1])
             below = [jnp.where(sub > j + 1, part, 0.0) for part in scaled[top]]
 
-            def pivots(value):
-                upper = spread(value[j:j + 1, :]) * first
-                return upper, (spread(value[j + 1:j + 2, :]) - cross * upper) * second
+            def pivots(value, slot):
+                slot = bank + GROUP + 3 * (j // 2) + slot
+                keep(value, slot)
+                upper = spread_row(slot, j) * first
+                return upper, (spread_row(slot, j + 1) - cross * upper) * second
 
             def replaced(value, upper, lower):
                 value = value - (below[0] * upper + below[1] * lower)
                 return jnp.where(sub == j, upper, jnp.where(sub == j + 1, lower, value))
 
-            diag = replaced(diag, *pivots(diag))
+            diag = replaced(diag, *pivots(diag, 2))
             for t in range(tiles):
-                upper, lower = pivots(rows[top, t])
+                upper, lower = pivots(rows[top, t], t)
                 rows[top, t] = replaced(rows[top, t], upper, lower)
                 for g in groups[1:]:
                     rows[g, t] = rows[g, t] - (scaled[g][0] * upper + scaled[g][1] * lower)
@@ -97,7 +108,7 @@
     a_ref[end:, :] = jnp.where((at >= base) & (at < end), 0.0, rest) - update
 
 
-def factorize(a_ref, factor_ref):
+def factorize(a_ref, factor_ref, buffer_ref):
     size = a_ref.shape[0]
     col = lax.broadcasted_iota(jnp.int32, (size, size), 1)
     row = lax.broadcasted_iota(jnp.int32, (size, size), 0)
@@ -105,7 +116,7 @@
     shrink = lax.rsqrt(largest)
     a_ref[...] = a_ref[...] * shrink * shrink
     for base in range(0, size, PANEL):
-        factor_panel(a_ref, factor_ref, base, PANEL, size)
+        factor_panel(a_ref, factor_ref, buffer_ref, base, PANEL, size)
         trailing(a_ref, base, PANEL, size)
     return jnp.where(col <= row, a_ref[...], 0.0) * shrink, largest * shrink
 
@@ -135,7 +146,7 @@
     return pl.ds(pl.multiple_of(block * height, GROUP), height)
 
 
-def local_kernel(features_hbm, sketch_hbm, sampled_ref, keep_ref, send_ref, gram_keep_ref, gram_send_ref, features_ref, sketch_ref, high_ref, low_ref, flip_high_ref, flip_low_ref, cross_ref, packed_ref, sems):
+def local_kernel(features_hbm, sketch_hbm, sampled_ref, keep_ref, send_ref, gram_keep_ref, gram_send_ref, features_ref, sketch_ref, cross_ref, packed_ref, sems):
     rows, depth = features_ref.shape
     rank = sketch_ref.shape[1]
     chunks = rows // BLOCK
@@ -148,19 +159,19 @@
     copies[0].wait()
     sketch = split(sketch_ref[...])
     gram = None
-    step = rows // 2
-    for top in range(0, rows, step):
-        span = slice(top, top + step)
-        for at in range(top // BLOCK, (top + step) // BLOCK):
-            copies[1 + at].wait()
+    for at in range(chunks):
+        span = slice(at * BLOCK, (at + 1) * BLOCK)
+        copies[1 + at].wait()
         features = split(features_ref[span, :])
-        high_ref[span, :], low_ref[span, :] = features
         sampled = product(features, sketch, 1, 0)
         sampled_ref[span, :] = sampled
         flipped = split(sampled.T)
-        flip_high_ref[:, span], flip_low_ref[:, span] = flipped
         term = product(flipped, split(sampled), 1, 0)
         gram = term if gram is None else gram + term
+        for left in range(0, depth, BLOCK):
+            columns = slice(left, left + BLOCK)
+            term = product(flipped, [part[:, columns] for part in features], 1, 0)
+            cross_ref[:, columns] = term if at == 0 else cross_ref[:, columns] + term
     packed_ref[:LANES, :] = gram[:LANES, :LANES]
     packed_ref[LANES:2 * LANES, :] = gram[:LANES, LANES:]
     packed_ref[2 * LANES:, :] = gram[LANES:, LANES:]
@@ -168,10 +179,8 @@
     core = core_bit()
     gram_keep_ref[...] = packed_ref[rows_of(core, half), :]
     gram_send_ref[...] = packed_ref[rows_of(1 - core, half), :]
-    flipped = flip_high_ref[...], flip_low_ref[...]
     own = own_block()
     height = rank // BLOCKS
-    cross_ref[...] = product(flipped, (high_ref[...], low_ref[...]), 1, 0)
     for at in range(BLOCKS):
         block = cross_ref[rows_of(at ^ own, height), :]
         if at < BLOCKS // 2:
@@ -197,8 +206,6 @@
         out_specs=(VMEM,) * 5,
         scratch_shapes=[
             pltpu.VMEM((rows, depth), jnp.float32), pltpu.VMEM((depth, rank), jnp.float32),
-            pltpu.VMEM((rows, depth), jnp.bfloat16), pltpu.VMEM((rows, depth), jnp.bfloat16),
-            pltpu.VMEM((rank, rows), jnp.bfloat16), pltpu.VMEM((rank, rows), jnp.bfloat16),
             pltpu.VMEM((rank, depth), jnp.float32), pltpu.VMEM((packed, LANES), jnp.float32),
             pltpu.SemaphoreType.DMA((rows // BLOCK + 1,)),
         ],
@@ -242,7 +249,7 @@
     return gram, outs
 
 
-def factor_kernel(scale, keep_ref, other_ref, inverse_ref, flipped_ref, factor_ref, a_ref, packed_ref):
+def factor_kernel(scale, keep_ref, other_ref, inverse_ref, flipped_ref, factor_ref, a_ref, packed_ref, buffer_ref):
     half = keep_ref.shape[0]
     core = core_bit()
     packed_ref[rows_of(core, half), :] = keep_ref[...]
@@ -251,7 +258,7 @@
     a_ref[:LANES, LANES:] = packed_ref[LANES:2 * LANES, :]
     a_ref[LANES:, :LANES] = jnp.zeros((LANES, LANES), jnp.float32)
     a_ref[LANES:, LANES:] = packed_ref[2 * LANES:, :]
-    inverse, grow = factorize(a_ref, factor_ref)
+    inverse, grow = factorize(a_ref, factor_ref, buffer_ref)
     inverse_ref[...] = inverse
     flipped_ref[...] = inverse.T * scale
     factor_ref[...] = factor_ref[...] * (grow / scale)
@@ -263,7 +270,7 @@
         out_shape=(f32(size, size),) * 3,
         in_specs=[VMEM] * 2,
         out_specs=(VMEM,) * 3,
-        scratch_shapes=[pltpu.VMEM((size, size), jnp.float32), pltpu.VMEM((3 * LANES, LANES), jnp.float32)],
+        scratch_shapes=[pltpu.VMEM((size, size), jnp.float32), pltpu.VMEM((3 * LANES, LANES), jnp.float32), pltpu.VMEM((40 * GROUP, LANES), jnp.float32)],
         compiler_params=pltpu.CompilerParams(vmem_limit_bytes=16 * 2**20),
         cost_estimate=pl.CostEstimate(flops=10 * 10**9, bytes_accessed=2**20, transcendentals=size),
         name="factor",

time: 62.1 us -> 60.4 us (0.973)
  Pallas kernels: 21.5 us -> 19.8 us
    pallas_call x1, Pallas kernels: 9.39 us -> 7.46 us  [factor(): pl.pallas_call(lambda *refs: factor_kernel(scale, *refs), out_shape=(f32(...]
  transfers between devices with their start and end apart: 23 -> 23, of which waited for: 8 -> 8; matrix products, arithmetic and copies ran while one was open for 0% -> 0% of each run, Pallas kernels for 18% -> 15%
where the time goes in v9:
time: 60.4 us; the launch traced here: 60.2 us
  starting transfers between devices  26.2 us (43%)
  Pallas kernels  19.8 us (33%)
  waiting for transfers between devices  13.6 us (23%)
  between operations  0.7 us (1%)
    ppermute x23, starting transfers between devices, send(): return lax.ppermute(value, AXES, pairs)  26.2 us
    ppermute x23, waiting for transfers between devices, send(): return lax.ppermute(value, AXES, pairs)  13.6 us
    pallas_call x1, Pallas kernels, local_terms(): pl.pallas_call(local_kernel, out_shape=(f32(rows, rank), f32(rank // 2, d...  8.96 us
    pallas_call x1, Pallas kernels, factor(): pl.pallas_call(lambda *refs: factor_kernel(scale, *refs), out_shape=(f32(...  7.46 us
    pallas_call x1, Pallas kernels, project(): pl.pallas_call(project_kernel, out_shape=jax.ShapeDtypeStruct((rank, dept...  1.65 us
    pallas_call x1, Pallas kernels, basis_of(): pl.pallas_call(basis_kernel, out_shape=f32(*sampled.shape), in_specs=[VME...  1.57 us
  transfers between devices with their start and end apart: 23, of which 8 were waited for; matrix products, arithmetic and copies ran while one was open for 0% of the time, Pallas kernels for 15%

profile of v9, /device:TPU:0, one launch (start us, length us, event | category | flops | bytes accessed | tf_op | source)
XLA Modules:
  0.0 60.2 jit_solution(12534420953388113281)
XLA Ops:
  0.6 9.0 %local_terms.1 = (f32[1024,256]{1,0:T(8,128)S(1)}, f32[128,1024]{1,0:T(8,128)S(1)}, f32[128,1024]{1,0:T(8,128)S(1)}, f32[192,128]{1,0:T(8,128)S(1)}, f32[192,128]{1,0:T(8,128)S(1)}) custom-call(f32[1024,1024]{1,0:T(8,128)} %features_hbm.1, f32[1024,256]{1,0:T(8,128)} %sketch_hbm.1), custom_call_target="tpu_custom_call" | custom-call | flops 4000000000 | bytes 8388608 | tf_op jit(solution)/shard_map/local_terms/pallas_call | solution.py:202
  9.6 0.5 collective-permute-start
  10.1 0.1 collective-permute-start.1
  10.2 1.6 %collective-permute-done.1.refs_3_ = f32[192,128]{1,0:T(8,128)S(1)} collective-permute-done((f32[192,128]{1,0:T(8,128)S(1)}, f32[192,128]{1,0:T(8,128)S(1)}, u32[]{:S(2)}, u32[]{:S(2)}) %collective-permute-start.1) | collective-permute-done | bytes 98336 | tf_op jit(solution)/shard_map/ppermute | solution.py:332
  11.8 0.0 collective-permute-done.refs_1_
  11.8 0.1 stage.3
  11.9 3.0 %collective-permute-start.5 = (f32[192,128]{1,0:T(8,128)S(1)}, f32[192,128]{1,0:T(8,128)S(1)}, u32[]{:S(2)}, u32[]{:S(2)}) collective-permute-start(f32[192,128]{1,0:T(8,128)S(1)} %get-tuple-element.34), channel_id=1, source_target_pairs={{0,8},{1,9},{2,10},{3,11},{4,12},{5,13},{6,14},{7,15},{8,0},{9,1},... | collective-permute-start | bytes 294920 | tf_op jit(solution)/shard_map/ppermute | solution.py:332
  14.9 1.5 %collective-permute-start.2 = (f32[32,1024]{1,0:T(8,128)S(1)}, f32[32,1024]{1,0:T(8,128)S(1)}, u32[]{:S(2)}, u32[]{:S(2)}) collective-permute-start(f32[32,1024]{1,0:T(8,128)S(1)} %get-tuple-element.31), channel_id=1, source_target_pairs={{0,1},{1,0},{2,3},{3,2},{4,5},{5,4},{6,7},{7,6},{8,9},{9,8},{10,11... | collective-permute-start | bytes 393224 | tf_op jit(solution)/shard_map/ppermute | solution.py:332
  16.4 1.5 %collective-permute-start.3 = (f32[32,1024]{1,0:T(8,128)S(1)}, f32[32,1024]{1,0:T(8,128)S(1)}, u32[]{:S(2)}, u32[]{:S(2)}) collective-permute-start(f32[32,1024]{1,0:T(8,128)S(1)} %get-tuple-element.32), channel_id=1, source_target_pairs={{0,4},{1,5},{2,6},{3,7},{4,0},{5,1},{6,2},{7,3},{8,12},{9,13},{10,... | collective-permute-start | bytes 393224 | tf_op jit(solution)/shard_map/ppermute | solution.py:332
  17.9 0.5 collective-permute-start.4
  18.4 0.0 collective-permute-done.5
  18.4 2.7 %collective-permute-start.6 = (f32[192,128]{1,0:T(8,128)S(1)}, f32[192,128]{1,0:T(8,128)S(1)}, u32[]{:S(2)}, u32[]{:S(2)}) collective-permute-start(f32[192,128]{1,0:T(8,128)S(1)} %add.3.refs_4_), channel_id=1, source_target_pairs={{0,16},{1,17},{2,18},{3,19},{4,20},{5,21},{6,22},{7,23},{8,24},{9,... | collective-permute-start | bytes 294920 | tf_op jit(solution)/shard_map/ppermute | solution.py:332
  21.0 0.0 collective-permute-done.2.refs_1_
  21.1 1.7 %collective-permute-done.3.refs_2_ = f32[32,1024]{1,0:T(8,128)S(1)} collective-permute-done((f32[32,1024]{1,0:T(8,128)S(1)}, f32[32,1024]{1,0:T(8,128)S(1)}, u32[]{:S(2)}, u32[]{:S(2)}) %collective-permute-start.3) | collective-permute-done | bytes 131104 | tf_op jit(solution)/shard_map/ppermute | solution.py:332
  22.8 1.4 %collective-permute-done.4.refs_3_ = f32[32,1024]{1,0:T(8,128)S(1)} collective-permute-done((f32[32,1024]{1,0:T(8,128)S(1)}, f32[32,1024]{1,0:T(8,128)S(1)}, u32[]{:S(2)}, u32[]{:S(2)}) %collective-permute-start.4) | collective-permute-done | bytes 131104 | tf_op jit(solution)/shard_map/ppermute | solution.py:332
  24.1 1.3 %collective-permute-done.6.refs_5_ = f32[192,128]{1,0:T(8,128)S(1)} collective-permute-done((f32[192,128]{1,0:T(8,128)S(1)}, f32[192,128]{1,0:T(8,128)S(1)}, u32[]{:S(2)}, u32[]{:S(2)}) %collective-permute-start.6) | collective-permute-done | bytes 98336 | tf_op jit(solution)/shard_map/ppermute | solution.py:332
  25.4 1.4 %collective-permute-start.10 = (f32[192,128]{1,0:T(8,128)S(1)}, f32[192,128]{1,0:T(8,128)S(1)}, u32[]{:S(2)}, u32[]{:S(2)}) collective-permute-start(f32[192,128]{1,0:T(8,128)S(1)} %get-tuple-element.39.refs_4_), channel_id=1, source_target_pairs={{0,1},{1,0},{2,3},{3,2},{4,5},{5,4},{6,7},{7,6},{8,9},{9,8},{10,11... | collective-permute-start | bytes 294920 | tf_op jit(solution)/shard_map/ppermute | solution.py:332
  26.9 0.7 %collective-permute-start.7 = (f32[8,1024]{1,0:T(8,128)S(1)}, f32[8,1024]{1,0:T(8,128)S(1)}, u32[]{:S(2)}, u32[]{:S(2)}) collective-permute-start(f32[8,1024]{1,0:T(8,128)S(1)} %get-tuple-element.36), channel_id=1, source_target_pairs={{0,8},{1,9},{2,10},{3,11},{4,12},{5,13},{6,14},{7,15},{8,0},{9,1},... | collective-permute-start | bytes 98312 | tf_op jit(solution)/shard_map/ppermute | solution.py:332
  27.5 3.4 %collective-permute-start.8 = (f32[8,1024]{1,0:T(8,128)S(1)}, f32[8,1024]{1,0:T(8,128)S(1)}, u32[]{:S(2)}, u32[]{:S(2)}) collective-permute-start(f32[8,1024]{1,0:T(8,128)S(1)} %get-tuple-element.37), channel_id=1, source_target_pairs={{0,16},{1,17},{2,18},{3,19},{4,20},{5,21},{6,22},{7,23},{8,24},{9,... | collective-permute-start | bytes 98312 | tf_op jit(solution)/shard_map/ppermute | solution.py:332
  30.9 0.3 collective-permute-start.9
  31.2 0.0 collective-permute-done.7.refs_1_
  31.3 1.6 %collective-permute-done.8.refs_2_ = f32[8,1024]{1,0:T(8,128)S(1)} collective-permute-done((f32[8,1024]{1,0:T(8,128)S(1)}, f32[8,1024]{1,0:T(8,128)S(1)}, u32[]{:S(2)}, u32[]{:S(2)}) %collective-permute-start.8) | collective-permute-done | bytes 32800 | tf_op jit(solution)/shard_map/ppermute | solution.py:332
  32.8 3.8 %collective-permute-done.9.refs_3_ = f32[8,1024]{1,0:T(8,128)S(1)} collective-permute-done((f32[8,1024]{1,0:T(8,128)S(1)}, f32[8,1024]{1,0:T(8,128)S(1)}, u32[]{:S(2)}, u32[]{:S(2)}) %collective-permute-start.9) | collective-permute-done | bytes 32800 | tf_op jit(solution)/shard_map/ppermute | solution.py:332
  36.6 0.0 collective-permute-done.10.refs_5_
  36.7 1.6 %collective-permute-start.14 = (f32[192,128]{1,0:T(8,128)S(1)}, f32[192,128]{1,0:T(8,128)S(1)}, u32[]{:S(2)}, u32[]{:S(2)}) collective-permute-start(f32[192,128]{1,0:T(8,128)S(1)} %get-tuple-element.41.refs_4_), channel_id=1, source_target_pairs={{0,4},{1,5},{2,6},{3,7},{4,0},{5,1},{6,2},{7,3},{8,12},{9,13},{10,... | collective-permute-start | bytes 294920 | tf_op jit(solution)/shard_map/ppermute | solution.py:332
  38.2 0.0 collective-permute-start.11
  38.2 0.9 %collective-permute-start.12 = (f32[8,1024]{1,0:T(8,128)S(1)}, f32[8,1024]{1,0:T(8,128)S(1)}, u32[]{:S(2)}, u32[]{:S(2)}) collective-permute-start(f32[8,1024]{1,0:T(8,128)S(1)} %get-tuple-element.40.refs_0_), channel_id=1, source_target_pairs={{0,16},{1,17},{2,18},{3,19},{4,20},{5,21},{6,22},{7,23},{8,24},{9,... | collective-permute-start | bytes 98312 | tf_op jit(solution)/shard_map/ppermute | solution.py:332
  39.1 3.5 %collective-permute-start.13 = (f32[8,1024]{1,0:T(8,128)S(1)}, f32[8,1024]{1,0:T(8,128)S(1)}, u32[]{:S(2)}, u32[]{:S(2)}) collective-permute-start(f32[8,1024]{1,0:T(8,128)S(1)} %get-tuple-element.40.refs_0_), channel_id=1, source_target_pairs={{0,24},{1,25},{2,26},{3,27},{4,28},{5,29},{6,30},{7,31},{8,16},{9,... | collective-permute-start | bytes 98312 | tf_op jit(solution)/shard_map/ppermute | solution.py:332
  42.6 0.0 collective-permute-done.11.refs_1_
  42.6 0.4 collective-permute-done.12.refs_2_
  43.0 1.8 %collective-permute-done.13.refs_3_ = f32[8,1024]{1,0:T(8,128)S(1)} collective-permute-done((f32[8,1024]{1,0:T(8,128)S(1)}, f32[8,1024]{1,0:T(8,128)S(1)}, u32[]{:S(2)}, u32[]{:S(2)}) %collective-permute-start.13) | collective-permute-done | bytes 32800 | tf_op jit(solution)/shard_map/ppermute | solution.py:332
  44.8 0.0 collective-permute-done.14.refs_5_
  44.9 0.1 collective-permute-start.15
  44.9 0.6 collective-permute-start.16
  45.5 0.7 %collective-permute-start.17 = (f32[32,1024]{1,0:T(8,128)S(1)}, f32[32,1024]{1,0:T(8,128)S(1)}, u32[]{:S(2)}, u32[]{:S(2)}) collective-permute-start(f32[32,1024]{1,0:T(8,128)S(1)} %get-tuple-element.46.refs_0_), channel_id=1, source_target_pairs={{0,4},{1,5},{2,6},{3,7},{4,0},{5,1},{6,2},{7,3},{8,12},{9,13},{10,... | collective-permute-start | bytes 393224 | tf_op jit(solution)/shard_map/ppermute | solution.py:332
  46.2 2.3 %collective-permute-start.18 = (f32[32,1024]{1,0:T(8,128)S(1)}, f32[32,1024]{1,0:T(8,128)S(1)}, u32[]{:S(2)}, u32[]{:S(2)}) collective-permute-start(f32[32,1024]{1,0:T(8,128)S(1)} %get-tuple-element.46.refs_0_), channel_id=1, source_target_pairs={{0,5},{1,4},{2,7},{3,6},{4,1},{5,0},{6,3},{7,2},{8,13},{9,12},{10,... | collective-permute-start | bytes 393224 | tf_op jit(solution)/shard_map/ppermute | solution.py:332
  48.5 0.0 collective-permute-start.19
  48.5 0.0 collective-permute-done.15.refs_1_
  48.5 7.5 %factor.1 = (f32[256,256]{1,0:T(8,128)S(1)}, f32[256,256]{1,0:T(8,128)S(1)}, f32[256,256]{1,0:T(8,128)}) custom-call(f32[192,128]{1,0:T(8,128)S(1)} %get-tuple-element.42.refs_0_, f32[192,128]{1,0:T(8,128)S(1)} %collective-permute-done.15.refs_1_), custom_call_target="tpu_custom_call" | custom-call | flops 10000000000 | bytes 1048576 | tf_op jit(solution)/shard_map/factor/pallas_call | solution.py:268
  56.0 0.0 collective-permute-done.16.refs_1_
  56.0 0.5 collective-permute-start.20
  56.5 0.0 collective-permute-done.17.refs_2_
  56.5 0.1 collective-permute-start.21
  56.5 0.0 collective-permute-done.18.refs_3_
  56.6 0.4 collective-permute-start.22
  57.0 1.6 %basis.1 = f32[1024,256]{1,0:T(8,128)} custom-call(f32[1024,256]{1,0:T(8,128)S(1)} %get-tuple-element.25.sampled_ref, f32[256,256]{1,0:T(8,128)S(1)} %get-tuple-element.43.flipped_ref), custom_call_target="tpu_custom_call" | custom-call | flops 2000000000 | bytes 2097152 | tf_op jit(solution)/shard_map/basis/pallas_call | solution.py:288
  58.6 0.0 collective-permute-done.19.refs_4_
  58.6 0.0 collective-permute-done.20.refs_5_
  58.6 0.0 collective-permute-done.21.refs_6_
  58.6 0.0 collective-permute-done.22.refs_7_
  58.6 1.7 %project.1 = f32[256,1024]{1,0:T(8,128)} custom-call(f32[256,256]{1,0:T(8,128)S(1)} %get-tuple-element.45.inverse_ref, f32[32,1024]{1,0:T(8,128)S(1)} %get-tuple-element.46.refs_0_, f32[32,1024]{1,0:T(8,128)S(1)} %collective-permute-done.16.refs_1_, f32[32,1024]{1,0:T(8,128)S(1)} %collective-permute-done.17.refs_2_, ...), custom_call_target="tpu_custom_call" | custom-call | flops 400000000 | bytes 2097152 | tf_op jit(solution)/shard_map/project/pallas_call | solution.py:317
  (4 shorter events, 0.1 us)
Async XLA Ops:
  9.6 2.2 %collective-permute-start = (f32[128,1024]{1,0:T(8,128)S(1)}, f32[128,1024]{1,0:T(8,128)S(1)}, u32[]{:S(2)}, u32[]{:S(2)}) collective-permute-start(f32[128,1024]{1,0:T(8,128)S(1)} %get-tuple-element.27), channel_id=1, source_target_pairs={{0,2},{1,3},{2,0},{3,1},{4,6},{5,7},{6,4},{7,5},{8,10},{9,11},{10,... | collective-permute-start | bytes 1572872 | tf_op jit(solution)/shard_map/ppermute | solution.py:332
  10.1 1.7 %collective-permute-start.1 = (f32[192,128]{1,0:T(8,128)S(1)}, f32[192,128]{1,0:T(8,128)S(1)}, u32[]{:S(2)}, u32[]{:S(2)}) collective-permute-start(f32[192,128]{1,0:T(8,128)S(1)} %get-tuple-element.29), channel_id=1, source_target_pairs={{0,2},{1,3},{2,0},{3,1},{4,6},{5,7},{6,4},{7,5},{8,10},{9,11},{10,... | collective-permute-start | bytes 294920 | tf_op jit(solution)/shard_map/ppermute | solution.py:332
  11.9 6.5 %collective-permute-start.5 = (f32[192,128]{1,0:T(8,128)S(1)}, f32[192,128]{1,0:T(8,128)S(1)}, u32[]{:S(2)}, u32[]{:S(2)}) collective-permute-start(f32[192,128]{1,0:T(8,128)S(1)} %get-tuple-element.34), channel_id=1, source_target_pairs={{0,8},{1,9},{2,10},{3,11},{4,12},{5,13},{6,14},{7,15},{8,0},{9,1},... | collective-permute-start | bytes 294920 | tf_op jit(solution)/shard_map/ppermute | solution.py:332
  14.9 6.2 %collective-permute-start.2 = (f32[32,1024]{1,0:T(8,128)S(1)}, f32[32,1024]{1,0:T(8,128)S(1)}, u32[]{:S(2)}, u32[]{:S(2)}) collective-permute-start(f32[32,1024]{1,0:T(8,128)S(1)} %get-tuple-element.31), channel_id=1, source_target_pairs={{0,1},{1,0},{2,3},{3,2},{4,5},{5,4},{6,7},{7,6},{8,9},{9,8},{10,11... | collective-permute-start | bytes 393224 | tf_op jit(solution)/shard_map/ppermute | solution.py:332
  16.4 6.4 %collective-permute-start.3 = (f32[32,1024]{1,0:T(8,128)S(1)}, f32[32,1024]{1,0:T(8,128)S(1)}, u32[]{:S(2)}, u32[]{:S(2)}) collective-permute-start(f32[32,1024]{1,0:T(8,128)S(1)} %get-tuple-element.32), channel_id=1, source_target_pairs={{0,4},{1,5},{2,6},{3,7},{4,0},{5,1},{6,2},{7,3},{8,12},{9,13},{10,... | collective-permute-start | bytes 393224 | tf_op jit(solution)/shard_map/ppermute | solution.py:332
  17.9 6.2 %collective-permute-start.4 = (f32[32,1024]{1,0:T(8,128)S(1)}, f32[32,1024]{1,0:T(8,128)S(1)}, u32[]{:S(2)}, u32[]{:S(2)}) collective-permute-start(f32[32,1024]{1,0:T(8,128)S(1)} %get-tuple-element.33), channel_id=1, source_target_pairs={{0,5},{1,4},{2,7},{3,6},{4,1},{5,0},{6,3},{7,2},{8,13},{9,12},{10,... | collective-permute-start | bytes 393224 | tf_op jit(solution)/shard_map/ppermute | solution.py:332
  18.4 7.0 %collective-permute-start.6 = (f32[192,128]{1,0:T(8,128)S(1)}, f32[192,128]{1,0:T(8,128)S(1)}, u32[]{:S(2)}, u32[]{:S(2)}) collective-permute-start(f32[192,128]{1,0:T(8,128)S(1)} %add.3.refs_4_), channel_id=1, source_target_pairs={{0,16},{1,17},{2,18},{3,19},{4,20},{5,21},{6,22},{7,23},{8,24},{9,... | collective-permute-start | bytes 294920 | tf_op jit(solution)/shard_map/ppermute | solution.py:332
  25.4 11.2 %collective-permute-start.10 = (f32[192,128]{1,0:T(8,128)S(1)}, f32[192,128]{1,0:T(8,128)S(1)}, u32[]{:S(2)}, u32[]{:S(2)}) collective-permute-start(f32[192,128]{1,0:T(8,128)S(1)} %get-tuple-element.39.refs_4_), channel_id=1, source_target_pairs={{0,1},{1,0},{2,3},{3,2},{4,5},{5,4},{6,7},{7,6},{8,9},{9,8},{10,11... | collective-permute-start | bytes 294920 | tf_op jit(solution)/shard_map/ppermute | solution.py:332
  26.9 4.4 %collective-permute-start.7 = (f32[8,1024]{1,0:T(8,128)S(1)}, f32[8,1024]{1,0:T(8,128)S(1)}, u32[]{:S(2)}, u32[]{:S(2)}) collective-permute-start(f32[8,1024]{1,0:T(8,128)S(1)} %get-tuple-element.36), channel_id=1, source_target_pairs={{0,8},{1,9},{2,10},{3,11},{4,12},{5,13},{6,14},{7,15},{8,0},{9,1},... | collective-permute-start | bytes 98312 | tf_op jit(solution)/shard_map/ppermute | solution.py:332
  27.5 5.3 %collective-permute-start.8 = (f32[8,1024]{1,0:T(8,128)S(1)}, f32[8,1024]{1,0:T(8,128)S(1)}, u32[]{:S(2)}, u32[]{:S(2)}) collective-permute-start(f32[8,1024]{1,0:T(8,128)S(1)} %get-tuple-element.37), channel_id=1, source_target_pairs={{0,16},{1,17},{2,18},{3,19},{4,20},{5,21},{6,22},{7,23},{8,24},{9,... | collective-permute-start | bytes 98312 | tf_op jit(solution)/shard_map/ppermute | solution.py:332
  30.9 5.7 %collective-permute-start.9 = (f32[8,1024]{1,0:T(8,128)S(1)}, f32[8,1024]{1,0:T(8,128)S(1)}, u32[]{:S(2)}, u32[]{:S(2)}) collective-permute-start(f32[8,1024]{1,0:T(8,128)S(1)} %get-tuple-element.38), channel_id=1, source_target_pairs={{0,24},{1,25},{2,26},{3,27},{4,28},{5,29},{6,30},{7,31},{8,16},{9,... | collective-permute-start | bytes 98312 | tf_op jit(solution)/shard_map/ppermute | solution.py:332
  36.7 8.2 %collective-permute-start.14 = (f32[192,128]{1,0:T(8,128)S(1)}, f32[192,128]{1,0:T(8,128)S(1)}, u32[]{:S(2)}, u32[]{:S(2)}) collective-permute-start(f32[192,128]{1,0:T(8,128)S(1)} %get-tuple-element.41.refs_4_), channel_id=1, source_target_pairs={{0,4},{1,5},{2,6},{3,7},{4,0},{5,1},{6,2},{7,3},{8,12},{9,13},{10,... | collective-permute-start | bytes 294920 | tf_op jit(solution)/shard_map/ppermute | solution.py:332
  38.2 4.4 %collective-permute-start.11 = (f32[8,1024]{1,0:T(8,128)S(1)}, f32[8,1024]{1,0:T(8,128)S(1)}, u32[]{:S(2)}, u32[]{:S(2)}) collective-permute-start(f32[8,1024]{1,0:T(8,128)S(1)} %get-tuple-element.40.refs_0_), channel_id=1, source_target_pairs={{0,8},{1,9},{2,10},{3,11},{4,12},{5,13},{6,14},{7,15},{8,0},{9,1},... | collective-permute-start | bytes 98312 | tf_op jit(solution)/shard_map/ppermute | solution.py:332
  38.2 4.8 %collective-permute-start.12 = (f32[8,1024]{1,0:T(8,128)S(1)}, f32[8,1024]{1,0:T(8,128)S(1)}, u32[]{:S(2)}, u32[]{:S(2)}) collective-permute-start(f32[8,1024]{1,0:T(8,128)S(1)} %get-tuple-element.40.refs_0_), channel_id=1, source_target_pairs={{0,16},{1,17},{2,18},{3,19},{4,20},{5,21},{6,22},{7,23},{8,24},{9,... | collective-permute-start | bytes 98312 | tf_op jit(solution)/shard_map/ppermute | solution.py:332
  39.1 5.7 %collective-permute-start.13 = (f32[8,1024]{1,0:T(8,128)S(1)}, f32[8,1024]{1,0:T(8,128)S(1)}, u32[]{:S(2)}, u32[]{:S(2)}) collective-permute-start(f32[8,1024]{1,0:T(8,128)S(1)} %get-tuple-element.40.refs_0_), channel_id=1, source_target_pairs={{0,24},{1,25},{2,26},{3,27},{4,28},{5,29},{6,30},{7,31},{8,16},{9,... | collective-permute-start | bytes 98312 | tf_op jit(solution)/shard_map/ppermute | solution.py:332
  44.9 3.6 %collective-permute-start.15 = (f32[192,128]{1,0:T(8,128)S(1)}, f32[192,128]{1,0:T(8,128)S(1)}, u32[]{:S(2)}, u32[]{:S(2)}) collective-permute-start(f32[192,128]{1,0:T(8,128)S(1)} %get-tuple-element.42.refs_0_), channel_id=1, source_target_pairs={{0,2},{1,3},{2,0},{3,1},{4,6},{5,7},{6,4},{7,5},{8,10},{9,11},{10,... | collective-permute-start | bytes 294920 | tf_op jit(solution)/shard_map/ppermute | solution.py:332
  44.9 11.0 %collective-permute-start.16 = (f32[32,1024]{1,0:T(8,128)S(1)}, f32[32,1024]{1,0:T(8,128)S(1)}, u32[]{:S(2)}, u32[]{:S(2)}) collective-permute-start(f32[32,1024]{1,0:T(8,128)S(1)} %get-tuple-element.46.refs_0_), channel_id=1, source_target_pairs={{0,1},{1,0},{2,3},{3,2},{4,5},{5,4},{6,7},{7,6},{8,9},{9,8},{10,11... | collective-permute-start | bytes 393224 | tf_op jit(solution)/shard_map/ppermute | solution.py:332
  45.5 11.0 %collective-permute-start.17 = (f32[32,1024]{1,0:T(8,128)S(1)}, f32[32,1024]{1,0:T(8,128)S(1)}, u32[]{:S(2)}, u32[]{:S(2)}) collective-permute-start(f32[32,1024]{1,0:T(8,128)S(1)} %get-tuple-element.46.refs_0_), channel_id=1, source_target_pairs={{0,4},{1,5},{2,6},{3,7},{4,0},{5,1},{6,2},{7,3},{8,12},{9,13},{10,... | collective-permute-start | bytes 393224 | tf_op jit(solution)/shard_map/ppermute | solution.py:332
  46.2 10.4 %collective-permute-start.18 = (f32[32,1024]{1,0:T(8,128)S(1)}, f32[32,1024]{1,0:T(8,128)S(1)}, u32[]{:S(2)}, u32[]{:S(2)}) collective-permute-start(f32[32,1024]{1,0:T(8,128)S(1)} %get-tuple-element.46.refs_0_), channel_id=1, source_target_pairs={{0,5},{1,4},{2,7},{3,6},{4,1},{5,0},{6,3},{7,2},{8,13},{9,12},{10,... | collective-permute-start | bytes 393224 | tf_op jit(solution)/shard_map/ppermute | solution.py:332
  48.5 10.1 %collective-permute-start.19 = (f32[32,1024]{1,0:T(8,128)S(1)}, f32[32,1024]{1,0:T(8,128)S(1)}, u32[]{:S(2)}, u32[]{:S(2)}) collective-permute-start(f32[32,1024]{1,0:T(8,128)S(1)} %get-tuple-element.46.refs_0_), channel_id=1, source_target_pairs={{0,2},{1,3},{2,0},{3,1},{4,6},{5,7},{6,4},{7,5},{8,10},{9,11},{10,... | collective-permute-start | bytes 393224 | tf_op jit(solution)/shard_map/ppermute | solution.py:332
  56.0 2.6 %collective-permute-start.20 = (f32[32,1024]{1,0:T(8,128)S(1)}, f32[32,1024]{1,0:T(8,128)S(1)}, u32[]{:S(2)}, u32[]{:S(2)}) collective-permute-start(f32[32,1024]{1,0:T(8,128)S(1)} %collective-permute-done.16.refs_1_), channel_id=1, source_target_pairs={{0,2},{1,3},{2,0},{3,1},{4,6},{5,7},{6,4},{7,5},{8,10},{9,11},{10,... | collective-permute-start | bytes 393224 | tf_op jit(solution)/shard_map/ppermute | solution.py:332
  56.5 2.1 %collective-permute-start.21 = (f32[32,1024]{1,0:T(8,128)S(1)}, f32[32,1024]{1,0:T(8,128)S(1)}, u32[]{:S(2)}, u32[]{:S(2)}) collective-permute-start(f32[32,1024]{1,0:T(8,128)S(1)} %collective-permute-done.17.refs_2_), channel_id=1, source_target_pairs={{0,2},{1,3},{2,0},{3,1},{4,6},{5,7},{6,4},{7,5},{8,10},{9,11},{10,... | collective-permute-start | bytes 393224 | tf_op jit(solution)/shard_map/ppermute | solution.py:332
  56.6 2.0 %collective-permute-start.22 = (f32[32,1024]{1,0:T(8,128)S(1)}, f32[32,1024]{1,0:T(8,128)S(1)}, u32[]{:S(2)}, u32[]{:S(2)}) collective-permute-start(f32[32,1024]{1,0:T(8,128)S(1)} %collective-permute-done.18.refs_3_), channel_id=1, source_target_pairs={{0,2},{1,3},{2,0},{3,1},{4,6},{5,7},{6,4},{7,5},{8,10},{9,11},{10,... | collective-permute-start | bytes 393224 | tf_op jit(solution)/shard_map/ppermute | solution.py:332

commit v10 on v9

--- a/solution.py
+++ b/solution.py
@@ -108,17 +108,21 @@
     a_ref[end:, :] = jnp.where((at >= base) & (at < end), 0.0, rest) - update
 
 
-def factorize(a_ref, factor_ref, buffer_ref):
+def normalize(a_ref):
     size = a_ref.shape[0]
     col = lax.broadcasted_iota(jnp.int32, (size, size), 1)
     row = lax.broadcasted_iota(jnp.int32, (size, size), 0)
     largest = jnp.max(jnp.where(col == row, a_ref[...], 0.0), axis=(0, 1), keepdims=True)
     shrink = lax.rsqrt(largest)
     a_ref[...] = a_ref[...] * shrink * shrink
-    for base in range(0, size, PANEL):
+    return shrink, largest * shrink
+
+
+def eliminate(a_ref, factor_ref, buffer_ref, first, last):
+    size = a_ref.shape[0]
+    for base in range(first, last, PANEL):
         factor_panel(a_ref, factor_ref, buffer_ref, base, PANEL, size)
         trailing(a_ref, base, PANEL, size)
-    return jnp.where(col <= row, a_ref[...], 0.0) * shrink, largest * shrink
 
 
 def split(value):
@@ -146,7 +150,7 @@
     return pl.ds(pl.multiple_of(block * height, GROUP), height)
 
 
-def local_kernel(features_hbm, sketch_hbm, sampled_ref, keep_ref, send_ref, gram_keep_ref, gram_send_ref, features_ref, sketch_ref, cross_ref, packed_ref, sems):
+def local_kernel(features_hbm, sketch_hbm, sampled_ref, keep_ref, send_ref, gram_keep_ref, gram_send_ref, features_ref, sketch_ref, high_ref, low_ref, flip_high_ref, flip_low_ref, cross_ref, packed_ref, sems):
     rows, depth = features_ref.shape
     rank = sketch_ref.shape[1]
     chunks = rows // BLOCK
@@ -163,15 +167,13 @@
         span = slice(at * BLOCK, (at + 1) * BLOCK)
         copies[1 + at].wait()
         features = split(features_ref[span, :])
+        high_ref[span, :], low_ref[span, :] = features
         sampled = product(features, sketch, 1, 0)
         sampled_ref[span, :] = sampled
         flipped = split(sampled.T)
+        flip_high_ref[:, span], flip_low_ref[:, span] = flipped
         term = product(flipped, split(sampled), 1, 0)
         gram = term if gram is None else gram + term
-        for left in range(0, depth, BLOCK):
-            columns = slice(left, left + BLOCK)
-            term = product(flipped, [part[:, columns] for part in features], 1, 0)
-            cross_ref[:, columns] = term if at == 0 else cross_ref[:, columns] + term
     packed_ref[:LANES, :] = gram[:LANES, :LANES]
     packed_ref[LANES:2 * LANES, :] = gram[:LANES, LANES:]
     packed_ref[2 * LANES:, :] = gram[LANES:, LANES:]
@@ -179,8 +181,12 @@
     core = core_bit()
     gram_keep_ref[...] = packed_ref[rows_of(core, half), :]
     gram_send_ref[...] = packed_ref[rows_of(1 - core, half), :]
+    flipped = flip_high_ref[...], flip_low_ref[...]
     own = own_block()
     height = rank // BLOCKS
+    for left in range(0, depth, BLOCK):
+        span = slice(left, left + BLOCK)
+        cross_ref[:, span] = product(flipped, (high_ref[:, span], low_ref[:, span]), 1, 0)
     for at in range(BLOCKS):
         block = cross_ref[rows_of(at ^ own, height), :]
         if at < BLOCKS // 2:
@@ -206,6 +212,8 @@
         out_specs=(VMEM,) * 5,
         scratch_shapes=[
             pltpu.VMEM((rows, depth), jnp.float32), pltpu.VMEM((depth, rank), jnp.float32),
+            pltpu.VMEM((rows, depth), jnp.bfloat16), pltpu.VMEM((rows, depth), jnp.bfloat16),
+            pltpu.VMEM((rank, rows), jnp.bfloat16), pltpu.VMEM((rank, rows), jnp.bfloat16),
             pltpu.VMEM((rank, depth), jnp.float32), pltpu.VMEM((packed, LANES), jnp.float32),
             pltpu.SemaphoreType.DMA((rows // BLOCK + 1,)),
         ],
@@ -215,41 +223,53 @@
     )(features, sketch)
 
 
-def stage_kernel(terms, *refs):
-    cross, (gram_ref, gram_other_ref, gram_out_ref), outs = refs[:terms], refs[terms:terms + 3], refs[terms + 3:]
-    gram_out_ref[...] = gram_ref[...] + gram_other_ref[...]
-    height = outs[0].shape[0]
-    for at, out_ref in enumerate(outs):
-        span = slice(at * height, (at + 1) * height)
-        out_ref[...] = sum(ref[span, :] for ref in cross)
-
-
-def join_kernel(*refs):
-    *cross, gram_ref, gram_other_ref, gram_out_ref, out_ref = refs
-    gram_out_ref[...] = gram_ref[...] + gram_other_ref[...]
-    top = 0
-    for ref in cross:
-        out_ref[top:top + ref.shape[0], :] = ref[...]
-        top += ref.shape[0]
-
-
-def stage(cross, gram, gram_other, pieces, join=False):
+def call(kernel, name, outs, *operands, after=(), scratch=(), flops=10**6):
+    return pl.pallas_call(
+        lambda *refs: kernel(*refs[:len(operands)], *refs[len(operands) + len(after):]),
+        out_shape=outs,
+        in_specs=[VMEM] * len(operands) + [pl.BlockSpec(memory_space=pl.ANY)] * len(after),
+        out_specs=jax.tree.map(lambda _: VMEM, outs),
+        scratch_shapes=list(scratch),
+        compiler_params=pltpu.CompilerParams(vmem_limit_bytes=16 * 2**20),
+        cost_estimate=pl.CostEstimate(flops=flops, bytes_accessed=10**6, transcendentals=0),
+        name=name,
+    )(*operands, *after)
+
+
+def sum_kernel(order, terms, *refs):
+    cross, (gram_ref, gram_other_ref), outs = refs[:terms], refs[terms:terms + 2], refs[terms + 2:]
+    outs[0][...] = gram_ref[...] + gram_other_ref[...]
+    at = 0
+    for out_ref in outs[1:]:
+        for top in range(0, out_ref.shape[0], GROUP):
+            span = slice(order[at] * GROUP, (order[at] + 1) * GROUP)
+            out_ref[top:top + GROUP, :] = sum(ref[span, :] for ref in cross)
+            at += 1
+
+
+def sums(cross, gram, gram_other, pieces, order=None):
     height, depth = cross[0].shape
-    outs = [f32(len(cross) * height, depth)] if join else [f32(height // pieces, depth)] * pieces
-    kernel = join_kernel if join else lambda *refs: stage_kernel(len(cross), *refs)
-    gram, *outs = pl.pallas_call(
-        kernel,
-        out_shape=(f32(*gram.shape), *outs),
-        in_specs=[VMEM] * (len(cross) + 2),
-        out_specs=(VMEM,) * (1 + len(outs)),
-        compiler_params=pltpu.CompilerParams(vmem_limit_bytes=16 * 2**20),
-        cost_estimate=pl.CostEstimate(flops=10**6, bytes_accessed=10**6, transcendentals=0),
-        name="join" if join else "stage",
-    )(*cross, gram, gram_other)
+    order = order or tuple(range(height // GROUP))
+    outs = (f32(*gram.shape), *[f32(height // pieces, depth)] * pieces)
+    kernel = lambda *refs: sum_kernel(order, len(cross), *refs)
+    gram, *outs = call(kernel, "sums", outs, *cross, gram, gram_other)
     return gram, outs
 
 
-def factor_kernel(scale, keep_ref, other_ref, inverse_ref, flipped_ref, factor_ref, a_ref, packed_ref, buffer_ref):
+def weave_kernel(*refs):
+    *parts, out_ref = refs
+    for top in range(0, out_ref.shape[0], GROUP):
+        block = top // GROUP
+        at = block // len(parts) * GROUP
+        out_ref[top:top + GROUP, :] = parts[block % len(parts)][at:at + GROUP, :]
+
+
+def weave(parts, after=()):
+    height, depth = parts[0].shape
+    return call(weave_kernel, "weave", f32(len(parts) * height, depth), *parts, after=after)
+
+
+def first_half_kernel(keep_ref, other_ref, a_ref, factor_ref, norm_ref, packed_ref, buffer_ref):
     half = keep_ref.shape[0]
     core = core_bit()
     packed_ref[rows_of(core, half), :] = keep_ref[...]
@@ -258,23 +278,37 @@
     a_ref[:LANES, LANES:] = packed_ref[LANES:2 * LANES, :]
     a_ref[LANES:, :LANES] = jnp.zeros((LANES, LANES), jnp.float32)
     a_ref[LANES:, LANES:] = packed_ref[2 * LANES:, :]
-    inverse, grow = factorize(a_ref, factor_ref, buffer_ref)
+    shrink, grow = normalize(a_ref)
+    norm_ref[:GROUP, :] = jnp.broadcast_to(shrink, (GROUP, LANES))
+    norm_ref[GROUP:, :] = jnp.broadcast_to(grow, (GROUP, LANES))
+    eliminate(a_ref, factor_ref, buffer_ref, 0, a_ref.shape[0] // 2)
+
+
+def second_half_kernel(scale, from_ref, upper_ref, norm_ref, inverse_ref, flipped_ref, factor_ref, a_ref, buffer_ref):
+    size = a_ref.shape[0]
+    a_ref[...] = from_ref[...]
+    eliminate(a_ref, factor_ref, buffer_ref, size // 2, size)
+    shrink, grow = norm_ref[:1, :1], norm_ref[GROUP:GROUP + 1, :1] / scale
+    factor_ref[:size // 2, :] = upper_ref[:size // 2, :] * grow
+    factor_ref[size // 2:, :] = factor_ref[size // 2:, :] * grow
+    col = lax.broadcasted_iota(jnp.int32, (size, size), 1)
+    row = lax.broadcasted_iota(jnp.int32, (size, size), 0)
+    inverse = jnp.where(col <= row, a_ref[...], 0.0) * shrink
     inverse_ref[...] = inverse
     flipped_ref[...] = inverse.T * scale
-    factor_ref[...] = factor_ref[...] * (grow / scale)
-
-
-def factor(keep, other, size, scale):
-    return pl.pallas_call(
-        lambda *refs: factor_kernel(scale, *refs),
-        out_shape=(f32(size, size),) * 3,
-        in_specs=[VMEM] * 2,
-        out_specs=(VMEM,) * 3,
-        scratch_shapes=[pltpu.VMEM((size, size), jnp.float32), pltpu.VMEM((3 * LANES, LANES), jnp.float32), pltpu.VMEM((40 * GROUP, LANES), jnp.float32)],
-        compiler_params=pltpu.CompilerParams(vmem_limit_bytes=16 * 2**20),
-        cost_estimate=pl.CostEstimate(flops=10 * 10**9, bytes_accessed=2**20, transcendentals=size),
-        name="factor",
-    )(keep, other)
+
+
+def first_half(keep, other, size, after):
+    square = f32(size, size)
+    scratch = pltpu.VMEM((3 * LANES, LANES), jnp.float32), pltpu.VMEM((40 * GROUP, LANES), jnp.float32)
+    return call(first_half_kernel, "first_half", (square, square, f32(2 * GROUP, LANES)), keep, other, after=after, scratch=scratch, flops=5 * 10**9)
+
+
+def second_half(state, size, scale, after):
+    square = f32(size, size)
+    scratch = pltpu.VMEM((size, size), jnp.float32), pltpu.VMEM((40 * GROUP, LANES), jnp.float32)
+    kernel = lambda *refs: second_half_kernel(scale, *refs)
+    return call(kernel, "second_half", (square, square, square), *state, after=after, scratch=scratch, flops=5 * 10**9)
 
 
 def basis_kernel(sampled_ref, flipped_ref, basis_ref):
@@ -334,7 +368,7 @@
 
 CORE = (1, 0)
 PLANE = [(0, 1), (2, 0), (2, 1)]
-LINE = [(4, 0), (8, 0), (12, 0)]
+NEAR, FAR = (4, 0), (8, 0)
 
 
 def spare_bits():
@@ -348,31 +382,27 @@
     return [first] + [send(part, *mask) for part, mask in zip(rest, masks)]
 
 
-def sums_and_factors(keep, other, gram_keep, gram_other, factors):
+def per_device(features, sketch):
+    scale = (features.shape[0] * lax.axis_size(AXES)) ** 0.5
+    size = sketch.shape[1]
+    sampled, keep, other, gram, gram_other = local_terms(features, sketch)
     cross = [keep, send(other, *CORE)]
-    gram, parts = stage(cross, gram_keep, send(gram_other, *CORE), 4)
+    gram, parts = sums(cross, gram, send(gram_other, *CORE), 4)
     cross = spread(parts, PLANE)
-    gram = gram + send(gram, *LINE[0])
-    gram, parts = stage(cross, gram, send(gram, *LINE[1]), 4)
-    cross = spread(parts, LINE)
-    gram, (own,) = stage(cross, gram, send(gram, *PLANE[0]), 1)
+    gram = gram + send(gram, *NEAR)
+    gram, (keep, other) = sums(cross, gram, send(gram, *FAR), 2, (0, 2, 1, 3))
+    gram, (keep, other) = sums([keep, send(other, *NEAR)], gram, send(gram, *PLANE[0]), 2)
+    gram, (own,) = sums([keep, send(other, *FAR)], gram, send(gram, *PLANE[1]), 1)
     for mask in spare_bits():
         own = own + send(own, *mask)
         gram = gram + send(gram, *mask)
-    line = [own] + [send(own, *mask) for mask in LINE]
-    gram, (line,) = stage(line, gram, send(gram, *PLANE[1]), 1, join=True)
+    pair = weave([own, send(own, *FAR)])
+    state = first_half(gram, send(gram, *CORE), size, (pair,))
+    line = weave([pair, send(pair, *NEAR)], state[:1])
     plane = [line] + [send(line, *mask) for mask in PLANE]
-    factors = factors(gram, send(gram, *CORE))
-    return plane + [send(part, *CORE) for part in plane], factors
-
-
-def per_device(features, sketch):
-    scale = (features.shape[0] * lax.axis_size(AXES)) ** 0.5
-    size = sketch.shape[1]
-
-    sampled, *terms = local_terms(features, sketch)
-    cross, (inverse, flipped, upper) = sums_and_factors(*terms, lambda *halves: factor(*halves, size, scale))
-    return (basis_of(sampled, flipped), upper, project(inverse, cross))
+    inverse, flipped, factor = second_half(state, size, scale, (line,))
+    cross = plane + [send(part, *CORE) for part in plane]
+    return (basis_of(sampled, flipped), factor, project(inverse, cross))
 
 
 def solution(mesh):

time: 60.4 us -> 59.3 us (0.982)
  starting transfers between devices: 26.2 us -> 23 us
  waiting for transfers between devices: 13.6 us -> 16.3 us
  Pallas kernels: 19.8 us -> 19.1 us
    ppermute x23 -> x21, starting transfers between devices: 26.2 us -> 23 us  [send(): return lax.ppermute(value, AXES, pairs)]
    ppermute x23 -> x21, waiting for transfers between devices: 13.6 us -> 16.3 us  [send(): return lax.ppermute(value, AXES, pairs)]
    pallas_call x1, Pallas kernels: 8.96 us -> 8.34 us  [local_terms(): pl.pallas_call(local_kernel, out_shape=(f32(rows, rank), f32(rank // 2, d...]
    pallas_call x5 -> x8, Pallas kernels: 7.6 us -> 7.57 us  [call(): pl.pallas_call(lambda *refs: kernel(*refs[:len(operands)], *refs[len(oper...]
  transfers between devices with their start and end apart: 23 -> 21, of which waited for: 8 -> 8; matrix products, arithmetic and copies ran while one was open for 0% -> 0% of each run, Pallas kernels for 15% -> 15%
where the time goes in v10:
time: 59.3 us; the launch traced here: 59.1 us
  starting transfers between devices  23 us (39%)
  Pallas kernels  19.1 us (32%)
  waiting for transfers between devices  16.3 us (27%)
  between operations  0.72 us (1%)
    ppermute x21, starting transfers between devices, send(): return lax.ppermute(value, AXES, pairs)  23 us
    ppermute x21, waiting for transfers between devices, send(): return lax.ppermute(value, AXES, pairs)  16.3 us
    pallas_call x1, Pallas kernels, local_terms(): pl.pallas_call(local_kernel, out_shape=(f32(rows, rank), f32(rank // 2, d...  8.34 us
    pallas_call x8, Pallas kernels, call(): pl.pallas_call(lambda *refs: kernel(*refs[:len(operands)], *refs[len(oper...  7.57 us
    pallas_call x1, Pallas kernels, project(): pl.pallas_call(project_kernel, out_shape=jax.ShapeDtypeStruct((rank, dept...  1.65 us
    pallas_call x1, Pallas kernels, basis_of(): pl.pallas_call(basis_kernel, out_shape=f32(*sampled.shape), in_specs=[VME...  1.56 us
  transfers between devices with their start and end apart: 21, of which 8 were waited for; matrix products, arithmetic and copies ran while one was open for 0% of the time, Pallas kernels for 15%

profile of v10, /device:TPU:0, one launch (start us, length us, event | category | flops | bytes accessed | tf_op | source)
XLA Modules:
  0.0 59.1 jit_solution(10325513919181420832)
XLA Ops:
  0.6 8.3 %local_terms.1 = (f32[1024,256]{1,0:T(8,128)S(1)}, f32[128,1024]{1,0:T(8,128)S(1)}, f32[128,1024]{1,0:T(8,128)S(1)}, f32[192,128]{1,0:T(8,128)S(1)}, f32[192,128]{1,0:T(8,128)S(1)}) custom-call(f32[1024,1024]{1,0:T(8,128)} %features_hbm.1, f32[1024,256]{1,0:T(8,128)} %sketch_hbm.1), custom_call_target="tpu_custom_call" | custom-call | flops 4000000000 | bytes 8388608 | tf_op jit(solution)/shard_map/local_terms/pallas_call | solution.py:208
  9.0 0.5 collective-permute-start
  9.5 0.1 collective-permute-start.1
  9.6 1.6 %collective-permute-done.1.refs_3_ = f32[192,128]{1,0:T(8,128)S(1)} collective-permute-done((f32[192,128]{1,0:T(8,128)S(1)}, f32[192,128]{1,0:T(8,128)S(1)}, u32[]{:S(2)}, u32[]{:S(2)}) %collective-permute-start.1) | collective-permute-done | bytes 98336 | tf_op jit(solution)/shard_map/ppermute | solution.py:366
  11.2 0.0 collective-permute-done.refs_1_
  11.2 0.1 sums.4
  11.2 3.0 %collective-permute-start.5 = (f32[192,128]{1,0:T(8,128)S(1)}, f32[192,128]{1,0:T(8,128)S(1)}, u32[]{:S(2)}, u32[]{:S(2)}) collective-permute-start(f32[192,128]{1,0:T(8,128)S(1)} %get-tuple-element.36), channel_id=1, source_target_pairs={{0,8},{1,9},{2,10},{3,11},{4,12},{5,13},{6,14},{7,15},{8,0},{9,1},... | collective-permute-start | bytes 294920 | tf_op jit(solution)/shard_map/ppermute | solution.py:366
  14.3 1.5 %collective-permute-start.2 = (f32[32,1024]{1,0:T(8,128)S(1)}, f32[32,1024]{1,0:T(8,128)S(1)}, u32[]{:S(2)}, u32[]{:S(2)}) collective-permute-start(f32[32,1024]{1,0:T(8,128)S(1)} %get-tuple-element.33), channel_id=1, source_target_pairs={{0,1},{1,0},{2,3},{3,2},{4,5},{5,4},{6,7},{7,6},{8,9},{9,8},{10,11... | collective-permute-start | bytes 393224 | tf_op jit(solution)/shard_map/ppermute | solution.py:366
  15.8 1.5 %collective-permute-start.3 = (f32[32,1024]{1,0:T(8,128)S(1)}, f32[32,1024]{1,0:T(8,128)S(1)}, u32[]{:S(2)}, u32[]{:S(2)}) collective-permute-start(f32[32,1024]{1,0:T(8,128)S(1)} %get-tuple-element.34), channel_id=1, source_target_pairs={{0,4},{1,5},{2,6},{3,7},{4,0},{5,1},{6,2},{7,3},{8,12},{9,13},{10,... | collective-permute-start | bytes 393224 | tf_op jit(solution)/shard_map/ppermute | solution.py:366
  17.3 0.5 collective-permute-start.4
  17.7 0.0 collective-permute-done.5
  17.8 2.7 %collective-permute-start.6 = (f32[192,128]{1,0:T(8,128)S(1)}, f32[192,128]{1,0:T(8,128)S(1)}, u32[]{:S(2)}, u32[]{:S(2)}) collective-permute-start(f32[192,128]{1,0:T(8,128)S(1)} %add.3.refs_4_), channel_id=1, source_target_pairs={{0,16},{1,17},{2,18},{3,19},{4,20},{5,21},{6,22},{7,23},{8,24},{9,... | collective-permute-start | bytes 294920 | tf_op jit(solution)/shard_map/ppermute | solution.py:366
  20.4 0.0 collective-permute-done.2.refs_1_
  20.4 1.7 %collective-permute-done.3.refs_2_ = f32[32,1024]{1,0:T(8,128)S(1)} collective-permute-done((f32[32,1024]{1,0:T(8,128)S(1)}, f32[32,1024]{1,0:T(8,128)S(1)}, u32[]{:S(2)}, u32[]{:S(2)}) %collective-permute-start.3) | collective-permute-done | bytes 131104 | tf_op jit(solution)/shard_map/ppermute | solution.py:366
  22.2 1.3 %collective-permute-done.4.refs_3_ = f32[32,1024]{1,0:T(8,128)S(1)} collective-permute-done((f32[32,1024]{1,0:T(8,128)S(1)}, f32[32,1024]{1,0:T(8,128)S(1)}, u32[]{:S(2)}, u32[]{:S(2)}) %collective-permute-start.4) | collective-permute-done | bytes 131104 | tf_op jit(solution)/shard_map/ppermute | solution.py:366
  23.5 1.3 %collective-permute-done.6.refs_5_ = f32[192,128]{1,0:T(8,128)S(1)} collective-permute-done((f32[192,128]{1,0:T(8,128)S(1)}, f32[192,128]{1,0:T(8,128)S(1)}, u32[]{:S(2)}, u32[]{:S(2)}) %collective-permute-start.6) | collective-permute-done | bytes 98336 | tf_op jit(solution)/shard_map/ppermute | solution.py:366
  24.8 1.4 %collective-permute-start.8 = (f32[192,128]{1,0:T(8,128)S(1)}, f32[192,128]{1,0:T(8,128)S(1)}, u32[]{:S(2)}, u32[]{:S(2)}) collective-permute-start(f32[192,128]{1,0:T(8,128)S(1)} %get-tuple-element.39.refs_2_), channel_id=1, source_target_pairs={{0,1},{1,0},{2,3},{3,2},{4,5},{5,4},{6,7},{7,6},{8,9},{9,8},{10,11... | collective-permute-start | bytes 294920 | tf_op jit(solution)/shard_map/ppermute | solution.py:366
  26.2 0.7 %collective-permute-start.7 = (f32[16,1024]{1,0:T(8,128)S(1)}, f32[16,1024]{1,0:T(8,128)S(1)}, u32[]{:S(2)}, u32[]{:S(2)}) collective-permute-start(f32[16,1024]{1,0:T(8,128)S(1)} %get-tuple-element.38), channel_id=1, source_target_pairs={{0,8},{1,9},{2,10},{3,11},{4,12},{5,13},{6,14},{7,15},{8,0},{9,1},... | collective-permute-start | bytes 196616 | tf_op jit(solution)/shard_map/ppermute | solution.py:366
  26.9 3.6 %collective-permute-done.7.refs_1_ = f32[16,1024]{1,0:T(8,128)S(1)} collective-permute-done((f32[16,1024]{1,0:T(8,128)S(1)}, f32[16,1024]{1,0:T(8,128)S(1)}, u32[]{:S(2)}, u32[]{:S(2)}) %collective-permute-start.7) | collective-permute-done | bytes 65568 | tf_op jit(solution)/shard_map/ppermute | solution.py:366
  30.5 0.0 collective-permute-done.8.refs_3_
  30.5 1.6 %collective-permute-start.10 = (f32[192,128]{1,0:T(8,128)S(1)}, f32[192,128]{1,0:T(8,128)S(1)}, u32[]{:S(2)}, u32[]{:S(2)}) collective-permute-start(f32[192,128]{1,0:T(8,128)S(1)} %get-tuple-element.42.refs_2_), channel_id=1, source_target_pairs={{0,4},{1,5},{2,6},{3,7},{4,0},{5,1},{6,2},{7,3},{8,12},{9,13},{10,... | collective-permute-start | bytes 294920 | tf_op jit(solution)/shard_map/ppermute | solution.py:366
  32.1 2.0 %collective-permute-start.9 = (f32[8,1024]{1,0:T(8,128)S(1)}, f32[8,1024]{1,0:T(8,128)S(1)}, u32[]{:S(2)}, u32[]{:S(2)}) collective-permute-start(f32[8,1024]{1,0:T(8,128)S(1)} %get-tuple-element.41), channel_id=1, source_target_pairs={{0,16},{1,17},{2,18},{3,19},{4,20},{5,21},{6,22},{7,23},{8,24},{9,... | collective-permute-start | bytes 98312 | tf_op jit(solution)/shard_map/ppermute | solution.py:366
  34.1 2.8 %collective-permute-done.9.refs_1_ = f32[8,1024]{1,0:T(8,128)S(1)} collective-permute-done((f32[8,1024]{1,0:T(8,128)S(1)}, f32[8,1024]{1,0:T(8,128)S(1)}, u32[]{:S(2)}, u32[]{:S(2)}) %collective-permute-start.9) | collective-permute-done | bytes 32800 | tf_op jit(solution)/shard_map/ppermute | solution.py:366
  36.9 0.0 collective-permute-done.10.refs_3_
  36.9 0.1 collective-permute-start.11
  37.0 2.1 %collective-permute-start.12 = (f32[8,1024]{1,0:T(8,128)S(1)}, f32[8,1024]{1,0:T(8,128)S(1)}, u32[]{:S(2)}, u32[]{:S(2)}) collective-permute-start(f32[8,1024]{1,0:T(8,128)S(1)} %get-tuple-element.44.refs_0_), channel_id=1, source_target_pairs={{0,16},{1,17},{2,18},{3,19},{4,20},{5,21},{6,22},{7,23},{8,24},{9,... | collective-permute-start | bytes 98312 | tf_op jit(solution)/shard_map/ppermute | solution.py:366
  39.1 2.8 %collective-permute-done.12.refs_1_ = f32[8,1024]{1,0:T(8,128)S(1)} collective-permute-done((f32[8,1024]{1,0:T(8,128)S(1)}, f32[8,1024]{1,0:T(8,128)S(1)}, u32[]{:S(2)}, u32[]{:S(2)}) %collective-permute-start.12) | collective-permute-done | bytes 32800 | tf_op jit(solution)/shard_map/ppermute | solution.py:366
  41.9 1.3 %collective-permute-start.13 = (f32[16,1024]{1,0:T(8,128)S(1)}, f32[16,1024]{1,0:T(8,128)S(1)}, u32[]{:S(2)}, u32[]{:S(2)}) collective-permute-start(f32[16,1024]{1,0:T(8,128)S(1)} %weave.2.refs_2_.refs_0_), channel_id=1, source_target_pairs={{0,8},{1,9},{2,10},{3,11},{4,12},{5,13},{6,14},{7,15},{8,0},{9,1},... | collective-permute-start | bytes 196616 | tf_op jit(solution)/shard_map/ppermute | solution.py:366
  43.2 0.0 collective-permute-done.11.refs_1_
  43.2 3.7 %first_half.1 = (f32[256,256]{1,0:T(8,128)S(1)}, f32[256,256]{1,0:T(8,128)S(1)}, f32[16,128]{1,0:T(8,128)S(1)}) custom-call(f32[192,128]{1,0:T(8,128)S(1)} %get-tuple-element.43.refs_0_, f32[192,128]{1,0:T(8,128)S(1)} %collective-permute-done.11.refs_1_, f32[16,1024]{1,0:T(8,128)S(1)} %weave.2.refs_2_.refs_0_), custom_call_target="tpu_custom_call" | custom-call | flops 5000000000 | bytes 1000000 | tf_op jit(solution)/shard_map/first_half/pallas_call | solution.py:227
  46.9 0.0 collective-permute-done.13.refs_1_
  46.9 0.6 collective-permute-start.14
  47.5 0.7 %collective-permute-start.15 = (f32[32,1024]{1,0:T(8,128)S(1)}, f32[32,1024]{1,0:T(8,128)S(1)}, u32[]{:S(2)}, u32[]{:S(2)}) collective-permute-start(f32[32,1024]{1,0:T(8,128)S(1)} %weave.3.refs_3_.refs_0_), channel_id=1, source_target_pairs={{0,4},{1,5},{2,6},{3,7},{4,0},{5,1},{6,2},{7,3},{8,12},{9,13},{10,... | collective-permute-start | bytes 393224 | tf_op jit(solution)/shard_map/ppermute | solution.py:366
  48.1 2.3 %collective-permute-start.16 = (f32[32,1024]{1,0:T(8,128)S(1)}, f32[32,1024]{1,0:T(8,128)S(1)}, u32[]{:S(2)}, u32[]{:S(2)}) collective-permute-start(f32[32,1024]{1,0:T(8,128)S(1)} %weave.3.refs_3_.refs_0_), channel_id=1, source_target_pairs={{0,5},{1,4},{2,7},{3,6},{4,1},{5,0},{6,3},{7,2},{8,13},{9,12},{10,... | collective-permute-start | bytes 393224 | tf_op jit(solution)/shard_map/ppermute | solution.py:366
  50.5 0.0 collective-permute-start.17
  50.5 3.7 %second_half.1 = (f32[256,256]{1,0:T(8,128)S(1)}, f32[256,256]{1,0:T(8,128)S(1)}, f32[256,256]{1,0:T(8,128)}) custom-call(f32[256,256]{1,0:T(8,128)S(1)} %get-tuple-element.45.refs_2_.refs_0_, f32[256,256]{1,0:T(8,128)S(1)} %get-tuple-element.46.refs_1_, f32[16,128]{1,0:T(8,128)S(1)} %get-tuple-element.47.refs_2_, f32[32,1024]{1,0:T(8,128)S(1)} %weave.3.refs_3_.refs_0_), custom_call_target="tpu_custom_call" | custom-call | flops 5000000000 | bytes 1000000 | tf_op jit(solution)/shard_map/second_half/pallas_call | solution.py:227
  54.2 0.0 collective-permute-done.14.refs_1_
  54.2 0.5 collective-permute-start.18
  54.7 0.0 collective-permute-done.15.refs_2_
  54.7 0.1 collective-permute-start.19
  54.8 1.1 %collective-permute-done.16.refs_3_ = f32[32,1024]{1,0:T(8,128)S(1)} collective-permute-done((f32[32,1024]{1,0:T(8,128)S(1)}, f32[32,1024]{1,0:T(8,128)S(1)}, u32[]{:S(2)}, u32[]{:S(2)}) %collective-permute-start.16) | collective-permute-done | bytes 131104 | tf_op jit(solution)/shard_map/ppermute | solution.py:366
  55.9 0.0 collective-permute-start.20
  55.9 1.6 %basis.1 = f32[1024,256]{1,0:T(8,128)} custom-call(f32[1024,256]{1,0:T(8,128)S(1)} %get-tuple-element.27.sampled_ref, f32[256,256]{1,0:T(8,128)S(1)} %get-tuple-element.48.flipped_ref), custom_call_target="tpu_custom_call" | custom-call | flops 2000000000 | bytes 2097152 | tf_op jit(solution)/shard_map/basis/pallas_call | solution.py:322
  57.5 0.0 collective-permute-done.17.refs_4_
  57.5 0.0 collective-permute-done.18.refs_5_
  57.5 0.0 collective-permute-done.19.refs_6_
  57.5 0.0 collective-permute-done.20.refs_7_
  57.5 1.7 %project.1 = f32[256,1024]{1,0:T(8,128)} custom-call(f32[256,256]{1,0:T(8,128)S(1)} %get-tuple-element.50.inverse_ref, f32[32,1024]{1,0:T(8,128)S(1)} %weave.3.refs_3_.refs_0_, f32[32,1024]{1,0:T(8,128)S(1)} %collective-permute-done.14.refs_1_, f32[32,1024]{1,0:T(8,128)S(1)} %collective-permute-done.15.refs_2_, ...), custom_call_target="tpu_custom_call" | custom-call | flops 400000000 | bytes 2097152 | tf_op jit(solution)/shard_map/project/pallas_call | solution.py:351
  (6 shorter events, 0.1 us)
Async XLA Ops:
  9.0 2.2 %collective-permute-start = (f32[128,1024]{1,0:T(8,128)S(1)}, f32[128,1024]{1,0:T(8,128)S(1)}, u32[]{:S(2)}, u32[]{:S(2)}) collective-permute-start(f32[128,1024]{1,0:T(8,128)S(1)} %get-tuple-element.29), channel_id=1, source_target_pairs={{0,2},{1,3},{2,0},{3,1},{4,6},{5,7},{6,4},{7,5},{8,10},{9,11},{10,... | collective-permute-start | bytes 1572872 | tf_op jit(solution)/shard_map/ppermute | solution.py:366
  9.5 1.7 %collective-permute-start.1 = (f32[192,128]{1,0:T(8,128)S(1)}, f32[192,128]{1,0:T(8,128)S(1)}, u32[]{:S(2)}, u32[]{:S(2)}) collective-permute-start(f32[192,128]{1,0:T(8,128)S(1)} %get-tuple-element.31), channel_id=1, source_target_pairs={{0,2},{1,3},{2,0},{3,1},{4,6},{5,7},{6,4},{7,5},{8,10},{9,11},{10,... | collective-permute-start | bytes 294920 | tf_op jit(solution)/shard_map/ppermute | solution.py:366
  11.2 6.5 %collective-permute-start.5 = (f32[192,128]{1,0:T(8,128)S(1)}, f32[192,128]{1,0:T(8,128)S(1)}, u32[]{:S(2)}, u32[]{:S(2)}) collective-permute-start(f32[192,128]{1,0:T(8,128)S(1)} %get-tuple-element.36), channel_id=1, source_target_pairs={{0,8},{1,9},{2,10},{3,11},{4,12},{5,13},{6,14},{7,15},{8,0},{9,1},... | collective-permute-start | bytes 294920 | tf_op jit(solution)/shard_map/ppermute | solution.py:366
  14.3 6.2 %collective-permute-start.2 = (f32[32,1024]{1,0:T(8,128)S(1)}, f32[32,1024]{1,0:T(8,128)S(1)}, u32[]{:S(2)}, u32[]{:S(2)}) collective-permute-start(f32[32,1024]{1,0:T(8,128)S(1)} %get-tuple-element.33), channel_id=1, source_target_pairs={{0,1},{1,0},{2,3},{3,2},{4,5},{5,4},{6,7},{7,6},{8,9},{9,8},{10,11... | collective-permute-start | bytes 393224 | tf_op jit(solution)/shard_map/ppermute | solution.py:366
  15.8 6.4 %collective-permute-start.3 = (f32[32,1024]{1,0:T(8,128)S(1)}, f32[32,1024]{1,0:T(8,128)S(1)}, u32[]{:S(2)}, u32[]{:S(2)}) collective-permute-start(f32[32,1024]{1,0:T(8,128)S(1)} %get-tuple-element.34), channel_id=1, source_target_pairs={{0,4},{1,5},{2,6},{3,7},{4,0},{5,1},{6,2},{7,3},{8,12},{9,13},{10,... | collective-permute-start | bytes 393224 | tf_op jit(solution)/shard_map/ppermute | solution.py:366
  17.3 6.2 %collective-permute-start.4 = (f32[32,1024]{1,0:T(8,128)S(1)}, f32[32,1024]{1,0:T(8,128)S(1)}, u32[]{:S(2)}, u32[]{:S(2)}) collective-permute-start(f32[32,1024]{1,0:T(8,128)S(1)} %get-tuple-element.35), channel_id=1, source_target_pairs={{0,5},{1,4},{2,7},{3,6},{4,1},{5,0},{6,3},{7,2},{8,13},{9,12},{10,... | collective-permute-start | bytes 393224 | tf_op jit(solution)/shard_map/ppermute | solution.py:366
  17.8 7.0 %collective-permute-start.6 = (f32[192,128]{1,0:T(8,128)S(1)}, f32[192,128]{1,0:T(8,128)S(1)}, u32[]{:S(2)}, u32[]{:S(2)}) collective-permute-start(f32[192,128]{1,0:T(8,128)S(1)} %add.3.refs_4_), channel_id=1, source_target_pairs={{0,16},{1,17},{2,18},{3,19},{4,20},{5,21},{6,22},{7,23},{8,24},{9,... | collective-permute-start | bytes 294920 | tf_op jit(solution)/shard_map/ppermute | solution.py:366
  24.8 5.7 %collective-permute-start.8 = (f32[192,128]{1,0:T(8,128)S(1)}, f32[192,128]{1,0:T(8,128)S(1)}, u32[]{:S(2)}, u32[]{:S(2)}) collective-permute-start(f32[192,128]{1,0:T(8,128)S(1)} %get-tuple-element.39.refs_2_), channel_id=1, source_target_pairs={{0,1},{1,0},{2,3},{3,2},{4,5},{5,4},{6,7},{7,6},{8,9},{9,8},{10,11... | collective-permute-start | bytes 294920 | tf_op jit(solution)/shard_map/ppermute | solution.py:366
  26.2 4.3 %collective-permute-start.7 = (f32[16,1024]{1,0:T(8,128)S(1)}, f32[16,1024]{1,0:T(8,128)S(1)}, u32[]{:S(2)}, u32[]{:S(2)}) collective-permute-start(f32[16,1024]{1,0:T(8,128)S(1)} %get-tuple-element.38), channel_id=1, source_target_pairs={{0,8},{1,9},{2,10},{3,11},{4,12},{5,13},{6,14},{7,15},{8,0},{9,1},... | collective-permute-start | bytes 196616 | tf_op jit(solution)/shard_map/ppermute | solution.py:366
  30.5 6.4 %collective-permute-start.10 = (f32[192,128]{1,0:T(8,128)S(1)}, f32[192,128]{1,0:T(8,128)S(1)}, u32[]{:S(2)}, u32[]{:S(2)}) collective-permute-start(f32[192,128]{1,0:T(8,128)S(1)} %get-tuple-element.42.refs_2_), channel_id=1, source_target_pairs={{0,4},{1,5},{2,6},{3,7},{4,0},{5,1},{6,2},{7,3},{8,12},{9,13},{10,... | collective-permute-start | bytes 294920 | tf_op jit(solution)/shard_map/ppermute | solution.py:366
  32.1 4.8 %collective-permute-start.9 = (f32[8,1024]{1,0:T(8,128)S(1)}, f32[8,1024]{1,0:T(8,128)S(1)}, u32[]{:S(2)}, u32[]{:S(2)}) collective-permute-start(f32[8,1024]{1,0:T(8,128)S(1)} %get-tuple-element.41), channel_id=1, source_target_pairs={{0,16},{1,17},{2,18},{3,19},{4,20},{5,21},{6,22},{7,23},{8,24},{9,... | collective-permute-start | bytes 98312 | tf_op jit(solution)/shard_map/ppermute | solution.py:366
  36.9 6.2 %collective-permute-start.11 = (f32[192,128]{1,0:T(8,128)S(1)}, f32[192,128]{1,0:T(8,128)S(1)}, u32[]{:S(2)}, u32[]{:S(2)}) collective-permute-start(f32[192,128]{1,0:T(8,128)S(1)} %get-tuple-element.43.refs_0_), channel_id=1, source_target_pairs={{0,2},{1,3},{2,0},{3,1},{4,6},{5,7},{6,4},{7,5},{8,10},{9,11},{10,... | collective-permute-start | bytes 294920 | tf_op jit(solution)/shard_map/ppermute | solution.py:366
  37.0 4.9 %collective-permute-start.12 = (f32[8,1024]{1,0:T(8,128)S(1)}, f32[8,1024]{1,0:T(8,128)S(1)}, u32[]{:S(2)}, u32[]{:S(2)}) collective-permute-start(f32[8,1024]{1,0:T(8,128)S(1)} %get-tuple-element.44.refs_0_), channel_id=1, source_target_pairs={{0,16},{1,17},{2,18},{3,19},{4,20},{5,21},{6,22},{7,23},{8,24},{9,... | collective-permute-start | bytes 98312 | tf_op jit(solution)/shard_map/ppermute | solution.py:366
  41.9 5.0 %collective-permute-start.13 = (f32[16,1024]{1,0:T(8,128)S(1)}, f32[16,1024]{1,0:T(8,128)S(1)}, u32[]{:S(2)}, u32[]{:S(2)}) collective-permute-start(f32[16,1024]{1,0:T(8,128)S(1)} %weave.2.refs_2_.refs_0_), channel_id=1, source_target_pairs={{0,8},{1,9},{2,10},{3,11},{4,12},{5,13},{6,14},{7,15},{8,0},{9,1},... | collective-permute-start | bytes 196616 | tf_op jit(solution)/shard_map/ppermute | solution.py:366
  46.9 7.3 %collective-permute-start.14 = (f32[32,1024]{1,0:T(8,128)S(1)}, f32[32,1024]{1,0:T(8,128)S(1)}, u32[]{:S(2)}, u32[]{:S(2)}) collective-permute-start(f32[32,1024]{1,0:T(8,128)S(1)} %weave.3.refs_3_.refs_0_), channel_id=1, source_target_pairs={{0,1},{1,0},{2,3},{3,2},{4,5},{5,4},{6,7},{7,6},{8,9},{9,8},{10,11... | collective-permute-start | bytes 393224 | tf_op jit(solution)/shard_map/ppermute | solution.py:366
  47.5 7.2 %collective-permute-start.15 = (f32[32,1024]{1,0:T(8,128)S(1)}, f32[32,1024]{1,0:T(8,128)S(1)}, u32[]{:S(2)}, u32[]{:S(2)}) collective-permute-start(f32[32,1024]{1,0:T(8,128)S(1)} %weave.3.refs_3_.refs_0_), channel_id=1, source_target_pairs={{0,4},{1,5},{2,6},{3,7},{4,0},{5,1},{6,2},{7,3},{8,12},{9,13},{10,... | collective-permute-start | bytes 393224 | tf_op jit(solution)/shard_map/ppermute | solution.py:366
  48.1 7.8 %collective-permute-start.16 = (f32[32,1024]{1,0:T(8,128)S(1)}, f32[32,1024]{1,0:T(8,128)S(1)}, u32[]{:S(2)}, u32[]{:S(2)}) collective-permute-start(f32[32,1024]{1,0:T(8,128)S(1)} %weave.3.refs_3_.refs_0_), channel_id=1, source_target_pairs={{0,5},{1,4},{2,7},{3,6},{4,1},{5,0},{6,3},{7,2},{8,13},{9,12},{10,... | collective-permute-start | bytes 393224 | tf_op jit(solution)/shard_map/ppermute | solution.py:366
  50.5 7.0 %collective-permute-start.17 = (f32[32,1024]{1,0:T(8,128)S(1)}, f32[32,1024]{1,0:T(8,128)S(1)}, u32[]{:S(2)}, u32[]{:S(2)}) collective-permute-start(f32[32,1024]{1,0:T(8,128)S(1)} %weave.3.refs_3_.refs_0_), channel_id=1, source_target_pairs={{0,2},{1,3},{2,0},{3,1},{4,6},{5,7},{6,4},{7,5},{8,10},{9,11},{10,... | collective-permute-start | bytes 393224 | tf_op jit(solution)/shard_map/ppermute | solution.py:366
  54.2 3.3 %collective-permute-start.18 = (f32[32,1024]{1,0:T(8,128)S(1)}, f32[32,1024]{1,0:T(8,128)S(1)}, u32[]{:S(2)}, u32[]{:S(2)}) collective-permute-start(f32[32,1024]{1,0:T(8,128)S(1)} %collective-permute-done.14.refs_1_), channel_id=1, source_target_pairs={{0,2},{1,3},{2,0},{3,1},{4,6},{5,7},{6,4},{7,5},{8,10},{9,11},{10,... | collective-permute-start | bytes 393224 | tf_op jit(solution)/shard_map/ppermute | solution.py:366
  54.7 2.8 %collective-permute-start.19 = (f32[32,1024]{1,0:T(8,128)S(1)}, f32[32,1024]{1,0:T(8,128)S(1)}, u32[]{:S(2)}, u32[]{:S(2)}) collective-permute-start(f32[32,1024]{1,0:T(8,128)S(1)} %collective-permute-done.15.refs_2_), channel_id=1, source_target_pairs={{0,2},{1,3},{2,0},{3,1},{4,6},{5,7},{6,4},{7,5},{8,10},{9,11},{10,... | collective-permute-start | bytes 393224 | tf_op jit(solution)/shard_map/ppermute | solution.py:366
  55.9 1.6 %collective-permute-start.20 = (f32[32,1024]{1,0:T(8,128)S(1)}, f32[32,1024]{1,0:T(8,128)S(1)}, u32[]{:S(2)}, u32[]{:S(2)}) collective-permute-start(f32[32,1024]{1,0:T(8,128)S(1)} %collective-permute-done.16.refs_3_), channel_id=1, source_target_pairs={{0,2},{1,3},{2,0},{3,1},{4,6},{5,7},{6,4},{7,5},{8,10},{9,11},{10,... | collective-permute-start | bytes 393224 | tf_op jit(solution)/shard_map/ppermute | solution.py:366

commit v11 on v10

--- a/solution.py
+++ b/solution.py
@@ -236,40 +236,32 @@
     )(*operands, *after)
 
 
-def sum_kernel(order, terms, *refs):
-    cross, (gram_ref, gram_other_ref), outs = refs[:terms], refs[terms:terms + 2], refs[terms + 2:]
-    outs[0][...] = gram_ref[...] + gram_other_ref[...]
+def sum_kernel(masks, *refs):
+    cross, outs = refs[:len(masks)], refs[len(masks):]
     at = 0
-    for out_ref in outs[1:]:
+    for out_ref in outs:
         for top in range(0, out_ref.shape[0], GROUP):
-            span = slice(order[at] * GROUP, (order[at] + 1) * GROUP)
-            out_ref[top:top + GROUP, :] = sum(ref[span, :] for ref in cross)
+            blocks = [ref[(at ^ mask) * GROUP:(at ^ mask) * GROUP + GROUP, :] for ref, mask in zip(cross, masks)]
+            out_ref[top:top + GROUP, :] = sum(blocks)
             at += 1
 
 
-def sums(cross, gram, gram_other, pieces, order=None):
+def sums(cross, pieces=1, masks=None, after=()):
     height, depth = cross[0].shape
-    order = order or tuple(range(height // GROUP))
-    outs = (f32(*gram.shape), *[f32(height // pieces, depth)] * pieces)
-    kernel = lambda *refs: sum_kernel(order, len(cross), *refs)
-    gram, *outs = call(kernel, "sums", outs, *cross, gram, gram_other)
-    return gram, outs
-
-
-def weave_kernel(*refs):
-    *parts, out_ref = refs
-    for top in range(0, out_ref.shape[0], GROUP):
-        block = top // GROUP
-        at = block // len(parts) * GROUP
-        out_ref[top:top + GROUP, :] = parts[block % len(parts)][at:at + GROUP, :]
-
-
-def weave(parts, after=()):
-    height, depth = parts[0].shape
-    return call(weave_kernel, "weave", f32(len(parts) * height, depth), *parts, after=after)
-
-
-def first_half_kernel(keep_ref, other_ref, a_ref, factor_ref, norm_ref, packed_ref, buffer_ref):
+    masks = masks or (0,) * len(cross)
+    outs = (f32(height // pieces, depth),) * pieces
+    return call(lambda *refs: sum_kernel(masks, *refs), "sums", outs, *cross, after=after)
+
+
+def add_kernel(left_ref, right_ref, out_ref):
+    out_ref[...] = left_ref[...] + right_ref[...]
+
+
+def add(left, right, after):
+    return call(add_kernel, "add", f32(*left.shape), left, right, after=after)
+
+
+def first_part_kernel(keep_ref, other_ref, a_ref, factor_ref, norm_ref, packed_ref, buffer_ref):
     half = keep_ref.shape[0]
     core = core_bit()
     packed_ref[rows_of(core, half), :] = keep_ref[...]
@@ -281,16 +273,22 @@
     shrink, grow = normalize(a_ref)
     norm_ref[:GROUP, :] = jnp.broadcast_to(shrink, (GROUP, LANES))
     norm_ref[GROUP:, :] = jnp.broadcast_to(grow, (GROUP, LANES))
-    eliminate(a_ref, factor_ref, buffer_ref, 0, a_ref.shape[0] // 2)
-
-
-def second_half_kernel(scale, from_ref, upper_ref, norm_ref, inverse_ref, flipped_ref, factor_ref, a_ref, buffer_ref):
+    eliminate(a_ref, factor_ref, buffer_ref, 0, PANEL)
+
+
+def middle_part_kernel(first, from_ref, upper_ref, a_ref, factor_ref, buffer_ref):
+    a_ref[...] = from_ref[...]
+    factor_ref[:first, :] = upper_ref[:first, :]
+    eliminate(a_ref, factor_ref, buffer_ref, first, first + PANEL)
+
+
+def last_part_kernel(scale, first, from_ref, upper_ref, norm_ref, inverse_ref, flipped_ref, factor_ref, a_ref, buffer_ref):
     size = a_ref.shape[0]
     a_ref[...] = from_ref[...]
-    eliminate(a_ref, factor_ref, buffer_ref, size // 2, size)
+    eliminate(a_ref, factor_ref, buffer_ref, first, size)
     shrink, grow = norm_ref[:1, :1], norm_ref[GROUP:GROUP + 1, :1] / scale
-    factor_ref[:size // 2, :] = upper_ref[:size // 2, :] * grow
-    factor_ref[size // 2:, :] = factor_ref[size // 2:, :] * grow
+    factor_ref[:first, :] = upper_ref[:first, :] * grow
+    factor_ref[first:, :] = factor_ref[first:, :] * grow
     col = lax.broadcasted_iota(jnp.int32, (size, size), 1)
     row = lax.broadcasted_iota(jnp.int32, (size, size), 0)
     inverse = jnp.where(col <= row, a_ref[...], 0.0) * shrink
@@ -298,17 +296,23 @@
     flipped_ref[...] = inverse.T * scale
 
 
-def first_half(keep, other, size, after):
-    square = f32(size, size)
-    scratch = pltpu.VMEM((3 * LANES, LANES), jnp.float32), pltpu.VMEM((40 * GROUP, LANES), jnp.float32)
-    return call(first_half_kernel, "first_half", (square, square, f32(2 * GROUP, LANES)), keep, other, after=after, scratch=scratch, flops=5 * 10**9)
-
-
-def second_half(state, size, scale, after):
-    square = f32(size, size)
-    scratch = pltpu.VMEM((size, size), jnp.float32), pltpu.VMEM((40 * GROUP, LANES), jnp.float32)
-    kernel = lambda *refs: second_half_kernel(scale, *refs)
-    return call(kernel, "second_half", (square, square, square), *state, after=after, scratch=scratch, flops=5 * 10**9)
+def buffers(*shapes):
+    return [pltpu.VMEM(shape, jnp.float32) for shape in (*shapes, (40 * GROUP, LANES))]
+
+
+def first_part(keep, other, size, after):
+    outs = f32(size, size), f32(size, size), f32(2 * GROUP, LANES)
+    return call(first_part_kernel, "first_part", outs, keep, other, after=after, scratch=buffers((3 * LANES, LANES)), flops=10**6)
+
+
+def middle_part(state, size, first, after):
+    kernel = lambda *refs: middle_part_kernel(first, *refs)
+    return call(kernel, "middle_part", (f32(size, size),) * 2, *state, after=after, scratch=buffers(), flops=3 * 10**9)
+
+
+def last_part(state, size, scale, first, after):
+    kernel = lambda *refs: last_part_kernel(scale, first, *refs)
+    return call(kernel, "last_part", (f32(size, size),) * 3, *state, after=after, scratch=buffers((size, size)), flops=3 * 10**9)
 
 
 def basis_kernel(sampled_ref, flipped_ref, basis_ref):
@@ -386,21 +390,27 @@
     scale = (features.shape[0] * lax.axis_size(AXES)) ** 0.5
     size = sketch.shape[1]
     sampled, keep, other, gram, gram_other = local_terms(features, sketch)
-    cross = [keep, send(other, *CORE)]
-    gram, parts = sums(cross, gram, send(gram_other, *CORE), 4)
+    gram_other = send(gram_other, *CORE)
+    parts = sums([keep, send(other, *CORE)], 4, after=(gram_other,))
     cross = spread(parts, PLANE)
+    gram = add(gram, gram_other, parts[-1:])
     gram = gram + send(gram, *NEAR)
-    gram, (keep, other) = sums(cross, gram, send(gram, *FAR), 2, (0, 2, 1, 3))
-    gram, (keep, other) = sums([keep, send(other, *NEAR)], gram, send(gram, *PLANE[0]), 2)
-    gram, (own,) = sums([keep, send(other, *FAR)], gram, send(gram, *PLANE[1]), 1)
+    gram_other = send(gram, *FAR)
+    (line,) = sums(cross, after=(gram_other,))
+    gram = add(gram, gram_other, (line,))
+    gram_other = send(gram, *PLANE[0])
+    (line,) = sums([line, send(line, *NEAR)], masks=(0, 1), after=(gram_other,))
+    gram = add(gram, gram_other, (line,))
+    gram = gram + send(gram, *PLANE[1])
     for mask in spare_bits():
-        own = own + send(own, *mask)
+        line = line + send(line, *mask)
         gram = gram + send(gram, *mask)
-    pair = weave([own, send(own, *FAR)])
-    state = first_half(gram, send(gram, *CORE), size, (pair,))
-    line = weave([pair, send(pair, *NEAR)], state[:1])
+    *state, norm = first_part(gram, send(gram, *CORE), size, ())
+    (line,) = sums([line, send(line, *FAR)], masks=(0, 2), after=state[:1])
     plane = [line] + [send(line, *mask) for mask in PLANE]
-    inverse, flipped, factor = second_half(state, size, scale, (line,))
+    state = middle_part(state, size, PANEL, (line,))
+    state = middle_part(state, size, 2 * PANEL, ())
+    inverse, flipped, factor = last_part((*state, norm), size, scale, 3 * PANEL, ())
     cross = plane + [send(part, *CORE) for part in plane]
     return (basis_of(sampled, flipped), factor, project(inverse, cross))
 

time: 59.3 us -> 52.8 us (0.89)
  waiting for transfers between devices: 16.3 us -> 11.4 us
  starting transfers between devices: 23 us -> 21.5 us
    ppermute x21 -> x19, waiting for transfers between devices: 16.3 us -> 11.4 us  [send(): return lax.ppermute(value, AXES, pairs)]
    ppermute x21 -> x19, starting transfers between devices: 23 us -> 21.5 us  [send(): return lax.ppermute(value, AXES, pairs)]
    pallas_call x8 -> x11, Pallas kernels: 7.57 us -> 7.46 us  [call(): pl.pallas_call(lambda *refs: kernel(*refs[:len(operands)], *refs[len(oper...]
  transfers between devices with their start and end apart: 21 -> 19, of which waited for: 8 -> 7; matrix products, arithmetic and copies ran while one was open for 0% -> 0% of each run, Pallas kernels for 15% -> 17%
where the time goes in v11:
time: 52.8 us; the launch traced here: 52.6 us
  starting transfers between devices  21.5 us (41%)
  Pallas kernels  19 us (36%)
  waiting for transfers between devices  11.4 us (22%)
  between operations  0.73 us (1%)
    ppermute x19, starting transfers between devices, send(): return lax.ppermute(value, AXES, pairs)  21.5 us
    ppermute x19, waiting for transfers between devices, send(): return lax.ppermute(value, AXES, pairs)  11.4 us
    pallas_call x1, Pallas kernels, local_terms(): pl.pallas_call(local_kernel, out_shape=(f32(rows, rank), f32(rank // 2, d...  8.34 us
    pallas_call x11, Pallas kernels, call(): pl.pallas_call(lambda *refs: kernel(*refs[:len(operands)], *refs[len(oper...  7.46 us
    pallas_call x1, Pallas kernels, project(): pl.pallas_call(project_kernel, out_shape=jax.ShapeDtypeStruct((rank, dept...  1.65 us
    pallas_call x1, Pallas kernels, basis_of(): pl.pallas_call(basis_kernel, out_shape=f32(*sampled.shape), in_specs=[VME...  1.55 us
  transfers between devices with their start and end apart: 19, of which 7 were waited for; matrix products, arithmetic and copies ran while one was open for 0% of the time, Pallas kernels for 17%

profile of v11, /device:TPU:0, one launch (start us, length us, event | category | flops | bytes accessed | tf_op | source)
XLA Modules:
  0.0 52.6 jit_solution(13336529909880669891)
XLA Ops:
  0.6 8.3 %local_terms.1 = (f32[1024,256]{1,0:T(8,128)S(1)}, f32[128,1024]{1,0:T(8,128)S(1)}, f32[128,1024]{1,0:T(8,128)S(1)}, f32[192,128]{1,0:T(8,128)S(1)}, f32[192,128]{1,0:T(8,128)S(1)}) custom-call(f32[1024,1024]{1,0:T(8,128)} %features_hbm.1, f32[1024,256]{1,0:T(8,128)} %sketch_hbm.1), custom_call_target="tpu_custom_call" | custom-call | flops 4000000000 | bytes 8388608 | tf_op jit(solution)/shard_map/local_terms/pallas_call | solution.py:208
  9.0 0.5 collective-permute-start.1
  9.5 0.1 collective-permute-start
  9.6 1.6 %collective-permute-done.refs_2_.refs_1_ = f32[192,128]{1,0:T(8,128)S(1)} collective-permute-done((f32[192,128]{1,0:T(8,128)S(1)}, f32[192,128]{1,0:T(8,128)S(1)}, u32[]{:S(2)}, u32[]{:S(2)}) %collective-permute-start) | collective-permute-done | bytes 98336 | tf_op jit(solution)/shard_map/ppermute | solution.py:370
  11.2 0.0 collective-permute-done.1.refs_1_
  11.2 0.1 sums.4
  11.3 3.0 %collective-permute-start.2 = (f32[192,128]{1,0:T(8,128)S(1)}, f32[192,128]{1,0:T(8,128)S(1)}, u32[]{:S(2)}, u32[]{:S(2)}) collective-permute-start(f32[192,128]{1,0:T(8,128)S(1)} %add.11), channel_id=1, source_target_pairs={{0,8},{1,9},{2,10},{3,11},{4,12},{5,13},{6,14},{7,15},{8,0},{9,1},... | collective-permute-start | bytes 294920 | tf_op jit(solution)/shard_map/ppermute | solution.py:370
  14.3 1.5 %collective-permute-start.4 = (f32[32,1024]{1,0:T(8,128)S(1)}, f32[32,1024]{1,0:T(8,128)S(1)}, u32[]{:S(2)}, u32[]{:S(2)}) collective-permute-start(f32[32,1024]{1,0:T(8,128)S(1)} %get-tuple-element.29), channel_id=1, source_target_pairs={{0,1},{1,0},{2,3},{3,2},{4,5},{5,4},{6,7},{7,6},{8,9},{9,8},{10,11... | collective-permute-start | bytes 393224 | tf_op jit(solution)/shard_map/ppermute | solution.py:370
  15.8 1.5 %collective-permute-start.5 = (f32[32,1024]{1,0:T(8,128)S(1)}, f32[32,1024]{1,0:T(8,128)S(1)}, u32[]{:S(2)}, u32[]{:S(2)}) collective-permute-start(f32[32,1024]{1,0:T(8,128)S(1)} %get-tuple-element.30), channel_id=1, source_target_pairs={{0,4},{1,5},{2,6},{3,7},{4,0},{5,1},{6,2},{7,3},{8,12},{9,13},{10,... | collective-permute-start | bytes 393224 | tf_op jit(solution)/shard_map/ppermute | solution.py:370
  17.3 0.5 collective-permute-start.6
  17.8 0.0 collective-permute-done.2
  17.8 2.7 %collective-permute-start.3 = (f32[192,128]{1,0:T(8,128)S(1)}, f32[192,128]{1,0:T(8,128)S(1)}, u32[]{:S(2)}, u32[]{:S(2)}) collective-permute-start(f32[192,128]{1,0:T(8,128)S(1)} %add.9.refs_0_), channel_id=1, source_target_pairs={{0,16},{1,17},{2,18},{3,19},{4,20},{5,21},{6,22},{7,23},{8,24},{9,... | collective-permute-start | bytes 294920 | tf_op jit(solution)/shard_map/ppermute | solution.py:370
  20.4 0.0 collective-permute-done.4.refs_1_
  20.4 1.7 %collective-permute-done.5.refs_2_ = f32[32,1024]{1,0:T(8,128)S(1)} collective-permute-done((f32[32,1024]{1,0:T(8,128)S(1)}, f32[32,1024]{1,0:T(8,128)S(1)}, u32[]{:S(2)}, u32[]{:S(2)}) %collective-permute-start.5) | collective-permute-done | bytes 131104 | tf_op jit(solution)/shard_map/ppermute | solution.py:370
  22.2 1.3 %collective-permute-done.6.refs_3_ = f32[32,1024]{1,0:T(8,128)S(1)} collective-permute-done((f32[32,1024]{1,0:T(8,128)S(1)}, f32[32,1024]{1,0:T(8,128)S(1)}, u32[]{:S(2)}, u32[]{:S(2)}) %collective-permute-start.6) | collective-permute-done | bytes 131104 | tf_op jit(solution)/shard_map/ppermute | solution.py:370
  23.5 1.3 %collective-permute-done.3.refs_4_.refs_1_ = f32[192,128]{1,0:T(8,128)S(1)} collective-permute-done((f32[192,128]{1,0:T(8,128)S(1)}, f32[192,128]{1,0:T(8,128)S(1)}, u32[]{:S(2)}, u32[]{:S(2)}) %collective-permute-start.3) | collective-permute-done | bytes 98336 | tf_op jit(solution)/shard_map/ppermute | solution.py:370
  24.8 0.6 %collective-permute-start.8 = (f32[32,1024]{1,0:T(8,128)S(1)}, f32[32,1024]{1,0:T(8,128)S(1)}, u32[]{:S(2)}, u32[]{:S(2)}) collective-permute-start(f32[32,1024]{1,0:T(8,128)S(1)} %sums.5.refs_2_.refs_0_), channel_id=1, source_target_pairs={{0,8},{1,9},{2,10},{3,11},{4,12},{5,13},{6,14},{7,15},{8,0},{9,1},... | collective-permute-start | bytes 393224 | tf_op jit(solution)/shard_map/ppermute | solution.py:370
  25.4 1.6 %collective-permute-start.7 = (f32[192,128]{1,0:T(8,128)S(1)}, f32[192,128]{1,0:T(8,128)S(1)}, u32[]{:S(2)}, u32[]{:S(2)}) collective-permute-start(f32[192,128]{1,0:T(8,128)S(1)} %add.12.refs_0_), channel_id=1, source_target_pairs={{0,1},{1,0},{2,3},{3,2},{4,5},{5,4},{6,7},{7,6},{8,9},{9,8},{10,11... | collective-permute-start | bytes 294920 | tf_op jit(solution)/shard_map/ppermute | solution.py:370
  27.0 3.1 %collective-permute-done.7.refs_2_.refs_1_ = f32[192,128]{1,0:T(8,128)S(1)} collective-permute-done((f32[192,128]{1,0:T(8,128)S(1)}, f32[192,128]{1,0:T(8,128)S(1)}, u32[]{:S(2)}, u32[]{:S(2)}) %collective-permute-start.7) | collective-permute-done | bytes 98336 | tf_op jit(solution)/shard_map/ppermute | solution.py:370
  30.1 0.0 collective-permute-done.8.refs_1_
  30.1 1.6 %collective-permute-start.9 = (f32[192,128]{1,0:T(8,128)S(1)}, f32[192,128]{1,0:T(8,128)S(1)}, u32[]{:S(2)}, u32[]{:S(2)}) collective-permute-start(f32[192,128]{1,0:T(8,128)S(1)} %add.13), channel_id=1, source_target_pairs={{0,4},{1,5},{2,6},{3,7},{4,0},{5,1},{6,2},{7,3},{8,12},{9,13},{10,... | collective-permute-start | bytes 294920 | tf_op jit(solution)/shard_map/ppermute | solution.py:370
  31.7 3.4 %collective-permute-start.11 = (f32[32,1024]{1,0:T(8,128)S(1)}, f32[32,1024]{1,0:T(8,128)S(1)}, u32[]{:S(2)}, u32[]{:S(2)}) collective-permute-start(f32[32,1024]{1,0:T(8,128)S(1)} %sums.6.refs_2_.refs_0_), channel_id=1, source_target_pairs={{0,16},{1,17},{2,18},{3,19},{4,20},{5,21},{6,22},{7,23},{8,24},{9,... | collective-permute-start | bytes 393224 | tf_op jit(solution)/shard_map/ppermute | solution.py:370
  35.1 0.0 collective-permute-done.9
  35.1 0.1 collective-permute-start.10
  35.2 1.3 %collective-permute-done.10.refs_1_ = f32[192,128]{1,0:T(8,128)S(1)} collective-permute-done((f32[192,128]{1,0:T(8,128)S(1)}, f32[192,128]{1,0:T(8,128)S(1)}, u32[]{:S(2)}, u32[]{:S(2)}) %collective-permute-start.10) | collective-permute-done | bytes 98336 | tf_op jit(solution)/shard_map/ppermute | solution.py:370
  36.5 1.9 %first_part.1 = (f32[256,256]{1,0:T(8,128)S(1)}, f32[256,256]{1,0:T(8,128)S(1)}, f32[16,128]{1,0:T(8,128)S(1)}) custom-call(f32[192,128]{1,0:T(8,128)S(1)} %add.10.refs_0_, f32[192,128]{1,0:T(8,128)S(1)} %collective-permute-done.10.refs_1_), custom_call_target="tpu_custom_call" | custom-call | flops 1000000 | bytes 1000000 | tf_op jit(solution)/shard_map/first_part/pallas_call | solution.py:227
  38.4 1.0 %collective-permute-done.11.refs_1_ = f32[32,1024]{1,0:T(8,128)S(1)} collective-permute-done((f32[32,1024]{1,0:T(8,128)S(1)}, f32[32,1024]{1,0:T(8,128)S(1)}, u32[]{:S(2)}, u32[]{:S(2)}) %collective-permute-start.11) | collective-permute-done | bytes 131104 | tf_op jit(solution)/shard_map/ppermute | solution.py:370
  39.4 1.6 %collective-permute-start.12 = (f32[32,1024]{1,0:T(8,128)S(1)}, f32[32,1024]{1,0:T(8,128)S(1)}, u32[]{:S(2)}, u32[]{:S(2)}) collective-permute-start(f32[32,1024]{1,0:T(8,128)S(1)} %sums.7.refs_2_.refs_0_), channel_id=1, source_target_pairs={{0,1},{1,0},{2,3},{3,2},{4,5},{5,4},{6,7},{7,6},{8,9},{9,8},{10,11... | collective-permute-start | bytes 393224 | tf_op jit(solution)/shard_map/ppermute | solution.py:370
  41.0 0.5 %collective-permute-start.13 = (f32[32,1024]{1,0:T(8,128)S(1)}, f32[32,1024]{1,0:T(8,128)S(1)}, u32[]{:S(2)}, u32[]{:S(2)}) collective-permute-start(f32[32,1024]{1,0:T(8,128)S(1)} %sums.7.refs_2_.refs_0_), channel_id=1, source_target_pairs={{0,4},{1,5},{2,6},{3,7},{4,0},{5,1},{6,2},{7,3},{8,12},{9,13},{10,... | collective-permute-start | bytes 393224 | tf_op jit(solution)/shard_map/ppermute | solution.py:370
  41.6 1.4 %collective-permute-start.14 = (f32[32,1024]{1,0:T(8,128)S(1)}, f32[32,1024]{1,0:T(8,128)S(1)}, u32[]{:S(2)}, u32[]{:S(2)}) collective-permute-start(f32[32,1024]{1,0:T(8,128)S(1)} %sums.7.refs_2_.refs_0_), channel_id=1, source_target_pairs={{0,5},{1,4},{2,7},{3,6},{4,1},{5,0},{6,3},{7,2},{8,13},{9,12},{10,... | collective-permute-start | bytes 393224 | tf_op jit(solution)/shard_map/ppermute | solution.py:370
  43.0 0.0 collective-permute-start.15
  43.0 1.6 %middle_part.2 = (f32[256,256]{1,0:T(8,128)S(1)}, f32[256,256]{1,0:T(8,128)S(1)}) custom-call(f32[256,256]{1,0:T(8,128)S(1)} %get-tuple-element.31.refs_2_.refs_0_, f32[256,256]{1,0:T(8,128)S(1)} %get-tuple-element.32.refs_1_, f32[32,1024]{1,0:T(8,128)S(1)} %sums.7.refs_2_.refs_0_), custom_call_target="tpu_custom_call" | custom-call | flops 3000000000 | bytes 1000000 | tf_op jit(solution)/shard_map/middle_part/pallas_call | solution.py:227
  44.7 1.7 %middle_part.3 = (f32[256,256]{1,0:T(8,128)S(1)}, f32[256,256]{1,0:T(8,128)S(1)}) custom-call(f32[256,256]{1,0:T(8,128)S(1)} %get-tuple-element.33.refs_0_, f32[256,256]{1,0:T(8,128)S(1)} %get-tuple-element.34.refs_1_), custom_call_target="tpu_custom_call" | custom-call | flops 3000000000 | bytes 1000000 | tf_op jit(solution)/shard_map/middle_part/pallas_call | solution.py:227
  46.3 2.1 %last_part.1 = (f32[256,256]{1,0:T(8,128)S(1)}, f32[256,256]{1,0:T(8,128)S(1)}, f32[256,256]{1,0:T(8,128)}) custom-call(f32[256,256]{1,0:T(8,128)S(1)} %get-tuple-element.35.refs_0_, f32[256,256]{1,0:T(8,128)S(1)} %get-tuple-element.36.refs_1_, f32[16,128]{1,0:T(8,128)S(1)} %get-tuple-element.37.refs_2_), custom_call_target="tpu_custom_call" | custom-call | flops 3000000000 | bytes 1000000 | tf_op jit(solution)/shard_map/last_part/pallas_call | solution.py:227
  48.4 0.0 collective-permute-done.12.refs_1_
  48.4 0.5 collective-permute-start.16
  48.9 0.0 collective-permute-done.13.refs_2_
  48.9 0.1 collective-permute-start.17
  49.0 0.0 collective-permute-done.14.refs_3_
  49.0 0.4 collective-permute-start.18
  49.4 1.5 %basis.1 = f32[1024,256]{1,0:T(8,128)} custom-call(f32[1024,256]{1,0:T(8,128)S(1)} %get-tuple-element.22.sampled_ref, f32[256,256]{1,0:T(8,128)S(1)} %get-tuple-element.38.flipped_ref), custom_call_target="tpu_custom_call" | custom-call | flops 2000000000 | bytes 2097152 | tf_op jit(solution)/shard_map/basis/pallas_call | solution.py:326
  51.0 0.0 collective-permute-done.15.refs_4_
  51.0 0.0 collective-permute-done.16.refs_5_
  51.0 0.0 collective-permute-done.17.refs_6_
  51.0 0.0 collective-permute-done.18.refs_7_
  51.0 1.7 %project.1 = f32[256,1024]{1,0:T(8,128)} custom-call(f32[256,256]{1,0:T(8,128)S(1)} %get-tuple-element.40.inverse_ref, f32[32,1024]{1,0:T(8,128)S(1)} %sums.7.refs_2_.refs_0_, f32[32,1024]{1,0:T(8,128)S(1)} %collective-permute-done.12.refs_1_, f32[32,1024]{1,0:T(8,128)S(1)} %collective-permute-done.13.refs_2_, ...), custom_call_target="tpu_custom_call" | custom-call | flops 400000000 | bytes 2097152 | tf_op jit(solution)/shard_map/project/pallas_call | solution.py:355
  (8 shorter events, 0.1 us)
Async XLA Ops:
  9.0 2.2 %collective-permute-start.1 = (f32[128,1024]{1,0:T(8,128)S(1)}, f32[128,1024]{1,0:T(8,128)S(1)}, u32[]{:S(2)}, u32[]{:S(2)}) collective-permute-start(f32[128,1024]{1,0:T(8,128)S(1)} %get-tuple-element.26), channel_id=1, source_target_pairs={{0,2},{1,3},{2,0},{3,1},{4,6},{5,7},{6,4},{7,5},{8,10},{9,11},{10,... | collective-permute-start | bytes 1572872 | tf_op jit(solution)/shard_map/ppermute | solution.py:370
  9.5 1.7 %collective-permute-start = (f32[192,128]{1,0:T(8,128)S(1)}, f32[192,128]{1,0:T(8,128)S(1)}, u32[]{:S(2)}, u32[]{:S(2)}) collective-permute-start(f32[192,128]{1,0:T(8,128)S(1)} %get-tuple-element.24), channel_id=1, source_target_pairs={{0,2},{1,3},{2,0},{3,1},{4,6},{5,7},{6,4},{7,5},{8,10},{9,11},{10,... | collective-permute-start | bytes 294920 | tf_op jit(solution)/shard_map/ppermute | solution.py:370
  11.3 6.5 %collective-permute-start.2 = (f32[192,128]{1,0:T(8,128)S(1)}, f32[192,128]{1,0:T(8,128)S(1)}, u32[]{:S(2)}, u32[]{:S(2)}) collective-permute-start(f32[192,128]{1,0:T(8,128)S(1)} %add.11), channel_id=1, source_target_pairs={{0,8},{1,9},{2,10},{3,11},{4,12},{5,13},{6,14},{7,15},{8,0},{9,1},... | collective-permute-start | bytes 294920 | tf_op jit(solution)/shard_map/ppermute | solution.py:370
  14.3 6.2 %collective-permute-start.4 = (f32[32,1024]{1,0:T(8,128)S(1)}, f32[32,1024]{1,0:T(8,128)S(1)}, u32[]{:S(2)}, u32[]{:S(2)}) collective-permute-start(f32[32,1024]{1,0:T(8,128)S(1)} %get-tuple-element.29), channel_id=1, source_target_pairs={{0,1},{1,0},{2,3},{3,2},{4,5},{5,4},{6,7},{7,6},{8,9},{9,8},{10,11... | collective-permute-start | bytes 393224 | tf_op jit(solution)/shard_map/ppermute | solution.py:370
  15.8 6.4 %collective-permute-start.5 = (f32[32,1024]{1,0:T(8,128)S(1)}, f32[32,1024]{1,0:T(8,128)S(1)}, u32[]{:S(2)}, u32[]{:S(2)}) collective-permute-start(f32[32,1024]{1,0:T(8,128)S(1)} %get-tuple-element.30), channel_id=1, source_target_pairs={{0,4},{1,5},{2,6},{3,7},{4,0},{5,1},{6,2},{7,3},{8,12},{9,13},{10,... | collective-permute-start | bytes 393224 | tf_op jit(solution)/shard_map/ppermute | solution.py:370
  17.3 6.2 %collective-permute-start.6 = (f32[32,1024]{1,0:T(8,128)S(1)}, f32[32,1024]{1,0:T(8,128)S(1)}, u32[]{:S(2)}, u32[]{:S(2)}) collective-permute-start(f32[32,1024]{1,0:T(8,128)S(1)} %get-tuple-element.27.refs_2_), channel_id=1, source_target_pairs={{0,5},{1,4},{2,7},{3,6},{4,1},{5,0},{6,3},{7,2},{8,13},{9,12},{10,... | collective-permute-start | bytes 393224 | tf_op jit(solution)/shard_map/ppermute | solution.py:370
  17.8 7.0 %collective-permute-start.3 = (f32[192,128]{1,0:T(8,128)S(1)}, f32[192,128]{1,0:T(8,128)S(1)}, u32[]{:S(2)}, u32[]{:S(2)}) collective-permute-start(f32[192,128]{1,0:T(8,128)S(1)} %add.9.refs_0_), channel_id=1, source_target_pairs={{0,16},{1,17},{2,18},{3,19},{4,20},{5,21},{6,22},{7,23},{8,24},{9,... | collective-permute-start | bytes 294920 | tf_op jit(solution)/shard_map/ppermute | solution.py:370
  24.8 5.3 %collective-permute-start.8 = (f32[32,1024]{1,0:T(8,128)S(1)}, f32[32,1024]{1,0:T(8,128)S(1)}, u32[]{:S(2)}, u32[]{:S(2)}) collective-permute-start(f32[32,1024]{1,0:T(8,128)S(1)} %sums.5.refs_2_.refs_0_), channel_id=1, source_target_pairs={{0,8},{1,9},{2,10},{3,11},{4,12},{5,13},{6,14},{7,15},{8,0},{9,1},... | collective-permute-start | bytes 393224 | tf_op jit(solution)/shard_map/ppermute | solution.py:370
  25.4 4.7 %collective-permute-start.7 = (f32[192,128]{1,0:T(8,128)S(1)}, f32[192,128]{1,0:T(8,128)S(1)}, u32[]{:S(2)}, u32[]{:S(2)}) collective-permute-start(f32[192,128]{1,0:T(8,128)S(1)} %add.12.refs_0_), channel_id=1, source_target_pairs={{0,1},{1,0},{2,3},{3,2},{4,5},{5,4},{6,7},{7,6},{8,9},{9,8},{10,11... | collective-permute-start | bytes 294920 | tf_op jit(solution)/shard_map/ppermute | solution.py:370
  30.1 4.9 %collective-permute-start.9 = (f32[192,128]{1,0:T(8,128)S(1)}, f32[192,128]{1,0:T(8,128)S(1)}, u32[]{:S(2)}, u32[]{:S(2)}) collective-permute-start(f32[192,128]{1,0:T(8,128)S(1)} %add.13), channel_id=1, source_target_pairs={{0,4},{1,5},{2,6},{3,7},{4,0},{5,1},{6,2},{7,3},{8,12},{9,13},{10,... | collective-permute-start | bytes 294920 | tf_op jit(solution)/shard_map/ppermute | solution.py:370
  31.7 7.7 %collective-permute-start.11 = (f32[32,1024]{1,0:T(8,128)S(1)}, f32[32,1024]{1,0:T(8,128)S(1)}, u32[]{:S(2)}, u32[]{:S(2)}) collective-permute-start(f32[32,1024]{1,0:T(8,128)S(1)} %sums.6.refs_2_.refs_0_), channel_id=1, source_target_pairs={{0,16},{1,17},{2,18},{3,19},{4,20},{5,21},{6,22},{7,23},{8,24},{9,... | collective-permute-start | bytes 393224 | tf_op jit(solution)/shard_map/ppermute | solution.py:370
  35.1 1.4 %collective-permute-start.10 = (f32[192,128]{1,0:T(8,128)S(1)}, f32[192,128]{1,0:T(8,128)S(1)}, u32[]{:S(2)}, u32[]{:S(2)}) collective-permute-start(f32[192,128]{1,0:T(8,128)S(1)} %add.10.refs_0_), channel_id=1, source_target_pairs={{0,2},{1,3},{2,0},{3,1},{4,6},{5,7},{6,4},{7,5},{8,10},{9,11},{10,... | collective-permute-start | bytes 294920 | tf_op jit(solution)/shard_map/ppermute | solution.py:370
  39.4 8.9 %collective-permute-start.12 = (f32[32,1024]{1,0:T(8,128)S(1)}, f32[32,1024]{1,0:T(8,128)S(1)}, u32[]{:S(2)}, u32[]{:S(2)}) collective-permute-start(f32[32,1024]{1,0:T(8,128)S(1)} %sums.7.refs_2_.refs_0_), channel_id=1, source_target_pairs={{0,1},{1,0},{2,3},{3,2},{4,5},{5,4},{6,7},{7,6},{8,9},{9,8},{10,11... | collective-permute-start | bytes 393224 | tf_op jit(solution)/shard_map/ppermute | solution.py:370
  41.0 7.9 %collective-permute-start.13 = (f32[32,1024]{1,0:T(8,128)S(1)}, f32[32,1024]{1,0:T(8,128)S(1)}, u32[]{:S(2)}, u32[]{:S(2)}) collective-permute-start(f32[32,1024]{1,0:T(8,128)S(1)} %sums.7.refs_2_.refs_0_), channel_id=1, source_target_pairs={{0,4},{1,5},{2,6},{3,7},{4,0},{5,1},{6,2},{7,3},{8,12},{9,13},{10,... | collective-permute-start | bytes 393224 | tf_op jit(solution)/shard_map/ppermute | solution.py:370
  41.6 7.4 %collective-permute-start.14 = (f32[32,1024]{1,0:T(8,128)S(1)}, f32[32,1024]{1,0:T(8,128)S(1)}, u32[]{:S(2)}, u32[]{:S(2)}) collective-permute-start(f32[32,1024]{1,0:T(8,128)S(1)} %sums.7.refs_2_.refs_0_), channel_id=1, source_target_pairs={{0,5},{1,4},{2,7},{3,6},{4,1},{5,0},{6,3},{7,2},{8,13},{9,12},{10,... | collective-permute-start | bytes 393224 | tf_op jit(solution)/shard_map/ppermute | solution.py:370
  43.0 8.0 %collective-permute-start.15 = (f32[32,1024]{1,0:T(8,128)S(1)}, f32[32,1024]{1,0:T(8,128)S(1)}, u32[]{:S(2)}, u32[]{:S(2)}) collective-permute-start(f32[32,1024]{1,0:T(8,128)S(1)} %sums.7.refs_2_.refs_0_), channel_id=1, source_target_pairs={{0,2},{1,3},{2,0},{3,1},{4,6},{5,7},{6,4},{7,5},{8,10},{9,11},{10,... | collective-permute-start | bytes 393224 | tf_op jit(solution)/shard_map/ppermute | solution.py:370
  48.4 2.6 %collective-permute-start.16 = (f32[32,1024]{1,0:T(8,128)S(1)}, f32[32,1024]{1,0:T(8,128)S(1)}, u32[]{:S(2)}, u32[]{:S(2)}) collective-permute-start(f32[32,1024]{1,0:T(8,128)S(1)} %collective-permute-done.12.refs_1_), channel_id=1, source_target_pairs={{0,2},{1,3},{2,0},{3,1},{4,6},{5,7},{6,4},{7,5},{8,10},{9,11},{10,... | collective-permute-start | bytes 393224 | tf_op jit(solution)/shard_map/ppermute | solution.py:370
  48.9 2.1 %collective-permute-start.17 = (f32[32,1024]{1,0:T(8,128)S(1)}, f32[32,1024]{1,0:T(8,128)S(1)}, u32[]{:S(2)}, u32[]{:S(2)}) collective-permute-start(f32[32,1024]{1,0:T(8,128)S(1)} %collective-permute-done.13.refs_2_), channel_id=1, source_target_pairs={{0,2},{1,3},{2,0},{3,1},{4,6},{5,7},{6,4},{7,5},{8,10},{9,11},{10,... | collective-permute-start | bytes 393224 | tf_op jit(solution)/shard_map/ppermute | solution.py:370
  49.0 2.0 %collective-permute-start.18 = (f32[32,1024]{1,0:T(8,128)S(1)}, f32[32,1024]{1,0:T(8,128)S(1)}, u32[]{:S(2)}, u32[]{:S(2)}) collective-permute-start(f32[32,1024]{1,0:T(8,128)S(1)} %collective-permute-done.14.refs_3_), channel_id=1, source_target_pairs={{0,2},{1,3},{2,0},{3,1},{4,6},{5,7},{6,4},{7,5},{8,10},{9,11},{10,... | collective-permute-start | bytes 393224 | tf_op jit(solution)/shard_map/ppermute | solution.py:370

commit v12 on v11

--- a/solution.py
+++ b/solution.py
@@ -150,7 +150,7 @@
     return pl.ds(pl.multiple_of(block * height, GROUP), height)
 
 
-def local_kernel(features_hbm, sketch_hbm, sampled_ref, keep_ref, send_ref, gram_keep_ref, gram_send_ref, features_ref, sketch_ref, high_ref, low_ref, flip_high_ref, flip_low_ref, cross_ref, packed_ref, sems):
+def local_kernel(features_hbm, sketch_hbm, sampled_ref, keep_ref, send_ref, gram_keep_ref, gram_send_ref, features_ref, sketch_ref, pair_ref, high_ref, low_ref, flip_high_ref, flip_low_ref, cross_ref, packed_ref, sems):
     rows, depth = features_ref.shape
     rank = sketch_ref.shape[1]
     chunks = rows // BLOCK
@@ -161,14 +161,15 @@
     for copy in copies:
         copy.start()
     copies[0].wait()
-    sketch = split(sketch_ref[...])
+    pair_ref[:, :rank], pair_ref[:, rank:] = split(sketch_ref[...])
     gram = None
     for at in range(chunks):
         span = slice(at * BLOCK, (at + 1) * BLOCK)
         copies[1 + at].wait()
         features = split(features_ref[span, :])
         high_ref[span, :], low_ref[span, :] = features
-        sampled = product(features, sketch, 1, 0)
+        both = lax.dot(features[0], pair_ref[...], preferred_element_type=jnp.float32)
+        sampled = both[:, :rank] + (both[:, rank:] + lax.dot(features[1], pair_ref[:, :rank], preferred_element_type=jnp.float32))
         sampled_ref[span, :] = sampled
         flipped = split(sampled.T)
         flip_high_ref[:, span], flip_low_ref[:, span] = flipped
@@ -212,6 +213,7 @@
         out_specs=(VMEM,) * 5,
         scratch_shapes=[
             pltpu.VMEM((rows, depth), jnp.float32), pltpu.VMEM((depth, rank), jnp.float32),
+            pltpu.VMEM((depth, 2 * rank), jnp.bfloat16),
             pltpu.VMEM((rows, depth), jnp.bfloat16), pltpu.VMEM((rows, depth), jnp.bfloat16),
             pltpu.VMEM((rank, rows), jnp.bfloat16), pltpu.VMEM((rank, rows), jnp.bfloat16),
             pltpu.VMEM((rank, depth), jnp.float32), pltpu.VMEM((packed, LANES), jnp.float32),
@@ -396,10 +398,10 @@
     gram = add(gram, gram_other, parts[-1:])
     gram = gram + send(gram, *NEAR)
     gram_other = send(gram, *FAR)
-    (line,) = sums(cross, after=(gram_other,))
+    (line,) = sums(cross)
     gram = add(gram, gram_other, (line,))
     gram_other = send(gram, *PLANE[0])
-    (line,) = sums([line, send(line, *NEAR)], masks=(0, 1), after=(gram_other,))
+    (line,) = sums([line, send(line, *NEAR)], masks=(0, 1))
     gram = add(gram, gram_other, (line,))
     gram = gram + send(gram, *PLANE[1])
     for mask in spare_bits():

time: 52.8 us -> 51.5 us (0.975)
  starting transfers between devices: 21.5 us -> 19.7 us
    ppermute x19, starting transfers between devices: 21.5 us -> 19.7 us  [send(): return lax.ppermute(value, AXES, pairs)]
    ppermute x19, waiting for transfers between devices: 11.4 us -> 11.9 us  [send(): return lax.ppermute(value, AXES, pairs)]
  transfers between devices with their start and end apart: 19 -> 19, of which waited for: 7 -> 9; matrix products, arithmetic and copies ran while one was open for 0% -> 0% of each run, Pallas kernels for 17% -> 17%
where the time goes in v12:
time: 51.5 us; the launch traced here: 51.4 us
  starting transfers between devices  19.7 us (38%)
  Pallas kernels  19 us (37%)
  waiting for transfers between devices  11.9 us (23%)
  between operations  0.73 us (1%)
    ppermute x19, starting transfers between devices, send(): return lax.ppermute(value, AXES, pairs)  19.7 us
    ppermute x19, waiting for transfers between devices, send(): return lax.ppermute(value, AXES, pairs)  11.9 us
    pallas_call x1, Pallas kernels, local_terms(): pl.pallas_call(local_kernel, out_shape=(f32(rows, rank), f32(rank // 2, d...  8.33 us
    pallas_call x11, Pallas kernels, call(): pl.pallas_call(lambda *refs: kernel(*refs[:len(operands)], *refs[len(oper...  7.44 us
    pallas_call x1, Pallas kernels, project(): pl.pallas_call(project_kernel, out_shape=jax.ShapeDtypeStruct((rank, dept...  1.66 us
    pallas_call x1, Pallas kernels, basis_of(): pl.pallas_call(basis_kernel, out_shape=f32(*sampled.shape), in_specs=[VME...  1.56 us
  transfers between devices with their start and end apart: 19, of which 9 were waited for; matrix products, arithmetic and copies ran while one was open for 0% of the time, Pallas kernels for 17%

profile of v12, /device:TPU:0, one launch (start us, length us, event | category | flops | bytes accessed | tf_op | source)
XLA Modules:
  0.0 51.4 jit_solution(14572035992590681615)
XLA Ops:
  0.6 8.3 %local_terms.1 = (f32[1024,256]{1,0:T(8,128)S(1)}, f32[128,1024]{1,0:T(8,128)S(1)}, f32[128,1024]{1,0:T(8,128)S(1)}, f32[192,128]{1,0:T(8,128)S(1)}, f32[192,128]{1,0:T(8,128)S(1)}) custom-call(f32[1024,1024]{1,0:T(8,128)} %features_hbm.1, f32[1024,256]{1,0:T(8,128)} %sketch_hbm.1), custom_call_target="tpu_custom_call" | custom-call | flops 4000000000 | bytes 8388608 | tf_op jit(solution)/shard_map/local_terms/pallas_call | solution.py:209
  9.0 0.5 %collective-permute-start.1 = (f32[128,1024]{1,0:T(8,128)S(1)}, f32[128,1024]{1,0:T(8,128)S(1)}, u32[]{:S(2)}, u32[]{:S(2)}) collective-permute-start(f32[128,1024]{1,0:T(8,128)S(1)} %get-tuple-element.26), channel_id=1, source_target_pairs={{0,2},{1,3},{2,0},{3,1},{4,6},{5,7},{6,4},{7,5},{8,10},{9,11},{10,... | collective-permute-start | bytes 1572872 | tf_op jit(solution)/shard_map/ppermute | solution.py:372
  9.5 0.1 collective-permute-start
  9.6 1.6 %collective-permute-done.refs_2_.refs_1_ = f32[192,128]{1,0:T(8,128)S(1)} collective-permute-done((f32[192,128]{1,0:T(8,128)S(1)}, f32[192,128]{1,0:T(8,128)S(1)}, u32[]{:S(2)}, u32[]{:S(2)}) %collective-permute-start) | collective-permute-done | bytes 98336 | tf_op jit(solution)/shard_map/ppermute | solution.py:372
  11.2 0.0 collective-permute-done.1.refs_1_
  11.2 0.1 sums.4
  11.3 3.0 %collective-permute-start.2 = (f32[192,128]{1,0:T(8,128)S(1)}, f32[192,128]{1,0:T(8,128)S(1)}, u32[]{:S(2)}, u32[]{:S(2)}) collective-permute-start(f32[192,128]{1,0:T(8,128)S(1)} %add.11), channel_id=1, source_target_pairs={{0,8},{1,9},{2,10},{3,11},{4,12},{5,13},{6,14},{7,15},{8,0},{9,1},... | collective-permute-start | bytes 294920 | tf_op jit(solution)/shard_map/ppermute | solution.py:372
  14.3 1.5 %collective-permute-start.4 = (f32[32,1024]{1,0:T(8,128)S(1)}, f32[32,1024]{1,0:T(8,128)S(1)}, u32[]{:S(2)}, u32[]{:S(2)}) collective-permute-start(f32[32,1024]{1,0:T(8,128)S(1)} %get-tuple-element.29), channel_id=1, source_target_pairs={{0,1},{1,0},{2,3},{3,2},{4,5},{5,4},{6,7},{7,6},{8,9},{9,8},{10,11... | collective-permute-start | bytes 393224 | tf_op jit(solution)/shard_map/ppermute | solution.py:372
  15.8 1.5 %collective-permute-start.5 = (f32[32,1024]{1,0:T(8,128)S(1)}, f32[32,1024]{1,0:T(8,128)S(1)}, u32[]{:S(2)}, u32[]{:S(2)}) collective-permute-start(f32[32,1024]{1,0:T(8,128)S(1)} %get-tuple-element.30), channel_id=1, source_target_pairs={{0,4},{1,5},{2,6},{3,7},{4,0},{5,1},{6,2},{7,3},{8,12},{9,13},{10,... | collective-permute-start | bytes 393224 | tf_op jit(solution)/shard_map/ppermute | solution.py:372
  17.3 0.5 collective-permute-start.6
  17.8 0.0 collective-permute-done.2
  17.8 2.7 %collective-permute-start.3 = (f32[192,128]{1,0:T(8,128)S(1)}, f32[192,128]{1,0:T(8,128)S(1)}, u32[]{:S(2)}, u32[]{:S(2)}) collective-permute-start(f32[192,128]{1,0:T(8,128)S(1)} %add.9.refs_0_), channel_id=1, source_target_pairs={{0,16},{1,17},{2,18},{3,19},{4,20},{5,21},{6,22},{7,23},{8,24},{9,... | collective-permute-start | bytes 294920 | tf_op jit(solution)/shard_map/ppermute | solution.py:372
  20.4 0.0 collective-permute-done.4.refs_1_
  20.4 1.7 %collective-permute-done.5.refs_2_ = f32[32,1024]{1,0:T(8,128)S(1)} collective-permute-done((f32[32,1024]{1,0:T(8,128)S(1)}, f32[32,1024]{1,0:T(8,128)S(1)}, u32[]{:S(2)}, u32[]{:S(2)}) %collective-permute-start.5) | collective-permute-done | bytes 131104 | tf_op jit(solution)/shard_map/ppermute | solution.py:372
  22.2 1.3 %collective-permute-done.6.refs_3_ = f32[32,1024]{1,0:T(8,128)S(1)} collective-permute-done((f32[32,1024]{1,0:T(8,128)S(1)}, f32[32,1024]{1,0:T(8,128)S(1)}, u32[]{:S(2)}, u32[]{:S(2)}) %collective-permute-start.6) | collective-permute-done | bytes 131104 | tf_op jit(solution)/shard_map/ppermute | solution.py:372
  23.5 0.4 collective-permute-start.8
  24.0 0.8 %collective-permute-done.3.refs_1_ = f32[192,128]{1,0:T(8,128)S(1)} collective-permute-done((f32[192,128]{1,0:T(8,128)S(1)}, f32[192,128]{1,0:T(8,128)S(1)}, u32[]{:S(2)}, u32[]{:S(2)}) %collective-permute-start.3) | collective-permute-done | bytes 98336 | tf_op jit(solution)/shard_map/ppermute | solution.py:372
  24.8 1.4 %collective-permute-start.7 = (f32[192,128]{1,0:T(8,128)S(1)}, f32[192,128]{1,0:T(8,128)S(1)}, u32[]{:S(2)}, u32[]{:S(2)}) collective-permute-start(f32[192,128]{1,0:T(8,128)S(1)} %add.12.refs_0_), channel_id=1, source_target_pairs={{0,1},{1,0},{2,3},{3,2},{4,5},{5,4},{6,7},{7,6},{8,9},{9,8},{10,11... | collective-permute-start | bytes 294920 | tf_op jit(solution)/shard_map/ppermute | solution.py:372
  26.2 2.4 %collective-permute-done.8.refs_1_ = f32[32,1024]{1,0:T(8,128)S(1)} collective-permute-done((f32[32,1024]{1,0:T(8,128)S(1)}, f32[32,1024]{1,0:T(8,128)S(1)}, u32[]{:S(2)}, u32[]{:S(2)}) %collective-permute-start.8) | collective-permute-done | bytes 131104 | tf_op jit(solution)/shard_map/ppermute | solution.py:372
  28.6 0.9 %collective-permute-done.7.refs_1_ = f32[192,128]{1,0:T(8,128)S(1)} collective-permute-done((f32[192,128]{1,0:T(8,128)S(1)}, f32[192,128]{1,0:T(8,128)S(1)}, u32[]{:S(2)}, u32[]{:S(2)}) %collective-permute-start.7) | collective-permute-done | bytes 98336 | tf_op jit(solution)/shard_map/ppermute | solution.py:372
  29.5 1.4 %collective-permute-start.9 = (f32[192,128]{1,0:T(8,128)S(1)}, f32[192,128]{1,0:T(8,128)S(1)}, u32[]{:S(2)}, u32[]{:S(2)}) collective-permute-start(f32[192,128]{1,0:T(8,128)S(1)} %add.13), channel_id=1, source_target_pairs={{0,4},{1,5},{2,6},{3,7},{4,0},{5,1},{6,2},{7,3},{8,12},{9,13},{10,... | collective-permute-start | bytes 294920 | tf_op jit(solution)/shard_map/ppermute | solution.py:372
  30.9 2.0 %collective-permute-start.11 = (f32[32,1024]{1,0:T(8,128)S(1)}, f32[32,1024]{1,0:T(8,128)S(1)}, u32[]{:S(2)}, u32[]{:S(2)}) collective-permute-start(f32[32,1024]{1,0:T(8,128)S(1)} %sums.6.refs_2_.refs_0_), channel_id=1, source_target_pairs={{0,16},{1,17},{2,18},{3,19},{4,20},{5,21},{6,22},{7,23},{8,24},{9,... | collective-permute-start | bytes 393224 | tf_op jit(solution)/shard_map/ppermute | solution.py:372
  32.9 1.2 %collective-permute-done.9 = f32[192,128]{1,0:T(8,128)S(1)} collective-permute-done((f32[192,128]{1,0:T(8,128)S(1)}, f32[192,128]{1,0:T(8,128)S(1)}, u32[]{:S(2)}, u32[]{:S(2)}) %collective-permute-start.9) | collective-permute-done | bytes 98336 | tf_op jit(solution)/shard_map/ppermute | solution.py:372
  34.2 0.1 collective-permute-start.10
  34.3 1.3 %collective-permute-done.10.refs_1_ = f32[192,128]{1,0:T(8,128)S(1)} collective-permute-done((f32[192,128]{1,0:T(8,128)S(1)}, f32[192,128]{1,0:T(8,128)S(1)}, u32[]{:S(2)}, u32[]{:S(2)}) %collective-permute-start.10) | collective-permute-done | bytes 98336 | tf_op jit(solution)/shard_map/ppermute | solution.py:372
  35.5 1.9 %first_part.1 = (f32[256,256]{1,0:T(8,128)S(1)}, f32[256,256]{1,0:T(8,128)S(1)}, f32[16,128]{1,0:T(8,128)S(1)}) custom-call(f32[192,128]{1,0:T(8,128)S(1)} %add.10.refs_0_, f32[192,128]{1,0:T(8,128)S(1)} %collective-permute-done.10.refs_1_), custom_call_target="tpu_custom_call" | custom-call | flops 1000000 | bytes 1000000 | tf_op jit(solution)/shard_map/first_part/pallas_call | solution.py:229
  37.5 0.7 %collective-permute-done.11.refs_1_ = f32[32,1024]{1,0:T(8,128)S(1)} collective-permute-done((f32[32,1024]{1,0:T(8,128)S(1)}, f32[32,1024]{1,0:T(8,128)S(1)}, u32[]{:S(2)}, u32[]{:S(2)}) %collective-permute-start.11) | collective-permute-done | bytes 131104 | tf_op jit(solution)/shard_map/ppermute | solution.py:372
  38.2 1.6 %collective-permute-start.12 = (f32[32,1024]{1,0:T(8,128)S(1)}, f32[32,1024]{1,0:T(8,128)S(1)}, u32[]{:S(2)}, u32[]{:S(2)}) collective-permute-start(f32[32,1024]{1,0:T(8,128)S(1)} %sums.7.refs_2_.refs_0_), channel_id=1, source_target_pairs={{0,1},{1,0},{2,3},{3,2},{4,5},{5,4},{6,7},{7,6},{8,9},{9,8},{10,11... | collective-permute-start | bytes 393224 | tf_op jit(solution)/shard_map/ppermute | solution.py:372
  39.8 0.7 %collective-permute-start.13 = (f32[32,1024]{1,0:T(8,128)S(1)}, f32[32,1024]{1,0:T(8,128)S(1)}, u32[]{:S(2)}, u32[]{:S(2)}) collective-permute-start(f32[32,1024]{1,0:T(8,128)S(1)} %sums.7.refs_2_.refs_0_), channel_id=1, source_target_pairs={{0,4},{1,5},{2,6},{3,7},{4,0},{5,1},{6,2},{7,3},{8,12},{9,13},{10,... | collective-permute-start | bytes 393224 | tf_op jit(solution)/shard_map/ppermute | solution.py:372
  40.4 1.3 %collective-permute-start.14 = (f32[32,1024]{1,0:T(8,128)S(1)}, f32[32,1024]{1,0:T(8,128)S(1)}, u32[]{:S(2)}, u32[]{:S(2)}) collective-permute-start(f32[32,1024]{1,0:T(8,128)S(1)} %sums.7.refs_2_.refs_0_), channel_id=1, source_target_pairs={{0,5},{1,4},{2,7},{3,6},{4,1},{5,0},{6,3},{7,2},{8,13},{9,12},{10,... | collective-permute-start | bytes 393224 | tf_op jit(solution)/shard_map/ppermute | solution.py:372
  41.7 0.0 collective-permute-start.15
  41.7 1.6 %middle_part.2 = (f32[256,256]{1,0:T(8,128)S(1)}, f32[256,256]{1,0:T(8,128)S(1)}) custom-call(f32[256,256]{1,0:T(8,128)S(1)} %get-tuple-element.31.refs_2_.refs_0_, f32[256,256]{1,0:T(8,128)S(1)} %get-tuple-element.32.refs_1_, f32[32,1024]{1,0:T(8,128)S(1)} %sums.7.refs_2_.refs_0_), custom_call_target="tpu_custom_call" | custom-call | flops 3000000000 | bytes 1000000 | tf_op jit(solution)/shard_map/middle_part/pallas_call | solution.py:229
  43.4 1.7 %middle_part.3 = (f32[256,256]{1,0:T(8,128)S(1)}, f32[256,256]{1,0:T(8,128)S(1)}) custom-call(f32[256,256]{1,0:T(8,128)S(1)} %get-tuple-element.33.refs_0_, f32[256,256]{1,0:T(8,128)S(1)} %get-tuple-element.34.refs_1_), custom_call_target="tpu_custom_call" | custom-call | flops 3000000000 | bytes 1000000 | tf_op jit(solution)/shard_map/middle_part/pallas_call | solution.py:229
  45.0 2.1 %last_part.1 = (f32[256,256]{1,0:T(8,128)S(1)}, f32[256,256]{1,0:T(8,128)S(1)}, f32[256,256]{1,0:T(8,128)}) custom-call(f32[256,256]{1,0:T(8,128)S(1)} %get-tuple-element.35.refs_0_, f32[256,256]{1,0:T(8,128)S(1)} %get-tuple-element.36.refs_1_, f32[16,128]{1,0:T(8,128)S(1)} %get-tuple-element.37.refs_2_), custom_call_target="tpu_custom_call" | custom-call | flops 3000000000 | bytes 1000000 | tf_op jit(solution)/shard_map/last_part/pallas_call | solution.py:229
  47.1 0.0 collective-permute-done.12.refs_1_
  47.1 0.5 collective-permute-start.16
  47.6 0.0 collective-permute-done.13.refs_2_
  47.6 0.1 collective-permute-start.17
  47.7 0.0 collective-permute-done.14.refs_3_
  47.7 0.4 collective-permute-start.18
  48.1 1.6 %basis.1 = f32[1024,256]{1,0:T(8,128)} custom-call(f32[1024,256]{1,0:T(8,128)S(1)} %get-tuple-element.22.sampled_ref, f32[256,256]{1,0:T(8,128)S(1)} %get-tuple-element.38.flipped_ref), custom_call_target="tpu_custom_call" | custom-call | flops 2000000000 | bytes 2097152 | tf_op jit(solution)/shard_map/basis/pallas_call | solution.py:328
  49.7 0.0 collective-permute-done.15.refs_4_
  49.7 0.0 collective-permute-done.16.refs_5_
  49.7 0.0 collective-permute-done.17.refs_6_
  49.7 0.0 collective-permute-done.18.refs_7_
  49.7 1.7 %project.1 = f32[256,1024]{1,0:T(8,128)} custom-call(f32[256,256]{1,0:T(8,128)S(1)} %get-tuple-element.40.inverse_ref, f32[32,1024]{1,0:T(8,128)S(1)} %sums.7.refs_2_.refs_0_, f32[32,1024]{1,0:T(8,128)S(1)} %collective-permute-done.12.refs_1_, f32[32,1024]{1,0:T(8,128)S(1)} %collective-permute-done.13.refs_2_, ...), custom_call_target="tpu_custom_call" | custom-call | flops 400000000 | bytes 2097152 | tf_op jit(solution)/shard_map/project/pallas_call | solution.py:357
  (8 shorter events, 0.1 us)
Async XLA Ops:
  9.0 2.2 %collective-permute-start.1 = (f32[128,1024]{1,0:T(8,128)S(1)}, f32[128,1024]{1,0:T(8,128)S(1)}, u32[]{:S(2)}, u32[]{:S(2)}) collective-permute-start(f32[128,1024]{1,0:T(8,128)S(1)} %get-tuple-element.26), channel_id=1, source_target_pairs={{0,2},{1,3},{2,0},{3,1},{4,6},{5,7},{6,4},{7,5},{8,10},{9,11},{10,... | collective-permute-start | bytes 1572872 | tf_op jit(solution)/shard_map/ppermute | solution.py:372
  9.5 1.7 %collective-permute-start = (f32[192,128]{1,0:T(8,128)S(1)}, f32[192,128]{1,0:T(8,128)S(1)}, u32[]{:S(2)}, u32[]{:S(2)}) collective-permute-start(f32[192,128]{1,0:T(8,128)S(1)} %get-tuple-element.24), channel_id=1, source_target_pairs={{0,2},{1,3},{2,0},{3,1},{4,6},{5,7},{6,4},{7,5},{8,10},{9,11},{10,... | collective-permute-start | bytes 294920 | tf_op jit(solution)/shard_map/ppermute | solution.py:372
  11.3 6.5 %collective-permute-start.2 = (f32[192,128]{1,0:T(8,128)S(1)}, f32[192,128]{1,0:T(8,128)S(1)}, u32[]{:S(2)}, u32[]{:S(2)}) collective-permute-start(f32[192,128]{1,0:T(8,128)S(1)} %add.11), channel_id=1, source_target_pairs={{0,8},{1,9},{2,10},{3,11},{4,12},{5,13},{6,14},{7,15},{8,0},{9,1},... | collective-permute-start | bytes 294920 | tf_op jit(solution)/shard_map/ppermute | solution.py:372
  14.3 6.2 %collective-permute-start.4 = (f32[32,1024]{1,0:T(8,128)S(1)}, f32[32,1024]{1,0:T(8,128)S(1)}, u32[]{:S(2)}, u32[]{:S(2)}) collective-permute-start(f32[32,1024]{1,0:T(8,128)S(1)} %get-tuple-element.29), channel_id=1, source_target_pairs={{0,1},{1,0},{2,3},{3,2},{4,5},{5,4},{6,7},{7,6},{8,9},{9,8},{10,11... | collective-permute-start | bytes 393224 | tf_op jit(solution)/shard_map/ppermute | solution.py:372
  15.8 6.4 %collective-permute-start.5 = (f32[32,1024]{1,0:T(8,128)S(1)}, f32[32,1024]{1,0:T(8,128)S(1)}, u32[]{:S(2)}, u32[]{:S(2)}) collective-permute-start(f32[32,1024]{1,0:T(8,128)S(1)} %get-tuple-element.30), channel_id=1, source_target_pairs={{0,4},{1,5},{2,6},{3,7},{4,0},{5,1},{6,2},{7,3},{8,12},{9,13},{10,... | collective-permute-start | bytes 393224 | tf_op jit(solution)/shard_map/ppermute | solution.py:372
  17.3 6.2 %collective-permute-start.6 = (f32[32,1024]{1,0:T(8,128)S(1)}, f32[32,1024]{1,0:T(8,128)S(1)}, u32[]{:S(2)}, u32[]{:S(2)}) collective-permute-start(f32[32,1024]{1,0:T(8,128)S(1)} %get-tuple-element.27.refs_2_), channel_id=1, source_target_pairs={{0,5},{1,4},{2,7},{3,6},{4,1},{5,0},{6,3},{7,2},{8,13},{9,12},{10,... | collective-permute-start | bytes 393224 | tf_op jit(solution)/shard_map/ppermute | solution.py:372
  17.8 7.0 %collective-permute-start.3 = (f32[192,128]{1,0:T(8,128)S(1)}, f32[192,128]{1,0:T(8,128)S(1)}, u32[]{:S(2)}, u32[]{:S(2)}) collective-permute-start(f32[192,128]{1,0:T(8,128)S(1)} %add.9.refs_0_), channel_id=1, source_target_pairs={{0,16},{1,17},{2,18},{3,19},{4,20},{5,21},{6,22},{7,23},{8,24},{9,... | collective-permute-start | bytes 294920 | tf_op jit(solution)/shard_map/ppermute | solution.py:372
  23.5 5.0 %collective-permute-start.8 = (f32[32,1024]{1,0:T(8,128)S(1)}, f32[32,1024]{1,0:T(8,128)S(1)}, u32[]{:S(2)}, u32[]{:S(2)}) collective-permute-start(f32[32,1024]{1,0:T(8,128)S(1)} %sums.5.refs_2_.refs_0_), channel_id=1, source_target_pairs={{0,8},{1,9},{2,10},{3,11},{4,12},{5,13},{6,14},{7,15},{8,0},{9,1},... | collective-permute-start | bytes 393224 | tf_op jit(solution)/shard_map/ppermute | solution.py:372
  24.8 4.7 %collective-permute-start.7 = (f32[192,128]{1,0:T(8,128)S(1)}, f32[192,128]{1,0:T(8,128)S(1)}, u32[]{:S(2)}, u32[]{:S(2)}) collective-permute-start(f32[192,128]{1,0:T(8,128)S(1)} %add.12.refs_0_), channel_id=1, source_target_pairs={{0,1},{1,0},{2,3},{3,2},{4,5},{5,4},{6,7},{7,6},{8,9},{9,8},{10,11... | collective-permute-start | bytes 294920 | tf_op jit(solution)/shard_map/ppermute | solution.py:372
  29.5 4.7 %collective-permute-start.9 = (f32[192,128]{1,0:T(8,128)S(1)}, f32[192,128]{1,0:T(8,128)S(1)}, u32[]{:S(2)}, u32[]{:S(2)}) collective-permute-start(f32[192,128]{1,0:T(8,128)S(1)} %add.13), channel_id=1, source_target_pairs={{0,4},{1,5},{2,6},{3,7},{4,0},{5,1},{6,2},{7,3},{8,12},{9,13},{10,... | collective-permute-start | bytes 294920 | tf_op jit(solution)/shard_map/ppermute | solution.py:372
  30.9 7.3 %collective-permute-start.11 = (f32[32,1024]{1,0:T(8,128)S(1)}, f32[32,1024]{1,0:T(8,128)S(1)}, u32[]{:S(2)}, u32[]{:S(2)}) collective-permute-start(f32[32,1024]{1,0:T(8,128)S(1)} %sums.6.refs_2_.refs_0_), channel_id=1, source_target_pairs={{0,16},{1,17},{2,18},{3,19},{4,20},{5,21},{6,22},{7,23},{8,24},{9,... | collective-permute-start | bytes 393224 | tf_op jit(solution)/shard_map/ppermute | solution.py:372
  34.2 1.4 %collective-permute-start.10 = (f32[192,128]{1,0:T(8,128)S(1)}, f32[192,128]{1,0:T(8,128)S(1)}, u32[]{:S(2)}, u32[]{:S(2)}) collective-permute-start(f32[192,128]{1,0:T(8,128)S(1)} %add.10.refs_0_), channel_id=1, source_target_pairs={{0,2},{1,3},{2,0},{3,1},{4,6},{5,7},{6,4},{7,5},{8,10},{9,11},{10,... | collective-permute-start | bytes 294920 | tf_op jit(solution)/shard_map/ppermute | solution.py:372
  38.2 8.9 %collective-permute-start.12 = (f32[32,1024]{1,0:T(8,128)S(1)}, f32[32,1024]{1,0:T(8,128)S(1)}, u32[]{:S(2)}, u32[]{:S(2)}) collective-permute-start(f32[32,1024]{1,0:T(8,128)S(1)} %sums.7.refs_2_.refs_0_), channel_id=1, source_target_pairs={{0,1},{1,0},{2,3},{3,2},{4,5},{5,4},{6,7},{7,6},{8,9},{9,8},{10,11... | collective-permute-start | bytes 393224 | tf_op jit(solution)/shard_map/ppermute | solution.py:372
  39.8 7.9 %collective-permute-start.13 = (f32[32,1024]{1,0:T(8,128)S(1)}, f32[32,1024]{1,0:T(8,128)S(1)}, u32[]{:S(2)}, u32[]{:S(2)}) collective-permute-start(f32[32,1024]{1,0:T(8,128)S(1)} %sums.7.refs_2_.refs_0_), channel_id=1, source_target_pairs={{0,4},{1,5},{2,6},{3,7},{4,0},{5,1},{6,2},{7,3},{8,12},{9,13},{10,... | collective-permute-start | bytes 393224 | tf_op jit(solution)/shard_map/ppermute | solution.py:372
  40.4 7.2 %collective-permute-start.14 = (f32[32,1024]{1,0:T(8,128)S(1)}, f32[32,1024]{1,0:T(8,128)S(1)}, u32[]{:S(2)}, u32[]{:S(2)}) collective-permute-start(f32[32,1024]{1,0:T(8,128)S(1)} %sums.7.refs_2_.refs_0_), channel_id=1, source_target_pairs={{0,5},{1,4},{2,7},{3,6},{4,1},{5,0},{6,3},{7,2},{8,13},{9,12},{10,... | collective-permute-start | bytes 393224 | tf_op jit(solution)/shard_map/ppermute | solution.py:372
  41.7 8.0 %collective-permute-start.15 = (f32[32,1024]{1,0:T(8,128)S(1)}, f32[32,1024]{1,0:T(8,128)S(1)}, u32[]{:S(2)}, u32[]{:S(2)}) collective-permute-start(f32[32,1024]{1,0:T(8,128)S(1)} %sums.7.refs_2_.refs_0_), channel_id=1, source_target_pairs={{0,2},{1,3},{2,0},{3,1},{4,6},{5,7},{6,4},{7,5},{8,10},{9,11},{10,... | collective-permute-start | bytes 393224 | tf_op jit(solution)/shard_map/ppermute | solution.py:372
  47.1 2.6 %collective-permute-start.16 = (f32[32,1024]{1,0:T(8,128)S(1)}, f32[32,1024]{1,0:T(8,128)S(1)}, u32[]{:S(2)}, u32[]{:S(2)}) collective-permute-start(f32[32,1024]{1,0:T(8,128)S(1)} %collective-permute-done.12.refs_1_), channel_id=1, source_target_pairs={{0,2},{1,3},{2,0},{3,1},{4,6},{5,7},{6,4},{7,5},{8,10},{9,11},{10,... | collective-permute-start | bytes 393224 | tf_op jit(solution)/shard_map/ppermute | solution.py:372
  47.6 2.1 %collective-permute-start.17 = (f32[32,1024]{1,0:T(8,128)S(1)}, f32[32,1024]{1,0:T(8,128)S(1)}, u32[]{:S(2)}, u32[]{:S(2)}) collective-permute-start(f32[32,1024]{1,0:T(8,128)S(1)} %collective-permute-done.13.refs_2_), channel_id=1, source_target_pairs={{0,2},{1,3},{2,0},{3,1},{4,6},{5,7},{6,4},{7,5},{8,10},{9,11},{10,... | collective-permute-start | bytes 393224 | tf_op jit(solution)/shard_map/ppermute | solution.py:372
  47.7 2.0 %collective-permute-start.18 = (f32[32,1024]{1,0:T(8,128)S(1)}, f32[32,1024]{1,0:T(8,128)S(1)}, u32[]{:S(2)}, u32[]{:S(2)}) collective-permute-start(f32[32,1024]{1,0:T(8,128)S(1)} %collective-permute-done.14.refs_3_), channel_id=1, source_target_pairs={{0,2},{1,3},{2,0},{3,1},{4,6},{5,7},{6,4},{7,5},{8,10},{9,11},{10,... | collective-permute-start | bytes 393224 | tf_op jit(solution)/shard_map/ppermute | solution.py:372

commit v13 on v12

--- a/solution.py
+++ b/solution.py
@@ -255,12 +255,13 @@
     return call(lambda *refs: sum_kernel(masks, *refs), "sums", outs, *cross, after=after)
 
 
-def add_kernel(left_ref, right_ref, out_ref):
-    out_ref[...] = left_ref[...] + right_ref[...]
-
-
-def add(left, right, after):
-    return call(add_kernel, "add", f32(*left.shape), left, right, after=after)
+def add_kernel(*refs):
+    *terms, out_ref = refs
+    out_ref[...] = sum(term[...] for term in terms)
+
+
+def add(terms, after):
+    return call(add_kernel, "add", f32(*terms[0].shape), *terms, after=after)
 
 
 def first_part_kernel(keep_ref, other_ref, a_ref, factor_ref, norm_ref, packed_ref, buffer_ref):
@@ -278,12 +279,6 @@
     eliminate(a_ref, factor_ref, buffer_ref, 0, PANEL)
 
 
-def middle_part_kernel(first, from_ref, upper_ref, a_ref, factor_ref, buffer_ref):
-    a_ref[...] = from_ref[...]
-    factor_ref[:first, :] = upper_ref[:first, :]
-    eliminate(a_ref, factor_ref, buffer_ref, first, first + PANEL)
-
-
 def last_part_kernel(scale, first, from_ref, upper_ref, norm_ref, inverse_ref, flipped_ref, factor_ref, a_ref, buffer_ref):
     size = a_ref.shape[0]
     a_ref[...] = from_ref[...]
@@ -307,37 +302,48 @@
     return call(first_part_kernel, "first_part", outs, keep, other, after=after, scratch=buffers((3 * LANES, LANES)), flops=10**6)
 
 
-def middle_part(state, size, first, after):
-    kernel = lambda *refs: middle_part_kernel(first, *refs)
-    return call(kernel, "middle_part", (f32(size, size),) * 2, *state, after=after, scratch=buffers(), flops=3 * 10**9)
-
-
 def last_part(state, size, scale, first, after):
     kernel = lambda *refs: last_part_kernel(scale, first, *refs)
     return call(kernel, "last_part", (f32(size, size),) * 3, *state, after=after, scratch=buffers((size, size)), flops=3 * 10**9)
 
 
-def basis_kernel(sampled_ref, flipped_ref, basis_ref):
+def copy_out(block_ref, out_hbm, span, sem):
+    copy = pltpu.make_async_copy(block_ref.at[span], out_hbm.at[span], sem)
+    copy.start()
+    return copy
+
+
+def basis_kernel(sampled_ref, flipped_ref, basis_hbm, basis_ref, sems):
     flipped = split(flipped_ref[...])
-    for top in range(0, sampled_ref.shape[0], BLOCK):
-        span = slice(top, top + BLOCK)
+    copies = []
+    for at in range(sampled_ref.shape[0] // BLOCK):
+        span = slice(at * BLOCK, (at + 1) * BLOCK)
         basis_ref[span, :] = product(split(sampled_ref[span, :]), flipped, 1, 0)
+        copies.append(copy_out(basis_ref, basis_hbm, (pl.ds(at * BLOCK, BLOCK), slice(None)), sems.at[at]))
+    for copy in copies:
+        copy.wait()
+
+
+def streamed(kernel, name, out, operands, scratch, flops):
+    blocks = max(out.shape) // BLOCK
+    return pl.pallas_call(
+        kernel,
+        out_shape=out,
+        in_specs=[VMEM] * len(operands),
+        out_specs=pl.BlockSpec(memory_space=pl.ANY),
+        scratch_shapes=[pltpu.VMEM(out.shape, jnp.float32), *scratch, pltpu.SemaphoreType.DMA((blocks,))],
+        compiler_params=pltpu.CompilerParams(vmem_limit_bytes=16 * 2**20),
+        cost_estimate=pl.CostEstimate(flops=flops, bytes_accessed=2 * 2**20, transcendentals=0),
+        name=name,
+    )(*operands)
 
 
 def basis_of(sampled, flipped):
-    return pl.pallas_call(
-        basis_kernel,
-        out_shape=f32(*sampled.shape),
-        in_specs=[VMEM] * 2,
-        out_specs=VMEM,
-        compiler_params=pltpu.CompilerParams(vmem_limit_bytes=16 * 2**20),
-        cost_estimate=pl.CostEstimate(flops=2 * 10**9, bytes_accessed=2 * 2**20, transcendentals=0),
-        name="basis",
-    )(sampled, flipped)
+    return streamed(basis_kernel, "basis", f32(*sampled.shape), (sampled, flipped), (), 2 * 10**9)
 
 
 def project_kernel(inverse_ref, *refs):
-    *pieces, projection_ref, cross_ref = refs
+    *pieces, projection_hbm, projection_ref, cross_ref, sems = refs
     own = own_block()
     height = cross_ref.shape[0] // BLOCKS
     at = 0
@@ -346,24 +352,19 @@
             cross_ref[rows_of(at ^ own, height), :] = piece[top:top + height, :]
             at += 1
     inverse = split(inverse_ref[...])
-    for left in range(0, cross_ref.shape[1], BLOCK):
-        span = slice(left, left + BLOCK)
+    copies = []
+    for at in range(cross_ref.shape[1] // BLOCK):
+        span = slice(at * BLOCK, (at + 1) * BLOCK)
         projection_ref[:, span] = product(inverse, split(cross_ref[:, span]), 1, 0)
+        copies.append(copy_out(projection_ref, projection_hbm, (slice(None), pl.ds(at * BLOCK, BLOCK)), sems.at[at]))
+    for copy in copies:
+        copy.wait()
 
 
 def project(inverse, pieces):
-    rank = inverse.shape[0]
-    depth = pieces[0].shape[1]
-    return pl.pallas_call(
-        project_kernel,
-        out_shape=jax.ShapeDtypeStruct((rank, depth), jnp.float32),
-        in_specs=[VMEM] * (1 + len(pieces)),
-        out_specs=VMEM,
-        scratch_shapes=[pltpu.VMEM((rank, depth), jnp.float32)],
-        compiler_params=pltpu.CompilerParams(vmem_limit_bytes=16 * 2**20),
-        cost_estimate=pl.CostEstimate(flops=4 * 10**8, bytes_accessed=2 * 2**20, transcendentals=0),
-        name="project",
-    )(inverse, *pieces)
+    rank, depth = inverse.shape[0], pieces[0].shape[1]
+    scratch = (pltpu.VMEM((rank, depth), jnp.float32),)
+    return streamed(project_kernel, "project", f32(rank, depth), (inverse, *pieces), scratch, 4 * 10**8)
 
 
 def send(value, wide, narrow):
@@ -395,24 +396,21 @@
     gram_other = send(gram_other, *CORE)
     parts = sums([keep, send(other, *CORE)], 4, after=(gram_other,))
     cross = spread(parts, PLANE)
-    gram = add(gram, gram_other, parts[-1:])
+    gram = add([gram, gram_other], parts[-1:])
     gram = gram + send(gram, *NEAR)
     gram_other = send(gram, *FAR)
     (line,) = sums(cross)
-    gram = add(gram, gram_other, (line,))
-    gram_other = send(gram, *PLANE[0])
+    gram = add([gram, gram_other], (line,))
+    grams = [gram] + [send(gram, *mask) for mask in PLANE]
     (line,) = sums([line, send(line, *NEAR)], masks=(0, 1))
-    gram = add(gram, gram_other, (line,))
-    gram = gram + send(gram, *PLANE[1])
+    gram = add(grams, (line,))
     for mask in spare_bits():
         line = line + send(line, *mask)
         gram = gram + send(gram, *mask)
     *state, norm = first_part(gram, send(gram, *CORE), size, ())
     (line,) = sums([line, send(line, *FAR)], masks=(0, 2), after=state[:1])
     plane = [line] + [send(line, *mask) for mask in PLANE]
-    state = middle_part(state, size, PANEL, (line,))
-    state = middle_part(state, size, 2 * PANEL, ())
-    inverse, flipped, factor = last_part((*state, norm), size, scale, 3 * PANEL, ())
+    inverse, flipped, factor = last_part((*state, norm), size, scale, PANEL, (line,))
     cross = plane + [send(part, *CORE) for part in plane]
     return (basis_of(sampled, flipped), factor, project(inverse, cross))
 

time: 51.5 us -> 49.7 us (0.965)
  waiting for transfers between devices: 11.9 us -> 9.06 us
  starting transfers between devices: 19.7 us -> 21 us
    ppermute x19 -> x20, waiting for transfers between devices: 11.9 us -> 9.06 us  [send(): return lax.ppermute(value, AXES, pairs)]
    ppermute x19 -> x20, starting transfers between devices: 19.7 us -> 21 us  [send(): return lax.ppermute(value, AXES, pairs)]
    pallas_call x11 -> x9, Pallas kernels: 7.44 us -> 7.52 us  [call(): pl.pallas_call(lambda *refs: kernel(*refs[:len(operands)], *refs[len(oper...]
  transfers between devices with their start and end apart: 19 -> 20, of which waited for: 9 -> 8; matrix products, arithmetic and copies ran while one was open for 0% -> 0% of each run, Pallas kernels for 17% -> 18%
where the time goes in v13:
time: 49.7 us; the launch traced here: 49.6 us
  starting transfers between devices  21 us (42%)
  Pallas kernels  18.8 us (38%)
  waiting for transfers between devices  9.06 us (18%)
  between operations  0.75 us (2%)
    ppermute x20, starting transfers between devices, send(): return lax.ppermute(value, AXES, pairs)  21 us
    ppermute x20, waiting for transfers between devices, send(): return lax.ppermute(value, AXES, pairs)  9.06 us
    pallas_call x1, Pallas kernels, local_terms(): pl.pallas_call(local_kernel, out_shape=(f32(rows, rank), f32(rank // 2, d...  8.33 us
    pallas_call x9, Pallas kernels, call(): pl.pallas_call(lambda *refs: kernel(*refs[:len(operands)], *refs[len(oper...  7.52 us
    pallas_call x2, Pallas kernels, streamed(): pl.pallas_call(kernel, out_shape=out, in_specs=[VMEM] * len(operands), ou...  2.93 us
  transfers between devices with their start and end apart: 20, of which 8 were waited for; matrix products, arithmetic and copies ran while one was open for 0% of the time, Pallas kernels for 18%

profile of v13, /device:TPU:0, one launch (start us, length us, event | category | flops | bytes accessed | tf_op | source)
XLA Modules:
  0.0 49.6 jit_solution(11020981003427343653)
XLA Ops:
  0.6 8.3 %local_terms.1 = (f32[1024,256]{1,0:T(8,128)S(1)}, f32[128,1024]{1,0:T(8,128)S(1)}, f32[128,1024]{1,0:T(8,128)S(1)}, f32[192,128]{1,0:T(8,128)S(1)}, f32[192,128]{1,0:T(8,128)S(1)}) custom-call(f32[1024,1024]{1,0:T(8,128)} %features_hbm.1, f32[1024,256]{1,0:T(8,128)} %sketch_hbm.1), custom_call_target="tpu_custom_call" | custom-call | flops 4000000000 | bytes 8388608 | tf_op jit(solution)/shard_map/local_terms/pallas_call | solution.py:209
  9.0 0.5 %collective-permute-start.1 = (f32[128,1024]{1,0:T(8,128)S(1)}, f32[128,1024]{1,0:T(8,128)S(1)}, u32[]{:S(2)}, u32[]{:S(2)}) collective-permute-start(f32[128,1024]{1,0:T(8,128)S(1)} %get-tuple-element.22), channel_id=1, source_target_pairs={{0,2},{1,3},{2,0},{3,1},{4,6},{5,7},{6,4},{7,5},{8,10},{9,11},{10,... | collective-permute-start | bytes 1572872 | tf_op jit(solution)/shard_map/ppermute | solution.py:373
  9.5 0.1 collective-permute-start
  9.6 1.6 %collective-permute-done.refs_2_.refs_1_ = f32[192,128]{1,0:T(8,128)S(1)} collective-permute-done((f32[192,128]{1,0:T(8,128)S(1)}, f32[192,128]{1,0:T(8,128)S(1)}, u32[]{:S(2)}, u32[]{:S(2)}) %collective-permute-start) | collective-permute-done | bytes 98336 | tf_op jit(solution)/shard_map/ppermute | solution.py:373
  11.2 0.0 collective-permute-done.1.refs_1_
  11.2 0.1 sums.4
  11.3 3.0 %collective-permute-start.2 = (f32[192,128]{1,0:T(8,128)S(1)}, f32[192,128]{1,0:T(8,128)S(1)}, u32[]{:S(2)}, u32[]{:S(2)}) collective-permute-start(f32[192,128]{1,0:T(8,128)S(1)} %add.7), channel_id=1, source_target_pairs={{0,8},{1,9},{2,10},{3,11},{4,12},{5,13},{6,14},{7,15},{8,0},{9,1},... | collective-permute-start | bytes 294920 | tf_op jit(solution)/shard_map/ppermute | solution.py:373
  14.3 1.5 %collective-permute-start.4 = (f32[32,1024]{1,0:T(8,128)S(1)}, f32[32,1024]{1,0:T(8,128)S(1)}, u32[]{:S(2)}, u32[]{:S(2)}) collective-permute-start(f32[32,1024]{1,0:T(8,128)S(1)} %get-tuple-element.25), channel_id=1, source_target_pairs={{0,1},{1,0},{2,3},{3,2},{4,5},{5,4},{6,7},{7,6},{8,9},{9,8},{10,11... | collective-permute-start | bytes 393224 | tf_op jit(solution)/shard_map/ppermute | solution.py:373
  15.8 1.5 %collective-permute-start.5 = (f32[32,1024]{1,0:T(8,128)S(1)}, f32[32,1024]{1,0:T(8,128)S(1)}, u32[]{:S(2)}, u32[]{:S(2)}) collective-permute-start(f32[32,1024]{1,0:T(8,128)S(1)} %get-tuple-element.26), channel_id=1, source_target_pairs={{0,4},{1,5},{2,6},{3,7},{4,0},{5,1},{6,2},{7,3},{8,12},{9,13},{10,... | collective-permute-start | bytes 393224 | tf_op jit(solution)/shard_map/ppermute | solution.py:373
  17.3 0.5 collective-permute-start.6
  17.8 0.0 collective-permute-done.2
  17.8 2.7 %collective-permute-start.3 = (f32[192,128]{1,0:T(8,128)S(1)}, f32[192,128]{1,0:T(8,128)S(1)}, u32[]{:S(2)}, u32[]{:S(2)}) collective-permute-start(f32[192,128]{1,0:T(8,128)S(1)} %add.6.refs_0_), channel_id=1, source_target_pairs={{0,16},{1,17},{2,18},{3,19},{4,20},{5,21},{6,22},{7,23},{8,24},{9,... | collective-permute-start | bytes 294920 | tf_op jit(solution)/shard_map/ppermute | solution.py:373
  20.4 0.0 collective-permute-done.4.refs_1_
  20.4 1.7 %collective-permute-done.5.refs_2_ = f32[32,1024]{1,0:T(8,128)S(1)} collective-permute-done((f32[32,1024]{1,0:T(8,128)S(1)}, f32[32,1024]{1,0:T(8,128)S(1)}, u32[]{:S(2)}, u32[]{:S(2)}) %collective-permute-start.5) | collective-permute-done | bytes 131104 | tf_op jit(solution)/shard_map/ppermute | solution.py:373
  22.2 1.3 %collective-permute-done.6.refs_3_ = f32[32,1024]{1,0:T(8,128)S(1)} collective-permute-done((f32[32,1024]{1,0:T(8,128)S(1)}, f32[32,1024]{1,0:T(8,128)S(1)}, u32[]{:S(2)}, u32[]{:S(2)}) %collective-permute-start.6) | collective-permute-done | bytes 131104 | tf_op jit(solution)/shard_map/ppermute | solution.py:373
  23.5 0.4 collective-permute-start.10
  24.0 0.8 %collective-permute-done.3.refs_1_ = f32[192,128]{1,0:T(8,128)S(1)} collective-permute-done((f32[192,128]{1,0:T(8,128)S(1)}, f32[192,128]{1,0:T(8,128)S(1)}, u32[]{:S(2)}, u32[]{:S(2)}) %collective-permute-start.3) | collective-permute-done | bytes 98336 | tf_op jit(solution)/shard_map/ppermute | solution.py:373
  24.8 1.4 %collective-permute-start.7 = (f32[192,128]{1,0:T(8,128)S(1)}, f32[192,128]{1,0:T(8,128)S(1)}, u32[]{:S(2)}, u32[]{:S(2)}) collective-permute-start(f32[192,128]{1,0:T(8,128)S(1)} %add.8.refs_0_), channel_id=1, source_target_pairs={{0,1},{1,0},{2,3},{3,2},{4,5},{5,4},{6,7},{7,6},{8,9},{9,8},{10,11... | collective-permute-start | bytes 294920 | tf_op jit(solution)/shard_map/ppermute | solution.py:373
  26.2 1.5 %collective-permute-start.8 = (f32[192,128]{1,0:T(8,128)S(1)}, f32[192,128]{1,0:T(8,128)S(1)}, u32[]{:S(2)}, u32[]{:S(2)}) collective-permute-start(f32[192,128]{1,0:T(8,128)S(1)} %add.8.refs_0_), channel_id=1, source_target_pairs={{0,4},{1,5},{2,6},{3,7},{4,0},{5,1},{6,2},{7,3},{8,12},{9,13},{10,... | collective-permute-start | bytes 294920 | tf_op jit(solution)/shard_map/ppermute | solution.py:373
  27.7 0.6 %collective-permute-start.9 = (f32[192,128]{1,0:T(8,128)S(1)}, f32[192,128]{1,0:T(8,128)S(1)}, u32[]{:S(2)}, u32[]{:S(2)}) collective-permute-start(f32[192,128]{1,0:T(8,128)S(1)} %add.8.refs_0_), channel_id=1, source_target_pairs={{0,5},{1,4},{2,7},{3,6},{4,1},{5,0},{6,3},{7,2},{8,13},{9,12},{10,... | collective-permute-start | bytes 294920 | tf_op jit(solution)/shard_map/ppermute | solution.py:373
  28.3 0.2 collective-permute-done.10.refs_1_
  28.6 2.7 %collective-permute-start.12 = (f32[32,1024]{1,0:T(8,128)S(1)}, f32[32,1024]{1,0:T(8,128)S(1)}, u32[]{:S(2)}, u32[]{:S(2)}) collective-permute-start(f32[32,1024]{1,0:T(8,128)S(1)} %sums.6.refs_4_.refs_0_), channel_id=1, source_target_pairs={{0,16},{1,17},{2,18},{3,19},{4,20},{5,21},{6,22},{7,23},{8,24},{9,... | collective-permute-start | bytes 393224 | tf_op jit(solution)/shard_map/ppermute | solution.py:373
  31.3 0.0 collective-permute-done.7.refs_1_
  31.3 0.0 collective-permute-done.8.refs_2_
  31.3 2.0 %collective-permute-done.9.refs_3_ = f32[192,128]{1,0:T(8,128)S(1)} collective-permute-done((f32[192,128]{1,0:T(8,128)S(1)}, f32[192,128]{1,0:T(8,128)S(1)}, u32[]{:S(2)}, u32[]{:S(2)}) %collective-permute-start.9) | collective-permute-done | bytes 98336 | tf_op jit(solution)/shard_map/ppermute | solution.py:373
  33.3 0.1 collective-permute-start.11
  33.3 1.3 %collective-permute-done.11.refs_1_ = f32[192,128]{1,0:T(8,128)S(1)} collective-permute-done((f32[192,128]{1,0:T(8,128)S(1)}, f32[192,128]{1,0:T(8,128)S(1)}, u32[]{:S(2)}, u32[]{:S(2)}) %collective-permute-start.11) | collective-permute-done | bytes 98336 | tf_op jit(solution)/shard_map/ppermute | solution.py:373
  34.6 1.9 %first_part.1 = (f32[256,256]{1,0:T(8,128)S(1)}, f32[256,256]{1,0:T(8,128)S(1)}, f32[16,128]{1,0:T(8,128)S(1)}) custom-call(f32[192,128]{1,0:T(8,128)S(1)} %add.9.refs_0_, f32[192,128]{1,0:T(8,128)S(1)} %collective-permute-done.11.refs_1_), custom_call_target="tpu_custom_call" | custom-call | flops 1000000 | bytes 1000000 | tf_op jit(solution)/shard_map/first_part/pallas_call | solution.py:229
  36.6 0.0 collective-permute-done.12.refs_1_
  36.6 0.9 %collective-permute-start.13 = (f32[32,1024]{1,0:T(8,128)S(1)}, f32[32,1024]{1,0:T(8,128)S(1)}, u32[]{:S(2)}, u32[]{:S(2)}) collective-permute-start(f32[32,1024]{1,0:T(8,128)S(1)} %sums.7.refs_3_.refs_0_), channel_id=1, source_target_pairs={{0,1},{1,0},{2,3},{3,2},{4,5},{5,4},{6,7},{7,6},{8,9},{9,8},{10,11... | collective-permute-start | bytes 393224 | tf_op jit(solution)/shard_map/ppermute | solution.py:373
  37.5 1.5 %collective-permute-start.14 = (f32[32,1024]{1,0:T(8,128)S(1)}, f32[32,1024]{1,0:T(8,128)S(1)}, u32[]{:S(2)}, u32[]{:S(2)}) collective-permute-start(f32[32,1024]{1,0:T(8,128)S(1)} %sums.7.refs_3_.refs_0_), channel_id=1, source_target_pairs={{0,4},{1,5},{2,6},{3,7},{4,0},{5,1},{6,2},{7,3},{8,12},{9,13},{10,... | collective-permute-start | bytes 393224 | tf_op jit(solution)/shard_map/ppermute | solution.py:373
  39.0 1.1 %collective-permute-start.15 = (f32[32,1024]{1,0:T(8,128)S(1)}, f32[32,1024]{1,0:T(8,128)S(1)}, u32[]{:S(2)}, u32[]{:S(2)}) collective-permute-start(f32[32,1024]{1,0:T(8,128)S(1)} %sums.7.refs_3_.refs_0_), channel_id=1, source_target_pairs={{0,5},{1,4},{2,7},{3,6},{4,1},{5,0},{6,3},{7,2},{8,13},{9,12},{10,... | collective-permute-start | bytes 393224 | tf_op jit(solution)/shard_map/ppermute | solution.py:373
  40.2 0.0 collective-permute-start.16
  40.2 5.4 %last_part.1 = (f32[256,256]{1,0:T(8,128)S(1)}, f32[256,256]{1,0:T(8,128)S(1)}, f32[256,256]{1,0:T(8,128)}) custom-call(f32[256,256]{1,0:T(8,128)S(1)} %get-tuple-element.27.refs_2_.refs_0_, f32[256,256]{1,0:T(8,128)S(1)} %get-tuple-element.28.refs_1_, f32[16,128]{1,0:T(8,128)S(1)} %get-tuple-element.29.refs_2_, f32[32,1024]{1,0:T(8,128)S(1)} %sums.7.refs_3_.refs_0_), custom_call_target="tpu_custom_call" | custom-call | flops 3000000000 | bytes 1000000 | tf_op jit(solution)/shard_map/last_part/pallas_call | solution.py:229
  45.6 0.0 collective-permute-done.13.refs_1_
  45.6 0.5 %collective-permute-start.17 = (f32[32,1024]{1,0:T(8,128)S(1)}, f32[32,1024]{1,0:T(8,128)S(1)}, u32[]{:S(2)}, u32[]{:S(2)}) collective-permute-start(f32[32,1024]{1,0:T(8,128)S(1)} %collective-permute-done.13.refs_1_), channel_id=1, source_target_pairs={{0,2},{1,3},{2,0},{3,1},{4,6},{5,7},{6,4},{7,5},{8,10},{9,11},{10,... | collective-permute-start | bytes 393224 | tf_op jit(solution)/shard_map/ppermute | solution.py:373
  46.1 0.0 collective-permute-done.14.refs_2_
  46.1 0.1 collective-permute-start.18
  46.2 0.1 collective-permute-done.15.refs_3_
  46.2 0.4 collective-permute-start.19
  46.6 1.4 %basis.1 = f32[1024,256]{1,0:T(8,128)} custom-call(f32[1024,256]{1,0:T(8,128)S(1)} %get-tuple-element.18.sampled_ref, f32[256,256]{1,0:T(8,128)S(1)} %get-tuple-element.30.flipped_ref), custom_call_target="tpu_custom_call" | custom-call | flops 2000000000 | bytes 2097152 | tf_op jit(solution)/shard_map/basis/pallas_call | solution.py:329
  48.0 0.0 collective-permute-done.16.refs_4_
  48.0 0.0 collective-permute-done.17.refs_5_
  48.0 0.0 collective-permute-done.18.refs_6_
  48.1 0.0 collective-permute-done.19.refs_7_
  48.1 1.5 %project.1 = f32[256,1024]{1,0:T(8,128)} custom-call(f32[256,256]{1,0:T(8,128)S(1)} %get-tuple-element.32.inverse_ref, f32[32,1024]{1,0:T(8,128)S(1)} %sums.7.refs_3_.refs_0_, f32[32,1024]{1,0:T(8,128)S(1)} %collective-permute-done.13.refs_1_, f32[32,1024]{1,0:T(8,128)S(1)} %collective-permute-done.14.refs_2_, ...), custom_call_target="tpu_custom_call" | custom-call | flops 400000000 | bytes 2097152 | tf_op jit(solution)/shard_map/project/pallas_call | solution.py:329
  (7 shorter events, 0.1 us)
Async XLA Ops:
  9.0 2.2 %collective-permute-start.1 = (f32[128,1024]{1,0:T(8,128)S(1)}, f32[128,1024]{1,0:T(8,128)S(1)}, u32[]{:S(2)}, u32[]{:S(2)}) collective-permute-start(f32[128,1024]{1,0:T(8,128)S(1)} %get-tuple-element.22), channel_id=1, source_target_pairs={{0,2},{1,3},{2,0},{3,1},{4,6},{5,7},{6,4},{7,5},{8,10},{9,11},{10,... | collective-permute-start | bytes 1572872 | tf_op jit(solution)/shard_map/ppermute | solution.py:373
  9.5 1.7 %collective-permute-start = (f32[192,128]{1,0:T(8,128)S(1)}, f32[192,128]{1,0:T(8,128)S(1)}, u32[]{:S(2)}, u32[]{:S(2)}) collective-permute-start(f32[192,128]{1,0:T(8,128)S(1)} %get-tuple-element.20), channel_id=1, source_target_pairs={{0,2},{1,3},{2,0},{3,1},{4,6},{5,7},{6,4},{7,5},{8,10},{9,11},{10,... | collective-permute-start | bytes 294920 | tf_op jit(solution)/shard_map/ppermute | solution.py:373
  11.3 6.5 %collective-permute-start.2 = (f32[192,128]{1,0:T(8,128)S(1)}, f32[192,128]{1,0:T(8,128)S(1)}, u32[]{:S(2)}, u32[]{:S(2)}) collective-permute-start(f32[192,128]{1,0:T(8,128)S(1)} %add.7), channel_id=1, source_target_pairs={{0,8},{1,9},{2,10},{3,11},{4,12},{5,13},{6,14},{7,15},{8,0},{9,1},... | collective-permute-start | bytes 294920 | tf_op jit(solution)/shard_map/ppermute | solution.py:373
  14.3 6.2 %collective-permute-start.4 = (f32[32,1024]{1,0:T(8,128)S(1)}, f32[32,1024]{1,0:T(8,128)S(1)}, u32[]{:S(2)}, u32[]{:S(2)}) collective-permute-start(f32[32,1024]{1,0:T(8,128)S(1)} %get-tuple-element.25), channel_id=1, source_target_pairs={{0,1},{1,0},{2,3},{3,2},{4,5},{5,4},{6,7},{7,6},{8,9},{9,8},{10,11... | collective-permute-start | bytes 393224 | tf_op jit(solution)/shard_map/ppermute | solution.py:373
  15.8 6.4 %collective-permute-start.5 = (f32[32,1024]{1,0:T(8,128)S(1)}, f32[32,1024]{1,0:T(8,128)S(1)}, u32[]{:S(2)}, u32[]{:S(2)}) collective-permute-start(f32[32,1024]{1,0:T(8,128)S(1)} %get-tuple-element.26), channel_id=1, source_target_pairs={{0,4},{1,5},{2,6},{3,7},{4,0},{5,1},{6,2},{7,3},{8,12},{9,13},{10,... | collective-permute-start | bytes 393224 | tf_op jit(solution)/shard_map/ppermute | solution.py:373
  17.3 6.2 %collective-permute-start.6 = (f32[32,1024]{1,0:T(8,128)S(1)}, f32[32,1024]{1,0:T(8,128)S(1)}, u32[]{:S(2)}, u32[]{:S(2)}) collective-permute-start(f32[32,1024]{1,0:T(8,128)S(1)} %get-tuple-element.23.refs_2_), channel_id=1, source_target_pairs={{0,5},{1,4},{2,7},{3,6},{4,1},{5,0},{6,3},{7,2},{8,13},{9,12},{10,... | collective-permute-start | bytes 393224 | tf_op jit(solution)/shard_map/ppermute | solution.py:373
  17.8 7.0 %collective-permute-start.3 = (f32[192,128]{1,0:T(8,128)S(1)}, f32[192,128]{1,0:T(8,128)S(1)}, u32[]{:S(2)}, u32[]{:S(2)}) collective-permute-start(f32[192,128]{1,0:T(8,128)S(1)} %add.6.refs_0_), channel_id=1, source_target_pairs={{0,16},{1,17},{2,18},{3,19},{4,20},{5,21},{6,22},{7,23},{8,24},{9,... | collective-permute-start | bytes 294920 | tf_op jit(solution)/shard_map/ppermute | solution.py:373
  23.5 5.0 %collective-permute-start.10 = (f32[32,1024]{1,0:T(8,128)S(1)}, f32[32,1024]{1,0:T(8,128)S(1)}, u32[]{:S(2)}, u32[]{:S(2)}) collective-permute-start(f32[32,1024]{1,0:T(8,128)S(1)} %sums.5.refs_2_.refs_0_), channel_id=1, source_target_pairs={{0,8},{1,9},{2,10},{3,11},{4,12},{5,13},{6,14},{7,15},{8,0},{9,1},... | collective-permute-start | bytes 393224 | tf_op jit(solution)/shard_map/ppermute | solution.py:373
  24.8 6.5 %collective-permute-start.7 = (f32[192,128]{1,0:T(8,128)S(1)}, f32[192,128]{1,0:T(8,128)S(1)}, u32[]{:S(2)}, u32[]{:S(2)}) collective-permute-start(f32[192,128]{1,0:T(8,128)S(1)} %add.8.refs_0_), channel_id=1, source_target_pairs={{0,1},{1,0},{2,3},{3,2},{4,5},{5,4},{6,7},{7,6},{8,9},{9,8},{10,11... | collective-permute-start | bytes 294920 | tf_op jit(solution)/shard_map/ppermute | solution.py:373
  26.2 5.0 %collective-permute-start.8 = (f32[192,128]{1,0:T(8,128)S(1)}, f32[192,128]{1,0:T(8,128)S(1)}, u32[]{:S(2)}, u32[]{:S(2)}) collective-permute-start(f32[192,128]{1,0:T(8,128)S(1)} %add.8.refs_0_), channel_id=1, source_target_pairs={{0,4},{1,5},{2,6},{3,7},{4,0},{5,1},{6,2},{7,3},{8,12},{9,13},{10,... | collective-permute-start | bytes 294920 | tf_op jit(solution)/shard_map/ppermute | solution.py:373
  27.7 5.5 %collective-permute-start.9 = (f32[192,128]{1,0:T(8,128)S(1)}, f32[192,128]{1,0:T(8,128)S(1)}, u32[]{:S(2)}, u32[]{:S(2)}) collective-permute-start(f32[192,128]{1,0:T(8,128)S(1)} %add.8.refs_0_), channel_id=1, source_target_pairs={{0,5},{1,4},{2,7},{3,6},{4,1},{5,0},{6,3},{7,2},{8,13},{9,12},{10,... | collective-permute-start | bytes 294920 | tf_op jit(solution)/shard_map/ppermute | solution.py:373
  28.6 8.0 %collective-permute-start.12 = (f32[32,1024]{1,0:T(8,128)S(1)}, f32[32,1024]{1,0:T(8,128)S(1)}, u32[]{:S(2)}, u32[]{:S(2)}) collective-permute-start(f32[32,1024]{1,0:T(8,128)S(1)} %sums.6.refs_4_.refs_0_), channel_id=1, source_target_pairs={{0,16},{1,17},{2,18},{3,19},{4,20},{5,21},{6,22},{7,23},{8,24},{9,... | collective-permute-start | bytes 393224 | tf_op jit(solution)/shard_map/ppermute | solution.py:373
  33.3 1.4 %collective-permute-start.11 = (f32[192,128]{1,0:T(8,128)S(1)}, f32[192,128]{1,0:T(8,128)S(1)}, u32[]{:S(2)}, u32[]{:S(2)}) collective-permute-start(f32[192,128]{1,0:T(8,128)S(1)} %add.9.refs_0_), channel_id=1, source_target_pairs={{0,2},{1,3},{2,0},{3,1},{4,6},{5,7},{6,4},{7,5},{8,10},{9,11},{10,... | collective-permute-start | bytes 294920 | tf_op jit(solution)/shard_map/ppermute | solution.py:373
  36.6 9.0 %collective-permute-start.13 = (f32[32,1024]{1,0:T(8,128)S(1)}, f32[32,1024]{1,0:T(8,128)S(1)}, u32[]{:S(2)}, u32[]{:S(2)}) collective-permute-start(f32[32,1024]{1,0:T(8,128)S(1)} %sums.7.refs_3_.refs_0_), channel_id=1, source_target_pairs={{0,1},{1,0},{2,3},{3,2},{4,5},{5,4},{6,7},{7,6},{8,9},{9,8},{10,11... | collective-permute-start | bytes 393224 | tf_op jit(solution)/shard_map/ppermute | solution.py:373
  37.5 8.6 %collective-permute-start.14 = (f32[32,1024]{1,0:T(8,128)S(1)}, f32[32,1024]{1,0:T(8,128)S(1)}, u32[]{:S(2)}, u32[]{:S(2)}) collective-permute-start(f32[32,1024]{1,0:T(8,128)S(1)} %sums.7.refs_3_.refs_0_), channel_id=1, source_target_pairs={{0,4},{1,5},{2,6},{3,7},{4,0},{5,1},{6,2},{7,3},{8,12},{9,13},{10,... | collective-permute-start | bytes 393224 | tf_op jit(solution)/shard_map/ppermute | solution.py:373
  39.0 7.2 %collective-permute-start.15 = (f32[32,1024]{1,0:T(8,128)S(1)}, f32[32,1024]{1,0:T(8,128)S(1)}, u32[]{:S(2)}, u32[]{:S(2)}) collective-permute-start(f32[32,1024]{1,0:T(8,128)S(1)} %sums.7.refs_3_.refs_0_), channel_id=1, source_target_pairs={{0,5},{1,4},{2,7},{3,6},{4,1},{5,0},{6,3},{7,2},{8,13},{9,12},{10,... | collective-permute-start | bytes 393224 | tf_op jit(solution)/shard_map/ppermute | solution.py:373
  40.2 7.9 %collective-permute-start.16 = (f32[32,1024]{1,0:T(8,128)S(1)}, f32[32,1024]{1,0:T(8,128)S(1)}, u32[]{:S(2)}, u32[]{:S(2)}) collective-permute-start(f32[32,1024]{1,0:T(8,128)S(1)} %sums.7.refs_3_.refs_0_), channel_id=1, source_target_pairs={{0,2},{1,3},{2,0},{3,1},{4,6},{5,7},{6,4},{7,5},{8,10},{9,11},{10,... | collective-permute-start | bytes 393224 | tf_op jit(solution)/shard_map/ppermute | solution.py:373
  45.6 2.5 %collective-permute-start.17 = (f32[32,1024]{1,0:T(8,128)S(1)}, f32[32,1024]{1,0:T(8,128)S(1)}, u32[]{:S(2)}, u32[]{:S(2)}) collective-permute-start(f32[32,1024]{1,0:T(8,128)S(1)} %collective-permute-done.13.refs_1_), channel_id=1, source_target_pairs={{0,2},{1,3},{2,0},{3,1},{4,6},{5,7},{6,4},{7,5},{8,10},{9,11},{10,... | collective-permute-start | bytes 393224 | tf_op jit(solution)/shard_map/ppermute | solution.py:373
  46.1 2.0 %collective-permute-start.18 = (f32[32,1024]{1,0:T(8,128)S(1)}, f32[32,1024]{1,0:T(8,128)S(1)}, u32[]{:S(2)}, u32[]{:S(2)}) collective-permute-start(f32[32,1024]{1,0:T(8,128)S(1)} %collective-permute-done.14.refs_2_), channel_id=1, source_target_pairs={{0,2},{1,3},{2,0},{3,1},{4,6},{5,7},{6,4},{7,5},{8,10},{9,11},{10,... | collective-permute-start | bytes 393224 | tf_op jit(solution)/shard_map/ppermute | solution.py:373
  46.2 1.8 %collective-permute-start.19 = (f32[32,1024]{1,0:T(8,128)S(1)}, f32[32,1024]{1,0:T(8,128)S(1)}, u32[]{:S(2)}, u32[]{:S(2)}) collective-permute-start(f32[32,1024]{1,0:T(8,128)S(1)} %collective-permute-done.15.refs_3_), channel_id=1, source_target_pairs={{0,2},{1,3},{2,0},{3,1},{4,6},{5,7},{6,4},{7,5},{8,10},{9,11},{10,... | collective-permute-start | bytes 393224 | tf_op jit(solution)/shard_map/ppermute | solution.py:373

commit v14 on v13

--- a/solution.py
+++ b/solution.py
@@ -279,7 +279,7 @@
     eliminate(a_ref, factor_ref, buffer_ref, 0, PANEL)
 
 
-def last_part_kernel(scale, first, from_ref, upper_ref, norm_ref, inverse_ref, flipped_ref, factor_ref, a_ref, buffer_ref):
+def last_part_kernel(scale, first, from_ref, upper_ref, norm_ref, inverse_ref, factor_ref, a_ref, buffer_ref):
     size = a_ref.shape[0]
     a_ref[...] = from_ref[...]
     eliminate(a_ref, factor_ref, buffer_ref, first, size)
@@ -288,9 +288,7 @@
     factor_ref[first:, :] = factor_ref[first:, :] * grow
     col = lax.broadcasted_iota(jnp.int32, (size, size), 1)
     row = lax.broadcasted_iota(jnp.int32, (size, size), 0)
-    inverse = jnp.where(col <= row, a_ref[...], 0.0) * shrink
-    inverse_ref[...] = inverse
-    flipped_ref[...] = inverse.T * scale
+    inverse_ref[...] = jnp.where(col <= row, a_ref[...], 0.0) * shrink
 
 
 def buffers(*shapes):
@@ -304,7 +302,7 @@
 
 def last_part(state, size, scale, first, after):
     kernel = lambda *refs: last_part_kernel(scale, first, *refs)
-    return call(kernel, "last_part", (f32(size, size),) * 3, *state, after=after, scratch=buffers((size, size)), flops=3 * 10**9)
+    return call(kernel, "last_part", (f32(size, size),) * 2, *state, after=after, scratch=buffers((size, size)), flops=3 * 10**9)
 
 
 def copy_out(block_ref, out_hbm, span, sem):
@@ -313,12 +311,12 @@
     return copy
 
 
-def basis_kernel(sampled_ref, flipped_ref, basis_hbm, basis_ref, sems):
-    flipped = split(flipped_ref[...])
+def basis_kernel(scale, sampled_ref, inverse_ref, basis_hbm, basis_ref, sems):
+    inverse = split(inverse_ref[...] * scale)
     copies = []
     for at in range(sampled_ref.shape[0] // BLOCK):
         span = slice(at * BLOCK, (at + 1) * BLOCK)
-        basis_ref[span, :] = product(split(sampled_ref[span, :]), flipped, 1, 0)
+        basis_ref[span, :] = product(split(sampled_ref[span, :]), inverse, 1, 1)
         copies.append(copy_out(basis_ref, basis_hbm, (pl.ds(at * BLOCK, BLOCK), slice(None)), sems.at[at]))
     for copy in copies:
         copy.wait()
@@ -338,8 +336,9 @@
     )(*operands)
 
 
-def basis_of(sampled, flipped):
-    return streamed(basis_kernel, "basis", f32(*sampled.shape), (sampled, flipped), (), 2 * 10**9)
+def basis_of(sampled, inverse, scale):
+    kernel = lambda *refs: basis_kernel(scale, *refs)
+    return streamed(kernel, "basis", f32(*sampled.shape), (sampled, inverse), (), 2 * 10**9)
 
 
 def project_kernel(inverse_ref, *refs):
@@ -384,9 +383,10 @@
     return wide + narrow
 
 
-def spread(parts, masks):
-    first, *rest = parts
-    return [first] + [send(part, *mask) for part, mask in zip(rest, masks)]
+def to_plane(parts):
+    order = sorted(range(len(PLANE)), key=lambda at: -PLANE[at][0] - PLANE[at][1])
+    sent = {at: send(parts[at], *PLANE[at]) for at in order}
+    return [sent[at] for at in range(len(PLANE))]
 
 
 def per_device(features, sketch):
@@ -395,13 +395,13 @@
     sampled, keep, other, gram, gram_other = local_terms(features, sketch)
     gram_other = send(gram_other, *CORE)
     parts = sums([keep, send(other, *CORE)], 4, after=(gram_other,))
-    cross = spread(parts, PLANE)
+    cross = [parts[0]] + to_plane(parts[1:])
     gram = add([gram, gram_other], parts[-1:])
     gram = gram + send(gram, *NEAR)
     gram_other = send(gram, *FAR)
     (line,) = sums(cross)
     gram = add([gram, gram_other], (line,))
-    grams = [gram] + [send(gram, *mask) for mask in PLANE]
+    grams = [gram] + to_plane([gram] * 3)
     (line,) = sums([line, send(line, *NEAR)], masks=(0, 1))
     gram = add(grams, (line,))
     for mask in spare_bits():
@@ -409,10 +409,10 @@
         gram = gram + send(gram, *mask)
     *state, norm = first_part(gram, send(gram, *CORE), size, ())
     (line,) = sums([line, send(line, *FAR)], masks=(0, 2), after=state[:1])
-    plane = [line] + [send(line, *mask) for mask in PLANE]
-    inverse, flipped, factor = last_part((*state, norm), size, scale, PANEL, (line,))
+    plane = [line] + to_plane([line] * 3)
+    inverse, factor = last_part((*state, norm), size, scale, PANEL, (line,))
     cross = plane + [send(part, *CORE) for part in plane]
-    return (basis_of(sampled, flipped), factor, project(inverse, cross))
+    return (basis_of(sampled, inverse, scale), factor, project(inverse, cross))
 
 
 def solution(mesh):

time: 49.7 us -> 49.4 us (level)
  transfers between devices with their start and end apart: 20 -> 20, of which waited for: 8 -> 10; matrix products, arithmetic and copies ran while one was open for 0% -> 0% of each run, Pallas kernels for 18% -> 18%
where the time goes in v14:
time: 49.4 us; the launch traced here: 49.3 us
  starting transfers between devices  20.6 us (42%)
  Pallas kernels  18.8 us (38%)
  waiting for transfers between devices  9.09 us (18%)
  between operations  0.75 us (2%)
    ppermute x20, starting transfers between devices, send(): return lax.ppermute(value, AXES, pairs)  20.6 us
    ppermute x20, waiting for transfers between devices, send(): return lax.ppermute(value, AXES, pairs)  9.09 us
    pallas_call x1, Pallas kernels, local_terms(): pl.pallas_call(local_kernel, out_shape=(f32(rows, rank), f32(rank // 2, d...  8.33 us
    pallas_call x9, Pallas kernels, call(): pl.pallas_call(lambda *refs: kernel(*refs[:len(operands)], *refs[len(oper...  7.53 us
    pallas_call x2, Pallas kernels, streamed(): pl.pallas_call(kernel, out_shape=out, in_specs=[VMEM] * len(operands), ou...  2.97 us
  transfers between devices with their start and end apart: 20, of which 10 were waited for; matrix products, arithmetic and copies ran while one was open for 0% of the time, Pallas kernels for 18%

profile of v14, /device:TPU:0, one launch (start us, length us, event | category | flops | bytes accessed | tf_op | source)
XLA Modules:
  0.0 49.3 jit_solution(14329469893911420580)
XLA Ops:
  0.6 8.3 %local_terms.1 = (f32[1024,256]{1,0:T(8,128)S(1)}, f32[128,1024]{1,0:T(8,128)S(1)}, f32[128,1024]{1,0:T(8,128)S(1)}, f32[192,128]{1,0:T(8,128)S(1)}, f32[192,128]{1,0:T(8,128)S(1)}) custom-call(f32[1024,1024]{1,0:T(8,128)} %features_hbm.1, f32[1024,256]{1,0:T(8,128)} %sketch_hbm.1), custom_call_target="tpu_custom_call" | custom-call | flops 4000000000 | bytes 8388608 | tf_op jit(solution)/shard_map/local_terms/pallas_call | solution.py:209
  9.0 0.5 %collective-permute-start.1 = (f32[128,1024]{1,0:T(8,128)S(1)}, f32[128,1024]{1,0:T(8,128)S(1)}, u32[]{:S(2)}, u32[]{:S(2)}) collective-permute-start(f32[128,1024]{1,0:T(8,128)S(1)} %get-tuple-element.21), channel_id=1, source_target_pairs={{0,2},{1,3},{2,0},{3,1},{4,6},{5,7},{6,4},{7,5},{8,10},{9,11},{10,... | collective-permute-start | bytes 1572872 | tf_op jit(solution)/shard_map/ppermute | solution.py:372
  9.5 0.1 collective-permute-start
  9.6 1.6 %collective-permute-done.refs_2_.refs_1_ = f32[192,128]{1,0:T(8,128)S(1)} collective-permute-done((f32[192,128]{1,0:T(8,128)S(1)}, f32[192,128]{1,0:T(8,128)S(1)}, u32[]{:S(2)}, u32[]{:S(2)}) %collective-permute-start) | collective-permute-done | bytes 98336 | tf_op jit(solution)/shard_map/ppermute | solution.py:372
  11.2 0.0 collective-permute-done.1.refs_1_
  11.2 0.1 sums.4
  11.3 3.0 %collective-permute-start.2 = (f32[192,128]{1,0:T(8,128)S(1)}, f32[192,128]{1,0:T(8,128)S(1)}, u32[]{:S(2)}, u32[]{:S(2)}) collective-permute-start(f32[192,128]{1,0:T(8,128)S(1)} %add.7), channel_id=1, source_target_pairs={{0,8},{1,9},{2,10},{3,11},{4,12},{5,13},{6,14},{7,15},{8,0},{9,1},... | collective-permute-start | bytes 294920 | tf_op jit(solution)/shard_map/ppermute | solution.py:372
  14.3 1.5 %collective-permute-start.4 = (f32[32,1024]{1,0:T(8,128)S(1)}, f32[32,1024]{1,0:T(8,128)S(1)}, u32[]{:S(2)}, u32[]{:S(2)}) collective-permute-start(f32[32,1024]{1,0:T(8,128)S(1)} %get-tuple-element.24), channel_id=1, source_target_pairs={{0,1},{1,0},{2,3},{3,2},{4,5},{5,4},{6,7},{7,6},{8,9},{9,8},{10,11... | collective-permute-start | bytes 393224 | tf_op jit(solution)/shard_map/ppermute | solution.py:372
  15.8 1.5 %collective-permute-start.5 = (f32[32,1024]{1,0:T(8,128)S(1)}, f32[32,1024]{1,0:T(8,128)S(1)}, u32[]{:S(2)}, u32[]{:S(2)}) collective-permute-start(f32[32,1024]{1,0:T(8,128)S(1)} %get-tuple-element.25), channel_id=1, source_target_pairs={{0,4},{1,5},{2,6},{3,7},{4,0},{5,1},{6,2},{7,3},{8,12},{9,13},{10,... | collective-permute-start | bytes 393224 | tf_op jit(solution)/shard_map/ppermute | solution.py:372
  17.3 0.5 collective-permute-start.6
  17.8 0.0 collective-permute-done.2
  17.8 2.7 %collective-permute-start.3 = (f32[192,128]{1,0:T(8,128)S(1)}, f32[192,128]{1,0:T(8,128)S(1)}, u32[]{:S(2)}, u32[]{:S(2)}) collective-permute-start(f32[192,128]{1,0:T(8,128)S(1)} %add.6.refs_0_), channel_id=1, source_target_pairs={{0,16},{1,17},{2,18},{3,19},{4,20},{5,21},{6,22},{7,23},{8,24},{9,... | collective-permute-start | bytes 294920 | tf_op jit(solution)/shard_map/ppermute | solution.py:372
  20.4 0.0 collective-permute-done.4.refs_1_
  20.4 1.7 %collective-permute-done.5.refs_2_ = f32[32,1024]{1,0:T(8,128)S(1)} collective-permute-done((f32[32,1024]{1,0:T(8,128)S(1)}, f32[32,1024]{1,0:T(8,128)S(1)}, u32[]{:S(2)}, u32[]{:S(2)}) %collective-permute-start.5) | collective-permute-done | bytes 131104 | tf_op jit(solution)/shard_map/ppermute | solution.py:372
  22.2 1.3 %collective-permute-done.6.refs_3_ = f32[32,1024]{1,0:T(8,128)S(1)} collective-permute-done((f32[32,1024]{1,0:T(8,128)S(1)}, f32[32,1024]{1,0:T(8,128)S(1)}, u32[]{:S(2)}, u32[]{:S(2)}) %collective-permute-start.6) | collective-permute-done | bytes 131104 | tf_op jit(solution)/shard_map/ppermute | solution.py:372
  23.5 0.4 collective-permute-start.10
  24.0 0.8 %collective-permute-done.3.refs_1_ = f32[192,128]{1,0:T(8,128)S(1)} collective-permute-done((f32[192,128]{1,0:T(8,128)S(1)}, f32[192,128]{1,0:T(8,128)S(1)}, u32[]{:S(2)}, u32[]{:S(2)}) %collective-permute-start.3) | collective-permute-done | bytes 98336 | tf_op jit(solution)/shard_map/ppermute | solution.py:372
  24.8 2.4 %collective-permute-start.9 = (f32[192,128]{1,0:T(8,128)S(1)}, f32[192,128]{1,0:T(8,128)S(1)}, u32[]{:S(2)}, u32[]{:S(2)}) collective-permute-start(f32[192,128]{1,0:T(8,128)S(1)} %add.8.refs_0_), channel_id=1, source_target_pairs={{0,5},{1,4},{2,7},{3,6},{4,1},{5,0},{6,3},{7,2},{8,13},{9,12},{10,... | collective-permute-start | bytes 294920 | tf_op jit(solution)/shard_map/ppermute | solution.py:372
  27.1 0.5 %collective-permute-start.8 = (f32[192,128]{1,0:T(8,128)S(1)}, f32[192,128]{1,0:T(8,128)S(1)}, u32[]{:S(2)}, u32[]{:S(2)}) collective-permute-start(f32[192,128]{1,0:T(8,128)S(1)} %add.8.refs_0_), channel_id=1, source_target_pairs={{0,4},{1,5},{2,6},{3,7},{4,0},{5,1},{6,2},{7,3},{8,12},{9,13},{10,... | collective-permute-start | bytes 294920 | tf_op jit(solution)/shard_map/ppermute | solution.py:372
  27.7 0.7 %collective-permute-start.7 = (f32[192,128]{1,0:T(8,128)S(1)}, f32[192,128]{1,0:T(8,128)S(1)}, u32[]{:S(2)}, u32[]{:S(2)}) collective-permute-start(f32[192,128]{1,0:T(8,128)S(1)} %add.8.refs_0_), channel_id=1, source_target_pairs={{0,1},{1,0},{2,3},{3,2},{4,5},{5,4},{6,7},{7,6},{8,9},{9,8},{10,11... | collective-permute-start | bytes 294920 | tf_op jit(solution)/shard_map/ppermute | solution.py:372
  28.3 0.2 collective-permute-done.10.refs_1_
  28.6 2.7 %collective-permute-start.12 = (f32[32,1024]{1,0:T(8,128)S(1)}, f32[32,1024]{1,0:T(8,128)S(1)}, u32[]{:S(2)}, u32[]{:S(2)}) collective-permute-start(f32[32,1024]{1,0:T(8,128)S(1)} %sums.6.refs_4_.refs_0_), channel_id=1, source_target_pairs={{0,16},{1,17},{2,18},{3,19},{4,20},{5,21},{6,22},{7,23},{8,24},{9,... | collective-permute-start | bytes 393224 | tf_op jit(solution)/shard_map/ppermute | solution.py:372
  31.3 0.0 collective-permute-done.9.refs_3_
  31.3 0.5 %collective-permute-done.8.refs_2_ = f32[192,128]{1,0:T(8,128)S(1)} collective-permute-done((f32[192,128]{1,0:T(8,128)S(1)}, f32[192,128]{1,0:T(8,128)S(1)}, u32[]{:S(2)}, u32[]{:S(2)}) %collective-permute-start.8) | collective-permute-done | bytes 98336 | tf_op jit(solution)/shard_map/ppermute | solution.py:372
  31.8 0.5 %collective-permute-done.7.refs_1_ = f32[192,128]{1,0:T(8,128)S(1)} collective-permute-done((f32[192,128]{1,0:T(8,128)S(1)}, f32[192,128]{1,0:T(8,128)S(1)}, u32[]{:S(2)}, u32[]{:S(2)}) %collective-permute-start.7) | collective-permute-done | bytes 98336 | tf_op jit(solution)/shard_map/ppermute | solution.py:372
  32.3 0.1 collective-permute-start.11
  32.4 1.3 %collective-permute-done.11.refs_1_ = f32[192,128]{1,0:T(8,128)S(1)} collective-permute-done((f32[192,128]{1,0:T(8,128)S(1)}, f32[192,128]{1,0:T(8,128)S(1)}, u32[]{:S(2)}, u32[]{:S(2)}) %collective-permute-start.11) | collective-permute-done | bytes 98336 | tf_op jit(solution)/shard_map/ppermute | solution.py:372
  33.7 1.9 %first_part.1 = (f32[256,256]{1,0:T(8,128)S(1)}, f32[256,256]{1,0:T(8,128)S(1)}, f32[16,128]{1,0:T(8,128)S(1)}) custom-call(f32[192,128]{1,0:T(8,128)S(1)} %add.9.refs_0_, f32[192,128]{1,0:T(8,128)S(1)} %collective-permute-done.11.refs_1_), custom_call_target="tpu_custom_call" | custom-call | flops 1000000 | bytes 1000000 | tf_op jit(solution)/shard_map/first_part/pallas_call | solution.py:229
  35.6 0.3 collective-permute-done.12.refs_1_
  36.0 0.1 collective-permute-start.16
  36.0 2.5 %collective-permute-start.15 = (f32[32,1024]{1,0:T(8,128)S(1)}, f32[32,1024]{1,0:T(8,128)S(1)}, u32[]{:S(2)}, u32[]{:S(2)}) collective-permute-start(f32[32,1024]{1,0:T(8,128)S(1)} %sums.7.refs_3_.refs_0_), channel_id=1, source_target_pairs={{0,5},{1,4},{2,7},{3,6},{4,1},{5,0},{6,3},{7,2},{8,13},{9,12},{10,... | collective-permute-start | bytes 393224 | tf_op jit(solution)/shard_map/ppermute | solution.py:372
  38.5 0.5 %collective-permute-start.14 = (f32[32,1024]{1,0:T(8,128)S(1)}, f32[32,1024]{1,0:T(8,128)S(1)}, u32[]{:S(2)}, u32[]{:S(2)}) collective-permute-start(f32[32,1024]{1,0:T(8,128)S(1)} %sums.7.refs_3_.refs_0_), channel_id=1, source_target_pairs={{0,4},{1,5},{2,6},{3,7},{4,0},{5,1},{6,2},{7,3},{8,12},{9,13},{10,... | collective-permute-start | bytes 393224 | tf_op jit(solution)/shard_map/ppermute | solution.py:372
  39.1 0.5 %collective-permute-start.13 = (f32[32,1024]{1,0:T(8,128)S(1)}, f32[32,1024]{1,0:T(8,128)S(1)}, u32[]{:S(2)}, u32[]{:S(2)}) collective-permute-start(f32[32,1024]{1,0:T(8,128)S(1)} %sums.7.refs_3_.refs_0_), channel_id=1, source_target_pairs={{0,1},{1,0},{2,3},{3,2},{4,5},{5,4},{6,7},{7,6},{8,9},{9,8},{10,11... | collective-permute-start | bytes 393224 | tf_op jit(solution)/shard_map/ppermute | solution.py:372
  39.6 5.4 %last_part.1 = (f32[256,256]{1,0:T(8,128)S(1)}, f32[256,256]{1,0:T(8,128)}) custom-call(f32[256,256]{1,0:T(8,128)S(1)} %get-tuple-element.26.refs_2_.refs_0_, f32[256,256]{1,0:T(8,128)S(1)} %get-tuple-element.27.refs_1_, f32[16,128]{1,0:T(8,128)S(1)} %get-tuple-element.28.refs_2_, f32[32,1024]{1,0:T(8,128)S(1)} %sums.7.refs_3_.refs_0_), custom_call_target="tpu_custom_call" | custom-call | flops 3000000000 | bytes 1000000 | tf_op jit(solution)/shard_map/last_part/pallas_call | solution.py:229
  45.0 0.0 collective-permute-done.15.refs_3_
  45.0 0.0 collective-permute-start.19
  45.0 0.7 %collective-permute-done.14.refs_2_ = f32[32,1024]{1,0:T(8,128)S(1)} collective-permute-done((f32[32,1024]{1,0:T(8,128)S(1)}, f32[32,1024]{1,0:T(8,128)S(1)}, u32[]{:S(2)}, u32[]{:S(2)}) %collective-permute-start.14) | collective-permute-done | bytes 131104 | tf_op jit(solution)/shard_map/ppermute | solution.py:372
  45.7 0.0 collective-permute-start.18
  45.7 0.0 collective-permute-done.13.refs_1_
  45.8 0.5 %collective-permute-start.17 = (f32[32,1024]{1,0:T(8,128)S(1)}, f32[32,1024]{1,0:T(8,128)S(1)}, u32[]{:S(2)}, u32[]{:S(2)}) collective-permute-start(f32[32,1024]{1,0:T(8,128)S(1)} %collective-permute-done.13.refs_1_), channel_id=1, source_target_pairs={{0,2},{1,3},{2,0},{3,1},{4,6},{5,7},{6,4},{7,5},{8,10},{9,11},{10,... | collective-permute-start | bytes 393224 | tf_op jit(solution)/shard_map/ppermute | solution.py:372
  46.3 1.5 %basis.1 = f32[1024,256]{1,0:T(8,128)} custom-call(f32[1024,256]{1,0:T(8,128)S(1)} %get-tuple-element.17.refs_0_, f32[256,256]{1,0:T(8,128)S(1)} %get-tuple-element.29.refs_1_.inverse_ref), custom_call_target="tpu_custom_call" | custom-call | flops 2000000000 | bytes 2097152 | tf_op jit(solution)/shard_map/basis/pallas_call | solution.py:327
  47.7 0.0 collective-permute-done.16.refs_4_
  47.7 0.0 collective-permute-done.19.refs_7_
  47.7 0.0 collective-permute-done.18.refs_6_
  47.8 0.0 collective-permute-done.17.refs_5_
  47.8 1.5 %project.1 = f32[256,1024]{1,0:T(8,128)} custom-call(f32[256,256]{1,0:T(8,128)S(1)} %get-tuple-element.29.refs_1_.inverse_ref, f32[32,1024]{1,0:T(8,128)S(1)} %sums.7.refs_3_.refs_0_, f32[32,1024]{1,0:T(8,128)S(1)} %collective-permute-done.13.refs_1_, f32[32,1024]{1,0:T(8,128)S(1)} %collective-permute-done.14.refs_2_, ...), custom_call_target="tpu_custom_call" | custom-call | flops 400000000 | bytes 2097152 | tf_op jit(solution)/shard_map/project/pallas_call | solution.py:327
  (7 shorter events, 0.1 us)
Async XLA Ops:
  9.0 2.2 %collective-permute-start.1 = (f32[128,1024]{1,0:T(8,128)S(1)}, f32[128,1024]{1,0:T(8,128)S(1)}, u32[]{:S(2)}, u32[]{:S(2)}) collective-permute-start(f32[128,1024]{1,0:T(8,128)S(1)} %get-tuple-element.21), channel_id=1, source_target_pairs={{0,2},{1,3},{2,0},{3,1},{4,6},{5,7},{6,4},{7,5},{8,10},{9,11},{10,... | collective-permute-start | bytes 1572872 | tf_op jit(solution)/shard_map/ppermute | solution.py:372
  9.5 1.7 %collective-permute-start = (f32[192,128]{1,0:T(8,128)S(1)}, f32[192,128]{1,0:T(8,128)S(1)}, u32[]{:S(2)}, u32[]{:S(2)}) collective-permute-start(f32[192,128]{1,0:T(8,128)S(1)} %get-tuple-element.19), channel_id=1, source_target_pairs={{0,2},{1,3},{2,0},{3,1},{4,6},{5,7},{6,4},{7,5},{8,10},{9,11},{10,... | collective-permute-start | bytes 294920 | tf_op jit(solution)/shard_map/ppermute | solution.py:372
  11.3 6.5 %collective-permute-start.2 = (f32[192,128]{1,0:T(8,128)S(1)}, f32[192,128]{1,0:T(8,128)S(1)}, u32[]{:S(2)}, u32[]{:S(2)}) collective-permute-start(f32[192,128]{1,0:T(8,128)S(1)} %add.7), channel_id=1, source_target_pairs={{0,8},{1,9},{2,10},{3,11},{4,12},{5,13},{6,14},{7,15},{8,0},{9,1},... | collective-permute-start | bytes 294920 | tf_op jit(solution)/shard_map/ppermute | solution.py:372
  14.3 6.2 %collective-permute-start.4 = (f32[32,1024]{1,0:T(8,128)S(1)}, f32[32,1024]{1,0:T(8,128)S(1)}, u32[]{:S(2)}, u32[]{:S(2)}) collective-permute-start(f32[32,1024]{1,0:T(8,128)S(1)} %get-tuple-element.24), channel_id=1, source_target_pairs={{0,1},{1,0},{2,3},{3,2},{4,5},{5,4},{6,7},{7,6},{8,9},{9,8},{10,11... | collective-permute-start | bytes 393224 | tf_op jit(solution)/shard_map/ppermute | solution.py:372
  15.8 6.4 %collective-permute-start.5 = (f32[32,1024]{1,0:T(8,128)S(1)}, f32[32,1024]{1,0:T(8,128)S(1)}, u32[]{:S(2)}, u32[]{:S(2)}) collective-permute-start(f32[32,1024]{1,0:T(8,128)S(1)} %get-tuple-element.25), channel_id=1, source_target_pairs={{0,4},{1,5},{2,6},{3,7},{4,0},{5,1},{6,2},{7,3},{8,12},{9,13},{10,... | collective-permute-start | bytes 393224 | tf_op jit(solution)/shard_map/ppermute | solution.py:372
  17.3 6.2 %collective-permute-start.6 = (f32[32,1024]{1,0:T(8,128)S(1)}, f32[32,1024]{1,0:T(8,128)S(1)}, u32[]{:S(2)}, u32[]{:S(2)}) collective-permute-start(f32[32,1024]{1,0:T(8,128)S(1)} %get-tuple-element.22.refs_2_), channel_id=1, source_target_pairs={{0,5},{1,4},{2,7},{3,6},{4,1},{5,0},{6,3},{7,2},{8,13},{9,12},{10,... | collective-permute-start | bytes 393224 | tf_op jit(solution)/shard_map/ppermute | solution.py:372
  17.8 7.0 %collective-permute-start.3 = (f32[192,128]{1,0:T(8,128)S(1)}, f32[192,128]{1,0:T(8,128)S(1)}, u32[]{:S(2)}, u32[]{:S(2)}) collective-permute-start(f32[192,128]{1,0:T(8,128)S(1)} %add.6.refs_0_), channel_id=1, source_target_pairs={{0,16},{1,17},{2,18},{3,19},{4,20},{5,21},{6,22},{7,23},{8,24},{9,... | collective-permute-start | bytes 294920 | tf_op jit(solution)/shard_map/ppermute | solution.py:372
  23.5 5.0 %collective-permute-start.10 = (f32[32,1024]{1,0:T(8,128)S(1)}, f32[32,1024]{1,0:T(8,128)S(1)}, u32[]{:S(2)}, u32[]{:S(2)}) collective-permute-start(f32[32,1024]{1,0:T(8,128)S(1)} %sums.5.refs_2_.refs_0_), channel_id=1, source_target_pairs={{0,8},{1,9},{2,10},{3,11},{4,12},{5,13},{6,14},{7,15},{8,0},{9,1},... | collective-permute-start | bytes 393224 | tf_op jit(solution)/shard_map/ppermute | solution.py:372
  24.8 6.5 %collective-permute-start.9 = (f32[192,128]{1,0:T(8,128)S(1)}, f32[192,128]{1,0:T(8,128)S(1)}, u32[]{:S(2)}, u32[]{:S(2)}) collective-permute-start(f32[192,128]{1,0:T(8,128)S(1)} %add.8.refs_0_), channel_id=1, source_target_pairs={{0,5},{1,4},{2,7},{3,6},{4,1},{5,0},{6,3},{7,2},{8,13},{9,12},{10,... | collective-permute-start | bytes 294920 | tf_op jit(solution)/shard_map/ppermute | solution.py:372
  27.1 4.6 %collective-permute-start.8 = (f32[192,128]{1,0:T(8,128)S(1)}, f32[192,128]{1,0:T(8,128)S(1)}, u32[]{:S(2)}, u32[]{:S(2)}) collective-permute-start(f32[192,128]{1,0:T(8,128)S(1)} %add.8.refs_0_), channel_id=1, source_target_pairs={{0,4},{1,5},{2,6},{3,7},{4,0},{5,1},{6,2},{7,3},{8,12},{9,13},{10,... | collective-permute-start | bytes 294920 | tf_op jit(solution)/shard_map/ppermute | solution.py:372
  27.7 4.6 %collective-permute-start.7 = (f32[192,128]{1,0:T(8,128)S(1)}, f32[192,128]{1,0:T(8,128)S(1)}, u32[]{:S(2)}, u32[]{:S(2)}) collective-permute-start(f32[192,128]{1,0:T(8,128)S(1)} %add.8.refs_0_), channel_id=1, source_target_pairs={{0,1},{1,0},{2,3},{3,2},{4,5},{5,4},{6,7},{7,6},{8,9},{9,8},{10,11... | collective-permute-start | bytes 294920 | tf_op jit(solution)/shard_map/ppermute | solution.py:372
  28.6 7.3 %collective-permute-start.12 = (f32[32,1024]{1,0:T(8,128)S(1)}, f32[32,1024]{1,0:T(8,128)S(1)}, u32[]{:S(2)}, u32[]{:S(2)}) collective-permute-start(f32[32,1024]{1,0:T(8,128)S(1)} %sums.6.refs_4_.refs_0_), channel_id=1, source_target_pairs={{0,16},{1,17},{2,18},{3,19},{4,20},{5,21},{6,22},{7,23},{8,24},{9,... | collective-permute-start | bytes 393224 | tf_op jit(solution)/shard_map/ppermute | solution.py:372
  32.3 1.4 %collective-permute-start.11 = (f32[192,128]{1,0:T(8,128)S(1)}, f32[192,128]{1,0:T(8,128)S(1)}, u32[]{:S(2)}, u32[]{:S(2)}) collective-permute-start(f32[192,128]{1,0:T(8,128)S(1)} %add.9.refs_0_), channel_id=1, source_target_pairs={{0,2},{1,3},{2,0},{3,1},{4,6},{5,7},{6,4},{7,5},{8,10},{9,11},{10,... | collective-permute-start | bytes 294920 | tf_op jit(solution)/shard_map/ppermute | solution.py:372
  36.0 11.8 %collective-permute-start.16 = (f32[32,1024]{1,0:T(8,128)S(1)}, f32[32,1024]{1,0:T(8,128)S(1)}, u32[]{:S(2)}, u32[]{:S(2)}) collective-permute-start(f32[32,1024]{1,0:T(8,128)S(1)} %sums.7.refs_3_.refs_0_), channel_id=1, source_target_pairs={{0,2},{1,3},{2,0},{3,1},{4,6},{5,7},{6,4},{7,5},{8,10},{9,11},{10,... | collective-permute-start | bytes 393224 | tf_op jit(solution)/shard_map/ppermute | solution.py:372
  36.0 9.0 %collective-permute-start.15 = (f32[32,1024]{1,0:T(8,128)S(1)}, f32[32,1024]{1,0:T(8,128)S(1)}, u32[]{:S(2)}, u32[]{:S(2)}) collective-permute-start(f32[32,1024]{1,0:T(8,128)S(1)} %sums.7.refs_3_.refs_0_), channel_id=1, source_target_pairs={{0,5},{1,4},{2,7},{3,6},{4,1},{5,0},{6,3},{7,2},{8,13},{9,12},{10,... | collective-permute-start | bytes 393224 | tf_op jit(solution)/shard_map/ppermute | solution.py:372
  38.5 7.2 %collective-permute-start.14 = (f32[32,1024]{1,0:T(8,128)S(1)}, f32[32,1024]{1,0:T(8,128)S(1)}, u32[]{:S(2)}, u32[]{:S(2)}) collective-permute-start(f32[32,1024]{1,0:T(8,128)S(1)} %sums.7.refs_3_.refs_0_), channel_id=1, source_target_pairs={{0,4},{1,5},{2,6},{3,7},{4,0},{5,1},{6,2},{7,3},{8,12},{9,13},{10,... | collective-permute-start | bytes 393224 | tf_op jit(solution)/shard_map/ppermute | solution.py:372
  39.1 6.7 %collective-permute-start.13 = (f32[32,1024]{1,0:T(8,128)S(1)}, f32[32,1024]{1,0:T(8,128)S(1)}, u32[]{:S(2)}, u32[]{:S(2)}) collective-permute-start(f32[32,1024]{1,0:T(8,128)S(1)} %sums.7.refs_3_.refs_0_), channel_id=1, source_target_pairs={{0,1},{1,0},{2,3},{3,2},{4,5},{5,4},{6,7},{7,6},{8,9},{9,8},{10,11... | collective-permute-start | bytes 393224 | tf_op jit(solution)/shard_map/ppermute | solution.py:372
  45.0 2.7 %collective-permute-start.19 = (f32[32,1024]{1,0:T(8,128)S(1)}, f32[32,1024]{1,0:T(8,128)S(1)}, u32[]{:S(2)}, u32[]{:S(2)}) collective-permute-start(f32[32,1024]{1,0:T(8,128)S(1)} %collective-permute-done.15.refs_3_), channel_id=1, source_target_pairs={{0,2},{1,3},{2,0},{3,1},{4,6},{5,7},{6,4},{7,5},{8,10},{9,11},{10,... | collective-permute-start | bytes 393224 | tf_op jit(solution)/shard_map/ppermute | solution.py:372
  45.7 2.0 %collective-permute-start.18 = (f32[32,1024]{1,0:T(8,128)S(1)}, f32[32,1024]{1,0:T(8,128)S(1)}, u32[]{:S(2)}, u32[]{:S(2)}) collective-permute-start(f32[32,1024]{1,0:T(8,128)S(1)} %collective-permute-done.14.refs_2_), channel_id=1, source_target_pairs={{0,2},{1,3},{2,0},{3,1},{4,6},{5,7},{6,4},{7,5},{8,10},{9,11},{10,... | collective-permute-start | bytes 393224 | tf_op jit(solution)/shard_map/ppermute | solution.py:372
  45.8 2.0 %collective-permute-start.17 = (f32[32,1024]{1,0:T(8,128)S(1)}, f32[32,1024]{1,0:T(8,128)S(1)}, u32[]{:S(2)}, u32[]{:S(2)}) collective-permute-start(f32[32,1024]{1,0:T(8,128)S(1)} %collective-permute-done.13.refs_1_), channel_id=1, source_target_pairs={{0,2},{1,3},{2,0},{3,1},{4,6},{5,7},{6,4},{7,5},{8,10},{9,11},{10,... | collective-permute-start | bytes 393224 | tf_op jit(solution)/shard_map/ppermute | solution.py:372

commit v15 on v14

--- a/solution.py
+++ b/solution.py
@@ -6,7 +6,9 @@
 
 GROUP = 8
 LANES = 128
-PANEL = 64
+PANEL = 32
+FIRST = 64
+PACKED = 272
 BLOCK = 256
 BLOCKS = 32
 AXES = ("wide", "narrow")
@@ -102,20 +104,10 @@
     row = lax.broadcasted_iota(jnp.int32, (height, size), 0) + base
     right = jnp.where((col <= row) | (col >= end), panel, 0.0)
     left = panel[:, end:]
-    update = lax.dot_general(left, right, (((0,), (0,)), ((), ())), precision=lax.Precision.HIGHEST, preferred_element_type=jnp.float32)
+    update = product(split(left), split(right), 0, 0)
     rest = a_ref[end:, :]
     at = lax.broadcasted_iota(jnp.int32, (size - end, size), 1)
     a_ref[end:, :] = jnp.where((at >= base) & (at < end), 0.0, rest) - update
-
-
-def normalize(a_ref):
-    size = a_ref.shape[0]
-    col = lax.broadcasted_iota(jnp.int32, (size, size), 1)
-    row = lax.broadcasted_iota(jnp.int32, (size, size), 0)
-    largest = jnp.max(jnp.where(col == row, a_ref[...], 0.0), axis=(0, 1), keepdims=True)
-    shrink = lax.rsqrt(largest)
-    a_ref[...] = a_ref[...] * shrink * shrink
-    return shrink, largest * shrink
 
 
 def eliminate(a_ref, factor_ref, buffer_ref, first, last):
@@ -175,9 +167,13 @@
         flip_high_ref[:, span], flip_low_ref[:, span] = flipped
         term = product(flipped, split(sampled), 1, 0)
         gram = term if gram is None else gram + term
-    packed_ref[:LANES, :] = gram[:LANES, :LANES]
-    packed_ref[LANES:2 * LANES, :] = gram[:LANES, LANES:]
-    packed_ref[2 * LANES:, :] = gram[LANES:, LANES:]
+    row = lax.broadcasted_iota(jnp.int32, (LANES, LANES), 0)
+    col = lax.broadcasted_iota(jnp.int32, (LANES, LANES), 1)
+    corner = gram[LANES:, LANES:]
+    packed_ref[:LANES, :] = gram[:LANES, LANES:]
+    packed_ref[LANES:2 * LANES, :] = jnp.where(col >= row, gram[:LANES, :LANES], corner)
+    diagonal = jnp.sum(jnp.where(col == row, corner, 0.0), axis=0, keepdims=True)
+    packed_ref[2 * LANES:, :] = jnp.broadcast_to(diagonal, (PACKED - 2 * LANES, LANES))
     half = packed_ref.shape[0] // 2
     core = core_bit()
     gram_keep_ref[...] = packed_ref[rows_of(core, half), :]
@@ -204,7 +200,7 @@
 def local_terms(features, sketch):
     rows, depth = features.shape
     rank = sketch.shape[1]
-    packed = 3 * LANES
+    packed = PACKED
     hbm = pl.BlockSpec(memory_space=pltpu.HBM)
     return pl.pallas_call(
         local_kernel,
@@ -269,14 +265,21 @@
     core = core_bit()
     packed_ref[rows_of(core, half), :] = keep_ref[...]
     packed_ref[rows_of(1 - core, half), :] = other_ref[...]
-    a_ref[:LANES, :LANES] = packed_ref[:LANES, :]
-    a_ref[:LANES, LANES:] = packed_ref[LANES:2 * LANES, :]
+    row = lax.broadcasted_iota(jnp.int32, (LANES, LANES), 0)
+    col = lax.broadcasted_iota(jnp.int32, (LANES, LANES), 1)
+    mixed = packed_ref[LANES:2 * LANES, :]
+    flipped = mixed.T
+    diagonal = packed_ref[2 * LANES:2 * LANES + 1, :]
+    largest = jnp.maximum(jnp.max(diagonal, axis=(0, 1), keepdims=True), jnp.max(jnp.where(col == row, mixed, 0.0), axis=(0, 1), keepdims=True))
+    shrink = lax.rsqrt(largest)
+    grow, square = largest * shrink, shrink * shrink
+    a_ref[:LANES, :LANES] = jnp.where(col >= row, mixed, flipped) * square
+    a_ref[:LANES, LANES:] = packed_ref[:LANES, :] * square
     a_ref[LANES:, :LANES] = jnp.zeros((LANES, LANES), jnp.float32)
-    a_ref[LANES:, LANES:] = packed_ref[2 * LANES:, :]
-    shrink, grow = normalize(a_ref)
+    a_ref[LANES:, LANES:] = jnp.where(col < row, mixed, jnp.where(col == row, diagonal, flipped)) * square
     norm_ref[:GROUP, :] = jnp.broadcast_to(shrink, (GROUP, LANES))
     norm_ref[GROUP:, :] = jnp.broadcast_to(grow, (GROUP, LANES))
-    eliminate(a_ref, factor_ref, buffer_ref, 0, PANEL)
+    eliminate(a_ref, factor_ref, buffer_ref, 0, FIRST)
 
 
 def last_part_kernel(scale, first, from_ref, upper_ref, norm_ref, inverse_ref, factor_ref, a_ref, buffer_ref):
@@ -297,7 +300,7 @@
 
 def first_part(keep, other, size, after):
     outs = f32(size, size), f32(size, size), f32(2 * GROUP, LANES)
-    return call(first_part_kernel, "first_part", outs, keep, other, after=after, scratch=buffers((3 * LANES, LANES)), flops=10**6)
+    return call(first_part_kernel, "first_part", outs, keep, other, after=after, scratch=buffers((PACKED, LANES)), flops=10**6)
 
 
 def last_part(state, size, scale, first, after):
@@ -410,7 +413,7 @@
     *state, norm = first_part(gram, send(gram, *CORE), size, ())
     (line,) = sums([line, send(line, *FAR)], masks=(0, 2), after=state[:1])
     plane = [line] + to_plane([line] * 3)
-    inverse, factor = last_part((*state, norm), size, scale, PANEL, (line,))
+    inverse, factor = last_part((*state, norm), size, scale, FIRST, (line,))
     cross = plane + [send(part, *CORE) for part in plane]
     return (basis_of(sampled, inverse, scale), factor, project(inverse, cross))
 

time: 49.4 us -> 53.5 us (1.083)
  waiting for transfers between devices: 9.09 us -> 11.3 us
  starting transfers between devices: 20.6 us -> 21.8 us
  Pallas kernels: 18.8 us -> 19.5 us
    ppermute x20, waiting for transfers between devices: 9.09 us -> 11.3 us  [send(): return lax.ppermute(value, AXES, pairs)]
    ppermute x20, starting transfers between devices: 20.6 us -> 21.8 us  [send(): return lax.ppermute(value, AXES, pairs)]
    pallas_call x9, Pallas kernels: 7.53 us -> 8.19 us  [call(): pl.pallas_call(lambda *refs: kernel(*refs[:len(operands)], *refs[len(oper...]
where the time goes in v15:
time: 53.5 us; the launch traced here: 53.3 us
  starting transfers between devices  21.8 us (41%)
  Pallas kernels  19.5 us (36%)
  waiting for transfers between devices  11.3 us (21%)
  between operations  0.74 us (1%)
    ppermute x20, starting transfers between devices, send(): return lax.ppermute(value, AXES, pairs)  21.8 us
    ppermute x20, waiting for transfers between devices, send(): return lax.ppermute(value, AXES, pairs)  11.3 us
    pallas_call x1, Pallas kernels, local_terms(): pl.pallas_call(local_kernel, out_shape=(f32(rows, rank), f32(rank // 2, d...  8.3 us
    pallas_call x9, Pallas kernels, call(): pl.pallas_call(lambda *refs: kernel(*refs[:len(operands)], *refs[len(oper...  8.19 us
    pallas_call x2, Pallas kernels, streamed(): pl.pallas_call(kernel, out_shape=out, in_specs=[VMEM] * len(operands), ou...  2.97 us
  transfers between devices with their start and end apart: 20, of which 10 were waited for; matrix products, arithmetic and copies ran while one was open for 0% of the time, Pallas kernels for 18%

profile of v15, /device:TPU:0, one launch (start us, length us, event | category | flops | bytes accessed | tf_op | source)
XLA Modules:
  0.0 53.3 jit_solution(4669058961958866098)
XLA Ops:
  0.6 8.3 %local_terms.1 = (f32[1024,256]{1,0:T(8,128)S(1)}, f32[128,1024]{1,0:T(8,128)S(1)}, f32[128,1024]{1,0:T(8,128)S(1)}, f32[136,128]{1,0:T(8,128)S(1)}, f32[136,128]{1,0:T(8,128)S(1)}) custom-call(f32[1024,1024]{1,0:T(8,128)} %features_hbm.1, f32[1024,256]{1,0:T(8,128)} %sketch_hbm.1), custom_call_target="tpu_custom_call" | custom-call | flops 4000000000 | bytes 8388608 | tf_op jit(solution)/shard_map/local_terms/pallas_call | solution.py:205
  8.9 0.5 collective-permute-start.1
  9.5 0.1 collective-permute-start
  9.5 1.6 %collective-permute-done.refs_2_.refs_1_ = f32[136,128]{1,0:T(8,128)S(1)} collective-permute-done((f32[136,128]{1,0:T(8,128)S(1)}, f32[136,128]{1,0:T(8,128)S(1)}, u32[]{:S(2)}, u32[]{:S(2)}) %collective-permute-start) | collective-permute-done | bytes 69664 | tf_op jit(solution)/shard_map/ppermute | solution.py:375
  11.1 0.0 collective-permute-done.1.refs_1_
  11.1 0.1 sums.4
  11.2 2.9 %collective-permute-start.4 = (f32[32,1024]{1,0:T(8,128)S(1)}, f32[32,1024]{1,0:T(8,128)S(1)}, u32[]{:S(2)}, u32[]{:S(2)}) collective-permute-start(f32[32,1024]{1,0:T(8,128)S(1)} %get-tuple-element.24), channel_id=1, source_target_pairs={{0,1},{1,0},{2,3},{3,2},{4,5},{5,4},{6,7},{7,6},{8,9},{9,8},{10,11... | collective-permute-start | bytes 393224 | tf_op jit(solution)/shard_map/ppermute | solution.py:375
  14.1 1.5 %collective-permute-start.5 = (f32[32,1024]{1,0:T(8,128)S(1)}, f32[32,1024]{1,0:T(8,128)S(1)}, u32[]{:S(2)}, u32[]{:S(2)}) collective-permute-start(f32[32,1024]{1,0:T(8,128)S(1)} %get-tuple-element.25), channel_id=1, source_target_pairs={{0,4},{1,5},{2,6},{3,7},{4,0},{5,1},{6,2},{7,3},{8,12},{9,13},{10,... | collective-permute-start | bytes 393224 | tf_op jit(solution)/shard_map/ppermute | solution.py:375
  15.6 0.0 collective-permute-start.6
  15.7 2.1 %collective-permute-start.2 = (f32[136,128]{1,0:T(8,128)S(1)}, f32[136,128]{1,0:T(8,128)S(1)}, u32[]{:S(2)}, u32[]{:S(2)}) collective-permute-start(f32[136,128]{1,0:T(8,128)S(1)} %add.7), channel_id=1, source_target_pairs={{0,8},{1,9},{2,10},{3,11},{4,12},{5,13},{6,14},{7,15},{8,0},{9,1},... | collective-permute-start | bytes 208904 | tf_op jit(solution)/shard_map/ppermute | solution.py:375
  17.7 0.2 collective-permute-done.4.refs_1_
  17.9 2.6 %collective-permute-done.5.refs_2_ = f32[32,1024]{1,0:T(8,128)S(1)} collective-permute-done((f32[32,1024]{1,0:T(8,128)S(1)}, f32[32,1024]{1,0:T(8,128)S(1)}, u32[]{:S(2)}, u32[]{:S(2)}) %collective-permute-start.5) | collective-permute-done | bytes 131104 | tf_op jit(solution)/shard_map/ppermute | solution.py:375
  20.5 1.5 %collective-permute-done.6.refs_3_ = f32[32,1024]{1,0:T(8,128)S(1)} collective-permute-done((f32[32,1024]{1,0:T(8,128)S(1)}, f32[32,1024]{1,0:T(8,128)S(1)}, u32[]{:S(2)}, u32[]{:S(2)}) %collective-permute-start.6) | collective-permute-done | bytes 131104 | tf_op jit(solution)/shard_map/ppermute | solution.py:375
  22.0 1.8 %collective-permute-start.10 = (f32[32,1024]{1,0:T(8,128)S(1)}, f32[32,1024]{1,0:T(8,128)S(1)}, u32[]{:S(2)}, u32[]{:S(2)}) collective-permute-start(f32[32,1024]{1,0:T(8,128)S(1)} %sums.5.refs_2_.refs_0_), channel_id=1, source_target_pairs={{0,8},{1,9},{2,10},{3,11},{4,12},{5,13},{6,14},{7,15},{8,0},{9,1},... | collective-permute-start | bytes 393224 | tf_op jit(solution)/shard_map/ppermute | solution.py:375
  23.8 0.0 collective-permute-done.2
  23.8 2.7 %collective-permute-start.3 = (f32[136,128]{1,0:T(8,128)S(1)}, f32[136,128]{1,0:T(8,128)S(1)}, u32[]{:S(2)}, u32[]{:S(2)}) collective-permute-start(f32[136,128]{1,0:T(8,128)S(1)} %add.6.refs_0_), channel_id=1, source_target_pairs={{0,16},{1,17},{2,18},{3,19},{4,20},{5,21},{6,22},{7,23},{8,24},{9,... | collective-permute-start | bytes 208904 | tf_op jit(solution)/shard_map/ppermute | solution.py:375
  26.5 2.8 %collective-permute-done.3.refs_1_ = f32[136,128]{1,0:T(8,128)S(1)} collective-permute-done((f32[136,128]{1,0:T(8,128)S(1)}, f32[136,128]{1,0:T(8,128)S(1)}, u32[]{:S(2)}, u32[]{:S(2)}) %collective-permute-start.3) | collective-permute-done | bytes 69664 | tf_op jit(solution)/shard_map/ppermute | solution.py:375
  29.3 2.3 %collective-permute-start.9 = (f32[136,128]{1,0:T(8,128)S(1)}, f32[136,128]{1,0:T(8,128)S(1)}, u32[]{:S(2)}, u32[]{:S(2)}) collective-permute-start(f32[136,128]{1,0:T(8,128)S(1)} %add.8.refs_0_), channel_id=1, source_target_pairs={{0,5},{1,4},{2,7},{3,6},{4,1},{5,0},{6,3},{7,2},{8,13},{9,12},{10,... | collective-permute-start | bytes 208904 | tf_op jit(solution)/shard_map/ppermute | solution.py:375
  31.6 0.5 %collective-permute-start.8 = (f32[136,128]{1,0:T(8,128)S(1)}, f32[136,128]{1,0:T(8,128)S(1)}, u32[]{:S(2)}, u32[]{:S(2)}) collective-permute-start(f32[136,128]{1,0:T(8,128)S(1)} %add.8.refs_0_), channel_id=1, source_target_pairs={{0,4},{1,5},{2,6},{3,7},{4,0},{5,1},{6,2},{7,3},{8,12},{9,13},{10,... | collective-permute-start | bytes 208904 | tf_op jit(solution)/shard_map/ppermute | solution.py:375
  32.2 0.7 %collective-permute-start.7 = (f32[136,128]{1,0:T(8,128)S(1)}, f32[136,128]{1,0:T(8,128)S(1)}, u32[]{:S(2)}, u32[]{:S(2)}) collective-permute-start(f32[136,128]{1,0:T(8,128)S(1)} %add.8.refs_0_), channel_id=1, source_target_pairs={{0,1},{1,0},{2,3},{3,2},{4,5},{5,4},{6,7},{7,6},{8,9},{9,8},{10,11... | collective-permute-start | bytes 208904 | tf_op jit(solution)/shard_map/ppermute | solution.py:375
  32.9 0.0 collective-permute-done.10.refs_1_
  32.9 2.5 %collective-permute-start.12 = (f32[32,1024]{1,0:T(8,128)S(1)}, f32[32,1024]{1,0:T(8,128)S(1)}, u32[]{:S(2)}, u32[]{:S(2)}) collective-permute-start(f32[32,1024]{1,0:T(8,128)S(1)} %sums.6.refs_4_.refs_0_), channel_id=1, source_target_pairs={{0,16},{1,17},{2,18},{3,19},{4,20},{5,21},{6,22},{7,23},{8,24},{9,... | collective-permute-start | bytes 393224 | tf_op jit(solution)/shard_map/ppermute | solution.py:375
  35.3 0.0 collective-permute-done.9.refs_3_
  35.3 0.6 %collective-permute-done.8.refs_2_ = f32[136,128]{1,0:T(8,128)S(1)} collective-permute-done((f32[136,128]{1,0:T(8,128)S(1)}, f32[136,128]{1,0:T(8,128)S(1)}, u32[]{:S(2)}, u32[]{:S(2)}) %collective-permute-start.8) | collective-permute-done | bytes 69664 | tf_op jit(solution)/shard_map/ppermute | solution.py:375
  35.9 0.5 %collective-permute-done.7.refs_1_ = f32[136,128]{1,0:T(8,128)S(1)} collective-permute-done((f32[136,128]{1,0:T(8,128)S(1)}, f32[136,128]{1,0:T(8,128)S(1)}, u32[]{:S(2)}, u32[]{:S(2)}) %collective-permute-start.7) | collective-permute-done | bytes 69664 | tf_op jit(solution)/shard_map/ppermute | solution.py:375
  36.5 0.1 collective-permute-start.11
  36.6 1.2 %collective-permute-done.11.refs_1_ = f32[136,128]{1,0:T(8,128)S(1)} collective-permute-done((f32[136,128]{1,0:T(8,128)S(1)}, f32[136,128]{1,0:T(8,128)S(1)}, u32[]{:S(2)}, u32[]{:S(2)}) %collective-permute-start.11) | collective-permute-done | bytes 69664 | tf_op jit(solution)/shard_map/ppermute | solution.py:375
  37.8 2.2 %first_part.1 = (f32[256,256]{1,0:T(8,128)S(1)}, f32[256,256]{1,0:T(8,128)S(1)}, f32[16,128]{1,0:T(8,128)S(1)}) custom-call(f32[136,128]{1,0:T(8,128)S(1)} %add.9.refs_0_, f32[136,128]{1,0:T(8,128)S(1)} %collective-permute-done.11.refs_1_), custom_call_target="tpu_custom_call" | custom-call | flops 1000000 | bytes 1000000 | tf_op jit(solution)/shard_map/first_part/pallas_call | solution.py:225
  40.0 0.2 collective-permute-done.12.refs_1_
  40.2 0.1 collective-permute-start.16
  40.3 2.3 %collective-permute-start.15 = (f32[32,1024]{1,0:T(8,128)S(1)}, f32[32,1024]{1,0:T(8,128)S(1)}, u32[]{:S(2)}, u32[]{:S(2)}) collective-permute-start(f32[32,1024]{1,0:T(8,128)S(1)} %sums.7.refs_3_.refs_0_), channel_id=1, source_target_pairs={{0,5},{1,4},{2,7},{3,6},{4,1},{5,0},{6,3},{7,2},{8,13},{9,12},{10,... | collective-permute-start | bytes 393224 | tf_op jit(solution)/shard_map/ppermute | solution.py:375
  42.6 0.5 %collective-permute-start.14 = (f32[32,1024]{1,0:T(8,128)S(1)}, f32[32,1024]{1,0:T(8,128)S(1)}, u32[]{:S(2)}, u32[]{:S(2)}) collective-permute-start(f32[32,1024]{1,0:T(8,128)S(1)} %sums.7.refs_3_.refs_0_), channel_id=1, source_target_pairs={{0,4},{1,5},{2,6},{3,7},{4,0},{5,1},{6,2},{7,3},{8,12},{9,13},{10,... | collective-permute-start | bytes 393224 | tf_op jit(solution)/shard_map/ppermute | solution.py:375
  43.2 0.7 %collective-permute-start.13 = (f32[32,1024]{1,0:T(8,128)S(1)}, f32[32,1024]{1,0:T(8,128)S(1)}, u32[]{:S(2)}, u32[]{:S(2)}) collective-permute-start(f32[32,1024]{1,0:T(8,128)S(1)} %sums.7.refs_3_.refs_0_), channel_id=1, source_target_pairs={{0,1},{1,0},{2,3},{3,2},{4,5},{5,4},{6,7},{7,6},{8,9},{9,8},{10,11... | collective-permute-start | bytes 393224 | tf_op jit(solution)/shard_map/ppermute | solution.py:375
  43.9 5.9 %last_part.1 = (f32[256,256]{1,0:T(8,128)S(1)}, f32[256,256]{1,0:T(8,128)}) custom-call(f32[256,256]{1,0:T(8,128)S(1)} %get-tuple-element.26.refs_2_.refs_0_, f32[256,256]{1,0:T(8,128)S(1)} %get-tuple-element.27.refs_1_, f32[16,128]{1,0:T(8,128)S(1)} %get-tuple-element.28.refs_2_, f32[32,1024]{1,0:T(8,128)S(1)} %sums.7.refs_3_.refs_0_), custom_call_target="tpu_custom_call" | custom-call | flops 3000000000 | bytes 1000000 | tf_op jit(solution)/shard_map/last_part/pallas_call | solution.py:225
  49.7 0.0 collective-permute-done.15.refs_3_
  49.7 0.0 collective-permute-start.19
  49.7 0.1 collective-permute-done.14.refs_2_
  49.8 0.4 collective-permute-start.18
  50.2 0.0 collective-permute-done.13.refs_1_
  50.3 0.1 collective-permute-start.17
  50.3 1.5 %basis.1 = f32[1024,256]{1,0:T(8,128)} custom-call(f32[1024,256]{1,0:T(8,128)S(1)} %get-tuple-element.17.refs_0_, f32[256,256]{1,0:T(8,128)S(1)} %get-tuple-element.29.refs_1_.inverse_ref), custom_call_target="tpu_custom_call" | custom-call | flops 2000000000 | bytes 2097152 | tf_op jit(solution)/shard_map/basis/pallas_call | solution.py:330
  51.8 0.0 collective-permute-done.16.refs_4_
  51.8 0.0 collective-permute-done.19.refs_7_
  51.8 0.0 collective-permute-done.18.refs_6_
  51.8 0.0 collective-permute-done.17.refs_5_
  51.8 1.5 %project.1 = f32[256,1024]{1,0:T(8,128)} custom-call(f32[256,256]{1,0:T(8,128)S(1)} %get-tuple-element.29.refs_1_.inverse_ref, f32[32,1024]{1,0:T(8,128)S(1)} %sums.7.refs_3_.refs_0_, f32[32,1024]{1,0:T(8,128)S(1)} %collective-permute-done.13.refs_1_, f32[32,1024]{1,0:T(8,128)S(1)} %collective-permute-done.14.refs_2_, ...), custom_call_target="tpu_custom_call" | custom-call | flops 400000000 | bytes 2097152 | tf_op jit(solution)/shard_map/project/pallas_call | solution.py:330
  (7 shorter events, 0.1 us)
Async XLA Ops:
  8.9 2.2 %collective-permute-start.1 = (f32[128,1024]{1,0:T(8,128)S(1)}, f32[128,1024]{1,0:T(8,128)S(1)}, u32[]{:S(2)}, u32[]{:S(2)}) collective-permute-start(f32[128,1024]{1,0:T(8,128)S(1)} %get-tuple-element.21), channel_id=1, source_target_pairs={{0,2},{1,3},{2,0},{3,1},{4,6},{5,7},{6,4},{7,5},{8,10},{9,11},{10,... | collective-permute-start | bytes 1572872 | tf_op jit(solution)/shard_map/ppermute | solution.py:375
  9.5 1.6 %collective-permute-start = (f32[136,128]{1,0:T(8,128)S(1)}, f32[136,128]{1,0:T(8,128)S(1)}, u32[]{:S(2)}, u32[]{:S(2)}) collective-permute-start(f32[136,128]{1,0:T(8,128)S(1)} %get-tuple-element.19), channel_id=1, source_target_pairs={{0,2},{1,3},{2,0},{3,1},{4,6},{5,7},{6,4},{7,5},{8,10},{9,11},{10,... | collective-permute-start | bytes 208904 | tf_op jit(solution)/shard_map/ppermute | solution.py:375
  11.2 6.7 %collective-permute-start.4 = (f32[32,1024]{1,0:T(8,128)S(1)}, f32[32,1024]{1,0:T(8,128)S(1)}, u32[]{:S(2)}, u32[]{:S(2)}) collective-permute-start(f32[32,1024]{1,0:T(8,128)S(1)} %get-tuple-element.24), channel_id=1, source_target_pairs={{0,1},{1,0},{2,3},{3,2},{4,5},{5,4},{6,7},{7,6},{8,9},{9,8},{10,11... | collective-permute-start | bytes 393224 | tf_op jit(solution)/shard_map/ppermute | solution.py:375
  14.1 6.4 %collective-permute-start.5 = (f32[32,1024]{1,0:T(8,128)S(1)}, f32[32,1024]{1,0:T(8,128)S(1)}, u32[]{:S(2)}, u32[]{:S(2)}) collective-permute-start(f32[32,1024]{1,0:T(8,128)S(1)} %get-tuple-element.25), channel_id=1, source_target_pairs={{0,4},{1,5},{2,6},{3,7},{4,0},{5,1},{6,2},{7,3},{8,12},{9,13},{10,... | collective-permute-start | bytes 393224 | tf_op jit(solution)/shard_map/ppermute | solution.py:375
  15.6 6.4 %collective-permute-start.6 = (f32[32,1024]{1,0:T(8,128)S(1)}, f32[32,1024]{1,0:T(8,128)S(1)}, u32[]{:S(2)}, u32[]{:S(2)}) collective-permute-start(f32[32,1024]{1,0:T(8,128)S(1)} %get-tuple-element.22.refs_2_), channel_id=1, source_target_pairs={{0,5},{1,4},{2,7},{3,6},{4,1},{5,0},{6,3},{7,2},{8,13},{9,12},{10,... | collective-permute-start | bytes 393224 | tf_op jit(solution)/shard_map/ppermute | solution.py:375
  15.7 8.1 %collective-permute-start.2 = (f32[136,128]{1,0:T(8,128)S(1)}, f32[136,128]{1,0:T(8,128)S(1)}, u32[]{:S(2)}, u32[]{:S(2)}) collective-permute-start(f32[136,128]{1,0:T(8,128)S(1)} %add.7), channel_id=1, source_target_pairs={{0,8},{1,9},{2,10},{3,11},{4,12},{5,13},{6,14},{7,15},{8,0},{9,1},... | collective-permute-start | bytes 208904 | tf_op jit(solution)/shard_map/ppermute | solution.py:375
  22.0 10.9 %collective-permute-start.10 = (f32[32,1024]{1,0:T(8,128)S(1)}, f32[32,1024]{1,0:T(8,128)S(1)}, u32[]{:S(2)}, u32[]{:S(2)}) collective-permute-start(f32[32,1024]{1,0:T(8,128)S(1)} %sums.5.refs_2_.refs_0_), channel_id=1, source_target_pairs={{0,8},{1,9},{2,10},{3,11},{4,12},{5,13},{6,14},{7,15},{8,0},{9,1},... | collective-permute-start | bytes 393224 | tf_op jit(solution)/shard_map/ppermute | solution.py:375
  23.8 5.5 %collective-permute-start.3 = (f32[136,128]{1,0:T(8,128)S(1)}, f32[136,128]{1,0:T(8,128)S(1)}, u32[]{:S(2)}, u32[]{:S(2)}) collective-permute-start(f32[136,128]{1,0:T(8,128)S(1)} %add.6.refs_0_), channel_id=1, source_target_pairs={{0,16},{1,17},{2,18},{3,19},{4,20},{5,21},{6,22},{7,23},{8,24},{9,... | collective-permute-start | bytes 208904 | tf_op jit(solution)/shard_map/ppermute | solution.py:375
  29.3 6.0 %collective-permute-start.9 = (f32[136,128]{1,0:T(8,128)S(1)}, f32[136,128]{1,0:T(8,128)S(1)}, u32[]{:S(2)}, u32[]{:S(2)}) collective-permute-start(f32[136,128]{1,0:T(8,128)S(1)} %add.8.refs_0_), channel_id=1, source_target_pairs={{0,5},{1,4},{2,7},{3,6},{4,1},{5,0},{6,3},{7,2},{8,13},{9,12},{10,... | collective-permute-start | bytes 208904 | tf_op jit(solution)/shard_map/ppermute | solution.py:375
  31.6 4.3 %collective-permute-start.8 = (f32[136,128]{1,0:T(8,128)S(1)}, f32[136,128]{1,0:T(8,128)S(1)}, u32[]{:S(2)}, u32[]{:S(2)}) collective-permute-start(f32[136,128]{1,0:T(8,128)S(1)} %add.8.refs_0_), channel_id=1, source_target_pairs={{0,4},{1,5},{2,6},{3,7},{4,0},{5,1},{6,2},{7,3},{8,12},{9,13},{10,... | collective-permute-start | bytes 208904 | tf_op jit(solution)/shard_map/ppermute | solution.py:375
  32.2 4.3 %collective-permute-start.7 = (f32[136,128]{1,0:T(8,128)S(1)}, f32[136,128]{1,0:T(8,128)S(1)}, u32[]{:S(2)}, u32[]{:S(2)}) collective-permute-start(f32[136,128]{1,0:T(8,128)S(1)} %add.8.refs_0_), channel_id=1, source_target_pairs={{0,1},{1,0},{2,3},{3,2},{4,5},{5,4},{6,7},{7,6},{8,9},{9,8},{10,11... | collective-permute-start | bytes 208904 | tf_op jit(solution)/shard_map/ppermute | solution.py:375
  32.9 7.3 %collective-permute-start.12 = (f32[32,1024]{1,0:T(8,128)S(1)}, f32[32,1024]{1,0:T(8,128)S(1)}, u32[]{:S(2)}, u32[]{:S(2)}) collective-permute-start(f32[32,1024]{1,0:T(8,128)S(1)} %sums.6.refs_4_.refs_0_), channel_id=1, source_target_pairs={{0,16},{1,17},{2,18},{3,19},{4,20},{5,21},{6,22},{7,23},{8,24},{9,... | collective-permute-start | bytes 393224 | tf_op jit(solution)/shard_map/ppermute | solution.py:375
  36.5 1.3 %collective-permute-start.11 = (f32[136,128]{1,0:T(8,128)S(1)}, f32[136,128]{1,0:T(8,128)S(1)}, u32[]{:S(2)}, u32[]{:S(2)}) collective-permute-start(f32[136,128]{1,0:T(8,128)S(1)} %add.9.refs_0_), channel_id=1, source_target_pairs={{0,2},{1,3},{2,0},{3,1},{4,6},{5,7},{6,4},{7,5},{8,10},{9,11},{10,... | collective-permute-start | bytes 208904 | tf_op jit(solution)/shard_map/ppermute | solution.py:375
  40.2 11.6 %collective-permute-start.16 = (f32[32,1024]{1,0:T(8,128)S(1)}, f32[32,1024]{1,0:T(8,128)S(1)}, u32[]{:S(2)}, u32[]{:S(2)}) collective-permute-start(f32[32,1024]{1,0:T(8,128)S(1)} %sums.7.refs_3_.refs_0_), channel_id=1, source_target_pairs={{0,2},{1,3},{2,0},{3,1},{4,6},{5,7},{6,4},{7,5},{8,10},{9,11},{10,... | collective-permute-start | bytes 393224 | tf_op jit(solution)/shard_map/ppermute | solution.py:375
  40.3 9.4 %collective-permute-start.15 = (f32[32,1024]{1,0:T(8,128)S(1)}, f32[32,1024]{1,0:T(8,128)S(1)}, u32[]{:S(2)}, u32[]{:S(2)}) collective-permute-start(f32[32,1024]{1,0:T(8,128)S(1)} %sums.7.refs_3_.refs_0_), channel_id=1, source_target_pairs={{0,5},{1,4},{2,7},{3,6},{4,1},{5,0},{6,3},{7,2},{8,13},{9,12},{10,... | collective-permute-start | bytes 393224 | tf_op jit(solution)/shard_map/ppermute | solution.py:375
  42.6 7.2 %collective-permute-start.14 = (f32[32,1024]{1,0:T(8,128)S(1)}, f32[32,1024]{1,0:T(8,128)S(1)}, u32[]{:S(2)}, u32[]{:S(2)}) collective-permute-start(f32[32,1024]{1,0:T(8,128)S(1)} %sums.7.refs_3_.refs_0_), channel_id=1, source_target_pairs={{0,4},{1,5},{2,6},{3,7},{4,0},{5,1},{6,2},{7,3},{8,12},{9,13},{10,... | collective-permute-start | bytes 393224 | tf_op jit(solution)/shard_map/ppermute | solution.py:375
  43.2 7.1 %collective-permute-start.13 = (f32[32,1024]{1,0:T(8,128)S(1)}, f32[32,1024]{1,0:T(8,128)S(1)}, u32[]{:S(2)}, u32[]{:S(2)}) collective-permute-start(f32[32,1024]{1,0:T(8,128)S(1)} %sums.7.refs_3_.refs_0_), channel_id=1, source_target_pairs={{0,1},{1,0},{2,3},{3,2},{4,5},{5,4},{6,7},{7,6},{8,9},{9,8},{10,11... | collective-permute-start | bytes 393224 | tf_op jit(solution)/shard_map/ppermute | solution.py:375
  49.7 2.1 %collective-permute-start.19 = (f32[32,1024]{1,0:T(8,128)S(1)}, f32[32,1024]{1,0:T(8,128)S(1)}, u32[]{:S(2)}, u32[]{:S(2)}) collective-permute-start(f32[32,1024]{1,0:T(8,128)S(1)} %collective-permute-done.15.refs_3_), channel_id=1, source_target_pairs={{0,2},{1,3},{2,0},{3,1},{4,6},{5,7},{6,4},{7,5},{8,10},{9,11},{10,... | collective-permute-start | bytes 393224 | tf_op jit(solution)/shard_map/ppermute | solution.py:375
  49.8 2.0 %collective-permute-start.18 = (f32[32,1024]{1,0:T(8,128)S(1)}, f32[32,1024]{1,0:T(8,128)S(1)}, u32[]{:S(2)}, u32[]{:S(2)}) collective-permute-start(f32[32,1024]{1,0:T(8,128)S(1)} %collective-permute-done.14.refs_2_), channel_id=1, source_target_pairs={{0,2},{1,3},{2,0},{3,1},{4,6},{5,7},{6,4},{7,5},{8,10},{9,11},{10,... | collective-permute-start | bytes 393224 | tf_op jit(solution)/shard_map/ppermute | solution.py:375
  50.3 1.6 %collective-permute-start.17 = (f32[32,1024]{1,0:T(8,128)S(1)}, f32[32,1024]{1,0:T(8,128)S(1)}, u32[]{:S(2)}, u32[]{:S(2)}) collective-permute-start(f32[32,1024]{1,0:T(8,128)S(1)} %collective-permute-done.13.refs_1_), channel_id=1, source_target_pairs={{0,2},{1,3},{2,0},{3,1},{4,6},{5,7},{6,4},{7,5},{8,10},{9,11},{10,... | collective-permute-start | bytes 393224 | tf_op jit(solution)/shard_map/ppermute | solution.py:375

commit v16 on v15

--- a/solution.py
+++ b/solution.py
@@ -6,8 +6,7 @@
 
 GROUP = 8
 LANES = 128
-PANEL = 32
-FIRST = 64
+PANEL = 64
 PACKED = 272
 BLOCK = 256
 BLOCKS = 32
@@ -257,7 +256,7 @@
 
 
 def add(terms, after):
-    return call(add_kernel, "add", f32(*terms[0].shape), *terms, after=after)
+    return call(add_kernel, "add", f32(*terms[0].shape), *terms, after=after, flops=10**9)
 
 
 def first_part_kernel(keep_ref, other_ref, a_ref, factor_ref, norm_ref, packed_ref, buffer_ref):
@@ -279,7 +278,7 @@
     a_ref[LANES:, LANES:] = jnp.where(col < row, mixed, jnp.where(col == row, diagonal, flipped)) * square
     norm_ref[:GROUP, :] = jnp.broadcast_to(shrink, (GROUP, LANES))
     norm_ref[GROUP:, :] = jnp.broadcast_to(grow, (GROUP, LANES))
-    eliminate(a_ref, factor_ref, buffer_ref, 0, FIRST)
+    eliminate(a_ref, factor_ref, buffer_ref, 0, PANEL)
 
 
 def last_part_kernel(scale, first, from_ref, upper_ref, norm_ref, inverse_ref, factor_ref, a_ref, buffer_ref):
@@ -413,7 +412,7 @@
     *state, norm = first_part(gram, send(gram, *CORE), size, ())
     (line,) = sums([line, send(line, *FAR)], masks=(0, 2), after=state[:1])
     plane = [line] + to_plane([line] * 3)
-    inverse, factor = last_part((*state, norm), size, scale, FIRST, (line,))
+    inverse, factor = last_part((*state, norm), size, scale, PANEL, (line,))
     cross = plane + [send(part, *CORE) for part in plane]
     return (basis_of(sampled, inverse, scale), factor, project(inverse, cross))
 

time: 53.5 us -> 49.4 us (0.923)
  waiting for transfers between devices: 11.3 us -> 8.88 us
  Pallas kernels: 19.5 us -> 18.5 us
  starting transfers between devices: 21.8 us -> 21.1 us
    ppermute x20, waiting for transfers between devices: 11.3 us -> 8.88 us  [send(): return lax.ppermute(value, AXES, pairs)]
    pallas_call x9, Pallas kernels: 8.19 us -> 7.27 us  [call(): pl.pallas_call(lambda *refs: kernel(*refs[:len(operands)], *refs[len(oper...]
    ppermute x20, starting transfers between devices: 21.8 us -> 21.1 us  [send(): return lax.ppermute(value, AXES, pairs)]
  transfers between devices with their start and end apart: 20 -> 20, of which waited for: 10 -> 7; matrix products, arithmetic and copies ran while one was open for 0% -> 0% of each run, Pallas kernels for 18% -> 18%
where the time goes in v16:
time: 49.4 us; the launch traced here: 49.3 us
  starting transfers between devices  21.1 us (43%)
  Pallas kernels  18.5 us (37%)
  waiting for transfers between devices  8.88 us (18%)
  between operations  0.75 us (2%)
    ppermute x20, starting transfers between devices, send(): return lax.ppermute(value, AXES, pairs)  21.1 us
    ppermute x20, waiting for transfers between devices, send(): return lax.ppermute(value, AXES, pairs)  8.88 us
    pallas_call x1, Pallas kernels, local_terms(): pl.pallas_call(local_kernel, out_shape=(f32(rows, rank), f32(rank // 2, d...  8.3 us
    pallas_call x9, Pallas kernels, call(): pl.pallas_call(lambda *refs: kernel(*refs[:len(operands)], *refs[len(oper...  7.27 us
    pallas_call x2, Pallas kernels, streamed(): pl.pallas_call(kernel, out_shape=out, in_specs=[VMEM] * len(operands), ou...  2.97 us
  transfers between devices with their start and end apart: 20, of which 7 were waited for; matrix products, arithmetic and copies ran while one was open for 0% of the time, Pallas kernels for 18%

profile of v16, /device:TPU:0, one launch (start us, length us, event | category | flops | bytes accessed | tf_op | source)
XLA Modules:
  0.0 49.3 jit_solution(11982857732893750003)
XLA Ops:
  0.6 8.3 %local_terms.1 = (f32[1024,256]{1,0:T(8,128)S(1)}, f32[128,1024]{1,0:T(8,128)S(1)}, f32[128,1024]{1,0:T(8,128)S(1)}, f32[136,128]{1,0:T(8,128)S(1)}, f32[136,128]{1,0:T(8,128)S(1)}) custom-call(f32[1024,1024]{1,0:T(8,128)} %features_hbm.1, f32[1024,256]{1,0:T(8,128)} %sketch_hbm.1), custom_call_target="tpu_custom_call" | custom-call | flops 4000000000 | bytes 8388608 | tf_op jit(solution)/shard_map/local_terms/pallas_call | solution.py:204
  8.9 0.5 %collective-permute-start.1 = (f32[128,1024]{1,0:T(8,128)S(1)}, f32[128,1024]{1,0:T(8,128)S(1)}, u32[]{:S(2)}, u32[]{:S(2)}) collective-permute-start(f32[128,1024]{1,0:T(8,128)S(1)} %get-tuple-element.21), channel_id=1, source_target_pairs={{0,2},{1,3},{2,0},{3,1},{4,6},{5,7},{6,4},{7,5},{8,10},{9,11},{10,... | collective-permute-start | bytes 1572872 | tf_op jit(solution)/shard_map/ppermute | solution.py:374
  9.5 0.1 collective-permute-start
  9.5 1.6 %collective-permute-done.refs_2_.refs_1_ = f32[136,128]{1,0:T(8,128)S(1)} collective-permute-done((f32[136,128]{1,0:T(8,128)S(1)}, f32[136,128]{1,0:T(8,128)S(1)}, u32[]{:S(2)}, u32[]{:S(2)}) %collective-permute-start) | collective-permute-done | bytes 69664 | tf_op jit(solution)/shard_map/ppermute | solution.py:374
  11.1 0.0 collective-permute-done.1.refs_1_
  11.1 0.1 sums.4
  11.2 3.0 %collective-permute-start.2 = (f32[136,128]{1,0:T(8,128)S(1)}, f32[136,128]{1,0:T(8,128)S(1)}, u32[]{:S(2)}, u32[]{:S(2)}) collective-permute-start(f32[136,128]{1,0:T(8,128)S(1)} %add.7), channel_id=1, source_target_pairs={{0,8},{1,9},{2,10},{3,11},{4,12},{5,13},{6,14},{7,15},{8,0},{9,1},... | collective-permute-start | bytes 208904 | tf_op jit(solution)/shard_map/ppermute | solution.py:374
  14.2 1.5 %collective-permute-start.4 = (f32[32,1024]{1,0:T(8,128)S(1)}, f32[32,1024]{1,0:T(8,128)S(1)}, u32[]{:S(2)}, u32[]{:S(2)}) collective-permute-start(f32[32,1024]{1,0:T(8,128)S(1)} %get-tuple-element.24), channel_id=1, source_target_pairs={{0,1},{1,0},{2,3},{3,2},{4,5},{5,4},{6,7},{7,6},{8,9},{9,8},{10,11... | collective-permute-start | bytes 393224 | tf_op jit(solution)/shard_map/ppermute | solution.py:374
  15.7 1.5 %collective-permute-start.5 = (f32[32,1024]{1,0:T(8,128)S(1)}, f32[32,1024]{1,0:T(8,128)S(1)}, u32[]{:S(2)}, u32[]{:S(2)}) collective-permute-start(f32[32,1024]{1,0:T(8,128)S(1)} %get-tuple-element.25), channel_id=1, source_target_pairs={{0,4},{1,5},{2,6},{3,7},{4,0},{5,1},{6,2},{7,3},{8,12},{9,13},{10,... | collective-permute-start | bytes 393224 | tf_op jit(solution)/shard_map/ppermute | solution.py:374
  17.2 0.5 collective-permute-start.6
  17.7 0.0 collective-permute-done.2
  17.7 2.7 %collective-permute-start.3 = (f32[136,128]{1,0:T(8,128)S(1)}, f32[136,128]{1,0:T(8,128)S(1)}, u32[]{:S(2)}, u32[]{:S(2)}) collective-permute-start(f32[136,128]{1,0:T(8,128)S(1)} %add.6.refs_0_), channel_id=1, source_target_pairs={{0,16},{1,17},{2,18},{3,19},{4,20},{5,21},{6,22},{7,23},{8,24},{9,... | collective-permute-start | bytes 208904 | tf_op jit(solution)/shard_map/ppermute | solution.py:374
  20.4 0.0 collective-permute-done.4.refs_1_
  20.4 1.7 %collective-permute-done.5.refs_2_ = f32[32,1024]{1,0:T(8,128)S(1)} collective-permute-done((f32[32,1024]{1,0:T(8,128)S(1)}, f32[32,1024]{1,0:T(8,128)S(1)}, u32[]{:S(2)}, u32[]{:S(2)}) %collective-permute-start.5) | collective-permute-done | bytes 131104 | tf_op jit(solution)/shard_map/ppermute | solution.py:374
  22.1 1.3 %collective-permute-done.6.refs_3_ = f32[32,1024]{1,0:T(8,128)S(1)} collective-permute-done((f32[32,1024]{1,0:T(8,128)S(1)}, f32[32,1024]{1,0:T(8,128)S(1)}, u32[]{:S(2)}, u32[]{:S(2)}) %collective-permute-start.6) | collective-permute-done | bytes 131104 | tf_op jit(solution)/shard_map/ppermute | solution.py:374
  23.5 0.4 collective-permute-start.10
  23.9 0.0 collective-permute-done.3.refs_1_
  23.9 2.6 %collective-permute-start.9 = (f32[136,128]{1,0:T(8,128)S(1)}, f32[136,128]{1,0:T(8,128)S(1)}, u32[]{:S(2)}, u32[]{:S(2)}) collective-permute-start(f32[136,128]{1,0:T(8,128)S(1)} %add.8.refs_0_), channel_id=1, source_target_pairs={{0,5},{1,4},{2,7},{3,6},{4,1},{5,0},{6,3},{7,2},{8,13},{9,12},{10,... | collective-permute-start | bytes 208904 | tf_op jit(solution)/shard_map/ppermute | solution.py:374
  26.5 0.5 %collective-permute-start.8 = (f32[136,128]{1,0:T(8,128)S(1)}, f32[136,128]{1,0:T(8,128)S(1)}, u32[]{:S(2)}, u32[]{:S(2)}) collective-permute-start(f32[136,128]{1,0:T(8,128)S(1)} %add.8.refs_0_), channel_id=1, source_target_pairs={{0,4},{1,5},{2,6},{3,7},{4,0},{5,1},{6,2},{7,3},{8,12},{9,13},{10,... | collective-permute-start | bytes 208904 | tf_op jit(solution)/shard_map/ppermute | solution.py:374
  27.0 0.4 collective-permute-start.7
  27.5 1.0 %collective-permute-done.10.refs_1_ = f32[32,1024]{1,0:T(8,128)S(1)} collective-permute-done((f32[32,1024]{1,0:T(8,128)S(1)}, f32[32,1024]{1,0:T(8,128)S(1)}, u32[]{:S(2)}, u32[]{:S(2)}) %collective-permute-start.10) | collective-permute-done | bytes 131104 | tf_op jit(solution)/shard_map/ppermute | solution.py:374
  28.5 3.2 %collective-permute-start.12 = (f32[32,1024]{1,0:T(8,128)S(1)}, f32[32,1024]{1,0:T(8,128)S(1)}, u32[]{:S(2)}, u32[]{:S(2)}) collective-permute-start(f32[32,1024]{1,0:T(8,128)S(1)} %sums.6.refs_4_.refs_0_), channel_id=1, source_target_pairs={{0,16},{1,17},{2,18},{3,19},{4,20},{5,21},{6,22},{7,23},{8,24},{9,... | collective-permute-start | bytes 393224 | tf_op jit(solution)/shard_map/ppermute | solution.py:374
  31.7 0.0 collective-permute-done.9.refs_3_
  31.7 0.0 collective-permute-done.8.refs_2_
  31.7 0.0 collective-permute-done.7.refs_1_
  31.7 0.1 collective-permute-start.11
  31.8 1.2 %collective-permute-done.11.refs_1_ = f32[136,128]{1,0:T(8,128)S(1)} collective-permute-done((f32[136,128]{1,0:T(8,128)S(1)}, f32[136,128]{1,0:T(8,128)S(1)}, u32[]{:S(2)}, u32[]{:S(2)}) %collective-permute-start.11) | collective-permute-done | bytes 69664 | tf_op jit(solution)/shard_map/ppermute | solution.py:374
  33.0 1.8 %first_part.1 = (f32[256,256]{1,0:T(8,128)S(1)}, f32[256,256]{1,0:T(8,128)S(1)}, f32[16,128]{1,0:T(8,128)S(1)}) custom-call(f32[136,128]{1,0:T(8,128)S(1)} %add.9.refs_0_, f32[136,128]{1,0:T(8,128)S(1)} %collective-permute-done.11.refs_1_), custom_call_target="tpu_custom_call" | custom-call | flops 1000000 | bytes 1000000 | tf_op jit(solution)/shard_map/first_part/pallas_call | solution.py:224
  34.9 1.0 %collective-permute-done.12.refs_1_ = f32[32,1024]{1,0:T(8,128)S(1)} collective-permute-done((f32[32,1024]{1,0:T(8,128)S(1)}, f32[32,1024]{1,0:T(8,128)S(1)}, u32[]{:S(2)}, u32[]{:S(2)}) %collective-permute-start.12) | collective-permute-done | bytes 131104 | tf_op jit(solution)/shard_map/ppermute | solution.py:374
  36.0 0.1 collective-permute-start.16
  36.0 2.5 %collective-permute-start.15 = (f32[32,1024]{1,0:T(8,128)S(1)}, f32[32,1024]{1,0:T(8,128)S(1)}, u32[]{:S(2)}, u32[]{:S(2)}) collective-permute-start(f32[32,1024]{1,0:T(8,128)S(1)} %sums.7.refs_3_.refs_0_), channel_id=1, source_target_pairs={{0,5},{1,4},{2,7},{3,6},{4,1},{5,0},{6,3},{7,2},{8,13},{9,12},{10,... | collective-permute-start | bytes 393224 | tf_op jit(solution)/shard_map/ppermute | solution.py:374
  38.5 0.5 %collective-permute-start.14 = (f32[32,1024]{1,0:T(8,128)S(1)}, f32[32,1024]{1,0:T(8,128)S(1)}, u32[]{:S(2)}, u32[]{:S(2)}) collective-permute-start(f32[32,1024]{1,0:T(8,128)S(1)} %sums.7.refs_3_.refs_0_), channel_id=1, source_target_pairs={{0,4},{1,5},{2,6},{3,7},{4,0},{5,1},{6,2},{7,3},{8,12},{9,13},{10,... | collective-permute-start | bytes 393224 | tf_op jit(solution)/shard_map/ppermute | solution.py:374
  39.1 0.5 %collective-permute-start.13 = (f32[32,1024]{1,0:T(8,128)S(1)}, f32[32,1024]{1,0:T(8,128)S(1)}, u32[]{:S(2)}, u32[]{:S(2)}) collective-permute-start(f32[32,1024]{1,0:T(8,128)S(1)} %sums.7.refs_3_.refs_0_), channel_id=1, source_target_pairs={{0,1},{1,0},{2,3},{3,2},{4,5},{5,4},{6,7},{7,6},{8,9},{9,8},{10,11... | collective-permute-start | bytes 393224 | tf_op jit(solution)/shard_map/ppermute | solution.py:374
  39.6 5.3 %last_part.1 = (f32[256,256]{1,0:T(8,128)S(1)}, f32[256,256]{1,0:T(8,128)}) custom-call(f32[256,256]{1,0:T(8,128)S(1)} %get-tuple-element.26.refs_2_.refs_0_, f32[256,256]{1,0:T(8,128)S(1)} %get-tuple-element.27.refs_1_, f32[16,128]{1,0:T(8,128)S(1)} %get-tuple-element.28.refs_2_, f32[32,1024]{1,0:T(8,128)S(1)} %sums.7.refs_3_.refs_0_), custom_call_target="tpu_custom_call" | custom-call | flops 3000000000 | bytes 1000000 | tf_op jit(solution)/shard_map/last_part/pallas_call | solution.py:224
  44.9 0.0 collective-permute-done.15.refs_3_
  44.9 0.0 collective-permute-start.19
  44.9 0.9 %collective-permute-done.14.refs_2_ = f32[32,1024]{1,0:T(8,128)S(1)} collective-permute-done((f32[32,1024]{1,0:T(8,128)S(1)}, f32[32,1024]{1,0:T(8,128)S(1)}, u32[]{:S(2)}, u32[]{:S(2)}) %collective-permute-start.14) | collective-permute-done | bytes 131104 | tf_op jit(solution)/shard_map/ppermute | solution.py:374
  45.7 0.0 collective-permute-start.18
  45.7 0.0 collective-permute-done.13.refs_1_
  45.8 0.5 %collective-permute-start.17 = (f32[32,1024]{1,0:T(8,128)S(1)}, f32[32,1024]{1,0:T(8,128)S(1)}, u32[]{:S(2)}, u32[]{:S(2)}) collective-permute-start(f32[32,1024]{1,0:T(8,128)S(1)} %collective-permute-done.13.refs_1_), channel_id=1, source_target_pairs={{0,2},{1,3},{2,0},{3,1},{4,6},{5,7},{6,4},{7,5},{8,10},{9,11},{10,... | collective-permute-start | bytes 393224 | tf_op jit(solution)/shard_map/ppermute | solution.py:374
  46.3 1.5 %basis.1 = f32[1024,256]{1,0:T(8,128)} custom-call(f32[1024,256]{1,0:T(8,128)S(1)} %get-tuple-element.17.refs_0_, f32[256,256]{1,0:T(8,128)S(1)} %get-tuple-element.29.refs_1_.inverse_ref), custom_call_target="tpu_custom_call" | custom-call | flops 2000000000 | bytes 2097152 | tf_op jit(solution)/shard_map/basis/pallas_call | solution.py:329
  47.7 0.0 collective-permute-done.16.refs_4_
  47.7 0.0 collective-permute-done.19.refs_7_
  47.7 0.0 collective-permute-done.18.refs_6_
  47.8 0.0 collective-permute-done.17.refs_5_
  47.8 1.5 %project.1 = f32[256,1024]{1,0:T(8,128)} custom-call(f32[256,256]{1,0:T(8,128)S(1)} %get-tuple-element.29.refs_1_.inverse_ref, f32[32,1024]{1,0:T(8,128)S(1)} %sums.7.refs_3_.refs_0_, f32[32,1024]{1,0:T(8,128)S(1)} %collective-permute-done.13.refs_1_, f32[32,1024]{1,0:T(8,128)S(1)} %collective-permute-done.14.refs_2_, ...), custom_call_target="tpu_custom_call" | custom-call | flops 400000000 | bytes 2097152 | tf_op jit(solution)/shard_map/project/pallas_call | solution.py:329
  (7 shorter events, 0.1 us)
Async XLA Ops:
  8.9 2.2 %collective-permute-start.1 = (f32[128,1024]{1,0:T(8,128)S(1)}, f32[128,1024]{1,0:T(8,128)S(1)}, u32[]{:S(2)}, u32[]{:S(2)}) collective-permute-start(f32[128,1024]{1,0:T(8,128)S(1)} %get-tuple-element.21), channel_id=1, source_target_pairs={{0,2},{1,3},{2,0},{3,1},{4,6},{5,7},{6,4},{7,5},{8,10},{9,11},{10,... | collective-permute-start | bytes 1572872 | tf_op jit(solution)/shard_map/ppermute | solution.py:374
  9.5 1.6 %collective-permute-start = (f32[136,128]{1,0:T(8,128)S(1)}, f32[136,128]{1,0:T(8,128)S(1)}, u32[]{:S(2)}, u32[]{:S(2)}) collective-permute-start(f32[136,128]{1,0:T(8,128)S(1)} %get-tuple-element.19), channel_id=1, source_target_pairs={{0,2},{1,3},{2,0},{3,1},{4,6},{5,7},{6,4},{7,5},{8,10},{9,11},{10,... | collective-permute-start | bytes 208904 | tf_op jit(solution)/shard_map/ppermute | solution.py:374
  11.2 6.5 %collective-permute-start.2 = (f32[136,128]{1,0:T(8,128)S(1)}, f32[136,128]{1,0:T(8,128)S(1)}, u32[]{:S(2)}, u32[]{:S(2)}) collective-permute-start(f32[136,128]{1,0:T(8,128)S(1)} %add.7), channel_id=1, source_target_pairs={{0,8},{1,9},{2,10},{3,11},{4,12},{5,13},{6,14},{7,15},{8,0},{9,1},... | collective-permute-start | bytes 208904 | tf_op jit(solution)/shard_map/ppermute | solution.py:374
  14.2 6.2 %collective-permute-start.4 = (f32[32,1024]{1,0:T(8,128)S(1)}, f32[32,1024]{1,0:T(8,128)S(1)}, u32[]{:S(2)}, u32[]{:S(2)}) collective-permute-start(f32[32,1024]{1,0:T(8,128)S(1)} %get-tuple-element.24), channel_id=1, source_target_pairs={{0,1},{1,0},{2,3},{3,2},{4,5},{5,4},{6,7},{7,6},{8,9},{9,8},{10,11... | collective-permute-start | bytes 393224 | tf_op jit(solution)/shard_map/ppermute | solution.py:374
  15.7 6.4 %collective-permute-start.5 = (f32[32,1024]{1,0:T(8,128)S(1)}, f32[32,1024]{1,0:T(8,128)S(1)}, u32[]{:S(2)}, u32[]{:S(2)}) collective-permute-start(f32[32,1024]{1,0:T(8,128)S(1)} %get-tuple-element.25), channel_id=1, source_target_pairs={{0,4},{1,5},{2,6},{3,7},{4,0},{5,1},{6,2},{7,3},{8,12},{9,13},{10,... | collective-permute-start | bytes 393224 | tf_op jit(solution)/shard_map/ppermute | solution.py:374
  17.2 6.2 %collective-permute-start.6 = (f32[32,1024]{1,0:T(8,128)S(1)}, f32[32,1024]{1,0:T(8,128)S(1)}, u32[]{:S(2)}, u32[]{:S(2)}) collective-permute-start(f32[32,1024]{1,0:T(8,128)S(1)} %get-tuple-element.22.refs_2_), channel_id=1, source_target_pairs={{0,5},{1,4},{2,7},{3,6},{4,1},{5,0},{6,3},{7,2},{8,13},{9,12},{10,... | collective-permute-start | bytes 393224 | tf_op jit(solution)/shard_map/ppermute | solution.py:374
  17.7 6.2 %collective-permute-start.3 = (f32[136,128]{1,0:T(8,128)S(1)}, f32[136,128]{1,0:T(8,128)S(1)}, u32[]{:S(2)}, u32[]{:S(2)}) collective-permute-start(f32[136,128]{1,0:T(8,128)S(1)} %add.6.refs_0_), channel_id=1, source_target_pairs={{0,16},{1,17},{2,18},{3,19},{4,20},{5,21},{6,22},{7,23},{8,24},{9,... | collective-permute-start | bytes 208904 | tf_op jit(solution)/shard_map/ppermute | solution.py:374
  23.5 5.0 %collective-permute-start.10 = (f32[32,1024]{1,0:T(8,128)S(1)}, f32[32,1024]{1,0:T(8,128)S(1)}, u32[]{:S(2)}, u32[]{:S(2)}) collective-permute-start(f32[32,1024]{1,0:T(8,128)S(1)} %sums.5.refs_2_.refs_0_), channel_id=1, source_target_pairs={{0,8},{1,9},{2,10},{3,11},{4,12},{5,13},{6,14},{7,15},{8,0},{9,1},... | collective-permute-start | bytes 393224 | tf_op jit(solution)/shard_map/ppermute | solution.py:374
  23.9 7.8 %collective-permute-start.9 = (f32[136,128]{1,0:T(8,128)S(1)}, f32[136,128]{1,0:T(8,128)S(1)}, u32[]{:S(2)}, u32[]{:S(2)}) collective-permute-start(f32[136,128]{1,0:T(8,128)S(1)} %add.8.refs_0_), channel_id=1, source_target_pairs={{0,5},{1,4},{2,7},{3,6},{4,1},{5,0},{6,3},{7,2},{8,13},{9,12},{10,... | collective-permute-start | bytes 208904 | tf_op jit(solution)/shard_map/ppermute | solution.py:374
  26.5 5.2 %collective-permute-start.8 = (f32[136,128]{1,0:T(8,128)S(1)}, f32[136,128]{1,0:T(8,128)S(1)}, u32[]{:S(2)}, u32[]{:S(2)}) collective-permute-start(f32[136,128]{1,0:T(8,128)S(1)} %add.8.refs_0_), channel_id=1, source_target_pairs={{0,4},{1,5},{2,6},{3,7},{4,0},{5,1},{6,2},{7,3},{8,12},{9,13},{10,... | collective-permute-start | bytes 208904 | tf_op jit(solution)/shard_map/ppermute | solution.py:374
  27.0 4.6 %collective-permute-start.7 = (f32[136,128]{1,0:T(8,128)S(1)}, f32[136,128]{1,0:T(8,128)S(1)}, u32[]{:S(2)}, u32[]{:S(2)}) collective-permute-start(f32[136,128]{1,0:T(8,128)S(1)} %add.8.refs_0_), channel_id=1, source_target_pairs={{0,1},{1,0},{2,3},{3,2},{4,5},{5,4},{6,7},{7,6},{8,9},{9,8},{10,11... | collective-permute-start | bytes 208904 | tf_op jit(solution)/shard_map/ppermute | solution.py:374
  28.5 7.4 %collective-permute-start.12 = (f32[32,1024]{1,0:T(8,128)S(1)}, f32[32,1024]{1,0:T(8,128)S(1)}, u32[]{:S(2)}, u32[]{:S(2)}) collective-permute-start(f32[32,1024]{1,0:T(8,128)S(1)} %sums.6.refs_4_.refs_0_), channel_id=1, source_target_pairs={{0,16},{1,17},{2,18},{3,19},{4,20},{5,21},{6,22},{7,23},{8,24},{9,... | collective-permute-start | bytes 393224 | tf_op jit(solution)/shard_map/ppermute | solution.py:374
  31.7 1.3 %collective-permute-start.11 = (f32[136,128]{1,0:T(8,128)S(1)}, f32[136,128]{1,0:T(8,128)S(1)}, u32[]{:S(2)}, u32[]{:S(2)}) collective-permute-start(f32[136,128]{1,0:T(8,128)S(1)} %add.9.refs_0_), channel_id=1, source_target_pairs={{0,2},{1,3},{2,0},{3,1},{4,6},{5,7},{6,4},{7,5},{8,10},{9,11},{10,... | collective-permute-start | bytes 208904 | tf_op jit(solution)/shard_map/ppermute | solution.py:374
  36.0 11.8 %collective-permute-start.16 = (f32[32,1024]{1,0:T(8,128)S(1)}, f32[32,1024]{1,0:T(8,128)S(1)}, u32[]{:S(2)}, u32[]{:S(2)}) collective-permute-start(f32[32,1024]{1,0:T(8,128)S(1)} %sums.7.refs_3_.refs_0_), channel_id=1, source_target_pairs={{0,2},{1,3},{2,0},{3,1},{4,6},{5,7},{6,4},{7,5},{8,10},{9,11},{10,... | collective-permute-start | bytes 393224 | tf_op jit(solution)/shard_map/ppermute | solution.py:374
  36.0 8.8 %collective-permute-start.15 = (f32[32,1024]{1,0:T(8,128)S(1)}, f32[32,1024]{1,0:T(8,128)S(1)}, u32[]{:S(2)}, u32[]{:S(2)}) collective-permute-start(f32[32,1024]{1,0:T(8,128)S(1)} %sums.7.refs_3_.refs_0_), channel_id=1, source_target_pairs={{0,5},{1,4},{2,7},{3,6},{4,1},{5,0},{6,3},{7,2},{8,13},{9,12},{10,... | collective-permute-start | bytes 393224 | tf_op jit(solution)/shard_map/ppermute | solution.py:374
  38.5 7.2 %collective-permute-start.14 = (f32[32,1024]{1,0:T(8,128)S(1)}, f32[32,1024]{1,0:T(8,128)S(1)}, u32[]{:S(2)}, u32[]{:S(2)}) collective-permute-start(f32[32,1024]{1,0:T(8,128)S(1)} %sums.7.refs_3_.refs_0_), channel_id=1, source_target_pairs={{0,4},{1,5},{2,6},{3,7},{4,0},{5,1},{6,2},{7,3},{8,12},{9,13},{10,... | collective-permute-start | bytes 393224 | tf_op jit(solution)/shard_map/ppermute | solution.py:374
  39.1 6.7 %collective-permute-start.13 = (f32[32,1024]{1,0:T(8,128)S(1)}, f32[32,1024]{1,0:T(8,128)S(1)}, u32[]{:S(2)}, u32[]{:S(2)}) collective-permute-start(f32[32,1024]{1,0:T(8,128)S(1)} %sums.7.refs_3_.refs_0_), channel_id=1, source_target_pairs={{0,1},{1,0},{2,3},{3,2},{4,5},{5,4},{6,7},{7,6},{8,9},{9,8},{10,11... | collective-permute-start | bytes 393224 | tf_op jit(solution)/shard_map/ppermute | solution.py:374
  44.9 2.9 %collective-permute-start.19 = (f32[32,1024]{1,0:T(8,128)S(1)}, f32[32,1024]{1,0:T(8,128)S(1)}, u32[]{:S(2)}, u32[]{:S(2)}) collective-permute-start(f32[32,1024]{1,0:T(8,128)S(1)} %collective-permute-done.15.refs_3_), channel_id=1, source_target_pairs={{0,2},{1,3},{2,0},{3,1},{4,6},{5,7},{6,4},{7,5},{8,10},{9,11},{10,... | collective-permute-start | bytes 393224 | tf_op jit(solution)/shard_map/ppermute | solution.py:374
  45.7 2.0 %collective-permute-start.18 = (f32[32,1024]{1,0:T(8,128)S(1)}, f32[32,1024]{1,0:T(8,128)S(1)}, u32[]{:S(2)}, u32[]{:S(2)}) collective-permute-start(f32[32,1024]{1,0:T(8,128)S(1)} %collective-permute-done.14.refs_2_), channel_id=1, source_target_pairs={{0,2},{1,3},{2,0},{3,1},{4,6},{5,7},{6,4},{7,5},{8,10},{9,11},{10,... | collective-permute-start | bytes 393224 | tf_op jit(solution)/shard_map/ppermute | solution.py:374
  45.8 2.0 %collective-permute-start.17 = (f32[32,1024]{1,0:T(8,128)S(1)}, f32[32,1024]{1,0:T(8,128)S(1)}, u32[]{:S(2)}, u32[]{:S(2)}) collective-permute-start(f32[32,1024]{1,0:T(8,128)S(1)} %collective-permute-done.13.refs_1_), channel_id=1, source_target_pairs={{0,2},{1,3},{2,0},{3,1},{4,6},{5,7},{6,4},{7,5},{8,10},{9,11},{10,... | collective-permute-start | bytes 393224 | tf_op jit(solution)/shard_map/ppermute | solution.py:374

commit v17 on v16

--- a/solution.py
+++ b/solution.py
@@ -102,11 +102,12 @@
     col = lax.broadcasted_iota(jnp.int32, (height, size), 1)
     row = lax.broadcasted_iota(jnp.int32, (height, size), 0) + base
     right = jnp.where((col <= row) | (col >= end), panel, 0.0)
-    left = panel[:, end:]
-    update = product(split(left), split(right), 0, 0)
-    rest = a_ref[end:, :]
-    at = lax.broadcasted_iota(jnp.int32, (size - end, size), 1)
-    a_ref[end:, :] = jnp.where((at >= base) & (at < end), 0.0, rest) - update
+    right = split(right)
+    at = lax.broadcasted_iota(jnp.int32, (height, size), 1)
+    for top in range(end, size, height):
+        rows = slice(top, top + height)
+        rest = jnp.where((at >= base) & (at < end), 0.0, a_ref[rows, :])
+        a_ref[rows, :] = rest - product(split(panel[:, rows]), right, 0, 0)
 
 
 def eliminate(a_ref, factor_ref, buffer_ref, first, last):
@@ -149,9 +150,11 @@
     for at in range(chunks):
         span = pl.ds(at * BLOCK, BLOCK)
         copies.append(pltpu.make_async_copy(features_hbm.at[span, :], features_ref.at[span, :], sems.at[at]))
-    for copy in copies:
+    for copy in copies[:2]:
         copy.start()
     copies[0].wait()
+    for copy in copies[2:]:
+        copy.start()
     pair_ref[:, :rank], pair_ref[:, rank:] = split(sketch_ref[...])
     gram = None
     for at in range(chunks):

time: 49.4 us -> 49.6 us (level)
  transfers between devices with their start and end apart: 20 -> 20, of which waited for: 7 -> 7; matrix products, arithmetic and copies ran while one was open for 0% -> 0% of each run, Pallas kernels for 18% -> 17%
where the time goes in v17:
time: 49.6 us; the launch traced here: 49.4 us
  starting transfers between devices  21.1 us (43%)
  Pallas kernels  18.7 us (38%)
  waiting for transfers between devices  8.9 us (18%)
  between operations  0.75 us (2%)
    ppermute x20, starting transfers between devices, send(): return lax.ppermute(value, AXES, pairs)  21.1 us
    ppermute x20, waiting for transfers between devices, send(): return lax.ppermute(value, AXES, pairs)  8.9 us
    pallas_call x1, Pallas kernels, local_terms(): pl.pallas_call(local_kernel, out_shape=(f32(rows, rank), f32(rank // 2, d...  8.47 us
    pallas_call x9, Pallas kernels, call(): pl.pallas_call(lambda *refs: kernel(*refs[:len(operands)], *refs[len(oper...  7.26 us
    pallas_call x2, Pallas kernels, streamed(): pl.pallas_call(kernel, out_shape=out, in_specs=[VMEM] * len(operands), ou...  2.97 us
  transfers between devices with their start and end apart: 20, of which 7 were waited for; matrix products, arithmetic and copies ran while one was open for 0% of the time, Pallas kernels for 17%

profile of v17, /device:TPU:0, one launch (start us, length us, event | category | flops | bytes accessed | tf_op | source)
XLA Modules:
  0.0 49.4 jit_solution(11431358234727271134)
XLA Ops:
  0.6 8.5 %local_terms.1 = (f32[1024,256]{1,0:T(8,128)S(1)}, f32[128,1024]{1,0:T(8,128)S(1)}, f32[128,1024]{1,0:T(8,128)S(1)}, f32[136,128]{1,0:T(8,128)S(1)}, f32[136,128]{1,0:T(8,128)S(1)}) custom-call(f32[1024,1024]{1,0:T(8,128)} %features_hbm.1, f32[1024,256]{1,0:T(8,128)} %sketch_hbm.1), custom_call_target="tpu_custom_call" | custom-call | flops 4000000000 | bytes 8388608 | tf_op jit(solution)/shard_map/local_terms/pallas_call | solution.py:207
  9.1 0.5 %collective-permute-start.1 = (f32[128,1024]{1,0:T(8,128)S(1)}, f32[128,1024]{1,0:T(8,128)S(1)}, u32[]{:S(2)}, u32[]{:S(2)}) collective-permute-start(f32[128,1024]{1,0:T(8,128)S(1)} %get-tuple-element.21), channel_id=1, source_target_pairs={{0,2},{1,3},{2,0},{3,1},{4,6},{5,7},{6,4},{7,5},{8,10},{9,11},{10,... | collective-permute-start | bytes 1572872 | tf_op jit(solution)/shard_map/ppermute | solution.py:377
  9.6 0.1 collective-permute-start
  9.7 1.6 %collective-permute-done.refs_2_.refs_1_ = f32[136,128]{1,0:T(8,128)S(1)} collective-permute-done((f32[136,128]{1,0:T(8,128)S(1)}, f32[136,128]{1,0:T(8,128)S(1)}, u32[]{:S(2)}, u32[]{:S(2)}) %collective-permute-start) | collective-permute-done | bytes 69664 | tf_op jit(solution)/shard_map/ppermute | solution.py:377
  11.3 0.0 collective-permute-done.1.refs_1_
  11.3 0.1 sums.4
  11.3 3.0 %collective-permute-start.2 = (f32[136,128]{1,0:T(8,128)S(1)}, f32[136,128]{1,0:T(8,128)S(1)}, u32[]{:S(2)}, u32[]{:S(2)}) collective-permute-start(f32[136,128]{1,0:T(8,128)S(1)} %add.7), channel_id=1, source_target_pairs={{0,8},{1,9},{2,10},{3,11},{4,12},{5,13},{6,14},{7,15},{8,0},{9,1},... | collective-permute-start | bytes 208904 | tf_op jit(solution)/shard_map/ppermute | solution.py:377
  14.4 1.5 %collective-permute-start.4 = (f32[32,1024]{1,0:T(8,128)S(1)}, f32[32,1024]{1,0:T(8,128)S(1)}, u32[]{:S(2)}, u32[]{:S(2)}) collective-permute-start(f32[32,1024]{1,0:T(8,128)S(1)} %get-tuple-element.24), channel_id=1, source_target_pairs={{0,1},{1,0},{2,3},{3,2},{4,5},{5,4},{6,7},{7,6},{8,9},{9,8},{10,11... | collective-permute-start | bytes 393224 | tf_op jit(solution)/shard_map/ppermute | solution.py:377
  15.9 1.5 %collective-permute-start.5 = (f32[32,1024]{1,0:T(8,128)S(1)}, f32[32,1024]{1,0:T(8,128)S(1)}, u32[]{:S(2)}, u32[]{:S(2)}) collective-permute-start(f32[32,1024]{1,0:T(8,128)S(1)} %get-tuple-element.25), channel_id=1, source_target_pairs={{0,4},{1,5},{2,6},{3,7},{4,0},{5,1},{6,2},{7,3},{8,12},{9,13},{10,... | collective-permute-start | bytes 393224 | tf_op jit(solution)/shard_map/ppermute | solution.py:377
  17.4 0.5 collective-permute-start.6
  17.8 0.0 collective-permute-done.2
  17.9 2.7 %collective-permute-start.3 = (f32[136,128]{1,0:T(8,128)S(1)}, f32[136,128]{1,0:T(8,128)S(1)}, u32[]{:S(2)}, u32[]{:S(2)}) collective-permute-start(f32[136,128]{1,0:T(8,128)S(1)} %add.6.refs_0_), channel_id=1, source_target_pairs={{0,16},{1,17},{2,18},{3,19},{4,20},{5,21},{6,22},{7,23},{8,24},{9,... | collective-permute-start | bytes 208904 | tf_op jit(solution)/shard_map/ppermute | solution.py:377
  20.5 0.0 collective-permute-done.4.refs_1_
  20.5 1.7 %collective-permute-done.5.refs_2_ = f32[32,1024]{1,0:T(8,128)S(1)} collective-permute-done((f32[32,1024]{1,0:T(8,128)S(1)}, f32[32,1024]{1,0:T(8,128)S(1)}, u32[]{:S(2)}, u32[]{:S(2)}) %collective-permute-start.5) | collective-permute-done | bytes 131104 | tf_op jit(solution)/shard_map/ppermute | solution.py:377
  22.3 1.3 %collective-permute-done.6.refs_3_ = f32[32,1024]{1,0:T(8,128)S(1)} collective-permute-done((f32[32,1024]{1,0:T(8,128)S(1)}, f32[32,1024]{1,0:T(8,128)S(1)}, u32[]{:S(2)}, u32[]{:S(2)}) %collective-permute-start.6) | collective-permute-done | bytes 131104 | tf_op jit(solution)/shard_map/ppermute | solution.py:377
  23.6 0.4 collective-permute-start.10
  24.1 0.0 collective-permute-done.3.refs_1_
  24.1 2.6 %collective-permute-start.9 = (f32[136,128]{1,0:T(8,128)S(1)}, f32[136,128]{1,0:T(8,128)S(1)}, u32[]{:S(2)}, u32[]{:S(2)}) collective-permute-start(f32[136,128]{1,0:T(8,128)S(1)} %add.8.refs_0_), channel_id=1, source_target_pairs={{0,5},{1,4},{2,7},{3,6},{4,1},{5,0},{6,3},{7,2},{8,13},{9,12},{10,... | collective-permute-start | bytes 208904 | tf_op jit(solution)/shard_map/ppermute | solution.py:377
  26.7 0.5 %collective-permute-start.8 = (f32[136,128]{1,0:T(8,128)S(1)}, f32[136,128]{1,0:T(8,128)S(1)}, u32[]{:S(2)}, u32[]{:S(2)}) collective-permute-start(f32[136,128]{1,0:T(8,128)S(1)} %add.8.refs_0_), channel_id=1, source_target_pairs={{0,4},{1,5},{2,6},{3,7},{4,0},{5,1},{6,2},{7,3},{8,12},{9,13},{10,... | collective-permute-start | bytes 208904 | tf_op jit(solution)/shard_map/ppermute | solution.py:377
  27.2 0.4 collective-permute-start.7
  27.6 1.0 %collective-permute-done.10.refs_1_ = f32[32,1024]{1,0:T(8,128)S(1)} collective-permute-done((f32[32,1024]{1,0:T(8,128)S(1)}, f32[32,1024]{1,0:T(8,128)S(1)}, u32[]{:S(2)}, u32[]{:S(2)}) %collective-permute-start.10) | collective-permute-done | bytes 131104 | tf_op jit(solution)/shard_map/ppermute | solution.py:377
  28.7 3.2 %collective-permute-start.12 = (f32[32,1024]{1,0:T(8,128)S(1)}, f32[32,1024]{1,0:T(8,128)S(1)}, u32[]{:S(2)}, u32[]{:S(2)}) collective-permute-start(f32[32,1024]{1,0:T(8,128)S(1)} %sums.6.refs_4_.refs_0_), channel_id=1, source_target_pairs={{0,16},{1,17},{2,18},{3,19},{4,20},{5,21},{6,22},{7,23},{8,24},{9,... | collective-permute-start | bytes 393224 | tf_op jit(solution)/shard_map/ppermute | solution.py:377
  31.8 0.0 collective-permute-done.9.refs_3_
  31.8 0.0 collective-permute-done.8.refs_2_
  31.8 0.0 collective-permute-done.7.refs_1_
  31.9 0.1 collective-permute-start.11
  32.0 1.2 %collective-permute-done.11.refs_1_ = f32[136,128]{1,0:T(8,128)S(1)} collective-permute-done((f32[136,128]{1,0:T(8,128)S(1)}, f32[136,128]{1,0:T(8,128)S(1)}, u32[]{:S(2)}, u32[]{:S(2)}) %collective-permute-start.11) | collective-permute-done | bytes 69664 | tf_op jit(solution)/shard_map/ppermute | solution.py:377
  33.2 1.9 %first_part.1 = (f32[256,256]{1,0:T(8,128)S(1)}, f32[256,256]{1,0:T(8,128)S(1)}, f32[16,128]{1,0:T(8,128)S(1)}) custom-call(f32[136,128]{1,0:T(8,128)S(1)} %add.9.refs_0_, f32[136,128]{1,0:T(8,128)S(1)} %collective-permute-done.11.refs_1_), custom_call_target="tpu_custom_call" | custom-call | flops 1000000 | bytes 1000000 | tf_op jit(solution)/shard_map/first_part/pallas_call | solution.py:227
  35.1 1.0 %collective-permute-done.12.refs_1_ = f32[32,1024]{1,0:T(8,128)S(1)} collective-permute-done((f32[32,1024]{1,0:T(8,128)S(1)}, f32[32,1024]{1,0:T(8,128)S(1)}, u32[]{:S(2)}, u32[]{:S(2)}) %collective-permute-start.12) | collective-permute-done | bytes 131104 | tf_op jit(solution)/shard_map/ppermute | solution.py:377
  36.1 0.1 collective-permute-start.16
  36.2 2.5 %collective-permute-start.15 = (f32[32,1024]{1,0:T(8,128)S(1)}, f32[32,1024]{1,0:T(8,128)S(1)}, u32[]{:S(2)}, u32[]{:S(2)}) collective-permute-start(f32[32,1024]{1,0:T(8,128)S(1)} %sums.7.refs_3_.refs_0_), channel_id=1, source_target_pairs={{0,5},{1,4},{2,7},{3,6},{4,1},{5,0},{6,3},{7,2},{8,13},{9,12},{10,... | collective-permute-start | bytes 393224 | tf_op jit(solution)/shard_map/ppermute | solution.py:377
  38.7 0.5 %collective-permute-start.14 = (f32[32,1024]{1,0:T(8,128)S(1)}, f32[32,1024]{1,0:T(8,128)S(1)}, u32[]{:S(2)}, u32[]{:S(2)}) collective-permute-start(f32[32,1024]{1,0:T(8,128)S(1)} %sums.7.refs_3_.refs_0_), channel_id=1, source_target_pairs={{0,4},{1,5},{2,6},{3,7},{4,0},{5,1},{6,2},{7,3},{8,12},{9,13},{10,... | collective-permute-start | bytes 393224 | tf_op jit(solution)/shard_map/ppermute | solution.py:377
  39.2 0.5 %collective-permute-start.13 = (f32[32,1024]{1,0:T(8,128)S(1)}, f32[32,1024]{1,0:T(8,128)S(1)}, u32[]{:S(2)}, u32[]{:S(2)}) collective-permute-start(f32[32,1024]{1,0:T(8,128)S(1)} %sums.7.refs_3_.refs_0_), channel_id=1, source_target_pairs={{0,1},{1,0},{2,3},{3,2},{4,5},{5,4},{6,7},{7,6},{8,9},{9,8},{10,11... | collective-permute-start | bytes 393224 | tf_op jit(solution)/shard_map/ppermute | solution.py:377
  39.7 5.2 %last_part.1 = (f32[256,256]{1,0:T(8,128)S(1)}, f32[256,256]{1,0:T(8,128)}) custom-call(f32[256,256]{1,0:T(8,128)S(1)} %get-tuple-element.26.refs_2_.refs_0_, f32[256,256]{1,0:T(8,128)S(1)} %get-tuple-element.27.refs_1_, f32[16,128]{1,0:T(8,128)S(1)} %get-tuple-element.28.refs_2_, f32[32,1024]{1,0:T(8,128)S(1)} %sums.7.refs_3_.refs_0_), custom_call_target="tpu_custom_call" | custom-call | flops 3000000000 | bytes 1000000 | tf_op jit(solution)/shard_map/last_part/pallas_call | solution.py:227
  45.0 0.0 collective-permute-done.15.refs_3_
  45.0 0.0 collective-permute-start.19
  45.0 0.9 %collective-permute-done.14.refs_2_ = f32[32,1024]{1,0:T(8,128)S(1)} collective-permute-done((f32[32,1024]{1,0:T(8,128)S(1)}, f32[32,1024]{1,0:T(8,128)S(1)}, u32[]{:S(2)}, u32[]{:S(2)}) %collective-permute-start.14) | collective-permute-done | bytes 131104 | tf_op jit(solution)/shard_map/ppermute | solution.py:377
  45.9 0.0 collective-permute-start.18
  45.9 0.0 collective-permute-done.13.refs_1_
  45.9 0.5 %collective-permute-start.17 = (f32[32,1024]{1,0:T(8,128)S(1)}, f32[32,1024]{1,0:T(8,128)S(1)}, u32[]{:S(2)}, u32[]{:S(2)}) collective-permute-start(f32[32,1024]{1,0:T(8,128)S(1)} %collective-permute-done.13.refs_1_), channel_id=1, source_target_pairs={{0,2},{1,3},{2,0},{3,1},{4,6},{5,7},{6,4},{7,5},{8,10},{9,11},{10,... | collective-permute-start | bytes 393224 | tf_op jit(solution)/shard_map/ppermute | solution.py:377
  46.4 1.5 %basis.1 = f32[1024,256]{1,0:T(8,128)} custom-call(f32[1024,256]{1,0:T(8,128)S(1)} %get-tuple-element.17.refs_0_, f32[256,256]{1,0:T(8,128)S(1)} %get-tuple-element.29.refs_1_.inverse_ref), custom_call_target="tpu_custom_call" | custom-call | flops 2000000000 | bytes 2097152 | tf_op jit(solution)/shard_map/basis/pallas_call | solution.py:332
  47.9 0.0 collective-permute-done.16.refs_4_
  47.9 0.0 collective-permute-done.19.refs_7_
  47.9 0.0 collective-permute-done.18.refs_6_
  47.9 0.0 collective-permute-done.17.refs_5_
  47.9 1.5 %project.1 = f32[256,1024]{1,0:T(8,128)} custom-call(f32[256,256]{1,0:T(8,128)S(1)} %get-tuple-element.29.refs_1_.inverse_ref, f32[32,1024]{1,0:T(8,128)S(1)} %sums.7.refs_3_.refs_0_, f32[32,1024]{1,0:T(8,128)S(1)} %collective-permute-done.13.refs_1_, f32[32,1024]{1,0:T(8,128)S(1)} %collective-permute-done.14.refs_2_, ...), custom_call_target="tpu_custom_call" | custom-call | flops 400000000 | bytes 2097152 | tf_op jit(solution)/shard_map/project/pallas_call | solution.py:332
  (7 shorter events, 0.1 us)
Async XLA Ops:
  9.1 2.2 %collective-permute-start.1 = (f32[128,1024]{1,0:T(8,128)S(1)}, f32[128,1024]{1,0:T(8,128)S(1)}, u32[]{:S(2)}, u32[]{:S(2)}) collective-permute-start(f32[128,1024]{1,0:T(8,128)S(1)} %get-tuple-element.21), channel_id=1, source_target_pairs={{0,2},{1,3},{2,0},{3,1},{4,6},{5,7},{6,4},{7,5},{8,10},{9,11},{10,... | collective-permute-start | bytes 1572872 | tf_op jit(solution)/shard_map/ppermute | solution.py:377
  9.6 1.6 %collective-permute-start = (f32[136,128]{1,0:T(8,128)S(1)}, f32[136,128]{1,0:T(8,128)S(1)}, u32[]{:S(2)}, u32[]{:S(2)}) collective-permute-start(f32[136,128]{1,0:T(8,128)S(1)} %get-tuple-element.19), channel_id=1, source_target_pairs={{0,2},{1,3},{2,0},{3,1},{4,6},{5,7},{6,4},{7,5},{8,10},{9,11},{10,... | collective-permute-start | bytes 208904 | tf_op jit(solution)/shard_map/ppermute | solution.py:377
  11.3 6.5 %collective-permute-start.2 = (f32[136,128]{1,0:T(8,128)S(1)}, f32[136,128]{1,0:T(8,128)S(1)}, u32[]{:S(2)}, u32[]{:S(2)}) collective-permute-start(f32[136,128]{1,0:T(8,128)S(1)} %add.7), channel_id=1, source_target_pairs={{0,8},{1,9},{2,10},{3,11},{4,12},{5,13},{6,14},{7,15},{8,0},{9,1},... | collective-permute-start | bytes 208904 | tf_op jit(solution)/shard_map/ppermute | solution.py:377
  14.4 6.2 %collective-permute-start.4 = (f32[32,1024]{1,0:T(8,128)S(1)}, f32[32,1024]{1,0:T(8,128)S(1)}, u32[]{:S(2)}, u32[]{:S(2)}) collective-permute-start(f32[32,1024]{1,0:T(8,128)S(1)} %get-tuple-element.24), channel_id=1, source_target_pairs={{0,1},{1,0},{2,3},{3,2},{4,5},{5,4},{6,7},{7,6},{8,9},{9,8},{10,11... | collective-permute-start | bytes 393224 | tf_op jit(solution)/shard_map/ppermute | solution.py:377
  15.9 6.4 %collective-permute-start.5 = (f32[32,1024]{1,0:T(8,128)S(1)}, f32[32,1024]{1,0:T(8,128)S(1)}, u32[]{:S(2)}, u32[]{:S(2)}) collective-permute-start(f32[32,1024]{1,0:T(8,128)S(1)} %get-tuple-element.25), channel_id=1, source_target_pairs={{0,4},{1,5},{2,6},{3,7},{4,0},{5,1},{6,2},{7,3},{8,12},{9,13},{10,... | collective-permute-start | bytes 393224 | tf_op jit(solution)/shard_map/ppermute | solution.py:377
  17.4 6.2 %collective-permute-start.6 = (f32[32,1024]{1,0:T(8,128)S(1)}, f32[32,1024]{1,0:T(8,128)S(1)}, u32[]{:S(2)}, u32[]{:S(2)}) collective-permute-start(f32[32,1024]{1,0:T(8,128)S(1)} %get-tuple-element.22.refs_2_), channel_id=1, source_target_pairs={{0,5},{1,4},{2,7},{3,6},{4,1},{5,0},{6,3},{7,2},{8,13},{9,12},{10,... | collective-permute-start | bytes 393224 | tf_op jit(solution)/shard_map/ppermute | solution.py:377
  17.9 6.2 %collective-permute-start.3 = (f32[136,128]{1,0:T(8,128)S(1)}, f32[136,128]{1,0:T(8,128)S(1)}, u32[]{:S(2)}, u32[]{:S(2)}) collective-permute-start(f32[136,128]{1,0:T(8,128)S(1)} %add.6.refs_0_), channel_id=1, source_target_pairs={{0,16},{1,17},{2,18},{3,19},{4,20},{5,21},{6,22},{7,23},{8,24},{9,... | collective-permute-start | bytes 208904 | tf_op jit(solution)/shard_map/ppermute | solution.py:377
  23.6 5.0 %collective-permute-start.10 = (f32[32,1024]{1,0:T(8,128)S(1)}, f32[32,1024]{1,0:T(8,128)S(1)}, u32[]{:S(2)}, u32[]{:S(2)}) collective-permute-start(f32[32,1024]{1,0:T(8,128)S(1)} %sums.5.refs_2_.refs_0_), channel_id=1, source_target_pairs={{0,8},{1,9},{2,10},{3,11},{4,12},{5,13},{6,14},{7,15},{8,0},{9,1},... | collective-permute-start | bytes 393224 | tf_op jit(solution)/shard_map/ppermute | solution.py:377
  24.1 7.8 %collective-permute-start.9 = (f32[136,128]{1,0:T(8,128)S(1)}, f32[136,128]{1,0:T(8,128)S(1)}, u32[]{:S(2)}, u32[]{:S(2)}) collective-permute-start(f32[136,128]{1,0:T(8,128)S(1)} %add.8.refs_0_), channel_id=1, source_target_pairs={{0,5},{1,4},{2,7},{3,6},{4,1},{5,0},{6,3},{7,2},{8,13},{9,12},{10,... | collective-permute-start | bytes 208904 | tf_op jit(solution)/shard_map/ppermute | solution.py:377
  26.7 5.2 %collective-permute-start.8 = (f32[136,128]{1,0:T(8,128)S(1)}, f32[136,128]{1,0:T(8,128)S(1)}, u32[]{:S(2)}, u32[]{:S(2)}) collective-permute-start(f32[136,128]{1,0:T(8,128)S(1)} %add.8.refs_0_), channel_id=1, source_target_pairs={{0,4},{1,5},{2,6},{3,7},{4,0},{5,1},{6,2},{7,3},{8,12},{9,13},{10,... | collective-permute-start | bytes 208904 | tf_op jit(solution)/shard_map/ppermute | solution.py:377
  27.2 4.6 %collective-permute-start.7 = (f32[136,128]{1,0:T(8,128)S(1)}, f32[136,128]{1,0:T(8,128)S(1)}, u32[]{:S(2)}, u32[]{:S(2)}) collective-permute-start(f32[136,128]{1,0:T(8,128)S(1)} %add.8.refs_0_), channel_id=1, source_target_pairs={{0,1},{1,0},{2,3},{3,2},{4,5},{5,4},{6,7},{7,6},{8,9},{9,8},{10,11... | collective-permute-start | bytes 208904 | tf_op jit(solution)/shard_map/ppermute | solution.py:377
  28.7 7.4 %collective-permute-start.12 = (f32[32,1024]{1,0:T(8,128)S(1)}, f32[32,1024]{1,0:T(8,128)S(1)}, u32[]{:S(2)}, u32[]{:S(2)}) collective-permute-start(f32[32,1024]{1,0:T(8,128)S(1)} %sums.6.refs_4_.refs_0_), channel_id=1, source_target_pairs={{0,16},{1,17},{2,18},{3,19},{4,20},{5,21},{6,22},{7,23},{8,24},{9,... | collective-permute-start | bytes 393224 | tf_op jit(solution)/shard_map/ppermute | solution.py:377
  31.9 1.3 %collective-permute-start.11 = (f32[136,128]{1,0:T(8,128)S(1)}, f32[136,128]{1,0:T(8,128)S(1)}, u32[]{:S(2)}, u32[]{:S(2)}) collective-permute-start(f32[136,128]{1,0:T(8,128)S(1)} %add.9.refs_0_), channel_id=1, source_target_pairs={{0,2},{1,3},{2,0},{3,1},{4,6},{5,7},{6,4},{7,5},{8,10},{9,11},{10,... | collective-permute-start | bytes 208904 | tf_op jit(solution)/shard_map/ppermute | solution.py:377
  36.1 11.8 %collective-permute-start.16 = (f32[32,1024]{1,0:T(8,128)S(1)}, f32[32,1024]{1,0:T(8,128)S(1)}, u32[]{:S(2)}, u32[]{:S(2)}) collective-permute-start(f32[32,1024]{1,0:T(8,128)S(1)} %sums.7.refs_3_.refs_0_), channel_id=1, source_target_pairs={{0,2},{1,3},{2,0},{3,1},{4,6},{5,7},{6,4},{7,5},{8,10},{9,11},{10,... | collective-permute-start | bytes 393224 | tf_op jit(solution)/shard_map/ppermute | solution.py:377
  36.2 8.8 %collective-permute-start.15 = (f32[32,1024]{1,0:T(8,128)S(1)}, f32[32,1024]{1,0:T(8,128)S(1)}, u32[]{:S(2)}, u32[]{:S(2)}) collective-permute-start(f32[32,1024]{1,0:T(8,128)S(1)} %sums.7.refs_3_.refs_0_), channel_id=1, source_target_pairs={{0,5},{1,4},{2,7},{3,6},{4,1},{5,0},{6,3},{7,2},{8,13},{9,12},{10,... | collective-permute-start | bytes 393224 | tf_op jit(solution)/shard_map/ppermute | solution.py:377
  38.7 7.2 %collective-permute-start.14 = (f32[32,1024]{1,0:T(8,128)S(1)}, f32[32,1024]{1,0:T(8,128)S(1)}, u32[]{:S(2)}, u32[]{:S(2)}) collective-permute-start(f32[32,1024]{1,0:T(8,128)S(1)} %sums.7.refs_3_.refs_0_), channel_id=1, source_target_pairs={{0,4},{1,5},{2,6},{3,7},{4,0},{5,1},{6,2},{7,3},{8,12},{9,13},{10,... | collective-permute-start | bytes 393224 | tf_op jit(solution)/shard_map/ppermute | solution.py:377
  39.2 6.7 %collective-permute-start.13 = (f32[32,1024]{1,0:T(8,128)S(1)}, f32[32,1024]{1,0:T(8,128)S(1)}, u32[]{:S(2)}, u32[]{:S(2)}) collective-permute-start(f32[32,1024]{1,0:T(8,128)S(1)} %sums.7.refs_3_.refs_0_), channel_id=1, source_target_pairs={{0,1},{1,0},{2,3},{3,2},{4,5},{5,4},{6,7},{7,6},{8,9},{9,8},{10,11... | collective-permute-start | bytes 393224 | tf_op jit(solution)/shard_map/ppermute | solution.py:377
  45.0 2.9 %collective-permute-start.19 = (f32[32,1024]{1,0:T(8,128)S(1)}, f32[32,1024]{1,0:T(8,128)S(1)}, u32[]{:S(2)}, u32[]{:S(2)}) collective-permute-start(f32[32,1024]{1,0:T(8,128)S(1)} %collective-permute-done.15.refs_3_), channel_id=1, source_target_pairs={{0,2},{1,3},{2,0},{3,1},{4,6},{5,7},{6,4},{7,5},{8,10},{9,11},{10,... | collective-permute-start | bytes 393224 | tf_op jit(solution)/shard_map/ppermute | solution.py:377
  45.9 2.0 %collective-permute-start.18 = (f32[32,1024]{1,0:T(8,128)S(1)}, f32[32,1024]{1,0:T(8,128)S(1)}, u32[]{:S(2)}, u32[]{:S(2)}) collective-permute-start(f32[32,1024]{1,0:T(8,128)S(1)} %collective-permute-done.14.refs_2_), channel_id=1, source_target_pairs={{0,2},{1,3},{2,0},{3,1},{4,6},{5,7},{6,4},{7,5},{8,10},{9,11},{10,... | collective-permute-start | bytes 393224 | tf_op jit(solution)/shard_map/ppermute | solution.py:377
  45.9 2.0 %collective-permute-start.17 = (f32[32,1024]{1,0:T(8,128)S(1)}, f32[32,1024]{1,0:T(8,128)S(1)}, u32[]{:S(2)}, u32[]{:S(2)}) collective-permute-start(f32[32,1024]{1,0:T(8,128)S(1)} %collective-permute-done.13.refs_1_), channel_id=1, source_target_pairs={{0,2},{1,3},{2,0},{3,1},{4,6},{5,7},{6,4},{7,5},{8,10},{9,11},{10,... | collective-permute-start | bytes 393224 | tf_op jit(solution)/shard_map/ppermute | solution.py:377

commit v18 on v17

--- a/solution.py
+++ b/solution.py
@@ -150,11 +150,9 @@
     for at in range(chunks):
         span = pl.ds(at * BLOCK, BLOCK)
         copies.append(pltpu.make_async_copy(features_hbm.at[span, :], features_ref.at[span, :], sems.at[at]))
-    for copy in copies[:2]:
+    for copy in copies:
         copy.start()
     copies[0].wait()
-    for copy in copies[2:]:
-        copy.start()
     pair_ref[:, :rank], pair_ref[:, rank:] = split(sketch_ref[...])
     gram = None
     for at in range(chunks):
@@ -407,13 +405,13 @@
     (line,) = sums(cross)
     gram = add([gram, gram_other], (line,))
     grams = [gram] + to_plane([gram] * 3)
-    (line,) = sums([line, send(line, *NEAR)], masks=(0, 1))
+    (line,) = sums([line, send(line, *FAR)], masks=(0, 2))
     gram = add(grams, (line,))
     for mask in spare_bits():
         line = line + send(line, *mask)
         gram = gram + send(gram, *mask)
     *state, norm = first_part(gram, send(gram, *CORE), size, ())
-    (line,) = sums([line, send(line, *FAR)], masks=(0, 2), after=state[:1])
+    (line,) = sums([line, send(line, *NEAR)], masks=(0, 1), after=state[:1])
     plane = [line] + to_plane([line] * 3)
     inverse, factor = last_part((*state, norm), size, scale, PANEL, (line,))
     cross = plane + [send(part, *CORE) for part in plane]

time: 49.6 us -> 49.7 us (level)
  waiting for transfers between devices: 8.9 us -> 9.83 us
  starting transfers between devices: 21.1 us -> 20.4 us
    ppermute x20, waiting for transfers between devices: 8.9 us -> 9.83 us  [send(): return lax.ppermute(value, AXES, pairs)]
    ppermute x20, starting transfers between devices: 21.1 us -> 20.4 us  [send(): return lax.ppermute(value, AXES, pairs)]
  transfers between devices with their start and end apart: 20 -> 20, of which waited for: 7 -> 8; matrix products, arithmetic and copies ran while one was open for 0% -> 0% of each run, Pallas kernels for 17% -> 17%
where the time goes in v18:
time: 49.7 us; the launch traced here: 49.5 us
  starting transfers between devices  20.4 us (41%)
  Pallas kernels  18.5 us (37%)
  waiting for transfers between devices  9.83 us (20%)
  between operations  0.77 us (2%)
    ppermute x20, starting transfers between devices, send(): return lax.ppermute(value, AXES, pairs)  20.4 us
    ppermute x20, waiting for transfers between devices, send(): return lax.ppermute(value, AXES, pairs)  9.83 us
    pallas_call x1, Pallas kernels, local_terms(): pl.pallas_call(local_kernel, out_shape=(f32(rows, rank), f32(rank // 2, d...  8.3 us
    pallas_call x9, Pallas kernels, call(): pl.pallas_call(lambda *refs: kernel(*refs[:len(operands)], *refs[len(oper...  7.26 us
    pallas_call x2, Pallas kernels, streamed(): pl.pallas_call(kernel, out_shape=out, in_specs=[VMEM] * len(operands), ou...  2.97 us
  transfers between devices with their start and end apart: 20, of which 8 were waited for; matrix products, arithmetic and copies ran while one was open for 0% of the time, Pallas kernels for 17%

profile of v18, /device:TPU:0, one launch (start us, length us, event | category | flops | bytes accessed | tf_op | source)
XLA Modules:
  0.0 49.5 jit_solution(17826715594442217660)
XLA Ops:
  0.6 8.3 %local_terms.1 = (f32[1024,256]{1,0:T(8,128)S(1)}, f32[128,1024]{1,0:T(8,128)S(1)}, f32[128,1024]{1,0:T(8,128)S(1)}, f32[136,128]{1,0:T(8,128)S(1)}, f32[136,128]{1,0:T(8,128)S(1)}) custom-call(f32[1024,1024]{1,0:T(8,128)} %features_hbm.1, f32[1024,256]{1,0:T(8,128)} %sketch_hbm.1), custom_call_target="tpu_custom_call" | custom-call | flops 4000000000 | bytes 8388608 | tf_op jit(solution)/shard_map/local_terms/pallas_call | solution.py:205
  8.9 0.5 %collective-permute-start.1 = (f32[128,1024]{1,0:T(8,128)S(1)}, f32[128,1024]{1,0:T(8,128)S(1)}, u32[]{:S(2)}, u32[]{:S(2)}) collective-permute-start(f32[128,1024]{1,0:T(8,128)S(1)} %get-tuple-element.21), channel_id=1, source_target_pairs={{0,2},{1,3},{2,0},{3,1},{4,6},{5,7},{6,4},{7,5},{8,10},{9,11},{10,... | collective-permute-start | bytes 1572872 | tf_op jit(solution)/shard_map/ppermute | solution.py:375
  9.5 0.1 collective-permute-start
  9.5 1.6 %collective-permute-done.refs_2_.refs_1_ = f32[136,128]{1,0:T(8,128)S(1)} collective-permute-done((f32[136,128]{1,0:T(8,128)S(1)}, f32[136,128]{1,0:T(8,128)S(1)}, u32[]{:S(2)}, u32[]{:S(2)}) %collective-permute-start) | collective-permute-done | bytes 69664 | tf_op jit(solution)/shard_map/ppermute | solution.py:375
  11.1 0.0 collective-permute-done.1.refs_1_
  11.1 0.1 sums.4
  11.2 3.0 %collective-permute-start.2 = (f32[136,128]{1,0:T(8,128)S(1)}, f32[136,128]{1,0:T(8,128)S(1)}, u32[]{:S(2)}, u32[]{:S(2)}) collective-permute-start(f32[136,128]{1,0:T(8,128)S(1)} %add.7), channel_id=1, source_target_pairs={{0,8},{1,9},{2,10},{3,11},{4,12},{5,13},{6,14},{7,15},{8,0},{9,1},... | collective-permute-start | bytes 208904 | tf_op jit(solution)/shard_map/ppermute | solution.py:375
  14.2 1.5 %collective-permute-start.4 = (f32[32,1024]{1,0:T(8,128)S(1)}, f32[32,1024]{1,0:T(8,128)S(1)}, u32[]{:S(2)}, u32[]{:S(2)}) collective-permute-start(f32[32,1024]{1,0:T(8,128)S(1)} %get-tuple-element.24), channel_id=1, source_target_pairs={{0,1},{1,0},{2,3},{3,2},{4,5},{5,4},{6,7},{7,6},{8,9},{9,8},{10,11... | collective-permute-start | bytes 393224 | tf_op jit(solution)/shard_map/ppermute | solution.py:375
  15.7 1.5 %collective-permute-start.5 = (f32[32,1024]{1,0:T(8,128)S(1)}, f32[32,1024]{1,0:T(8,128)S(1)}, u32[]{:S(2)}, u32[]{:S(2)}) collective-permute-start(f32[32,1024]{1,0:T(8,128)S(1)} %get-tuple-element.25), channel_id=1, source_target_pairs={{0,4},{1,5},{2,6},{3,7},{4,0},{5,1},{6,2},{7,3},{8,12},{9,13},{10,... | collective-permute-start | bytes 393224 | tf_op jit(solution)/shard_map/ppermute | solution.py:375
  17.2 0.5 collective-permute-start.6
  17.7 0.0 collective-permute-done.2
  17.7 2.7 %collective-permute-start.3 = (f32[136,128]{1,0:T(8,128)S(1)}, f32[136,128]{1,0:T(8,128)S(1)}, u32[]{:S(2)}, u32[]{:S(2)}) collective-permute-start(f32[136,128]{1,0:T(8,128)S(1)} %add.6.refs_0_), channel_id=1, source_target_pairs={{0,16},{1,17},{2,18},{3,19},{4,20},{5,21},{6,22},{7,23},{8,24},{9,... | collective-permute-start | bytes 208904 | tf_op jit(solution)/shard_map/ppermute | solution.py:375
  20.4 0.0 collective-permute-done.4.refs_1_
  20.4 1.7 %collective-permute-done.5.refs_2_ = f32[32,1024]{1,0:T(8,128)S(1)} collective-permute-done((f32[32,1024]{1,0:T(8,128)S(1)}, f32[32,1024]{1,0:T(8,128)S(1)}, u32[]{:S(2)}, u32[]{:S(2)}) %collective-permute-start.5) | collective-permute-done | bytes 131104 | tf_op jit(solution)/shard_map/ppermute | solution.py:375
  22.1 1.3 %collective-permute-done.6.refs_3_ = f32[32,1024]{1,0:T(8,128)S(1)} collective-permute-done((f32[32,1024]{1,0:T(8,128)S(1)}, f32[32,1024]{1,0:T(8,128)S(1)}, u32[]{:S(2)}, u32[]{:S(2)}) %collective-permute-start.6) | collective-permute-done | bytes 131104 | tf_op jit(solution)/shard_map/ppermute | solution.py:375
  23.5 2.7 %collective-permute-start.10 = (f32[32,1024]{1,0:T(8,128)S(1)}, f32[32,1024]{1,0:T(8,128)S(1)}, u32[]{:S(2)}, u32[]{:S(2)}) collective-permute-start(f32[32,1024]{1,0:T(8,128)S(1)} %sums.5.refs_2_.refs_0_), channel_id=1, source_target_pairs={{0,16},{1,17},{2,18},{3,19},{4,20},{5,21},{6,22},{7,23},{8,24},{9,... | collective-permute-start | bytes 393224 | tf_op jit(solution)/shard_map/ppermute | solution.py:375
  26.1 0.0 collective-permute-done.3.refs_1_
  26.1 2.5 %collective-permute-start.9 = (f32[136,128]{1,0:T(8,128)S(1)}, f32[136,128]{1,0:T(8,128)S(1)}, u32[]{:S(2)}, u32[]{:S(2)}) collective-permute-start(f32[136,128]{1,0:T(8,128)S(1)} %add.8.refs_0_), channel_id=1, source_target_pairs={{0,5},{1,4},{2,7},{3,6},{4,1},{5,0},{6,3},{7,2},{8,13},{9,12},{10,... | collective-permute-start | bytes 208904 | tf_op jit(solution)/shard_map/ppermute | solution.py:375
  28.7 0.5 %collective-permute-start.8 = (f32[136,128]{1,0:T(8,128)S(1)}, f32[136,128]{1,0:T(8,128)S(1)}, u32[]{:S(2)}, u32[]{:S(2)}) collective-permute-start(f32[136,128]{1,0:T(8,128)S(1)} %add.8.refs_0_), channel_id=1, source_target_pairs={{0,4},{1,5},{2,6},{3,7},{4,0},{5,1},{6,2},{7,3},{8,12},{9,13},{10,... | collective-permute-start | bytes 208904 | tf_op jit(solution)/shard_map/ppermute | solution.py:375
  29.2 0.5 %collective-permute-start.7 = (f32[136,128]{1,0:T(8,128)S(1)}, f32[136,128]{1,0:T(8,128)S(1)}, u32[]{:S(2)}, u32[]{:S(2)}) collective-permute-start(f32[136,128]{1,0:T(8,128)S(1)} %add.8.refs_0_), channel_id=1, source_target_pairs={{0,1},{1,0},{2,3},{3,2},{4,5},{5,4},{6,7},{7,6},{8,9},{9,8},{10,11... | collective-permute-start | bytes 208904 | tf_op jit(solution)/shard_map/ppermute | solution.py:375
  29.7 1.8 %collective-permute-done.10.refs_1_ = f32[32,1024]{1,0:T(8,128)S(1)} collective-permute-done((f32[32,1024]{1,0:T(8,128)S(1)}, f32[32,1024]{1,0:T(8,128)S(1)}, u32[]{:S(2)}, u32[]{:S(2)}) %collective-permute-start.10) | collective-permute-done | bytes 131104 | tf_op jit(solution)/shard_map/ppermute | solution.py:375
  31.5 0.1 collective-permute-start.12
  31.6 0.0 collective-permute-done.9.refs_3_
  31.6 1.3 %collective-permute-done.8.refs_2_ = f32[136,128]{1,0:T(8,128)S(1)} collective-permute-done((f32[136,128]{1,0:T(8,128)S(1)}, f32[136,128]{1,0:T(8,128)S(1)}, u32[]{:S(2)}, u32[]{:S(2)}) %collective-permute-start.8) | collective-permute-done | bytes 69664 | tf_op jit(solution)/shard_map/ppermute | solution.py:375
  33.0 0.5 %collective-permute-done.7.refs_1_ = f32[136,128]{1,0:T(8,128)S(1)} collective-permute-done((f32[136,128]{1,0:T(8,128)S(1)}, f32[136,128]{1,0:T(8,128)S(1)}, u32[]{:S(2)}, u32[]{:S(2)}) %collective-permute-start.7) | collective-permute-done | bytes 69664 | tf_op jit(solution)/shard_map/ppermute | solution.py:375
  33.5 0.1 collective-permute-start.11
  33.6 1.2 %collective-permute-done.11.refs_1_ = f32[136,128]{1,0:T(8,128)S(1)} collective-permute-done((f32[136,128]{1,0:T(8,128)S(1)}, f32[136,128]{1,0:T(8,128)S(1)}, u32[]{:S(2)}, u32[]{:S(2)}) %collective-permute-start.11) | collective-permute-done | bytes 69664 | tf_op jit(solution)/shard_map/ppermute | solution.py:375
  34.9 1.9 %first_part.1 = (f32[256,256]{1,0:T(8,128)S(1)}, f32[256,256]{1,0:T(8,128)S(1)}, f32[16,128]{1,0:T(8,128)S(1)}) custom-call(f32[136,128]{1,0:T(8,128)S(1)} %add.9.refs_0_, f32[136,128]{1,0:T(8,128)S(1)} %collective-permute-done.11.refs_1_), custom_call_target="tpu_custom_call" | custom-call | flops 1000000 | bytes 1000000 | tf_op jit(solution)/shard_map/first_part/pallas_call | solution.py:225
  36.7 0.0 collective-permute-done.12.refs_1_
  36.8 0.2 collective-permute-start.16
  37.0 1.6 %collective-permute-start.15 = (f32[32,1024]{1,0:T(8,128)S(1)}, f32[32,1024]{1,0:T(8,128)S(1)}, u32[]{:S(2)}, u32[]{:S(2)}) collective-permute-start(f32[32,1024]{1,0:T(8,128)S(1)} %sums.7.refs_3_.refs_0_), channel_id=1, source_target_pairs={{0,5},{1,4},{2,7},{3,6},{4,1},{5,0},{6,3},{7,2},{8,13},{9,12},{10,... | collective-permute-start | bytes 393224 | tf_op jit(solution)/shard_map/ppermute | solution.py:375
  38.6 0.5 %collective-permute-start.14 = (f32[32,1024]{1,0:T(8,128)S(1)}, f32[32,1024]{1,0:T(8,128)S(1)}, u32[]{:S(2)}, u32[]{:S(2)}) collective-permute-start(f32[32,1024]{1,0:T(8,128)S(1)} %sums.7.refs_3_.refs_0_), channel_id=1, source_target_pairs={{0,4},{1,5},{2,6},{3,7},{4,0},{5,1},{6,2},{7,3},{8,12},{9,13},{10,... | collective-permute-start | bytes 393224 | tf_op jit(solution)/shard_map/ppermute | solution.py:375
  39.1 1.4 %collective-permute-start.13 = (f32[32,1024]{1,0:T(8,128)S(1)}, f32[32,1024]{1,0:T(8,128)S(1)}, u32[]{:S(2)}, u32[]{:S(2)}) collective-permute-start(f32[32,1024]{1,0:T(8,128)S(1)} %sums.7.refs_3_.refs_0_), channel_id=1, source_target_pairs={{0,1},{1,0},{2,3},{3,2},{4,5},{5,4},{6,7},{7,6},{8,9},{9,8},{10,11... | collective-permute-start | bytes 393224 | tf_op jit(solution)/shard_map/ppermute | solution.py:375
  40.5 5.2 %last_part.1 = (f32[256,256]{1,0:T(8,128)S(1)}, f32[256,256]{1,0:T(8,128)}) custom-call(f32[256,256]{1,0:T(8,128)S(1)} %get-tuple-element.26.refs_2_.refs_0_, f32[256,256]{1,0:T(8,128)S(1)} %get-tuple-element.27.refs_1_, f32[16,128]{1,0:T(8,128)S(1)} %get-tuple-element.28.refs_2_, f32[32,1024]{1,0:T(8,128)S(1)} %sums.7.refs_3_.refs_0_), custom_call_target="tpu_custom_call" | custom-call | flops 3000000000 | bytes 1000000 | tf_op jit(solution)/shard_map/last_part/pallas_call | solution.py:225
  45.7 0.0 collective-permute-done.15.refs_3_
  45.7 0.0 collective-permute-start.19
  45.7 0.0 collective-permute-done.14.refs_2_
  45.7 0.5 %collective-permute-start.18 = (f32[32,1024]{1,0:T(8,128)S(1)}, f32[32,1024]{1,0:T(8,128)S(1)}, u32[]{:S(2)}, u32[]{:S(2)}) collective-permute-start(f32[32,1024]{1,0:T(8,128)S(1)} %collective-permute-done.14.refs_2_), channel_id=1, source_target_pairs={{0,2},{1,3},{2,0},{3,1},{4,6},{5,7},{6,4},{7,5},{8,10},{9,11},{10,... | collective-permute-start | bytes 393224 | tf_op jit(solution)/shard_map/ppermute | solution.py:375
  46.2 0.2 collective-permute-done.13.refs_1_
  46.5 0.0 collective-permute-start.17
  46.5 1.5 %basis.1 = f32[1024,256]{1,0:T(8,128)} custom-call(f32[1024,256]{1,0:T(8,128)S(1)} %get-tuple-element.17.refs_0_, f32[256,256]{1,0:T(8,128)S(1)} %get-tuple-element.29.refs_1_.inverse_ref), custom_call_target="tpu_custom_call" | custom-call | flops 2000000000 | bytes 2097152 | tf_op jit(solution)/shard_map/basis/pallas_call | solution.py:330
  47.9 0.0 collective-permute-done.16.refs_4_
  47.9 0.0 collective-permute-done.19.refs_7_
  48.0 0.0 collective-permute-done.18.refs_6_
  48.0 0.0 collective-permute-done.17.refs_5_
  48.0 1.5 %project.1 = f32[256,1024]{1,0:T(8,128)} custom-call(f32[256,256]{1,0:T(8,128)S(1)} %get-tuple-element.29.refs_1_.inverse_ref, f32[32,1024]{1,0:T(8,128)S(1)} %sums.7.refs_3_.refs_0_, f32[32,1024]{1,0:T(8,128)S(1)} %collective-permute-done.13.refs_1_, f32[32,1024]{1,0:T(8,128)S(1)} %collective-permute-done.14.refs_2_, ...), custom_call_target="tpu_custom_call" | custom-call | flops 400000000 | bytes 2097152 | tf_op jit(solution)/shard_map/project/pallas_call | solution.py:330
  (7 shorter events, 0.1 us)
Async XLA Ops:
  8.9 2.2 %collective-permute-start.1 = (f32[128,1024]{1,0:T(8,128)S(1)}, f32[128,1024]{1,0:T(8,128)S(1)}, u32[]{:S(2)}, u32[]{:S(2)}) collective-permute-start(f32[128,1024]{1,0:T(8,128)S(1)} %get-tuple-element.21), channel_id=1, source_target_pairs={{0,2},{1,3},{2,0},{3,1},{4,6},{5,7},{6,4},{7,5},{8,10},{9,11},{10,... | collective-permute-start | bytes 1572872 | tf_op jit(solution)/shard_map/ppermute | solution.py:375
  9.5 1.6 %collective-permute-start = (f32[136,128]{1,0:T(8,128)S(1)}, f32[136,128]{1,0:T(8,128)S(1)}, u32[]{:S(2)}, u32[]{:S(2)}) collective-permute-start(f32[136,128]{1,0:T(8,128)S(1)} %get-tuple-element.19), channel_id=1, source_target_pairs={{0,2},{1,3},{2,0},{3,1},{4,6},{5,7},{6,4},{7,5},{8,10},{9,11},{10,... | collective-permute-start | bytes 208904 | tf_op jit(solution)/shard_map/ppermute | solution.py:375
  11.2 6.5 %collective-permute-start.2 = (f32[136,128]{1,0:T(8,128)S(1)}, f32[136,128]{1,0:T(8,128)S(1)}, u32[]{:S(2)}, u32[]{:S(2)}) collective-permute-start(f32[136,128]{1,0:T(8,128)S(1)} %add.7), channel_id=1, source_target_pairs={{0,8},{1,9},{2,10},{3,11},{4,12},{5,13},{6,14},{7,15},{8,0},{9,1},... | collective-permute-start | bytes 208904 | tf_op jit(solution)/shard_map/ppermute | solution.py:375
  14.2 6.2 %collective-permute-start.4 = (f32[32,1024]{1,0:T(8,128)S(1)}, f32[32,1024]{1,0:T(8,128)S(1)}, u32[]{:S(2)}, u32[]{:S(2)}) collective-permute-start(f32[32,1024]{1,0:T(8,128)S(1)} %get-tuple-element.24), channel_id=1, source_target_pairs={{0,1},{1,0},{2,3},{3,2},{4,5},{5,4},{6,7},{7,6},{8,9},{9,8},{10,11... | collective-permute-start | bytes 393224 | tf_op jit(solution)/shard_map/ppermute | solution.py:375
  15.7 6.4 %collective-permute-start.5 = (f32[32,1024]{1,0:T(8,128)S(1)}, f32[32,1024]{1,0:T(8,128)S(1)}, u32[]{:S(2)}, u32[]{:S(2)}) collective-permute-start(f32[32,1024]{1,0:T(8,128)S(1)} %get-tuple-element.25), channel_id=1, source_target_pairs={{0,4},{1,5},{2,6},{3,7},{4,0},{5,1},{6,2},{7,3},{8,12},{9,13},{10,... | collective-permute-start | bytes 393224 | tf_op jit(solution)/shard_map/ppermute | solution.py:375
  17.2 6.2 %collective-permute-start.6 = (f32[32,1024]{1,0:T(8,128)S(1)}, f32[32,1024]{1,0:T(8,128)S(1)}, u32[]{:S(2)}, u32[]{:S(2)}) collective-permute-start(f32[32,1024]{1,0:T(8,128)S(1)} %get-tuple-element.22.refs_2_), channel_id=1, source_target_pairs={{0,5},{1,4},{2,7},{3,6},{4,1},{5,0},{6,3},{7,2},{8,13},{9,12},{10,... | collective-permute-start | bytes 393224 | tf_op jit(solution)/shard_map/ppermute | solution.py:375
  17.7 8.4 %collective-permute-start.3 = (f32[136,128]{1,0:T(8,128)S(1)}, f32[136,128]{1,0:T(8,128)S(1)}, u32[]{:S(2)}, u32[]{:S(2)}) collective-permute-start(f32[136,128]{1,0:T(8,128)S(1)} %add.6.refs_0_), channel_id=1, source_target_pairs={{0,16},{1,17},{2,18},{3,19},{4,20},{5,21},{6,22},{7,23},{8,24},{9,... | collective-permute-start | bytes 208904 | tf_op jit(solution)/shard_map/ppermute | solution.py:375
  23.5 8.0 %collective-permute-start.10 = (f32[32,1024]{1,0:T(8,128)S(1)}, f32[32,1024]{1,0:T(8,128)S(1)}, u32[]{:S(2)}, u32[]{:S(2)}) collective-permute-start(f32[32,1024]{1,0:T(8,128)S(1)} %sums.5.refs_2_.refs_0_), channel_id=1, source_target_pairs={{0,16},{1,17},{2,18},{3,19},{4,20},{5,21},{6,22},{7,23},{8,24},{9,... | collective-permute-start | bytes 393224 | tf_op jit(solution)/shard_map/ppermute | solution.py:375
  26.1 5.5 %collective-permute-start.9 = (f32[136,128]{1,0:T(8,128)S(1)}, f32[136,128]{1,0:T(8,128)S(1)}, u32[]{:S(2)}, u32[]{:S(2)}) collective-permute-start(f32[136,128]{1,0:T(8,128)S(1)} %add.8.refs_0_), channel_id=1, source_target_pairs={{0,5},{1,4},{2,7},{3,6},{4,1},{5,0},{6,3},{7,2},{8,13},{9,12},{10,... | collective-permute-start | bytes 208904 | tf_op jit(solution)/shard_map/ppermute | solution.py:375
  28.7 4.3 %collective-permute-start.8 = (f32[136,128]{1,0:T(8,128)S(1)}, f32[136,128]{1,0:T(8,128)S(1)}, u32[]{:S(2)}, u32[]{:S(2)}) collective-permute-start(f32[136,128]{1,0:T(8,128)S(1)} %add.8.refs_0_), channel_id=1, source_target_pairs={{0,4},{1,5},{2,6},{3,7},{4,0},{5,1},{6,2},{7,3},{8,12},{9,13},{10,... | collective-permute-start | bytes 208904 | tf_op jit(solution)/shard_map/ppermute | solution.py:375
  29.2 4.3 %collective-permute-start.7 = (f32[136,128]{1,0:T(8,128)S(1)}, f32[136,128]{1,0:T(8,128)S(1)}, u32[]{:S(2)}, u32[]{:S(2)}) collective-permute-start(f32[136,128]{1,0:T(8,128)S(1)} %add.8.refs_0_), channel_id=1, source_target_pairs={{0,1},{1,0},{2,3},{3,2},{4,5},{5,4},{6,7},{7,6},{8,9},{9,8},{10,11... | collective-permute-start | bytes 208904 | tf_op jit(solution)/shard_map/ppermute | solution.py:375
  31.5 5.2 %collective-permute-start.12 = (f32[32,1024]{1,0:T(8,128)S(1)}, f32[32,1024]{1,0:T(8,128)S(1)}, u32[]{:S(2)}, u32[]{:S(2)}) collective-permute-start(f32[32,1024]{1,0:T(8,128)S(1)} %sums.6.refs_4_.refs_0_), channel_id=1, source_target_pairs={{0,8},{1,9},{2,10},{3,11},{4,12},{5,13},{6,14},{7,15},{8,0},{9,1},... | collective-permute-start | bytes 393224 | tf_op jit(solution)/shard_map/ppermute | solution.py:375
  33.5 1.3 %collective-permute-start.11 = (f32[136,128]{1,0:T(8,128)S(1)}, f32[136,128]{1,0:T(8,128)S(1)}, u32[]{:S(2)}, u32[]{:S(2)}) collective-permute-start(f32[136,128]{1,0:T(8,128)S(1)} %add.9.refs_0_), channel_id=1, source_target_pairs={{0,2},{1,3},{2,0},{3,1},{4,6},{5,7},{6,4},{7,5},{8,10},{9,11},{10,... | collective-permute-start | bytes 208904 | tf_op jit(solution)/shard_map/ppermute | solution.py:375
  36.8 11.2 %collective-permute-start.16 = (f32[32,1024]{1,0:T(8,128)S(1)}, f32[32,1024]{1,0:T(8,128)S(1)}, u32[]{:S(2)}, u32[]{:S(2)}) collective-permute-start(f32[32,1024]{1,0:T(8,128)S(1)} %sums.7.refs_3_.refs_0_), channel_id=1, source_target_pairs={{0,2},{1,3},{2,0},{3,1},{4,6},{5,7},{6,4},{7,5},{8,10},{9,11},{10,... | collective-permute-start | bytes 393224 | tf_op jit(solution)/shard_map/ppermute | solution.py:375
  37.0 8.7 %collective-permute-start.15 = (f32[32,1024]{1,0:T(8,128)S(1)}, f32[32,1024]{1,0:T(8,128)S(1)}, u32[]{:S(2)}, u32[]{:S(2)}) collective-permute-start(f32[32,1024]{1,0:T(8,128)S(1)} %sums.7.refs_3_.refs_0_), channel_id=1, source_target_pairs={{0,5},{1,4},{2,7},{3,6},{4,1},{5,0},{6,3},{7,2},{8,13},{9,12},{10,... | collective-permute-start | bytes 393224 | tf_op jit(solution)/shard_map/ppermute | solution.py:375
  38.6 7.2 %collective-permute-start.14 = (f32[32,1024]{1,0:T(8,128)S(1)}, f32[32,1024]{1,0:T(8,128)S(1)}, u32[]{:S(2)}, u32[]{:S(2)}) collective-permute-start(f32[32,1024]{1,0:T(8,128)S(1)} %sums.7.refs_3_.refs_0_), channel_id=1, source_target_pairs={{0,4},{1,5},{2,6},{3,7},{4,0},{5,1},{6,2},{7,3},{8,12},{9,13},{10,... | collective-permute-start | bytes 393224 | tf_op jit(solution)/shard_map/ppermute | solution.py:375
  39.1 7.4 %collective-permute-start.13 = (f32[32,1024]{1,0:T(8,128)S(1)}, f32[32,1024]{1,0:T(8,128)S(1)}, u32[]{:S(2)}, u32[]{:S(2)}) collective-permute-start(f32[32,1024]{1,0:T(8,128)S(1)} %sums.7.refs_3_.refs_0_), channel_id=1, source_target_pairs={{0,1},{1,0},{2,3},{3,2},{4,5},{5,4},{6,7},{7,6},{8,9},{9,8},{10,11... | collective-permute-start | bytes 393224 | tf_op jit(solution)/shard_map/ppermute | solution.py:375
  45.7 2.2 %collective-permute-start.19 = (f32[32,1024]{1,0:T(8,128)S(1)}, f32[32,1024]{1,0:T(8,128)S(1)}, u32[]{:S(2)}, u32[]{:S(2)}) collective-permute-start(f32[32,1024]{1,0:T(8,128)S(1)} %collective-permute-done.15.refs_3_), channel_id=1, source_target_pairs={{0,2},{1,3},{2,0},{3,1},{4,6},{5,7},{6,4},{7,5},{8,10},{9,11},{10,... | collective-permute-start | bytes 393224 | tf_op jit(solution)/shard_map/ppermute | solution.py:375
  45.7 2.2 %collective-permute-start.18 = (f32[32,1024]{1,0:T(8,128)S(1)}, f32[32,1024]{1,0:T(8,128)S(1)}, u32[]{:S(2)}, u32[]{:S(2)}) collective-permute-start(f32[32,1024]{1,0:T(8,128)S(1)} %collective-permute-done.14.refs_2_), channel_id=1, source_target_pairs={{0,2},{1,3},{2,0},{3,1},{4,6},{5,7},{6,4},{7,5},{8,10},{9,11},{10,... | collective-permute-start | bytes 393224 | tf_op jit(solution)/shard_map/ppermute | solution.py:375
  46.5 1.5 %collective-permute-start.17 = (f32[32,1024]{1,0:T(8,128)S(1)}, f32[32,1024]{1,0:T(8,128)S(1)}, u32[]{:S(2)}, u32[]{:S(2)}) collective-permute-start(f32[32,1024]{1,0:T(8,128)S(1)} %collective-permute-done.13.refs_1_), channel_id=1, source_target_pairs={{0,2},{1,3},{2,0},{3,1},{4,6},{5,7},{6,4},{7,5},{8,10},{9,11},{10,... | collective-permute-start | bytes 393224 | tf_op jit(solution)/shard_map/ppermute | solution.py:375

commit v19 on v18

--- a/solution.py
+++ b/solution.py
@@ -142,7 +142,7 @@
     return pl.ds(pl.multiple_of(block * height, GROUP), height)
 
 
-def local_kernel(features_hbm, sketch_hbm, sampled_ref, keep_ref, send_ref, gram_keep_ref, gram_send_ref, features_ref, sketch_ref, pair_ref, high_ref, low_ref, flip_high_ref, flip_low_ref, cross_ref, packed_ref, sems):
+def local_kernel(features_hbm, sketch_hbm, sampled_high_ref, sampled_low_ref, keep_ref, send_ref, gram_keep_ref, gram_send_ref, features_ref, sketch_ref, pair_ref, high_ref, low_ref, flip_high_ref, flip_low_ref, cross_ref, packed_ref, sems):
     rows, depth = features_ref.shape
     rank = sketch_ref.shape[1]
     chunks = rows // BLOCK
@@ -162,10 +162,11 @@
         high_ref[span, :], low_ref[span, :] = features
         both = lax.dot(features[0], pair_ref[...], preferred_element_type=jnp.float32)
         sampled = both[:, :rank] + (both[:, rank:] + lax.dot(features[1], pair_ref[:, :rank], preferred_element_type=jnp.float32))
-        sampled_ref[span, :] = sampled
+        parts = split(sampled)
+        sampled_high_ref[span, :], sampled_low_ref[span, :] = parts
         flipped = split(sampled.T)
         flip_high_ref[:, span], flip_low_ref[:, span] = flipped
-        term = product(flipped, split(sampled), 1, 0)
+        term = product(flipped, parts, 1, 0)
         gram = term if gram is None else gram + term
     row = lax.broadcasted_iota(jnp.int32, (LANES, LANES), 0)
     col = lax.broadcasted_iota(jnp.int32, (LANES, LANES), 1)
@@ -201,12 +202,13 @@
     rows, depth = features.shape
     rank = sketch.shape[1]
     packed = PACKED
+    half = jax.ShapeDtypeStruct((rows, rank), jnp.bfloat16)
     hbm = pl.BlockSpec(memory_space=pltpu.HBM)
     return pl.pallas_call(
         local_kernel,
-        out_shape=(f32(rows, rank), f32(rank // 2, depth), f32(rank // 2, depth), f32(packed // 2, LANES), f32(packed // 2, LANES)),
+        out_shape=(half, half, f32(rank // 2, depth), f32(rank // 2, depth), f32(packed // 2, LANES), f32(packed // 2, LANES)),
         in_specs=[hbm, hbm],
-        out_specs=(VMEM,) * 5,
+        out_specs=(VMEM,) * 6,
         scratch_shapes=[
             pltpu.VMEM((rows, depth), jnp.float32), pltpu.VMEM((depth, rank), jnp.float32),
             pltpu.VMEM((depth, 2 * rank), jnp.bfloat16),
@@ -314,12 +316,12 @@
     return copy
 
 
-def basis_kernel(scale, sampled_ref, inverse_ref, basis_hbm, basis_ref, sems):
+def basis_kernel(scale, high_ref, low_ref, inverse_ref, basis_hbm, basis_ref, sems):
     inverse = split(inverse_ref[...] * scale)
     copies = []
-    for at in range(sampled_ref.shape[0] // BLOCK):
+    for at in range(high_ref.shape[0] // BLOCK):
         span = slice(at * BLOCK, (at + 1) * BLOCK)
-        basis_ref[span, :] = product(split(sampled_ref[span, :]), inverse, 1, 1)
+        basis_ref[span, :] = product((high_ref[span, :], low_ref[span, :]), inverse, 1, 1)
         copies.append(copy_out(basis_ref, basis_hbm, (pl.ds(at * BLOCK, BLOCK), slice(None)), sems.at[at]))
     for copy in copies:
         copy.wait()
@@ -341,7 +343,7 @@
 
 def basis_of(sampled, inverse, scale):
     kernel = lambda *refs: basis_kernel(scale, *refs)
-    return streamed(kernel, "basis", f32(*sampled.shape), (sampled, inverse), (), 2 * 10**9)
+    return streamed(kernel, "basis", f32(*sampled[0].shape), (*sampled, inverse), (), 2 * 10**9)
 
 
 def project_kernel(inverse_ref, *refs):
@@ -395,7 +397,7 @@
 def per_device(features, sketch):
     scale = (features.shape[0] * lax.axis_size(AXES)) ** 0.5
     size = sketch.shape[1]
-    sampled, keep, other, gram, gram_other = local_terms(features, sketch)
+    *sampled, keep, other, gram, gram_other = local_terms(features, sketch)
     gram_other = send(gram_other, *CORE)
     parts = sums([keep, send(other, *CORE)], 4, after=(gram_other,))
     cross = [parts[0]] + to_plane(parts[1:])
@@ -405,13 +407,13 @@
     (line,) = sums(cross)
     gram = add([gram, gram_other], (line,))
     grams = [gram] + to_plane([gram] * 3)
-    (line,) = sums([line, send(line, *FAR)], masks=(0, 2))
+    (line,) = sums([line, send(line, *NEAR)], masks=(0, 1))
     gram = add(grams, (line,))
     for mask in spare_bits():
         line = line + send(line, *mask)
         gram = gram + send(gram, *mask)
     *state, norm = first_part(gram, send(gram, *CORE), size, ())
-    (line,) = sums([line, send(line, *NEAR)], masks=(0, 1), after=state[:1])
+    (line,) = sums([line, send(line, *FAR)], masks=(0, 2), after=state[:1])
     plane = [line] + to_plane([line] * 3)
     inverse, factor = last_part((*state, norm), size, scale, PANEL, (line,))
     cross = plane + [send(part, *CORE) for part in plane]

time: 49.7 us -> 49.4 us (level)
  waiting for transfers between devices: 9.83 us -> 8.9 us
  starting transfers between devices: 20.4 us -> 21.1 us
    ppermute x20, waiting for transfers between devices: 9.83 us -> 8.9 us  [send(): return lax.ppermute(value, AXES, pairs)]
    ppermute x20, starting transfers between devices: 20.4 us -> 21.1 us  [send(): return lax.ppermute(value, AXES, pairs)]
  transfers between devices with their start and end apart: 20 -> 20, of which waited for: 8 -> 7; matrix products, arithmetic and copies ran while one was open for 0% -> 0% of each run, Pallas kernels for 17% -> 17%
where the time goes in v19:
time: 49.4 us; the launch traced here: 49.3 us
  starting transfers between devices  21.1 us (43%)
  Pallas kernels  18.5 us (37%)
  waiting for transfers between devices  8.9 us (18%)
  between operations  0.75 us (2%)
    ppermute x20, starting transfers between devices, send(): return lax.ppermute(value, AXES, pairs)  21.1 us
    ppermute x20, waiting for transfers between devices, send(): return lax.ppermute(value, AXES, pairs)  8.9 us
    pallas_call x1, Pallas kernels, local_terms(): pl.pallas_call(local_kernel, out_shape=(half, half, f32(rank // 2, depth)...  8.3 us
    pallas_call x9, Pallas kernels, call(): pl.pallas_call(lambda *refs: kernel(*refs[:len(operands)], *refs[len(oper...  7.25 us
    pallas_call x2, Pallas kernels, streamed(): pl.pallas_call(kernel, out_shape=out, in_specs=[VMEM] * len(operands), ou...  2.95 us
  transfers between devices with their start and end apart: 20, of which 7 were waited for; matrix products, arithmetic and copies ran while one was open for 0% of the time, Pallas kernels for 17%

profile of v19, /device:TPU:0, one launch (start us, length us, event | category | flops | bytes accessed | tf_op | source)
XLA Modules:
  0.0 49.3 jit_solution(14490415560155916522)
XLA Ops:
  0.6 8.3 %local_terms.1 = (bf16[1024,256]{1,0:T(8,128)(2,1)S(1)}, bf16[1024,256]{1,0:T(8,128)(2,1)S(1)}, f32[128,1024]{1,0:T(8,128)S(1)}, f32[128,1024]{1,0:T(8,128)S(1)}...) custom-call(f32[1024,1024]{1,0:T(8,128)} %features_hbm.1, f32[1024,256]{1,0:T(8,128)} %sketch_hbm.1), custom_call_target="tpu_custom_call" | custom-call | flops 4000000000 | bytes 8388608 | tf_op jit(solution)/shard_map/local_terms/pallas_call | solution.py:207
  8.9 0.5 %collective-permute-start.1 = (f32[128,1024]{1,0:T(8,128)S(1)}, f32[128,1024]{1,0:T(8,128)S(1)}, u32[]{:S(2)}, u32[]{:S(2)}) collective-permute-start(f32[128,1024]{1,0:T(8,128)S(1)} %get-tuple-element.23), channel_id=1, source_target_pairs={{0,2},{1,3},{2,0},{3,1},{4,6},{5,7},{6,4},{7,5},{8,10},{9,11},{10,... | collective-permute-start | bytes 1572872 | tf_op jit(solution)/shard_map/ppermute | solution.py:377
  9.5 0.1 collective-permute-start
  9.5 1.6 %collective-permute-done.refs_2_.refs_1_ = f32[136,128]{1,0:T(8,128)S(1)} collective-permute-done((f32[136,128]{1,0:T(8,128)S(1)}, f32[136,128]{1,0:T(8,128)S(1)}, u32[]{:S(2)}, u32[]{:S(2)}) %collective-permute-start) | collective-permute-done | bytes 69664 | tf_op jit(solution)/shard_map/ppermute | solution.py:377
  11.1 0.0 collective-permute-done.1.refs_1_
  11.1 0.1 sums.4
  11.2 3.0 %collective-permute-start.2 = (f32[136,128]{1,0:T(8,128)S(1)}, f32[136,128]{1,0:T(8,128)S(1)}, u32[]{:S(2)}, u32[]{:S(2)}) collective-permute-start(f32[136,128]{1,0:T(8,128)S(1)} %add.7), channel_id=1, source_target_pairs={{0,8},{1,9},{2,10},{3,11},{4,12},{5,13},{6,14},{7,15},{8,0},{9,1},... | collective-permute-start | bytes 208904 | tf_op jit(solution)/shard_map/ppermute | solution.py:377
  14.2 1.5 %collective-permute-start.4 = (f32[32,1024]{1,0:T(8,128)S(1)}, f32[32,1024]{1,0:T(8,128)S(1)}, u32[]{:S(2)}, u32[]{:S(2)}) collective-permute-start(f32[32,1024]{1,0:T(8,128)S(1)} %get-tuple-element.26), channel_id=1, source_target_pairs={{0,1},{1,0},{2,3},{3,2},{4,5},{5,4},{6,7},{7,6},{8,9},{9,8},{10,11... | collective-permute-start | bytes 393224 | tf_op jit(solution)/shard_map/ppermute | solution.py:377
  15.7 1.5 %collective-permute-start.5 = (f32[32,1024]{1,0:T(8,128)S(1)}, f32[32,1024]{1,0:T(8,128)S(1)}, u32[]{:S(2)}, u32[]{:S(2)}) collective-permute-start(f32[32,1024]{1,0:T(8,128)S(1)} %get-tuple-element.27), channel_id=1, source_target_pairs={{0,4},{1,5},{2,6},{3,7},{4,0},{5,1},{6,2},{7,3},{8,12},{9,13},{10,... | collective-permute-start | bytes 393224 | tf_op jit(solution)/shard_map/ppermute | solution.py:377
  17.2 0.5 collective-permute-start.6
  17.7 0.0 collective-permute-done.2
  17.7 2.7 %collective-permute-start.3 = (f32[136,128]{1,0:T(8,128)S(1)}, f32[136,128]{1,0:T(8,128)S(1)}, u32[]{:S(2)}, u32[]{:S(2)}) collective-permute-start(f32[136,128]{1,0:T(8,128)S(1)} %add.6.refs_0_), channel_id=1, source_target_pairs={{0,16},{1,17},{2,18},{3,19},{4,20},{5,21},{6,22},{7,23},{8,24},{9,... | collective-permute-start | bytes 208904 | tf_op jit(solution)/shard_map/ppermute | solution.py:377
  20.4 0.0 collective-permute-done.4.refs_1_
  20.4 1.7 %collective-permute-done.5.refs_2_ = f32[32,1024]{1,0:T(8,128)S(1)} collective-permute-done((f32[32,1024]{1,0:T(8,128)S(1)}, f32[32,1024]{1,0:T(8,128)S(1)}, u32[]{:S(2)}, u32[]{:S(2)}) %collective-permute-start.5) | collective-permute-done | bytes 131104 | tf_op jit(solution)/shard_map/ppermute | solution.py:377
  22.1 1.3 %collective-permute-done.6.refs_3_ = f32[32,1024]{1,0:T(8,128)S(1)} collective-permute-done((f32[32,1024]{1,0:T(8,128)S(1)}, f32[32,1024]{1,0:T(8,128)S(1)}, u32[]{:S(2)}, u32[]{:S(2)}) %collective-permute-start.6) | collective-permute-done | bytes 131104 | tf_op jit(solution)/shard_map/ppermute | solution.py:377
  23.5 0.4 collective-permute-start.10
  23.9 0.0 collective-permute-done.3.refs_1_
  23.9 2.6 %collective-permute-start.9 = (f32[136,128]{1,0:T(8,128)S(1)}, f32[136,128]{1,0:T(8,128)S(1)}, u32[]{:S(2)}, u32[]{:S(2)}) collective-permute-start(f32[136,128]{1,0:T(8,128)S(1)} %add.8.refs_0_), channel_id=1, source_target_pairs={{0,5},{1,4},{2,7},{3,6},{4,1},{5,0},{6,3},{7,2},{8,13},{9,12},{10,... | collective-permute-start | bytes 208904 | tf_op jit(solution)/shard_map/ppermute | solution.py:377
  26.5 0.5 %collective-permute-start.8 = (f32[136,128]{1,0:T(8,128)S(1)}, f32[136,128]{1,0:T(8,128)S(1)}, u32[]{:S(2)}, u32[]{:S(2)}) collective-permute-start(f32[136,128]{1,0:T(8,128)S(1)} %add.8.refs_0_), channel_id=1, source_target_pairs={{0,4},{1,5},{2,6},{3,7},{4,0},{5,1},{6,2},{7,3},{8,12},{9,13},{10,... | collective-permute-start | bytes 208904 | tf_op jit(solution)/shard_map/ppermute | solution.py:377
  27.0 0.4 collective-permute-start.7
  27.5 1.0 %collective-permute-done.10.refs_1_ = f32[32,1024]{1,0:T(8,128)S(1)} collective-permute-done((f32[32,1024]{1,0:T(8,128)S(1)}, f32[32,1024]{1,0:T(8,128)S(1)}, u32[]{:S(2)}, u32[]{:S(2)}) %collective-permute-start.10) | collective-permute-done | bytes 131104 | tf_op jit(solution)/shard_map/ppermute | solution.py:377
  28.5 3.2 %collective-permute-start.12 = (f32[32,1024]{1,0:T(8,128)S(1)}, f32[32,1024]{1,0:T(8,128)S(1)}, u32[]{:S(2)}, u32[]{:S(2)}) collective-permute-start(f32[32,1024]{1,0:T(8,128)S(1)} %sums.6.refs_4_.refs_0_), channel_id=1, source_target_pairs={{0,16},{1,17},{2,18},{3,19},{4,20},{5,21},{6,22},{7,23},{8,24},{9,... | collective-permute-start | bytes 393224 | tf_op jit(solution)/shard_map/ppermute | solution.py:377
  31.7 0.0 collective-permute-done.9.refs_3_
  31.7 0.0 collective-permute-done.8.refs_2_
  31.7 0.0 collective-permute-done.7.refs_1_
  31.7 0.1 collective-permute-start.11
  31.8 1.2 %collective-permute-done.11.refs_1_ = f32[136,128]{1,0:T(8,128)S(1)} collective-permute-done((f32[136,128]{1,0:T(8,128)S(1)}, f32[136,128]{1,0:T(8,128)S(1)}, u32[]{:S(2)}, u32[]{:S(2)}) %collective-permute-start.11) | collective-permute-done | bytes 69664 | tf_op jit(solution)/shard_map/ppermute | solution.py:377
  33.0 1.9 %first_part.1 = (f32[256,256]{1,0:T(8,128)S(1)}, f32[256,256]{1,0:T(8,128)S(1)}, f32[16,128]{1,0:T(8,128)S(1)}) custom-call(f32[136,128]{1,0:T(8,128)S(1)} %add.9.refs_0_, f32[136,128]{1,0:T(8,128)S(1)} %collective-permute-done.11.refs_1_), custom_call_target="tpu_custom_call" | custom-call | flops 1000000 | bytes 1000000 | tf_op jit(solution)/shard_map/first_part/pallas_call | solution.py:227
  34.9 1.0 %collective-permute-done.12.refs_1_ = f32[32,1024]{1,0:T(8,128)S(1)} collective-permute-done((f32[32,1024]{1,0:T(8,128)S(1)}, f32[32,1024]{1,0:T(8,128)S(1)}, u32[]{:S(2)}, u32[]{:S(2)}) %collective-permute-start.12) | collective-permute-done | bytes 131104 | tf_op jit(solution)/shard_map/ppermute | solution.py:377
  36.0 0.1 collective-permute-start.16
  36.0 2.5 %collective-permute-start.15 = (f32[32,1024]{1,0:T(8,128)S(1)}, f32[32,1024]{1,0:T(8,128)S(1)}, u32[]{:S(2)}, u32[]{:S(2)}) collective-permute-start(f32[32,1024]{1,0:T(8,128)S(1)} %sums.7.refs_3_.refs_0_), channel_id=1, source_target_pairs={{0,5},{1,4},{2,7},{3,6},{4,1},{5,0},{6,3},{7,2},{8,13},{9,12},{10,... | collective-permute-start | bytes 393224 | tf_op jit(solution)/shard_map/ppermute | solution.py:377
  38.5 0.5 %collective-permute-start.14 = (f32[32,1024]{1,0:T(8,128)S(1)}, f32[32,1024]{1,0:T(8,128)S(1)}, u32[]{:S(2)}, u32[]{:S(2)}) collective-permute-start(f32[32,1024]{1,0:T(8,128)S(1)} %sums.7.refs_3_.refs_0_), channel_id=1, source_target_pairs={{0,4},{1,5},{2,6},{3,7},{4,0},{5,1},{6,2},{7,3},{8,12},{9,13},{10,... | collective-permute-start | bytes 393224 | tf_op jit(solution)/shard_map/ppermute | solution.py:377
  39.1 0.5 %collective-permute-start.13 = (f32[32,1024]{1,0:T(8,128)S(1)}, f32[32,1024]{1,0:T(8,128)S(1)}, u32[]{:S(2)}, u32[]{:S(2)}) collective-permute-start(f32[32,1024]{1,0:T(8,128)S(1)} %sums.7.refs_3_.refs_0_), channel_id=1, source_target_pairs={{0,1},{1,0},{2,3},{3,2},{4,5},{5,4},{6,7},{7,6},{8,9},{9,8},{10,11... | collective-permute-start | bytes 393224 | tf_op jit(solution)/shard_map/ppermute | solution.py:377
  39.6 5.2 %last_part.1 = (f32[256,256]{1,0:T(8,128)S(1)}, f32[256,256]{1,0:T(8,128)}) custom-call(f32[256,256]{1,0:T(8,128)S(1)} %get-tuple-element.28.refs_2_.refs_0_, f32[256,256]{1,0:T(8,128)S(1)} %get-tuple-element.29.refs_1_, f32[16,128]{1,0:T(8,128)S(1)} %get-tuple-element.30.refs_2_, f32[32,1024]{1,0:T(8,128)S(1)} %sums.7.refs_3_.refs_0_), custom_call_target="tpu_custom_call" | custom-call | flops 3000000000 | bytes 1000000 | tf_op jit(solution)/shard_map/last_part/pallas_call | solution.py:227
  44.8 0.0 collective-permute-done.15.refs_3_
  44.8 0.0 collective-permute-start.19
  44.8 0.9 %collective-permute-done.14.refs_2_ = f32[32,1024]{1,0:T(8,128)S(1)} collective-permute-done((f32[32,1024]{1,0:T(8,128)S(1)}, f32[32,1024]{1,0:T(8,128)S(1)}, u32[]{:S(2)}, u32[]{:S(2)}) %collective-permute-start.14) | collective-permute-done | bytes 131104 | tf_op jit(solution)/shard_map/ppermute | solution.py:377
  45.7 0.0 collective-permute-start.18
  45.7 0.0 collective-permute-done.13.refs_1_
  45.8 0.5 %collective-permute-start.17 = (f32[32,1024]{1,0:T(8,128)S(1)}, f32[32,1024]{1,0:T(8,128)S(1)}, u32[]{:S(2)}, u32[]{:S(2)}) collective-permute-start(f32[32,1024]{1,0:T(8,128)S(1)} %collective-permute-done.13.refs_1_), channel_id=1, source_target_pairs={{0,2},{1,3},{2,0},{3,1},{4,6},{5,7},{6,4},{7,5},{8,10},{9,11},{10,... | collective-permute-start | bytes 393224 | tf_op jit(solution)/shard_map/ppermute | solution.py:377
  46.3 1.4 %basis.1 = f32[1024,256]{1,0:T(8,128)} custom-call(bf16[1024,256]{1,0:T(8,128)(2,1)S(1)} %get-tuple-element.18.refs_0_, bf16[1024,256]{1,0:T(8,128)(2,1)S(1)} %get-tuple-element.19.refs_1_, f32[256,256]{1,0:T(8,128)S(1)} %get-tuple-element.31.refs_2_.inverse_ref), custom_call_target="tpu_custom_call" | custom-call | flops 2000000000 | bytes 2097152 | tf_op jit(solution)/shard_map/basis/pallas_call | solution.py:332
  47.7 0.0 collective-permute-done.16.refs_4_
  47.7 0.0 collective-permute-done.19.refs_7_
  47.7 0.0 collective-permute-done.18.refs_6_
  47.7 0.0 collective-permute-done.17.refs_5_
  47.7 1.5 %project.1 = f32[256,1024]{1,0:T(8,128)} custom-call(f32[256,256]{1,0:T(8,128)S(1)} %get-tuple-element.31.refs_2_.inverse_ref, f32[32,1024]{1,0:T(8,128)S(1)} %sums.7.refs_3_.refs_0_, f32[32,1024]{1,0:T(8,128)S(1)} %collective-permute-done.13.refs_1_, f32[32,1024]{1,0:T(8,128)S(1)} %collective-permute-done.14.refs_2_, ...), custom_call_target="tpu_custom_call" | custom-call | flops 400000000 | bytes 2097152 | tf_op jit(solution)/shard_map/project/pallas_call | solution.py:332
  (7 shorter events, 0.1 us)
Async XLA Ops:
  8.9 2.2 %collective-permute-start.1 = (f32[128,1024]{1,0:T(8,128)S(1)}, f32[128,1024]{1,0:T(8,128)S(1)}, u32[]{:S(2)}, u32[]{:S(2)}) collective-permute-start(f32[128,1024]{1,0:T(8,128)S(1)} %get-tuple-element.23), channel_id=1, source_target_pairs={{0,2},{1,3},{2,0},{3,1},{4,6},{5,7},{6,4},{7,5},{8,10},{9,11},{10,... | collective-permute-start | bytes 1572872 | tf_op jit(solution)/shard_map/ppermute | solution.py:377
  9.5 1.6 %collective-permute-start = (f32[136,128]{1,0:T(8,128)S(1)}, f32[136,128]{1,0:T(8,128)S(1)}, u32[]{:S(2)}, u32[]{:S(2)}) collective-permute-start(f32[136,128]{1,0:T(8,128)S(1)} %get-tuple-element.21), channel_id=1, source_target_pairs={{0,2},{1,3},{2,0},{3,1},{4,6},{5,7},{6,4},{7,5},{8,10},{9,11},{10,... | collective-permute-start | bytes 208904 | tf_op jit(solution)/shard_map/ppermute | solution.py:377
  11.2 6.5 %collective-permute-start.2 = (f32[136,128]{1,0:T(8,128)S(1)}, f32[136,128]{1,0:T(8,128)S(1)}, u32[]{:S(2)}, u32[]{:S(2)}) collective-permute-start(f32[136,128]{1,0:T(8,128)S(1)} %add.7), channel_id=1, source_target_pairs={{0,8},{1,9},{2,10},{3,11},{4,12},{5,13},{6,14},{7,15},{8,0},{9,1},... | collective-permute-start | bytes 208904 | tf_op jit(solution)/shard_map/ppermute | solution.py:377
  14.2 6.2 %collective-permute-start.4 = (f32[32,1024]{1,0:T(8,128)S(1)}, f32[32,1024]{1,0:T(8,128)S(1)}, u32[]{:S(2)}, u32[]{:S(2)}) collective-permute-start(f32[32,1024]{1,0:T(8,128)S(1)} %get-tuple-element.26), channel_id=1, source_target_pairs={{0,1},{1,0},{2,3},{3,2},{4,5},{5,4},{6,7},{7,6},{8,9},{9,8},{10,11... | collective-permute-start | bytes 393224 | tf_op jit(solution)/shard_map/ppermute | solution.py:377
  15.7 6.4 %collective-permute-start.5 = (f32[32,1024]{1,0:T(8,128)S(1)}, f32[32,1024]{1,0:T(8,128)S(1)}, u32[]{:S(2)}, u32[]{:S(2)}) collective-permute-start(f32[32,1024]{1,0:T(8,128)S(1)} %get-tuple-element.27), channel_id=1, source_target_pairs={{0,4},{1,5},{2,6},{3,7},{4,0},{5,1},{6,2},{7,3},{8,12},{9,13},{10,... | collective-permute-start | bytes 393224 | tf_op jit(solution)/shard_map/ppermute | solution.py:377
  17.2 6.2 %collective-permute-start.6 = (f32[32,1024]{1,0:T(8,128)S(1)}, f32[32,1024]{1,0:T(8,128)S(1)}, u32[]{:S(2)}, u32[]{:S(2)}) collective-permute-start(f32[32,1024]{1,0:T(8,128)S(1)} %get-tuple-element.24.refs_2_), channel_id=1, source_target_pairs={{0,5},{1,4},{2,7},{3,6},{4,1},{5,0},{6,3},{7,2},{8,13},{9,12},{10,... | collective-permute-start | bytes 393224 | tf_op jit(solution)/shard_map/ppermute | solution.py:377
  17.7 6.2 %collective-permute-start.3 = (f32[136,128]{1,0:T(8,128)S(1)}, f32[136,128]{1,0:T(8,128)S(1)}, u32[]{:S(2)}, u32[]{:S(2)}) collective-permute-start(f32[136,128]{1,0:T(8,128)S(1)} %add.6.refs_0_), channel_id=1, source_target_pairs={{0,16},{1,17},{2,18},{3,19},{4,20},{5,21},{6,22},{7,23},{8,24},{9,... | collective-permute-start | bytes 208904 | tf_op jit(solution)/shard_map/ppermute | solution.py:377
  23.5 5.0 %collective-permute-start.10 = (f32[32,1024]{1,0:T(8,128)S(1)}, f32[32,1024]{1,0:T(8,128)S(1)}, u32[]{:S(2)}, u32[]{:S(2)}) collective-permute-start(f32[32,1024]{1,0:T(8,128)S(1)} %sums.5.refs_2_.refs_0_), channel_id=1, source_target_pairs={{0,8},{1,9},{2,10},{3,11},{4,12},{5,13},{6,14},{7,15},{8,0},{9,1},... | collective-permute-start | bytes 393224 | tf_op jit(solution)/shard_map/ppermute | solution.py:377
  23.9 7.8 %collective-permute-start.9 = (f32[136,128]{1,0:T(8,128)S(1)}, f32[136,128]{1,0:T(8,128)S(1)}, u32[]{:S(2)}, u32[]{:S(2)}) collective-permute-start(f32[136,128]{1,0:T(8,128)S(1)} %add.8.refs_0_), channel_id=1, source_target_pairs={{0,5},{1,4},{2,7},{3,6},{4,1},{5,0},{6,3},{7,2},{8,13},{9,12},{10,... | collective-permute-start | bytes 208904 | tf_op jit(solution)/shard_map/ppermute | solution.py:377
  26.5 5.2 %collective-permute-start.8 = (f32[136,128]{1,0:T(8,128)S(1)}, f32[136,128]{1,0:T(8,128)S(1)}, u32[]{:S(2)}, u32[]{:S(2)}) collective-permute-start(f32[136,128]{1,0:T(8,128)S(1)} %add.8.refs_0_), channel_id=1, source_target_pairs={{0,4},{1,5},{2,6},{3,7},{4,0},{5,1},{6,2},{7,3},{8,12},{9,13},{10,... | collective-permute-start | bytes 208904 | tf_op jit(solution)/shard_map/ppermute | solution.py:377
  27.0 4.6 %collective-permute-start.7 = (f32[136,128]{1,0:T(8,128)S(1)}, f32[136,128]{1,0:T(8,128)S(1)}, u32[]{:S(2)}, u32[]{:S(2)}) collective-permute-start(f32[136,128]{1,0:T(8,128)S(1)} %add.8.refs_0_), channel_id=1, source_target_pairs={{0,1},{1,0},{2,3},{3,2},{4,5},{5,4},{6,7},{7,6},{8,9},{9,8},{10,11... | collective-permute-start | bytes 208904 | tf_op jit(solution)/shard_map/ppermute | solution.py:377
  28.5 7.4 %collective-permute-start.12 = (f32[32,1024]{1,0:T(8,128)S(1)}, f32[32,1024]{1,0:T(8,128)S(1)}, u32[]{:S(2)}, u32[]{:S(2)}) collective-permute-start(f32[32,1024]{1,0:T(8,128)S(1)} %sums.6.refs_4_.refs_0_), channel_id=1, source_target_pairs={{0,16},{1,17},{2,18},{3,19},{4,20},{5,21},{6,22},{7,23},{8,24},{9,... | collective-permute-start | bytes 393224 | tf_op jit(solution)/shard_map/ppermute | solution.py:377
  31.7 1.3 %collective-permute-start.11 = (f32[136,128]{1,0:T(8,128)S(1)}, f32[136,128]{1,0:T(8,128)S(1)}, u32[]{:S(2)}, u32[]{:S(2)}) collective-permute-start(f32[136,128]{1,0:T(8,128)S(1)} %add.9.refs_0_), channel_id=1, source_target_pairs={{0,2},{1,3},{2,0},{3,1},{4,6},{5,7},{6,4},{7,5},{8,10},{9,11},{10,... | collective-permute-start | bytes 208904 | tf_op jit(solution)/shard_map/ppermute | solution.py:377
  36.0 11.8 %collective-permute-start.16 = (f32[32,1024]{1,0:T(8,128)S(1)}, f32[32,1024]{1,0:T(8,128)S(1)}, u32[]{:S(2)}, u32[]{:S(2)}) collective-permute-start(f32[32,1024]{1,0:T(8,128)S(1)} %sums.7.refs_3_.refs_0_), channel_id=1, source_target_pairs={{0,2},{1,3},{2,0},{3,1},{4,6},{5,7},{6,4},{7,5},{8,10},{9,11},{10,... | collective-permute-start | bytes 393224 | tf_op jit(solution)/shard_map/ppermute | solution.py:377
  36.0 8.8 %collective-permute-start.15 = (f32[32,1024]{1,0:T(8,128)S(1)}, f32[32,1024]{1,0:T(8,128)S(1)}, u32[]{:S(2)}, u32[]{:S(2)}) collective-permute-start(f32[32,1024]{1,0:T(8,128)S(1)} %sums.7.refs_3_.refs_0_), channel_id=1, source_target_pairs={{0,5},{1,4},{2,7},{3,6},{4,1},{5,0},{6,3},{7,2},{8,13},{9,12},{10,... | collective-permute-start | bytes 393224 | tf_op jit(solution)/shard_map/ppermute | solution.py:377
  38.5 7.2 %collective-permute-start.14 = (f32[32,1024]{1,0:T(8,128)S(1)}, f32[32,1024]{1,0:T(8,128)S(1)}, u32[]{:S(2)}, u32[]{:S(2)}) collective-permute-start(f32[32,1024]{1,0:T(8,128)S(1)} %sums.7.refs_3_.refs_0_), channel_id=1, source_target_pairs={{0,4},{1,5},{2,6},{3,7},{4,0},{5,1},{6,2},{7,3},{8,12},{9,13},{10,... | collective-permute-start | bytes 393224 | tf_op jit(solution)/shard_map/ppermute | solution.py:377
  39.1 6.7 %collective-permute-start.13 = (f32[32,1024]{1,0:T(8,128)S(1)}, f32[32,1024]{1,0:T(8,128)S(1)}, u32[]{:S(2)}, u32[]{:S(2)}) collective-permute-start(f32[32,1024]{1,0:T(8,128)S(1)} %sums.7.refs_3_.refs_0_), channel_id=1, source_target_pairs={{0,1},{1,0},{2,3},{3,2},{4,5},{5,4},{6,7},{7,6},{8,9},{9,8},{10,11... | collective-permute-start | bytes 393224 | tf_op jit(solution)/shard_map/ppermute | solution.py:377
  44.8 2.9 %collective-permute-start.19 = (f32[32,1024]{1,0:T(8,128)S(1)}, f32[32,1024]{1,0:T(8,128)S(1)}, u32[]{:S(2)}, u32[]{:S(2)}) collective-permute-start(f32[32,1024]{1,0:T(8,128)S(1)} %collective-permute-done.15.refs_3_), channel_id=1, source_target_pairs={{0,2},{1,3},{2,0},{3,1},{4,6},{5,7},{6,4},{7,5},{8,10},{9,11},{10,... | collective-permute-start | bytes 393224 | tf_op jit(solution)/shard_map/ppermute | solution.py:377
  45.7 2.0 %collective-permute-start.18 = (f32[32,1024]{1,0:T(8,128)S(1)}, f32[32,1024]{1,0:T(8,128)S(1)}, u32[]{:S(2)}, u32[]{:S(2)}) collective-permute-start(f32[32,1024]{1,0:T(8,128)S(1)} %collective-permute-done.14.refs_2_), channel_id=1, source_target_pairs={{0,2},{1,3},{2,0},{3,1},{4,6},{5,7},{6,4},{7,5},{8,10},{9,11},{10,... | collective-permute-start | bytes 393224 | tf_op jit(solution)/shard_map/ppermute | solution.py:377
  45.8 2.0 %collective-permute-start.17 = (f32[32,1024]{1,0:T(8,128)S(1)}, f32[32,1024]{1,0:T(8,128)S(1)}, u32[]{:S(2)}, u32[]{:S(2)}) collective-permute-start(f32[32,1024]{1,0:T(8,128)S(1)} %collective-permute-done.13.refs_1_), channel_id=1, source_target_pairs={{0,2},{1,3},{2,0},{3,1},{4,6},{5,7},{6,4},{7,5},{8,10},{9,11},{10,... | collective-permute-start | bytes 393224 | tf_op jit(solution)/shard_map/ppermute | solution.py:377
